TPU v7x, 32 devices: a whole 2x2x4 slice. The times are simulated.
32 devices in a mesh: ctx: 4 (over x, core), tp: 8 (over z, y).
Axes of the slice: x: 2, y: 2, z: 4, core: 2. Of those that a mesh axis runs over, the one named last changes fastest.
Arguments:
- tokens: bfloat16 [512, 8192], P('ctx', 'tp'), may hold values from -6 to 6
- in_weight: bfloat16 [8192, 3, 8192], P(None, None, 'tp'), may hold values from -0.0625 to 0.0625
- filter_taps: float32 [3, 3, 8192], P(None, None, 'tp'), may hold values from -2.4 to 2.4
- decay_rate: float32 [16, 8192], P(None, 'tp'), may hold values from 0.000390625 to 0.08, as said below
- residue: float32 [16, 8192], P(None, 'tp'), may hold values from -80 to 80
Outputs:
- gated: bfloat16 [512, 8192], P('ctx', 'tp')
Inputs may be any that keep to these rules, and one draw needn't show every extreme that they name: `decay_rate`: every decay rate lies between 0.2 / 512 and 0.08.
All inputs are finite; a program needn't handle non-finite values.
Results may differ from a plain program's by a relative error of at most 0.015.
Values may be sent and summed in bfloat16 or wider, within the bound.
No kernel may reach another device: no remote copies, remote signals or barrier semaphores. Data moves between devices by JAX's collectives and lax.ppermute only.
A program may use at most 192 MiB of HBM per device.

v0:
```python
import jax
import jax.numpy as jnp
from jax import lax
from jax.sharding import PartitionSpec as P

BLOCK = 128


def passed_along(value, axis, steps):
    count = lax.axis_size(axis)
    first, last = (max(0, -steps), min(count, count - steps))
    return lax.ppermute(value, axis, [(source, source + steps) for source in range(first, last)])


def entering(value, axis, join, neutral):
    count, mine = (lax.axis_size(axis), lax.axis_index(axis))
    pieces = jax.tree.map(lambda part: lax.all_gather(part, axis), value)
    total = jax.tree.map(
        lambda part, zero: jnp.full_like(part, 0) + jnp.asarray(zero, part.dtype), value, neutral
    )

    def step(position, total):
        longer = join(total, jax.tree.map(lambda part: part[position], pieces))
        return jax.tree.map(lambda new, old: jnp.where(position < mine, new, old), longer, total)

    return lax.fori_loop(0, count - 1, step, total)


def project(row_block, in_weight):
    weight_flat = in_weight.reshape(in_weight.shape[0], -1)
    gathered = lax.all_gather(row_block, "tp", axis=1, tiled=True)
    summed = jnp.dot(gathered, weight_flat, preferred_element_type=jnp.float32)
    return summed.astype(jnp.bfloat16).reshape(row_block.shape[0], 3, -1)


def combine_modes(earlier, later):
    return (earlier[0] * later[0], later[0] * earlier[1] + later[1])


def on_device(tokens, in_weight, filter_taps, decay_rate, residue):
    row_count = tokens.shape[0]
    lead_rows = filter_taps.shape[0] - 1
    projected = project(tokens, in_weight)
    rim_rows = passed_along(projected[row_count - lead_rows :], "ctx", 1)
    padded = jnp.concatenate([rim_rows, projected], axis=0)
    features = jnp.zeros((row_count,) + padded.shape[1:], jnp.float32)
    for lag_index in range(lead_rows + 1):
        window = padded[lead_rows - lag_index : lead_rows - lag_index + row_count].astype(
            jnp.float32
        )
        features = features + filter_taps[lag_index] * window
    query_part = features[:, 0]
    source = features[:, 1] * features[:, 2]
    chan_count = source.shape[1]
    block_count = row_count // BLOCK
    coeffs = residue * jnp.sqrt(1.0 - jnp.exp(-2.0 * decay_rate))
    offsets = jnp.arange(BLOCK, dtype=jnp.float32)
    falling = jnp.exp(-decay_rate[None] * offsets[:, None, None])
    rising = jnp.exp(decay_rate[None] * offsets[:, None, None])
    toeplitz = jnp.einsum(
        "inc,jnc->ijc", falling * coeffs[None], rising, precision=lax.Precision.HIGHEST
    )
    lower_mask = (offsets[:, None] >= offsets[None, :])[:, :, None]
    toeplitz = jnp.where(lower_mask, toeplitz, 0.0)
    blocks = source.reshape(block_count, BLOCK, chan_count)
    inner_part = jnp.einsum("ijc,bjc->bic", toeplitz, blocks, precision=lax.Precision.HIGHEST)
    end_weights = falling[::-1]
    partial_states = jnp.einsum(
        "jnc,bjc->bnc", end_weights, blocks, precision=lax.Precision.HIGHEST
    )
    block_decay = jnp.exp(-decay_rate * BLOCK)

    def advance(carry_state, block_term):
        return (block_decay * carry_state + block_term, carry_state)

    local_end, local_starts = lax.scan(advance, jnp.zeros_like(block_decay), partial_states)
    device_decay = jnp.exp(-decay_rate * row_count)
    identity = (jnp.ones_like(local_end), jnp.zeros_like(local_end))
    prefix = entering((device_decay, local_end), "ctx", combine_modes, identity)
    incoming = prefix[1]
    start_offsets = jnp.arange(block_count, dtype=jnp.float32) * BLOCK
    start_states = (
        local_starts + jnp.exp(-decay_rate[None] * start_offsets[:, None, None]) * incoming[None]
    )
    read_weights = coeffs[None] * jnp.exp(-decay_rate[None] * (offsets + 1.0)[:, None, None])
    carried = jnp.einsum(
        "inc,bnc->bic", read_weights, start_states, precision=lax.Precision.HIGHEST
    )
    response = (inner_part + carried).reshape(row_count, chan_count)
    return (query_part * response).astype(jnp.bfloat16)


def solution(mesh):
    return jax.shard_map(
        on_device,
        mesh=mesh,
        in_specs=(
            P("ctx", "tp"),
            P(None, None, "tp"),
            P(None, None, "tp"),
            P(None, "tp"),
            P(None, "tp"),
        ),
        out_specs=P("ctx", "tp"),
        check_vma=False,
    )
```

profile of v0, /device:TPU:0, one launch (start us, length us, event | category | flops | bytes accessed | tf_op | source)
XLA Modules:
  0.0 356.9 jit_solution(2000796973372073112)
XLA Ops:
  6.5 0.7 all-gather.4.cloned.1.call-update
  7.3 62.2 %copy.13 = bf16[8192,3,1024]{0,2,1:T(8,128)(2,1)} copy(bf16[8192,3,1024]{2,0,1:T(8,128)(2,1)} %param.8) | data formatting | bytes 100663296 | tf_op args[1]
  69.5 0.2 copy.18
  69.8 6.0 %multiply_exponential_fusion = f32[128,16,1024]{0,1,2:T(8,128)} fusion(f32[16,1024]{0,1:T(8,128)S(1)} %copy.18), kind=kLoop, calls=%fused_computation.13 | loop fusion | flops 2097152 | bytes 8454144 | tf_op jit(solution)/shard_map/exp | solution.py:58
  75.8 22.7 %convolution_convert_fusion = bf16[128,3072]{1,0:T(8,128)(2,1)S(1)} fusion(bf16[128,8192]{1,0:T(8,128)(2,1)} %all-gather.4.cloned.1.call-done, bf16[8192,3072]{0,1:T(8,128)(2,1)} %bitcast.62), kind=kOutput, calls=%fused_computation.22 | convolution fusion | flops 6442844160 | bytes 53215232 | tf_op jit(solution)/shard_map/dot_general | solution.py:32
  98.5 2.4 collective-permute-start
  100.9 0.6 iota_add_fusion
  101.5 1.0 copy.17
  102.5 13.2 %rev.3 = f32[128,16,1024]{0,1,2:T(8,128)} reverse(f32[128,16,1024]{0,1,2:T(8,128)} %multiply_exponential_fusion), dimensions={0} | reverse | bytes 16777216 | tf_op jit(solution)/shard_map/rev | solution.py:67
  115.7 0.4 copy.14
  116.1 0.0 collective-permute-done
  116.1 1.3 copy.16
  117.4 3.7 %multiply_add_fusion = f32[128,3,1024]{0,2,1:T(8,128)S(1)} fusion(bf16[128,3,1024]{0,2,1:T(8,128)(2,1)S(1)} %bitcast.66, bf16[2,3,1024]{0,2,1:T(8,128)(2,1)} %copy.16, f32[3,1024]{1,0:T(4,128)S(1)} %get-tuple-element.148, f32[3,1024]{1,0:T(4,128)S(1)} %get-tuple-element.149, f32[3,1024]{1,0:T(4,128)S(1)} %get-tuple-element.147), kind=kLoop, calls=%fused_computation.25 | loop fusion | flops 5505024 | bytes 2408448 | tf_op jit(solution)/shard_map/add | solution.py:51
  121.1 0.1 slice_multiply_fusion
  121.2 16.0 %fusion.22 = f32[1024,1,16]{2,1,0:T(1,128)} fusion(f32[128,1024,1]{0,2,1:T(1,128)S(1)} %bitcast.63, f32[128,16,1024]{0,1,2:T(8,128)} %rev.3), kind=kOutput, calls=%fused_computation.42 | convolution fusion | flops 25165824 | bytes 8978432 | tf_op jit(solution)/shard_map/jnc,bjc->bnc/dot_general | solution.py:68
  137.2 1.1 copy.23
  138.4 10.2 %all-gather = f32[64,1024]{1,0:T(8,128)S(1)} all-gather(f32[16,1024]{1,0:T(8,128)S(1)} %get-tuple-element.146), channel_id=2, replica_groups=mesh['ctx'=4,'tp'=8] {'ctx'}, dimensions={0}, use_global_device_ids=true | all-gather | bytes 327680 | tf_op jit(solution)/shard_map/all_gather | solution.py:17
  148.5 6.3 %all-gather.1 = f32[64,1024]{1,0:T(8,128)} all-gather(f32[16,1024]{1,0:T(8,128)S(1)} %get-tuple-element.145), channel_id=3, replica_groups=mesh['ctx'=4,'tp'=8] {'ctx'}, dimensions={0}, use_global_device_ids=true | all-gather | bytes 327680 | tf_op jit(solution)/shard_map/all_gather | solution.py:17
  154.8 2.7 while.9
  154.8 0.9 fusion.37
  155.7 0.9 fusion.37
  156.6 0.9 fusion.37
  157.5 0.9 multiply_bitcast_fusion
  158.4 1.0 copy.19
  159.4 1.0 copy.24
  160.4 116.7 %fusion.8 = f32[1024,128,128]{2,1,0:T(8,128)} fusion(f32[16,1024]{0,1:T(8,128)} %copy.19, f32[16,1024]{0,1:T(8,128)S(1)} %copy-done, f32[16,1024]{0,1:T(8,128)S(1)} %copy.18), kind=kOutput, calls=%fused_computation.11 | convolution fusion | flops 3227516928 | bytes 67305472 | tf_op jit(solution)/shard_map/inc,jnc->ijc/dot_general | solution.py:60
  277.1 0.0 copy-start.5
  277.1 60.6 %fusion.1 = f32[1024,1,128]{2,1,0:T(1,128)S(1)} fusion(f32[128,1024,1]{0,2,1:T(1,128)S(1)} %bitcast.64, f32[1024,128,128]{2,1,0:T(8,128)} %fusion.8, pred[128,128]{0,1:T(8,128)(4,1)S(1)} %iota_compare_fusion), kind=kOutput, calls=%fused_computation.4 | convolution fusion | flops 218103808 | bytes 68173824 | tf_op jit(solution)/shard_map/ijc,bjc->bic/dot_general | solution.py:66
  337.7 0.0 copy-done.1
  337.7 11.3 %fusion.4 = f32[1024,1,128]{2,1,0:T(1,128)S(1)} fusion(f32[16,1024,1]{0,2,1:T(1,128)S(1)} %copy-done.3, f32[128]{0:T(128)S(1)} %copy-done.5, f32[16,1024]{0,1:T(8,128)S(1)} %copy-done.1, f32[16,1024]{0,1:T(8,128)S(1)} %copy.18), kind=kOutput, calls=%fused_computation.7 | convolution fusion | flops 29360128 | bytes 721408 | tf_op jit(solution)/shard_map/inc,bnc->bic/dot_general | solution.py:86
  349.1 0.1 fusion.20
  349.2 0.9 copy.20
  (18 shorter events, 0.1 us)
Async XLA Ops:
  6.5 69.3 %all-gather.4.cloned.1.call-start = ((), (), s32[]{:S(2)}) async-start(), calls=%async_computation | async-start | bytes 2359296 | tf_op jit(solution)/shard_map/all_gather | solution.py:31
  7.3 62.3 %copy-start.2 = (f32[16,1024]{1,0:T(8,128)S(1)}, f32[16,1024]{1,0:T(8,128)}, u32[]{:S(2)}) copy-start(f32[16,1024]{1,0:T(8,128)} %param.10) | copy-start | bytes 196612
  7.3 62.5 %copy-start.4 = (f32[3,3,1024]{2,1,0:T(4,128)S(1)}, f32[3,3,1024]{2,1,0:T(4,128)}, u32[]{:S(2)}) copy-start(f32[3,3,1024]{2,1,0:T(4,128)} %param.9) | copy-start | bytes 110596
  98.5 17.5 %collective-permute-start = (bf16[2,3,1024]{2,0,1:T(2,128)(2,1)S(1)}, bf16[2,3,1024]{2,0,1:T(2,128)(2,1)S(1)}, u32[]{:S(2)}, u32[]{:S(2)}) collective-permute-start(bf16[2,3,1024]{2,0,1:T(2,128)(2,1)S(1)} %bitcast.70), channel_id=1, source_target_pairs={{0,8},{8,16},{16,24},{1,9},{9,17},{17,25},{2,10},{10,18},{18,26},{... | collective-permute-start | bytes 36872 | tf_op jit(solution)/shard_map/ppermute | solution.py:12
  121.1 39.3 %copy-start = (f32[16,1024]{0,1:T(8,128)S(1)}, f32[16,1024]{0,1:T(8,128)}, u32[]{:S(2)}) copy-start(f32[16,1024]{0,1:T(8,128)} %copy.17) | copy-start | bytes 196612
  277.1 60.6 %copy-start.1 = (f32[16,1024]{0,1:T(8,128)S(1)}, f32[16,1024]{0,1:T(8,128)}, u32[]{:S(2)}) copy-start(f32[16,1024]{0,1:T(8,128)} %copy.19) | copy-start | bytes 196612
  277.1 60.6 %copy-start.3 = (f32[16,1024,1]{0,2,1:T(1,128)S(1)}, f32[16,1024,1]{0,2,1:T(1,128)}, u32[]{:S(2)}) copy-start(f32[16,1024,1]{0,2,1:T(1,128)} %copy.24) | copy-start | bytes 196612
  277.1 60.6 %copy-start.5 = (f32[128]{0:T(128)S(1)}, f32[128]{0:T(128)}, u32[]{:S(2)}) copy-start(f32[128]{0:T(128)} %iota_add_fusion) | copy-start | bytes 1540
Sparse Core Ops, SparseCore 0:
  9.5 51.9 all-gather.3
where the time goes:
time: 359 us; the launch traced here: 357 us
  matrix products  227 us (63%)
  local copies, waits for them, and re-layouts  82.3 us (23%)
  blocking collectives  16.5 us (5%)
  other arithmetic  14.1 us (4%)
  between operations  13.6 us (4%)
    dot_general x1, matrix products, on_device(): jnp.einsum('inc,jnc->ijc', falling * coeffs[None], rising, precision=lax....  117 us
    unnamed x14, local copies, waits for them, and re-layouts  63.3 us
    dot_general x1, matrix products, on_device(): jnp.einsum('ijc,bjc->bic', toeplitz, blocks, precision=lax.Precision.HIGH...  60.6 us
    dot_general x1, matrix products, project(): summed = jnp.dot(gathered, weight_flat, preferred_element_type=jnp.float32)  22.7 us
    all_gather x2, blocking collectives, entering(): pieces = jax.tree.map(lambda part: lax.all_gather(part, axis), value)  16.5 us
    dot_general x1, matrix products, on_device(): jnp.einsum('jnc,bjc->bnc', end_weights, blocks, precision=lax.Precision.H...  16 us
    rev x1, local copies, waits for them, and re-layouts, on_device(): end_weights = falling[::-1]  13.2 us
    dot_general x1, matrix products, on_device(): jnp.einsum('inc,bnc->bic', read_weights, start_states, precision=lax.Prec...  11.3 us
  transfers between devices with their start and end apart: 2, of which 0 were waited for; matrix products, arithmetic and copies ran while one was open for 23% of the time, Pallas kernels for 0%

commit v1 on v0

v1 whole, which is shorter than its diff:
```python
import functools

import jax
import jax.numpy as jnp
from jax import lax
from jax.experimental import pallas as pl
from jax.experimental.pallas import tpu as pltpu
from jax.sharding import PartitionSpec as P

LANES = 128
DEPTH = 256
SLOTS = 6
GRID_ROWS = 4
VMEM = pl.BlockSpec(memory_space=pltpu.VMEM)
ANY = pl.BlockSpec(memory_space=pl.ANY)


def ring_order(count):
    if count % (2 * GRID_ROWS):
        return list(range(count))
    cols = count // GRID_ROWS
    cells = [(0, c) for c in range(cols)]
    for r in range(1, GRID_ROWS):
        inner = list(range(1, cols))
        cells += [(r, c) for c in (reversed(inner) if r % 2 else inner)]
    cells += [(r, 0) for r in range(GRID_ROWS - 1, 0, -1)]
    return [r * cols + c for r, c in cells]


def owner_at(order, step):
    me = lax.axis_index("tp")
    owner = jnp.int32(0)
    for place, index in enumerate(order):
        owner = jnp.where(me == index, order[(place - step) % len(order)], owner)
    return owner


def accumulate(order, steps, xs, w_ref, total, buf, sem, fresh):
    width = xs[0][0].shape[1]
    depth = min(DEPTH, width)
    jobs = [(b, k) for b in range(len(xs)) for k in range(width // depth)]
    owners = [owner_at(order, step) for step in steps]

    def copy(i):
        b, k = jobs[i]
        start = pl.multiple_of(owners[b] * width + k * depth, depth)
        slot = i % SLOTS
        return pltpu.make_async_copy(
            w_ref.at[:, pl.ds(start, depth), :], buf.at[slot], sem.at[slot]
        )

    for i in range(min(SLOTS, len(jobs))):
        copy(i).start()
    for i, (b, k) in enumerate(jobs):
        copy(i).wait()
        row = 0
        for part in xs[b]:
            rows = part.shape[0]
            x = part[:, k * depth : (k + 1) * depth]
            for s in range(total.shape[0]):
                term = jnp.dot(x, buf[i % SLOTS, s], preferred_element_type=jnp.float32)
                if fresh and i == 0:
                    total[s, row : row + rows] = term
                else:
                    total[s, row : row + rows] += term
            row += rows
        if i + SLOTS < len(jobs):
            copy(i + SLOTS).start()


def first_kernel(order, x_ref, w_ref, total, buf, sem):
    accumulate(order, [0], [[x_ref]], w_ref, total, buf, sem, True)


def middle_kernel(order, steps, count, *refs):
    xs = [[ref] for ref in refs[:count]]
    w_ref, _, total, buf, sem = refs[count:]
    accumulate(order, steps, xs, w_ref, total, buf, sem, False)


def last_kernel(order, step, xa_ref, xb_ref, w_ref, taps, decay, _, total, p_ref, out_ref, buf, sem):
    accumulate(order, [step], [[xa_ref, xb_ref]], w_ref, total, buf, sem, False)
    streams, rows, groups, lanes = p_ref.shape
    modes = decay.shape[0]
    for s in range(streams):
        value = total[s].astype(jnp.bfloat16).astype(jnp.float32)
        for g in range(groups):
            p_ref[s, :, g, :] = value[:, g * lanes : (g + 1) * lanes]
    rate = [decay[n] for n in range(modes)]

    def step_row(t, state):
        u = filtered(taps, p_ref, 1, t) * filtered(taps, p_ref, 2, t)
        return [r * s + u for r, s in zip(rate, state)]

    state = [jnp.zeros((groups, lanes), jnp.float32)] * modes
    for t in range(2, 8):
        state = step_row(t, state)

    def eight(i, state):
        for j in range(8):
            state = step_row(i * 8 + j, state)
        return state

    state = lax.fori_loop(1, rows // 8, eight, state)
    for n in range(modes):
        out_ref[n] = state[n]
    for s in (1, 2):
        for j, t in enumerate((0, 1)):
            out_ref[modes + (s - 1) * 2 + j] = p_ref[s, t]
    for s in range(streams):
        for j, t in enumerate((rows - 2, rows - 1)):
            out_ref[modes + 4 + s * 2 + j] = p_ref[s, t]


def filtered(taps, p_ref, s, t):
    return taps[0, s] * p_ref[s, t] + taps[1, s] * p_ref[s, t - 1] + taps[2, s] * p_ref[s, t - 2]


def edge(taps, s, first, second, before, last):
    return (
        taps[0, s] * first + taps[1, s] * last + taps[2, s] * before,
        taps[0, s] * second + taps[1, s] * first + taps[2, s] * last,
    )


def final_kernel(count, *refs):
    sent = refs[:count]
    p_ref, taps, table, out_ref, work = refs[count:]
    streams, rows, groups, lanes = p_ref.shape
    modes = table.shape[1]
    zero = jnp.zeros((groups, lanes), jnp.float32)

    def rim(d, s):
        if d >= count:
            return zero, zero
        return sent[d][modes + 4 + s * 2], sent[d][modes + 4 + s * 2 + 1]

    state = [zero] * modes
    for d in reversed(range(count)):
        ends = []
        for s in (1, 2):
            first, second = sent[d][modes + (s - 1) * 2], sent[d][modes + (s - 1) * 2 + 1]
            ends.append(edge(taps, s, first, second, *rim(d + 1, s)))
        u0, u1 = ends[0][0] * ends[1][0], ends[0][1] * ends[1][1]
        state = [
            table[1, n] * state[n] + (sent[d][n] + table[2, n] * u0 + table[3, n] * u1)
            for n in range(modes)
        ]

    def advance(t, q, u, state):
        state = [table[0, n] * state[n] + u for n in range(modes)]
        terms = [table[4, n] * state[n] for n in range(modes)]
        while len(terms) > 1:
            terms = [a + b for a, b in zip(terms[::2], terms[1::2])] + terms[len(terms) & ~1 :]
        work[t] = q * terms[0]
        return state

    edges = [edge(taps, s, p_ref[s, 0], p_ref[s, 1], *rim(0, s)) for s in range(streams)]
    for t in range(2):
        state = advance(t, edges[0][t], edges[1][t] * edges[2][t], state)

    def row(t, state):
        q, f1, f2 = [filtered(taps, p_ref, s, t) for s in range(3)]
        return advance(t, q, f1 * f2, state)

    for t in range(2, 8):
        state = row(t, state)

    def eight(i, state):
        for j in range(8):
            state = row(i * 8 + j, state)
        return state

    lax.fori_loop(1, rows // 8, eight, state)
    for g in range(groups):
        out_ref[:, g * lanes : (g + 1) * lanes] = work[:, g, :].astype(out_ref.dtype)


def on_device(tokens, in_weight, filter_taps, decay_rate, residue):
    rows, width = tokens.shape
    streams, chans = in_weight.shape[1:]
    modes = decay_rate.shape[0]
    groups = chans // LANES
    tp, ctx = lax.axis_size("tp"), lax.axis_size("ctx")
    order = ring_order(tp)
    weight = jnp.transpose(in_weight, (1, 0, 2))
    half = tp // 2
    ahead = [(order[i], order[(i + 1) % tp]) for i in range(tp)]
    back = [(b, a) for a, b in ahead]

    taps = filter_taps.reshape(filter_taps.shape[0], streams, groups, LANES)
    coeffs = residue * jnp.sqrt(1.0 - jnp.exp(-2.0 * decay_rate))
    table = jnp.stack(
        [jnp.exp(-decay_rate * k) for k in (1, rows, rows - 1, rows - 2)] + [coeffs]
    ).reshape(5, modes, groups, LANES)

    depth = min(DEPTH, width)
    stream_scratch = [
        pltpu.VMEM((SLOTS, streams, depth, chans), jnp.bfloat16),
        pltpu.SemaphoreType.DMA((SLOTS,)),
    ]
    sums = jax.ShapeDtypeStruct((streams, rows, chans), jnp.float32)
    params = pltpu.CompilerParams(vmem_limit_bytes=24 << 20)

    def cost(blocks):
        work = blocks * width * streams * chans
        return pl.CostEstimate(flops=2 * rows * work, bytes_accessed=2 * work, transcendentals=0)

    fore, aft = tokens, tokens
    total = pl.pallas_call(
        functools.partial(first_kernel, order),
        out_shape=sums,
        in_specs=[VMEM, ANY],
        out_specs=VMEM,
        scratch_shapes=stream_scratch,
        compiler_params=params,
        cost_estimate=cost(1),
        name="project_own",
    )(tokens, weight)
    for step in range(1, half):
        fore = lax.ppermute(fore, "tp", ahead)
        aft = lax.ppermute(aft, "tp", back)
        total = pl.pallas_call(
            functools.partial(middle_kernel, order, [step, -step], 2),
            out_shape=sums,
            in_specs=[VMEM, VMEM, ANY, VMEM],
            out_specs=VMEM,
            scratch_shapes=stream_scratch,
            input_output_aliases={3: 0},
            compiler_params=params,
            cost_estimate=cost(2),
            name="project_pair",
        )(fore, aft, weight, total)
    fore = lax.ppermute(fore[: rows // 2], "tp", ahead)
    aft = lax.ppermute(aft[rows // 2 :], "tp", back)
    _, projected, local = pl.pallas_call(
        functools.partial(last_kernel, order, half),
        out_shape=[
            sums,
            jax.ShapeDtypeStruct((streams, rows, groups, LANES), jnp.float32),
            jax.ShapeDtypeStruct((modes + 10, groups, LANES), jnp.float32),
        ],
        in_specs=[VMEM, VMEM, ANY, VMEM, VMEM, VMEM],
        out_specs=[VMEM, VMEM, VMEM],
        scratch_shapes=stream_scratch,
        input_output_aliases={5: 0},
        compiler_params=params,
        cost_estimate=cost(1),
        name="project_last",
    )(fore, aft, weight, taps, table[0], total)

    sent = [
        lax.ppermute(local, "ctx", [(j, j + d) for j in range(ctx - d)]) for d in range(1, ctx)
    ]
    return pl.pallas_call(
        functools.partial(final_kernel, len(sent)),
        out_shape=jax.ShapeDtypeStruct((rows, chans), jnp.bfloat16),
        in_specs=[VMEM] * (len(sent) + 3),
        out_specs=VMEM,
        scratch_shapes=[pltpu.VMEM((rows, groups, LANES), jnp.float32)],
        compiler_params=params,
        name="long_filter",
    )(*sent, projected, taps, table)


def solution(mesh):
    return jax.shard_map(
        on_device,
        mesh=mesh,
        in_specs=(
            P("ctx", "tp"),
            P(None, None, "tp"),
            P(None, None, "tp"),
            P(None, "tp"),
            P(None, "tp"),
        ),
        out_specs=P("ctx", "tp"),
        check_vma=False,
    )
```

time: 359 us -> 53.9 us (0.15)
  matrix products: 227 us -> 0 us
  local copies, waits for them, and re-layouts: 82.3 us -> 1.1 us
  Pallas kernels: 0 us -> 27.5 us
  blocking collectives: 16.5 us -> 0 us
  between operations: 13.6 us -> 0.22 us
  other arithmetic: 14.1 us -> 0.94 us
  starting transfers between devices: 2.4 us -> 15 us
  waiting for transfers between devices: 0.71 us -> 8.85 us
    dot_general x5 -> x0, matrix products: 227 us -> none  [the longest x1 117 us: on_device(): jnp.einsum('inc,jnc->ijc', falling * coeffs[None], rising, precision=lax....]
    unnamed x14 -> x13, local copies, waits for them, and re-layouts: 63.3 us -> 1.06 us
    pallas_call x0 -> x6, Pallas kernels: none -> 27.5 us  [the longest x3 15.9 us: on_device(): pl.pallas_call(functools.partial(middle_kernel, order, [step, -step], 2),...]
    all_gather x2 -> x0, blocking collectives: 16.5 us -> none  [entering(): pieces = jax.tree.map(lambda part: lax.all_gather(part, axis), value)]
    rev x1 -> x0, local copies, waits for them, and re-layouts: 13.2 us -> none  [on_device(): end_weights = falling[::-1]]
    ppermute x1 -> x11, starting transfers between devices: 2.4 us -> 15 us  [the longest x3 6.02 us: on_device(): fore = lax.ppermute(fore, 'tp', ahead)]
    ppermute x1 -> x11, waiting for transfers between devices: 0.01 us -> 8.85 us  [the longest x3 6.6 us: on_device(): fore = lax.ppermute(fore, 'tp', ahead)]
    exp x1 -> x0, other arithmetic: 6.01 us -> none  [on_device(): falling = jnp.exp(-decay_rate[None] * offsets[:, None, None])]
  transfers between devices with their start and end apart: 2 -> 11, of which waited for: 0 -> 3; matrix products, arithmetic and copies ran while one was open for 23% -> 2% of each run, Pallas kernels for 0% -> 36%
where the time goes in v1:
time: 53.9 us; the launch traced here: 53.6 us
  Pallas kernels  27.5 us (51%)
  starting transfers between devices  15 us (28%)
  waiting for transfers between devices  8.85 us (16%)
  local copies, waits for them, and re-layouts  1.1 us (2%)
  other arithmetic  0.94 us (2%)
    pallas_call x3, Pallas kernels, on_device(): pl.pallas_call(functools.partial(middle_kernel, order, [step, -step], 2),...  15.9 us
    ppermute x3, waiting for transfers between devices, on_device(): fore = lax.ppermute(fore, 'tp', ahead)  6.6 us
    ppermute x3, starting transfers between devices, on_device(): fore = lax.ppermute(fore, 'tp', ahead)  6.02 us
    ppermute x3, starting transfers between devices, on_device(): lax.ppermute(local, 'ctx', [(j, j + d) for j in range(ctx - d)])  5.84 us
    pallas_call x1, Pallas kernels, on_device(): pl.pallas_call(functools.partial(last_kernel, order, half), out_shape=[su...  5.34 us
    pallas_call x1, Pallas kernels, on_device(): pl.pallas_call(functools.partial(first_kernel, order), out_shape=sums, in...  3.26 us
    pallas_call x1, Pallas kernels, on_device(): pl.pallas_call(functools.partial(final_kernel, len(sent)), out_shape=jax....  3.01 us
    ppermute x3, waiting for transfers between devices, on_device(): lax.ppermute(local, 'ctx', [(j, j + d) for j in range(ctx - d)])  2.24 us
  transfers between devices with their start and end apart: 11, of which 3 were waited for; matrix products, arithmetic and copies ran while one was open for 2% of the time, Pallas kernels for 36%

profile of v1, /device:TPU:0, one launch (start us, length us, event | category | flops | bytes accessed | tf_op | source)
XLA Modules:
  0.0 53.6 jit_solution(16248865476994212954)
XLA Ops:
  0.0 3.0 %collective-permute-start = (bf16[128,1024]{1,0:T(8,128)(2,1)}, bf16[128,1024]{1,0:T(8,128)(2,1)S(1)}, u32[]{:S(2)}, u32[]{:S(2)}) collective-permute-start(bf16[128,1024]{1,0:T(8,128)(2,1)} %x_ref.1), channel_id=1, source_target_pairs={{0,1},{1,3},{3,5},{5,7},{7,6},{6,4},{4,2},{2,0},{8,9},{9,11},{11,1... | collective-permute-start | bytes 786440 | tf_op jit(solution)/shard_map/ppermute | solution.py:221
  3.0 0.1 collective-permute-start.4
  3.0 0.9 %multiply_bitcast_fusion = (f32[2,8,8,128]{3,1,2,0:T(8,128)S(1)}, f32[2,8,8,128]{3,1,2,0:T(8,128)S(1)}, f32[2,8,8,128]{3,1,2,0:T(8,128)S(1)}, f32[2,8,8,128]{3,1,2,0:T(8,128)S(1)}, f32[2,8,8,128]{3,1,2,0:T(8,128)S(1)}) fusion(f32[16,1024]{1,0:T(8,128)} %param.9, f32[16,1024]{1,0:T(8,128)} %param.8), kind=kLoop, calls=%fused_computation.5 | loop fusion | flops 114688 | bytes 458752
  4.0 5.5 %collective-permute-done.refs_0_ = bf16[128,1024]{1,0:T(8,128)(2,1)S(1)} collective-permute-done((bf16[128,1024]{1,0:T(8,128)(2,1)}, bf16[128,1024]{1,0:T(8,128)(2,1)S(1)}, u32[]{:S(2)}, u32[]{:S(2)}) %collective-permute-start) | collective-permute-done | bytes 262176 | tf_op jit(solution)/shard_map/ppermute | solution.py:221
  9.5 1.7 %collective-permute-start.1 = (bf16[128,1024]{1,0:T(8,128)(2,1)S(1)}, bf16[128,1024]{1,0:T(8,128)(2,1)S(1)}, u32[]{:S(2)}, u32[]{:S(2)}) collective-permute-start(bf16[128,1024]{1,0:T(8,128)(2,1)S(1)} %collective-permute-done.refs_0_), channel_id=1, source_target_pairs={{0,1},{1,3},{3,5},{5,7},{7,6},{6,4},{4,2},{2,0},{8,9},{9,11},{11,1... | collective-permute-start | bytes 786440 | tf_op jit(solution)/shard_map/ppermute | solution.py:221
  11.2 0.0 collective-permute-done.4.refs_1_
  11.2 0.3 collective-permute-start.5
  11.6 0.0 copy-start
  11.6 0.9 %copy-done = bf16[128,1024]{1,0:T(8,128)(2,1)S(1)} copy-done((bf16[128,1024]{1,0:T(8,128)(2,1)S(1)}, bf16[128,1024]{1,0:T(8,128)(2,1)}, u32[]{:S(2)}) %copy-start) | copy-done | bytes 262168
  12.5 3.3 %project_own.1.refs_3_ = f32[3,128,1024]{2,1,0:T(8,128)S(1)} custom-call(bf16[128,1024]{1,0:T(8,128)(2,1)S(1)} %copy-done, bf16[3,8192,1024]{2,1,0:T(8,128)(2,1)} %bitcast.35), custom_call_target="tpu_custom_call" | custom-call | flops 805306368 | bytes 6291456 | tf_op jit(solution)/shard_map/project_own/pallas_call | solution.py:210
  15.8 0.0 copy-done.1
  15.9 1.1 %collective-permute-done.1.refs_0_ = bf16[128,1024]{1,0:T(8,128)(2,1)S(1)} collective-permute-done((bf16[128,1024]{1,0:T(8,128)(2,1)S(1)}, bf16[128,1024]{1,0:T(8,128)(2,1)S(1)}, u32[]{:S(2)}, u32[]{:S(2)}) %collective-permute-start.1) | collective-permute-done | bytes 262176 | tf_op jit(solution)/shard_map/ppermute | solution.py:221
  17.0 1.4 %collective-permute-start.2 = (bf16[128,1024]{1,0:T(8,128)(2,1)S(1)}, bf16[128,1024]{1,0:T(8,128)(2,1)S(1)}, u32[]{:S(2)}, u32[]{:S(2)}) collective-permute-start(bf16[128,1024]{1,0:T(8,128)(2,1)S(1)} %collective-permute-done.1.refs_0_), channel_id=1, source_target_pairs={{0,1},{1,3},{3,5},{5,7},{7,6},{6,4},{4,2},{2,0},{8,9},{9,11},{11,1... | collective-permute-start | bytes 786440 | tf_op jit(solution)/shard_map/ppermute | solution.py:221
  18.4 0.0 collective-permute-done.5.refs_1_
  18.4 0.7 %collective-permute-start.6 = (bf16[128,1024]{1,0:T(8,128)(2,1)S(1)}, bf16[128,1024]{1,0:T(8,128)(2,1)S(1)}, u32[]{:S(2)}, u32[]{:S(2)}) collective-permute-start(bf16[128,1024]{1,0:T(8,128)(2,1)S(1)} %collective-permute-done.5.refs_1_), channel_id=1, source_target_pairs={{1,0},{3,1},{5,3},{7,5},{6,7},{4,6},{2,4},{0,2},{9,8},{11,9},{13,1... | collective-permute-start | bytes 786440 | tf_op jit(solution)/shard_map/ppermute | solution.py:222
  19.1 5.3 %project_pair.3.refs_3_ = f32[3,128,1024]{2,1,0:T(8,128)S(1)} custom-call(bf16[128,1024]{1,0:T(8,128)(2,1)S(1)} %collective-permute-done.refs_0_, bf16[128,1024]{1,0:T(8,128)(2,1)S(1)} %collective-permute-done.4.refs_1_, bf16[3,8192,1024]{2,1,0:T(8,128)(2,1)} %bitcast.36, f32[3,128,1024]{2,1,0:T(8,128)S(1)} %project_own.1.refs_3_), custom_call_target="tpu_custom_call", output_to_operand_aliasing={{}: (3, {})} | custom-call | flops 1610612736 | bytes 12582912 | tf_op jit(solution)/shard_map/project_pair/pallas_call | solution.py:223
  24.4 5.3 %project_pair.4.refs_3_ = f32[3,128,1024]{2,1,0:T(8,128)S(1)} custom-call(bf16[128,1024]{1,0:T(8,128)(2,1)S(1)} %collective-permute-done.1.refs_0_, bf16[128,1024]{1,0:T(8,128)(2,1)S(1)} %collective-permute-done.5.refs_1_, bf16[3,8192,1024]{2,1,0:T(8,128)(2,1)} %bitcast.37, f32[3,128,1024]{2,1,0:T(8,128)S(1)} %project_pair.3.refs_3_), custom_call_target="tpu_custom_call", output_to_operand_aliasing={{}: (3, {})} | custom-call | flops 1610612736 | bytes 12582912 | tf_op jit(solution)/shard_map/project_pair/pallas_call | solution.py:223
  29.7 0.0 collective-permute-done.2.refs_0_
  29.7 1.4 %collective-permute-start.3 = (bf16[64,1024]{1,0:T(8,128)(2,1)S(1)}, bf16[64,1024]{1,0:T(8,128)(2,1)S(1)}, u32[]{:S(2)}, u32[]{:S(2)}) collective-permute-start(bf16[64,1024]{1,0:T(8,128)(2,1)S(1)} %slice.10), channel_id=1, source_target_pairs={{0,1},{1,3},{3,5},{5,7},{7,6},{6,4},{4,2},{2,0},{8,9},{9,11},{11,1... | collective-permute-start | bytes 393224 | tf_op jit(solution)/shard_map/ppermute | solution.py:234
  31.1 0.0 collective-permute-done.6.refs_1_
  31.1 0.7 %collective-permute-start.7 = (bf16[64,1024]{1,0:T(8,128)(2,1)S(1)}, bf16[64,1024]{1,0:T(8,128)(2,1)S(1)}, u32[]{:S(2)}, u32[]{:S(2)}) collective-permute-start(bf16[64,1024]{1,0:T(8,128)(2,1)S(1)} %slice.11), channel_id=1, source_target_pairs={{1,0},{3,1},{5,3},{7,5},{6,7},{4,6},{2,4},{0,2},{9,8},{11,9},{13,1... | collective-permute-start | bytes 393224 | tf_op jit(solution)/shard_map/ppermute | solution.py:235
  31.8 5.3 %project_pair.5._ = f32[3,128,1024]{2,1,0:T(8,128)S(1)} custom-call(bf16[128,1024]{1,0:T(8,128)(2,1)S(1)} %collective-permute-done.2.refs_0_, bf16[128,1024]{1,0:T(8,128)(2,1)S(1)} %collective-permute-done.6.refs_1_, bf16[3,8192,1024]{2,1,0:T(8,128)(2,1)} %bitcast.38, f32[3,128,1024]{2,1,0:T(8,128)S(1)} %project_pair.4.refs_3_), custom_call_target="tpu_custom_call", output_to_operand_aliasing={{}: (3, {})} | custom-call | flops 1610612736 | bytes 12582912 | tf_op jit(solution)/shard_map/project_pair/pallas_call | solution.py:223
  37.1 0.0 collective-permute-done.3.xa_ref
  37.1 0.0 collective-permute-done.7.xb_ref
  37.1 5.3 %project_last.1 = (f32[3,128,1024]{2,1,0:T(8,128)S(1)}, f32[3,128,8,128]{3,2,1,0:T(8,128)S(1)}, f32[26,8,128]{2,1,0:T(8,128)S(1)}) custom-call(bf16[64,1024]{1,0:T(8,128)(2,1)S(1)} %collective-permute-done.3.xa_ref, bf16[64,1024]{1,0:T(8,128)(2,1)S(1)} %collective-permute-done.7.xb_ref, ...), custom_call_target="tpu_custom_call", output_to_operand_aliasing={{0}: (5, {})} | custom-call | flops 805306368 | bytes 6291456 | tf_op jit(solution)/shard_map/project_last/pallas_call | solution.py:236
  42.5 1.3 %collective-permute-start.10 = (f32[26,8,128]{2,1,0:T(8,128)S(1)}, f32[26,8,128]{2,1,0:T(8,128)S(1)}, u32[]{:S(2)}, u32[]{:S(2)}) collective-permute-start(f32[26,8,128]{2,1,0:T(8,128)S(1)} %get-tuple-element.7), channel_id=1, source_target_pairs={{0,24},{1,25},{2,26},{3,27},{4,28},{5,29},{6,30},{7,31}} | collective-permute-start | bytes 319496 | tf_op jit(solution)/shard_map/ppermute | solution.py:253
  43.8 1.3 %collective-permute-start.8 = (f32[26,8,128]{2,1,0:T(8,128)S(1)}, f32[26,8,128]{2,1,0:T(8,128)S(1)}, u32[]{:S(2)}, u32[]{:S(2)}) collective-permute-start(f32[26,8,128]{2,1,0:T(8,128)S(1)} %get-tuple-element.7), channel_id=1, source_target_pairs={{0,8},{8,16},{16,24},{1,9},{9,17},{17,25},{2,10},{10,18},{18,26},{... | collective-permute-start | bytes 319496 | tf_op jit(solution)/shard_map/ppermute | solution.py:253
  45.1 3.2 %collective-permute-start.9 = (f32[26,8,128]{2,1,0:T(8,128)S(1)}, f32[26,8,128]{2,1,0:T(8,128)S(1)}, u32[]{:S(2)}, u32[]{:S(2)}) collective-permute-start(f32[26,8,128]{2,1,0:T(8,128)S(1)} %get-tuple-element.7), channel_id=1, source_target_pairs={{0,16},{8,24},{1,17},{9,25},{2,18},{10,26},{3,19},{11,27},{4,20},{... | collective-permute-start | bytes 319496 | tf_op jit(solution)/shard_map/ppermute | solution.py:253
  48.4 0.0 collective-permute-done.10.refs_2_
  48.4 0.0 collective-permute-done.8.refs_0_
  48.4 2.2 %collective-permute-done.9.refs_1_ = f32[26,8,128]{2,1,0:T(8,128)S(1)} collective-permute-done((f32[26,8,128]{2,1,0:T(8,128)S(1)}, f32[26,8,128]{2,1,0:T(8,128)S(1)}, u32[]{:S(2)}, u32[]{:S(2)}) %collective-permute-start.9) | collective-permute-done | bytes 106528 | tf_op jit(solution)/shard_map/ppermute | solution.py:253
  50.6 3.0 %long_filter.1 = bf16[128,1024]{1,0:T(8,128)(2,1)} custom-call(f32[26,8,128]{2,1,0:T(8,128)S(1)} %collective-permute-done.8.refs_0_, f32[26,8,128]{2,1,0:T(8,128)S(1)} %collective-permute-done.9.refs_1_, f32[26,8,128]{2,1,0:T(8,128)S(1)} %collective-permute-done.10.refs_2_, f32[3,128,8,128]{3,2,1,0:T(8,128)S(1)} %get-tuple-element.8.refs_3_, ...), custom_call_target="tpu_custom_call" | custom-call | tf_op jit(solution)/shard_map/long_filter/pallas_call | solution.py:255
  (14 shorter events, 0.2 us)
Async XLA Ops:
  0.0 9.5 %collective-permute-start = (bf16[128,1024]{1,0:T(8,128)(2,1)}, bf16[128,1024]{1,0:T(8,128)(2,1)S(1)}, u32[]{:S(2)}, u32[]{:S(2)}) collective-permute-start(bf16[128,1024]{1,0:T(8,128)(2,1)} %x_ref.1), channel_id=1, source_target_pairs={{0,1},{1,3},{3,5},{5,7},{7,6},{6,4},{4,2},{2,0},{8,9},{9,11},{11,1... | collective-permute-start | bytes 786440 | tf_op jit(solution)/shard_map/ppermute | solution.py:221
  3.0 8.3 %collective-permute-start.4 = (bf16[128,1024]{1,0:T(8,128)(2,1)}, bf16[128,1024]{1,0:T(8,128)(2,1)S(1)}, u32[]{:S(2)}, u32[]{:S(2)}) collective-permute-start(bf16[128,1024]{1,0:T(8,128)(2,1)} %x_ref.1), channel_id=1, source_target_pairs={{1,0},{3,1},{5,3},{7,5},{6,7},{4,6},{2,4},{0,2},{9,8},{11,9},{13,1... | collective-permute-start | bytes 786440 | tf_op jit(solution)/shard_map/ppermute | solution.py:222
  9.5 7.5 %collective-permute-start.1 = (bf16[128,1024]{1,0:T(8,128)(2,1)S(1)}, bf16[128,1024]{1,0:T(8,128)(2,1)S(1)}, u32[]{:S(2)}, u32[]{:S(2)}) collective-permute-start(bf16[128,1024]{1,0:T(8,128)(2,1)S(1)} %collective-permute-done.refs_0_), channel_id=1, source_target_pairs={{0,1},{1,3},{3,5},{5,7},{7,6},{6,4},{4,2},{2,0},{8,9},{9,11},{11,1... | collective-permute-start | bytes 786440 | tf_op jit(solution)/shard_map/ppermute | solution.py:221
  11.2 7.2 %collective-permute-start.5 = (bf16[128,1024]{1,0:T(8,128)(2,1)S(1)}, bf16[128,1024]{1,0:T(8,128)(2,1)S(1)}, u32[]{:S(2)}, u32[]{:S(2)}) collective-permute-start(bf16[128,1024]{1,0:T(8,128)(2,1)S(1)} %collective-permute-done.4.refs_1_), channel_id=1, source_target_pairs={{1,0},{3,1},{5,3},{7,5},{6,7},{4,6},{2,4},{0,2},{9,8},{11,9},{13,1... | collective-permute-start | bytes 786440 | tf_op jit(solution)/shard_map/ppermute | solution.py:222
  11.6 0.9 %copy-start = (bf16[128,1024]{1,0:T(8,128)(2,1)S(1)}, bf16[128,1024]{1,0:T(8,128)(2,1)}, u32[]{:S(2)}) copy-start(bf16[128,1024]{1,0:T(8,128)(2,1)} %x_ref.1) | copy-start | bytes 786436
  12.5 3.3 %copy-start.1 = (f32[3,3,1024]{2,1,0:T(4,128)S(1)}, f32[3,3,1024]{2,1,0:T(4,128)}, u32[]{:S(2)}) copy-start(f32[3,3,1024]{2,1,0:T(4,128)} %param.7) | copy-start | bytes 110596
  17.0 12.6 %collective-permute-start.2 = (bf16[128,1024]{1,0:T(8,128)(2,1)S(1)}, bf16[128,1024]{1,0:T(8,128)(2,1)S(1)}, u32[]{:S(2)}, u32[]{:S(2)}) collective-permute-start(bf16[128,1024]{1,0:T(8,128)(2,1)S(1)} %collective-permute-done.1.refs_0_), channel_id=1, source_target_pairs={{0,1},{1,3},{3,5},{5,7},{7,6},{6,4},{4,2},{2,0},{8,9},{9,11},{11,1... | collective-permute-start | bytes 786440 | tf_op jit(solution)/shard_map/ppermute | solution.py:221
  18.4 12.7 %collective-permute-start.6 = (bf16[128,1024]{1,0:T(8,128)(2,1)S(1)}, bf16[128,1024]{1,0:T(8,128)(2,1)S(1)}, u32[]{:S(2)}, u32[]{:S(2)}) collective-permute-start(bf16[128,1024]{1,0:T(8,128)(2,1)S(1)} %collective-permute-done.5.refs_1_), channel_id=1, source_target_pairs={{1,0},{3,1},{5,3},{7,5},{6,7},{4,6},{2,4},{0,2},{9,8},{11,9},{13,1... | collective-permute-start | bytes 786440 | tf_op jit(solution)/shard_map/ppermute | solution.py:222
  29.7 7.4 %collective-permute-start.3 = (bf16[64,1024]{1,0:T(8,128)(2,1)S(1)}, bf16[64,1024]{1,0:T(8,128)(2,1)S(1)}, u32[]{:S(2)}, u32[]{:S(2)}) collective-permute-start(bf16[64,1024]{1,0:T(8,128)(2,1)S(1)} %slice.10), channel_id=1, source_target_pairs={{0,1},{1,3},{3,5},{5,7},{7,6},{6,4},{4,2},{2,0},{8,9},{9,11},{11,1... | collective-permute-start | bytes 393224 | tf_op jit(solution)/shard_map/ppermute | solution.py:234
  31.1 6.0 %collective-permute-start.7 = (bf16[64,1024]{1,0:T(8,128)(2,1)S(1)}, bf16[64,1024]{1,0:T(8,128)(2,1)S(1)}, u32[]{:S(2)}, u32[]{:S(2)}) collective-permute-start(bf16[64,1024]{1,0:T(8,128)(2,1)S(1)} %slice.11), channel_id=1, source_target_pairs={{1,0},{3,1},{5,3},{7,5},{6,7},{4,6},{2,4},{0,2},{9,8},{11,9},{13,1... | collective-permute-start | bytes 393224 | tf_op jit(solution)/shard_map/ppermute | solution.py:235
  42.5 5.9 %collective-permute-start.10 = (f32[26,8,128]{2,1,0:T(8,128)S(1)}, f32[26,8,128]{2,1,0:T(8,128)S(1)}, u32[]{:S(2)}, u32[]{:S(2)}) collective-permute-start(f32[26,8,128]{2,1,0:T(8,128)S(1)} %get-tuple-element.7), channel_id=1, source_target_pairs={{0,24},{1,25},{2,26},{3,27},{4,28},{5,29},{6,30},{7,31}} | collective-permute-start | bytes 319496 | tf_op jit(solution)/shard_map/ppermute | solution.py:253
  43.8 4.6 %collective-permute-start.8 = (f32[26,8,128]{2,1,0:T(8,128)S(1)}, f32[26,8,128]{2,1,0:T(8,128)S(1)}, u32[]{:S(2)}, u32[]{:S(2)}) collective-permute-start(f32[26,8,128]{2,1,0:T(8,128)S(1)} %get-tuple-element.7), channel_id=1, source_target_pairs={{0,8},{8,16},{16,24},{1,9},{9,17},{17,25},{2,10},{10,18},{18,26},{... | collective-permute-start | bytes 319496 | tf_op jit(solution)/shard_map/ppermute | solution.py:253
  45.1 5.5 %collective-permute-start.9 = (f32[26,8,128]{2,1,0:T(8,128)S(1)}, f32[26,8,128]{2,1,0:T(8,128)S(1)}, u32[]{:S(2)}, u32[]{:S(2)}) collective-permute-start(f32[26,8,128]{2,1,0:T(8,128)S(1)} %get-tuple-element.7), channel_id=1, source_target_pairs={{0,16},{8,24},{1,17},{9,25},{2,18},{10,26},{3,19},{11,27},{4,20},{... | collective-permute-start | bytes 319496 | tf_op jit(solution)/shard_map/ppermute | solution.py:253

commit v2 on v1

v2 whole, which is shorter than its diff:
```python
import functools

import jax
import jax.numpy as jnp
from jax import lax
from jax.experimental import pallas as pl
from jax.experimental.pallas import tpu as pltpu
from jax.sharding import PartitionSpec as P

LANES = 128
COLS = 256
DEPTH = 256
GRID_ROWS = 4
EDGE = 10
VMEM = pl.BlockSpec(memory_space=pltpu.VMEM)
HBM = pl.BlockSpec(memory_space=pltpu.HBM)


def ring_order(count):
    if count % (2 * GRID_ROWS):
        return list(range(count))
    cols = count // GRID_ROWS
    cells = [(0, c) for c in range(cols)]
    for r in range(1, GRID_ROWS):
        inner = list(range(1, cols))
        cells += [(r, c) for c in (reversed(inner) if r % 2 else inner)]
    cells += [(r, 0) for r in range(GRID_ROWS - 1, 0, -1)]
    return [r * cols + c for r, c in cells]


def owner_at(order, step):
    me = lax.axis_index("tp")
    owner = jnp.int32(0)
    for place, index in enumerate(order):
        owner = jnp.where(me == index, order[(place - step) % len(order)], owner)
    return owner


def block_loads(order, steps, w_ref, held, sem):
    count, streams, width, _ = held.shape
    copies = []
    for b, step in enumerate(steps):
        start = pl.multiple_of(owner_at(order, step) * width, width)
        for s in range(streams):
            copies.append(
                pltpu.make_async_copy(
                    w_ref.at[s, pl.ds(start, width), :], held.at[b, s], sem.at[b, s]
                )
            )
    return copies


def add_products(xs, held, total):
    streams, _, chans = total.shape
    for s in range(streams):
        for c in range(0, chans, COLS):
            at = slice(c, c + COLS)
            terms = [
                jnp.dot(x, held[b, s, :, at], preferred_element_type=jnp.float32)
                for b, x in enumerate(xs)
            ]
            total[s, :, at] += sum(terms)


def spread(out_ref, value):
    groups, lanes = out_ref.shape[-2:]
    for g in range(groups):
        out_ref[..., g, :] = value[..., g * lanes : (g + 1) * lanes]


def first_kernel(order, steps, x_ref, w_ref, total, held, own, own_sem, held_sem):
    width = x_ref.shape[1]
    depth = min(DEPTH, width)
    start = pl.multiple_of(owner_at(order, 0) * width, width)
    chunks = [
        pltpu.make_async_copy(
            w_ref.at[:, pl.ds(start + k * depth, depth), :],
            own.at[:, pl.ds(k * depth, depth), :],
            own_sem.at[k],
        )
        for k in range(width // depth)
    ]
    ahead = block_loads(order, steps, w_ref, held, held_sem)
    for copy in chunks + ahead:
        copy.start()
    for k, copy in enumerate(chunks):
        copy.wait()
        at = slice(k * depth, (k + 1) * depth)
        for s in range(total.shape[0]):
            for c in range(0, total.shape[2], COLS):
                to = slice(c, c + COLS)
                term = jnp.dot(x_ref[:, at], own[s, at, to], preferred_element_type=jnp.float32)
                if k:
                    total[s, :, to] += term
                else:
                    total[s, :, to] = term
    for copy in ahead:
        copy.wait()


def middle_kernel(order, steps, xa_ref, xb_ref, held, w_ref, _, total, next_held, sem):
    ahead = block_loads(order, steps, w_ref, next_held, sem)
    for copy in ahead:
        copy.start()
    add_products([xa_ref[...], xb_ref[...]], held, total)
    for copy in ahead:
        copy.wait()


def second_kernel(
    order, steps, xa_ref, xb_ref, held, w_ref, _, taps_in, decay, residue,
    total, next_held, taps, table, sem,
):
    ahead = block_loads(order, steps, w_ref, next_held, sem)
    for copy in ahead:
        copy.start()
    rate = decay[...]
    rows = total.shape[1]
    for i, power in enumerate((1, rows, rows - 1, rows - 2)):
        spread(table.at[i], jnp.exp(-rate * power))
    spread(table.at[4], residue[...] * jnp.sqrt(1.0 - jnp.exp(-2.0 * rate)))
    spread(taps, taps_in[...])
    add_products([xa_ref[...], xb_ref[...]], held, total)
    for copy in ahead:
        copy.wait()


def filtered(taps, p_ref, s, t):
    return (
        taps[0, s] * p_ref[s - 1, t]
        + taps[1, s] * p_ref[s - 1, t - 1]
        + taps[2, s] * p_ref[s - 1, t - 2]
    )


def last_kernel(xa_ref, xb_ref, held, taps, table, _, total, source, out_ref, p_ref, tail):
    add_products([jnp.concatenate([xa_ref[...], xb_ref[...]], axis=0)], held, total)
    rows, groups, lanes = source.shape
    modes = table.shape[1]
    for s in (1, 2):
        spread(p_ref.at[s - 1], rounded(total[s]))
    spread(tail, rounded(total[0, rows - 8 :]))
    rate = [table[0, n] for n in range(modes)]

    def step_row(t, state):
        u = filtered(taps, p_ref, 1, t) * filtered(taps, p_ref, 2, t)
        source[t] = u
        return [r * s + u for r, s in zip(rate, state)]

    state = [jnp.zeros((groups, lanes), jnp.float32)] * modes
    for t in range(2, 8):
        state = step_row(t, state)

    def eight(i, state):
        for j in range(8):
            state = step_row(i * 8 + j, state)
        return state

    state = lax.fori_loop(1, rows // 8, eight, state)
    for n in range(modes):
        out_ref[n] = state[n]
    for s in (1, 2):
        for j in range(2):
            out_ref[modes + (s - 1) * 2 + j] = p_ref[s - 1, j]
            out_ref[modes + 4 + s * 2 + j] = p_ref[s - 1, rows - 2 + j]
    for j in range(2):
        out_ref[modes + 4 + j] = tail[6 + j]


def rounded(value):
    return value.astype(jnp.bfloat16).astype(jnp.float32)


def tree_sum(terms):
    while len(terms) > 1:
        terms = [a + b for a, b in zip(terms[::2], terms[1::2])] + terms[len(terms) & ~1 :]
    return terms[0]


def local_kernel(total, source, taps, table, query, response, p_ref):
    rows, groups, lanes = source.shape
    modes = table.shape[1]
    spread(p_ref, rounded(total[0]))
    for j in range(2):
        query[j] = p_ref[j]

    def step_row(t, state):
        query[t] = taps[0, 0] * p_ref[t] + taps[1, 0] * p_ref[t - 1] + taps[2, 0] * p_ref[t - 2]
        u = source[t]
        state = [table[0, n] * state[n] + u for n in range(modes)]
        response[t] = tree_sum([table[4, n] * state[n] for n in range(modes)])
        return state

    state = [jnp.zeros((groups, lanes), jnp.float32)] * modes
    for t in range(2, 8):
        state = step_row(t, state)

    def eight(i, state):
        for j in range(8):
            state = step_row(i * 8 + j, state)
        return state

    lax.fori_loop(1, rows // 8, eight, state)


def edge(taps, s, first, second, before, last):
    return (
        taps[0, s] * first + taps[1, s] * last + taps[2, s] * before,
        taps[0, s] * second + taps[1, s] * first + taps[2, s] * last,
    )


def final_kernel(count, *refs):
    sent = refs[:count]
    local, query, response, taps, table, out_ref, work = refs[count:]
    rows, groups, lanes = query.shape
    modes = table.shape[1]
    zero = jnp.zeros((groups, lanes), jnp.float32)

    def rim(d, s):
        if d >= count:
            return zero, zero
        return sent[d][modes + 4 + s * 2], sent[d][modes + 4 + s * 2 + 1]

    def sources(block, d):
        ends = [
            edge(taps, s, block[modes + s * 2 - 2], block[modes + s * 2 - 1], *rim(d, s))
            for s in (1, 2)
        ]
        return ends[0][0] * ends[1][0], ends[0][1] * ends[1][1]

    state = [zero] * modes
    for d in reversed(range(count)):
        u0, u1 = sources(sent[d], d + 1)
        state = [
            table[1, n] * state[n] + (sent[d][n] + table[2, n] * u0 + table[3, n] * u1)
            for n in range(modes)
        ]
    heads = edge(taps, 0, query[0], query[1], *rim(0, 0))
    for t, u in enumerate(sources(local, 0)):
        state = [table[0, n] * state[n] + u for n in range(modes)]
        work[t] = heads[t] * tree_sum([table[4, n] * state[n] for n in range(modes)])
    carried = [table[4, n] * state[n] for n in range(modes)]

    def row(t, carried):
        carried = [table[0, n] * carried[n] for n in range(modes)]
        work[t] = query[t] * (response[t] + tree_sum(carried))
        return carried

    for t in range(2, 8):
        carried = row(t, carried)

    def eight(i, carried):
        for j in range(8):
            carried = row(i * 8 + j, carried)
        return carried

    lax.fori_loop(1, rows // 8, eight, carried)
    for g in range(groups):
        out_ref[:, g * lanes : (g + 1) * lanes] = work[:, g, :].astype(out_ref.dtype)


def on_device(tokens, in_weight, filter_taps, decay_rate, residue):
    rows, width = tokens.shape
    streams, chans = in_weight.shape[1:]
    lags = filter_taps.shape[0]
    modes = decay_rate.shape[0]
    groups = chans // LANES
    tp, ctx = lax.axis_size("tp"), lax.axis_size("ctx")
    order = ring_order(tp)
    weight = jnp.transpose(in_weight, (1, 0, 2))
    half = tp // 2
    ahead = [(order[i], order[(i + 1) % tp]) for i in range(tp)]
    back = [(b, a) for a, b in ahead]

    def f32(*shape):
        return jax.ShapeDtypeStruct(shape, jnp.float32)

    def held(count):
        return jax.ShapeDtypeStruct((count, streams, width, chans), jnp.bfloat16)

    def loads(step):
        return [step, -step] if step < half else [step]

    sums = f32(streams, rows, chans)
    wide = f32(rows, groups, LANES)
    params = pltpu.CompilerParams(vmem_limit_bytes=12 << 20)
    cost = pl.CostEstimate(flops=0, bytes_accessed=16 << 20, transcendentals=0)

    depth = min(DEPTH, width)
    total, weights = pl.pallas_call(
        functools.partial(first_kernel, order, loads(1)),
        out_shape=[sums, held(len(loads(1)))],
        in_specs=[VMEM, HBM],
        out_specs=[VMEM] * 2,
        scratch_shapes=[
            pltpu.VMEM((streams, width, chans), jnp.bfloat16),
            pltpu.SemaphoreType.DMA((width // depth,)),
            pltpu.SemaphoreType.DMA((len(loads(1)), streams)),
        ],
        compiler_params=params,
        cost_estimate=cost,
        name="project_own",
    )(tokens, weight)
    fore, aft = tokens, tokens
    for step in range(1, half):
        fore = lax.ppermute(fore, "tp", ahead)
        aft = lax.ppermute(aft, "tp", back)
        fore, aft, total, weights = lax.optimization_barrier((fore, aft, total, weights))
        coming = loads(step + 1)
        tables = [f32(lags, streams, groups, LANES), f32(5, modes, groups, LANES)]
        with_tables = step == 1
        total, weights, *made = pl.pallas_call(
            functools.partial(second_kernel if with_tables else middle_kernel, order, coming),
            out_shape=[sums, held(len(coming))] + tables * with_tables,
            in_specs=[VMEM, VMEM, VMEM, HBM, VMEM] + [VMEM] * 3 * with_tables,
            out_specs=[VMEM, VMEM] + [VMEM] * 2 * with_tables,
            scratch_shapes=[pltpu.SemaphoreType.DMA((len(coming), streams))],
            input_output_aliases={4: 0},
            compiler_params=params,
            cost_estimate=cost,
            name="project_pair",
        )(fore, aft, weights, weight, total, *[filter_taps, decay_rate, residue][: 3 * with_tables])
        if with_tables:
            taps, table = made
    fore = lax.ppermute(fore[: rows // 2], "tp", ahead)
    aft = lax.ppermute(aft[rows // 2 :], "tp", back)
    total, source, local = pl.pallas_call(
        last_kernel,
        out_shape=[sums, wide, f32(modes + EDGE, groups, LANES)],
        in_specs=[VMEM] * 6,
        out_specs=[VMEM] * 3,
        scratch_shapes=[
            pltpu.VMEM((2, rows, groups, LANES), jnp.float32),
            pltpu.VMEM((8, groups, LANES), jnp.float32),
        ],
        input_output_aliases={5: 0},
        compiler_params=params,
        cost_estimate=cost,
        name="project_last",
    )(fore, aft, weights, taps, table, total)

    sent = [
        lax.ppermute(local, "ctx", [(j, j + d) for j in range(ctx - d)]) for d in range(1, ctx)
    ]
    query, response = pl.pallas_call(
        local_kernel,
        out_shape=[wide, wide],
        in_specs=[VMEM] * 4,
        out_specs=[VMEM] * 2,
        scratch_shapes=[pltpu.VMEM((rows, groups, LANES), jnp.float32)],
        compiler_params=params,
        cost_estimate=cost,
        name="local_response",
    )(total, source, taps, table)
    return pl.pallas_call(
        functools.partial(final_kernel, len(sent)),
        out_shape=jax.ShapeDtypeStruct((rows, chans), jnp.bfloat16),
        in_specs=[VMEM] * (len(sent) + 5),
        out_specs=VMEM,
        scratch_shapes=[pltpu.VMEM((rows, groups, LANES), jnp.float32)],
        compiler_params=params,
        name="carried_response",
    )(*sent, local, query, response, taps, table)


def solution(mesh):
    return jax.shard_map(
        on_device,
        mesh=mesh,
        in_specs=(
            P("ctx", "tp"),
            P(None, None, "tp"),
            P(None, None, "tp"),
            P(None, "tp"),
            P(None, "tp"),
        ),
        out_specs=P("ctx", "tp"),
        check_vma=False,
    )
```

time: 53.9 us -> 47.9 us (0.89)
  waiting for transfers between devices: 8.85 us -> 1.32 us
  Pallas kernels: 27.5 us -> 30 us
  other arithmetic: 0.94 us -> 0 us
    ppermute x3, waiting for transfers between devices: 6.6 us -> 0.01 us  [on_device(): fore = lax.ppermute(fore, 'tp', ahead)]
    pallas_call x5 -> x6, Pallas kernels: 24.5 us -> 28.1 us  [the longest x3 17.4 us: on_device(): pl.pallas_call(functools.partial(second_kernel if with_tables else middle...]
    ppermute x3, waiting for transfers between devices: 2.24 us -> 0.55 us  [on_device(): lax.ppermute(local, 'ctx', [(j, j + d) for j in range(ctx - d)])]
    pallas_call x1, Pallas kernels: 3.01 us -> 1.95 us  [on_device(): pl.pallas_call(functools.partial(final_kernel, len(sent)), out_shape=jax....]
    unnamed x1 -> x0, other arithmetic: 0.94 us -> none
    ppermute x3, waiting for transfers between devices: 0.01 us -> 0.76 us  [on_device(): aft = lax.ppermute(aft, 'tp', back)]
  transfers between devices with their start and end apart: 11 -> 11, of which waited for: 3 -> 3; matrix products, arithmetic and copies ran while one was open for 2% -> 0% of each run, Pallas kernels for 36% -> 54%
where the time goes in v2:
time: 47.9 us; the launch traced here: 47.7 us
  Pallas kernels  30 us (63%)
  starting transfers between devices  15.2 us (32%)
  waiting for transfers between devices  1.32 us (3%)
  local copies, waits for them, and re-layouts  1.03 us (2%)
    pallas_call x3, Pallas kernels, on_device(): pl.pallas_call(functools.partial(second_kernel if with_tables else middle...  17.4 us
    pallas_call x1, Pallas kernels, on_device(): pl.pallas_call(functools.partial(first_kernel, order, loads(1)), out_shap...  6.57 us
    ppermute x3, starting transfers between devices, on_device(): fore = lax.ppermute(fore, 'tp', ahead)  6.23 us
    ppermute x3, starting transfers between devices, on_device(): lax.ppermute(local, 'ctx', [(j, j + d) for j in range(ctx - d)])  5.99 us
    pallas_call x1, Pallas kernels, on_device(): pl.pallas_call(last_kernel, out_shape=[sums, wide, f32(modes + EDGE, grou...  2.38 us
    pallas_call x1, Pallas kernels, on_device(): pl.pallas_call(functools.partial(final_kernel, len(sent)), out_shape=jax....  1.95 us
    pallas_call x1, Pallas kernels, on_device(): pl.pallas_call(local_kernel, out_shape=[wide, wide], in_specs=[VMEM] * 4,...  1.7 us
    ppermute x1, starting transfers between devices, on_device(): fore = lax.ppermute(fore[:rows // 2], 'tp', ahead)  1.62 us
  transfers between devices with their start and end apart: 11, of which 3 were waited for; matrix products, arithmetic and copies ran while one was open for 0% of the time, Pallas kernels for 54%

profile of v2, /device:TPU:0, one launch (start us, length us, event | category | flops | bytes accessed | tf_op | source)
XLA Modules:
  0.0 47.7 jit_solution(9175134238608046510)
XLA Ops:
  0.0 3.0 %collective-permute-start = (bf16[128,1024]{1,0:T(8,128)(2,1)}, bf16[128,1024]{1,0:T(8,128)(2,1)S(1)}, u32[]{:S(2)}, u32[]{:S(2)}) collective-permute-start(bf16[128,1024]{1,0:T(8,128)(2,1)} %x_ref.1), channel_id=1, source_target_pairs={{0,1},{1,3},{3,5},{5,7},{7,6},{6,4},{4,2},{2,0},{8,9},{9,11},{11,1... | collective-permute-start | bytes 786440 | tf_op jit(solution)/shard_map/ppermute | solution.py:307
  3.0 0.1 collective-permute-start.1
  3.0 1.0 %copy-done = bf16[128,1024]{1,0:T(8,128)(2,1)S(1)} copy-done((bf16[128,1024]{1,0:T(8,128)(2,1)S(1)}, bf16[128,1024]{1,0:T(8,128)(2,1)}, u32[]{:S(2)}) %copy-start) | copy-done | bytes 262168
  4.0 6.6 %project_own.1 = (f32[3,128,1024]{2,1,0:T(8,128)S(1)}, bf16[2,3,1024,1024]{3,2,1,0:T(8,128)(2,1)S(1)}) custom-call(bf16[128,1024]{1,0:T(8,128)(2,1)S(1)} %copy-done, bf16[3,8192,1024]{2,1,0:T(8,128)(2,1)} %bitcast.1), custom_call_target="tpu_custom_call" | custom-call | bytes 16777216 | tf_op jit(solution)/shard_map/project_own/pallas_call | solution.py:291
  10.6 0.0 collective-permute-done.xa_ref
  10.6 0.3 collective-permute-done.1.xb_ref
  10.9 1.7 %collective-permute-start.2 = (bf16[128,1024]{1,0:T(8,128)(2,1)S(1)}, bf16[128,1024]{1,0:T(8,128)(2,1)S(1)}, u32[]{:S(2)}, u32[]{:S(2)}) collective-permute-start(bf16[128,1024]{1,0:T(8,128)(2,1)S(1)} %collective-permute-done.xa_ref), channel_id=1, source_target_pairs={{0,1},{1,3},{3,5},{5,7},{7,6},{6,4},{4,2},{2,0},{8,9},{9,11},{11,1... | collective-permute-start | bytes 786440 | tf_op jit(solution)/shard_map/ppermute | solution.py:307
  12.6 0.3 collective-permute-start.3
  13.0 0.0 copy-done.1
  13.0 0.0 copy-done.3
  13.0 6.4 %project_pair.3 = (f32[3,128,1024]{2,1,0:T(8,128)S(1)}, bf16[2,3,1024,1024]{3,2,1,0:T(8,128)(2,1)S(1)}, f32[3,3,8,128]{3,2,1,0:T(8,128)S(1)}, f32[5,16,8,128]{3,2,1,0:T(8,128)S(1)}) custom-call(bf16[128,1024]{1,0:T(8,128)(2,1)S(1)} %collective-permute-done.xa_ref, ...), custom_call_target="tpu_custom_call", output_to_operand_aliasing={{0}: (4, {})} | custom-call | bytes 16777216 | tf_op jit(solution)/shard_map/project_pair/pallas_call | solution.py:313
  19.4 0.0 collective-permute-done.2.xa_ref
  19.4 0.4 collective-permute-done.3.xb_ref
  19.8 1.6 %collective-permute-start.4 = (bf16[128,1024]{1,0:T(8,128)(2,1)S(1)}, bf16[128,1024]{1,0:T(8,128)(2,1)S(1)}, u32[]{:S(2)}, u32[]{:S(2)}) collective-permute-start(bf16[128,1024]{1,0:T(8,128)(2,1)S(1)} %collective-permute-done.2.xa_ref), channel_id=1, source_target_pairs={{0,1},{1,3},{3,5},{5,7},{7,6},{6,4},{4,2},{2,0},{8,9},{9,11},{11,1... | collective-permute-start | bytes 786440 | tf_op jit(solution)/shard_map/ppermute | solution.py:307
  21.4 0.4 collective-permute-start.5
  21.9 6.4 %project_pair.4 = (f32[3,128,1024]{2,1,0:T(8,128)S(1)}, bf16[2,3,1024,1024]{3,2,1,0:T(8,128)(2,1)S(1)}) custom-call(bf16[128,1024]{1,0:T(8,128)(2,1)S(1)} %collective-permute-done.2.xa_ref, bf16[128,1024]{1,0:T(8,128)(2,1)S(1)} %collective-permute-done.3.xb_ref, ...), custom_call_target="tpu_custom_call", output_to_operand_aliasing={{0}: (4, {})} | custom-call | bytes 16777216 | tf_op jit(solution)/shard_map/project_pair/pallas_call | solution.py:313
  28.3 0.0 collective-permute-done.4.xa_ref
  28.3 0.0 collective-permute-done.5.xb_ref
  28.3 1.6 %collective-permute-start.6 = (bf16[64,1024]{1,0:T(8,128)(2,1)S(1)}, bf16[64,1024]{1,0:T(8,128)(2,1)S(1)}, u32[]{:S(2)}, u32[]{:S(2)}) collective-permute-start(bf16[64,1024]{1,0:T(8,128)(2,1)S(1)} %slice.6), channel_id=1, source_target_pairs={{0,1},{1,3},{3,5},{5,7},{7,6},{6,4},{4,2},{2,0},{8,9},{9,11},{11,1... | collective-permute-start | bytes 393224 | tf_op jit(solution)/shard_map/ppermute | solution.py:326
  30.0 0.5 %collective-permute-start.7 = (bf16[64,1024]{1,0:T(8,128)(2,1)S(1)}, bf16[64,1024]{1,0:T(8,128)(2,1)S(1)}, u32[]{:S(2)}, u32[]{:S(2)}) collective-permute-start(bf16[64,1024]{1,0:T(8,128)(2,1)S(1)} %slice.7), channel_id=1, source_target_pairs={{1,0},{3,1},{5,3},{7,5},{6,7},{4,6},{2,4},{0,2},{9,8},{11,9},{13,1... | collective-permute-start | bytes 393224 | tf_op jit(solution)/shard_map/ppermute | solution.py:327
  30.5 4.6 %project_pair.5 = (f32[3,128,1024]{2,1,0:T(8,128)S(1)}, bf16[1,3,1024,1024]{3,2,1,0:T(8,128)(2,1)S(1)}) custom-call(bf16[128,1024]{1,0:T(8,128)(2,1)S(1)} %collective-permute-done.4.xa_ref, bf16[128,1024]{1,0:T(8,128)(2,1)S(1)} %collective-permute-done.5.xb_ref, ...), custom_call_target="tpu_custom_call", output_to_operand_aliasing={{0}: (4, {})} | custom-call | bytes 16777216 | tf_op jit(solution)/shard_map/project_pair/pallas_call | solution.py:313
  35.1 0.0 collective-permute-done.6.xa_ref
  35.1 0.0 collective-permute-done.7.xb_ref
  35.1 2.4 %project_last.1 = (f32[3,128,1024]{2,1,0:T(8,128)S(1)}, f32[128,8,128]{2,1,0:T(8,128)S(1)}, f32[26,8,128]{2,1,0:T(8,128)S(1)}) custom-call(bf16[64,1024]{1,0:T(8,128)(2,1)S(1)} %collective-permute-done.6.xa_ref, bf16[64,1024]{1,0:T(8,128)(2,1)S(1)} %collective-permute-done.7.xb_ref, ...), custom_call_target="tpu_custom_call", output_to_operand_aliasing={{0}: (5, {})} | custom-call | bytes 16777216 | tf_op jit(solution)/shard_map/project_last/pallas_call | solution.py:328
  37.5 1.3 %collective-permute-start.10 = (f32[26,8,128]{2,1,0:T(8,128)S(1)}, f32[26,8,128]{2,1,0:T(8,128)S(1)}, u32[]{:S(2)}, u32[]{:S(2)}) collective-permute-start(f32[26,8,128]{2,1,0:T(8,128)S(1)} %get-tuple-element.54.refs_3_), channel_id=1, source_target_pairs={{0,24},{1,25},{2,26},{3,27},{4,28},{5,29},{6,30},{7,31}} | collective-permute-start | bytes 319496 | tf_op jit(solution)/shard_map/ppermute | solution.py:344
  38.8 1.3 %collective-permute-start.8 = (f32[26,8,128]{2,1,0:T(8,128)S(1)}, f32[26,8,128]{2,1,0:T(8,128)S(1)}, u32[]{:S(2)}, u32[]{:S(2)}) collective-permute-start(f32[26,8,128]{2,1,0:T(8,128)S(1)} %get-tuple-element.54.refs_3_), channel_id=1, source_target_pairs={{0,8},{8,16},{16,24},{1,9},{9,17},{17,25},{2,10},{10,18},{18,26},{... | collective-permute-start | bytes 319496 | tf_op jit(solution)/shard_map/ppermute | solution.py:344
  40.1 3.4 %collective-permute-start.9 = (f32[26,8,128]{2,1,0:T(8,128)S(1)}, f32[26,8,128]{2,1,0:T(8,128)S(1)}, u32[]{:S(2)}, u32[]{:S(2)}) collective-permute-start(f32[26,8,128]{2,1,0:T(8,128)S(1)} %get-tuple-element.54.refs_3_), channel_id=1, source_target_pairs={{0,16},{8,24},{1,17},{9,25},{2,18},{10,26},{3,19},{11,27},{4,20},{... | collective-permute-start | bytes 319496 | tf_op jit(solution)/shard_map/ppermute | solution.py:344
  43.5 1.7 %local_response.1 = (f32[128,8,128]{2,1,0:T(8,128)S(1)}, f32[128,8,128]{2,1,0:T(8,128)S(1)}) custom-call(f32[3,128,1024]{2,1,0:T(8,128)S(1)} %get-tuple-element.55.total, f32[128,8,128]{2,1,0:T(8,128)S(1)} %get-tuple-element.56.source, f32[3,3,8,128]{3,2,1,0:T(8,128)S(1)} %get-tuple-element.51.taps.refs_6_, f32[5,16,8,128]{3,2,1,0:T(8,128)S(1)} %get-tuple-element.52.table.refs_7_), custom_call_target="tpu_custom_call" | custom-call | bytes 16777216 | tf_op jit(solution)/shard_map/local_response/pallas_call | solution.py:346
  45.2 0.0 collective-permute-done.10.refs_2_
  45.2 0.0 collective-permute-done.8.refs_0_
  45.2 0.5 %collective-permute-done.9.refs_1_ = f32[26,8,128]{2,1,0:T(8,128)S(1)} collective-permute-done((f32[26,8,128]{2,1,0:T(8,128)S(1)}, f32[26,8,128]{2,1,0:T(8,128)S(1)}, u32[]{:S(2)}, u32[]{:S(2)}) %collective-permute-start.9) | collective-permute-done | bytes 106528 | tf_op jit(solution)/shard_map/ppermute | solution.py:344
  45.8 1.9 %carried_response.1 = bf16[128,1024]{1,0:T(8,128)(2,1)} custom-call(f32[26,8,128]{2,1,0:T(8,128)S(1)} %collective-permute-done.8.refs_0_, f32[26,8,128]{2,1,0:T(8,128)S(1)} %collective-permute-done.9.refs_1_, f32[26,8,128]{2,1,0:T(8,128)S(1)} %collective-permute-done.10.refs_2_, f32[26,8,128]{2,1,0:T(8,128)S(1)} %get-tuple-element.54.refs_3_, ...), custom_call_target="tpu_custom_call" | custom-call | tf_op jit(solution)/shard_map/carried_response/pallas_call | solution.py:356
  (7 shorter events, 0.0 us)
Async XLA Ops:
  0.0 10.6 %collective-permute-start = (bf16[128,1024]{1,0:T(8,128)(2,1)}, bf16[128,1024]{1,0:T(8,128)(2,1)S(1)}, u32[]{:S(2)}, u32[]{:S(2)}) collective-permute-start(bf16[128,1024]{1,0:T(8,128)(2,1)} %x_ref.1), channel_id=1, source_target_pairs={{0,1},{1,3},{3,5},{5,7},{7,6},{6,4},{4,2},{2,0},{8,9},{9,11},{11,1... | collective-permute-start | bytes 786440 | tf_op jit(solution)/shard_map/ppermute | solution.py:307
  3.0 8.0 %collective-permute-start.1 = (bf16[128,1024]{1,0:T(8,128)(2,1)}, bf16[128,1024]{1,0:T(8,128)(2,1)S(1)}, u32[]{:S(2)}, u32[]{:S(2)}) collective-permute-start(bf16[128,1024]{1,0:T(8,128)(2,1)} %x_ref.1), channel_id=1, source_target_pairs={{1,0},{3,1},{5,3},{7,5},{6,7},{4,6},{2,4},{0,2},{9,8},{11,9},{13,1... | collective-permute-start | bytes 786440 | tf_op jit(solution)/shard_map/ppermute | solution.py:308
  3.0 1.0 %copy-start = (bf16[128,1024]{1,0:T(8,128)(2,1)S(1)}, bf16[128,1024]{1,0:T(8,128)(2,1)}, u32[]{:S(2)}) copy-start(bf16[128,1024]{1,0:T(8,128)(2,1)} %x_ref.1) | copy-start | bytes 786436
  4.0 8.9 %copy-start.1 = (f32[16,1024]{1,0:T(8,128)S(1)}, f32[16,1024]{1,0:T(8,128)}, u32[]{:S(2)}) copy-start(f32[16,1024]{1,0:T(8,128)} %decay.1) | copy-start | bytes 196612
  4.0 8.9 %copy-start.2 = (f32[16,1024]{1,0:T(8,128)S(1)}, f32[16,1024]{1,0:T(8,128)}, u32[]{:S(2)}) copy-start(f32[16,1024]{1,0:T(8,128)} %residue.1) | copy-start | bytes 196612
  4.0 8.9 %copy-start.3 = (f32[3,3,1024]{2,1,0:T(4,128)S(1)}, f32[3,3,1024]{2,1,0:T(4,128)}, u32[]{:S(2)}) copy-start(f32[3,3,1024]{2,1,0:T(4,128)} %taps_in.1) | copy-start | bytes 110596
  10.9 8.5 %collective-permute-start.2 = (bf16[128,1024]{1,0:T(8,128)(2,1)S(1)}, bf16[128,1024]{1,0:T(8,128)(2,1)S(1)}, u32[]{:S(2)}, u32[]{:S(2)}) collective-permute-start(bf16[128,1024]{1,0:T(8,128)(2,1)S(1)} %collective-permute-done.xa_ref), channel_id=1, source_target_pairs={{0,1},{1,3},{3,5},{5,7},{7,6},{6,4},{4,2},{2,0},{8,9},{9,11},{11,1... | collective-permute-start | bytes 786440 | tf_op jit(solution)/shard_map/ppermute | solution.py:307
  12.6 7.2 %collective-permute-start.3 = (bf16[128,1024]{1,0:T(8,128)(2,1)S(1)}, bf16[128,1024]{1,0:T(8,128)(2,1)S(1)}, u32[]{:S(2)}, u32[]{:S(2)}) collective-permute-start(bf16[128,1024]{1,0:T(8,128)(2,1)S(1)} %collective-permute-done.1.xb_ref), channel_id=1, source_target_pairs={{1,0},{3,1},{5,3},{7,5},{6,7},{4,6},{2,4},{0,2},{9,8},{11,9},{13,1... | collective-permute-start | bytes 786440 | tf_op jit(solution)/shard_map/ppermute | solution.py:308
  19.8 8.4 %collective-permute-start.4 = (bf16[128,1024]{1,0:T(8,128)(2,1)S(1)}, bf16[128,1024]{1,0:T(8,128)(2,1)S(1)}, u32[]{:S(2)}, u32[]{:S(2)}) collective-permute-start(bf16[128,1024]{1,0:T(8,128)(2,1)S(1)} %collective-permute-done.2.xa_ref), channel_id=1, source_target_pairs={{0,1},{1,3},{3,5},{5,7},{7,6},{6,4},{4,2},{2,0},{8,9},{9,11},{11,1... | collective-permute-start | bytes 786440 | tf_op jit(solution)/shard_map/ppermute | solution.py:307
  21.4 6.9 %collective-permute-start.5 = (bf16[128,1024]{1,0:T(8,128)(2,1)S(1)}, bf16[128,1024]{1,0:T(8,128)(2,1)S(1)}, u32[]{:S(2)}, u32[]{:S(2)}) collective-permute-start(bf16[128,1024]{1,0:T(8,128)(2,1)S(1)} %collective-permute-done.3.xb_ref), channel_id=1, source_target_pairs={{1,0},{3,1},{5,3},{7,5},{6,7},{4,6},{2,4},{0,2},{9,8},{11,9},{13,1... | collective-permute-start | bytes 786440 | tf_op jit(solution)/shard_map/ppermute | solution.py:308
  28.3 6.8 %collective-permute-start.6 = (bf16[64,1024]{1,0:T(8,128)(2,1)S(1)}, bf16[64,1024]{1,0:T(8,128)(2,1)S(1)}, u32[]{:S(2)}, u32[]{:S(2)}) collective-permute-start(bf16[64,1024]{1,0:T(8,128)(2,1)S(1)} %slice.6), channel_id=1, source_target_pairs={{0,1},{1,3},{3,5},{5,7},{7,6},{6,4},{4,2},{2,0},{8,9},{9,11},{11,1... | collective-permute-start | bytes 393224 | tf_op jit(solution)/shard_map/ppermute | solution.py:326
  30.0 5.1 %collective-permute-start.7 = (bf16[64,1024]{1,0:T(8,128)(2,1)S(1)}, bf16[64,1024]{1,0:T(8,128)(2,1)S(1)}, u32[]{:S(2)}, u32[]{:S(2)}) collective-permute-start(bf16[64,1024]{1,0:T(8,128)(2,1)S(1)} %slice.7), channel_id=1, source_target_pairs={{1,0},{3,1},{5,3},{7,5},{6,7},{4,6},{2,4},{0,2},{9,8},{11,9},{13,1... | collective-permute-start | bytes 393224 | tf_op jit(solution)/shard_map/ppermute | solution.py:327
  37.5 7.7 %collective-permute-start.10 = (f32[26,8,128]{2,1,0:T(8,128)S(1)}, f32[26,8,128]{2,1,0:T(8,128)S(1)}, u32[]{:S(2)}, u32[]{:S(2)}) collective-permute-start(f32[26,8,128]{2,1,0:T(8,128)S(1)} %get-tuple-element.54.refs_3_), channel_id=1, source_target_pairs={{0,24},{1,25},{2,26},{3,27},{4,28},{5,29},{6,30},{7,31}} | collective-permute-start | bytes 319496 | tf_op jit(solution)/shard_map/ppermute | solution.py:344
  38.8 6.4 %collective-permute-start.8 = (f32[26,8,128]{2,1,0:T(8,128)S(1)}, f32[26,8,128]{2,1,0:T(8,128)S(1)}, u32[]{:S(2)}, u32[]{:S(2)}) collective-permute-start(f32[26,8,128]{2,1,0:T(8,128)S(1)} %get-tuple-element.54.refs_3_), channel_id=1, source_target_pairs={{0,8},{8,16},{16,24},{1,9},{9,17},{17,25},{2,10},{10,18},{18,26},{... | collective-permute-start | bytes 319496 | tf_op jit(solution)/shard_map/ppermute | solution.py:344
  40.1 5.7 %collective-permute-start.9 = (f32[26,8,128]{2,1,0:T(8,128)S(1)}, f32[26,8,128]{2,1,0:T(8,128)S(1)}, u32[]{:S(2)}, u32[]{:S(2)}) collective-permute-start(f32[26,8,128]{2,1,0:T(8,128)S(1)} %get-tuple-element.54.refs_3_), channel_id=1, source_target_pairs={{0,16},{8,24},{1,17},{9,25},{2,18},{10,26},{3,19},{11,27},{4,20},{... | collective-permute-start | bytes 319496 | tf_op jit(solution)/shard_map/ppermute | solution.py:344

commit v3 on v2

--- a/solution.py
+++ b/solution.py
@@ -50,16 +50,23 @@
     return copies
 
 
-def add_products(xs, held, total):
-    streams, _, chans = total.shape
-    for s in range(streams):
-        for c in range(0, chans, COLS):
-            at = slice(c, c + COLS)
-            terms = [
-                jnp.dot(x, held[b, s, :, at], preferred_element_type=jnp.float32)
-                for b, x in enumerate(xs)
-            ]
-            total[s, :, at] += sum(terms)
+def add_products(xs, held, total, s):
+    for c in range(0, total.shape[2], COLS):
+        at = slice(c, c + COLS)
+        terms = [
+            jnp.dot(x, held[b, s, :, at], preferred_element_type=jnp.float32)
+            for b, x in enumerate(xs)
+        ]
+        total[s, :, at] += sum(terms)
+
+
+def multiply_beside(loads, xa_ref, xb_ref, held, total):
+    @pl.loop(0, total.shape[0])
+    def _(s):
+        add_products([xa_ref[...], xb_ref[...]], held, total, s)
+
+    for copy in loads:
+        copy.wait()
 
 
 def spread(out_ref, value):
@@ -102,9 +109,7 @@
     ahead = block_loads(order, steps, w_ref, next_held, sem)
     for copy in ahead:
         copy.start()
-    add_products([xa_ref[...], xb_ref[...]], held, total)
-    for copy in ahead:
-        copy.wait()
+    multiply_beside(ahead, xa_ref, xb_ref, held, total)
 
 
 def second_kernel(
@@ -120,9 +125,7 @@
         spread(table.at[i], jnp.exp(-rate * power))
     spread(table.at[4], residue[...] * jnp.sqrt(1.0 - jnp.exp(-2.0 * rate)))
     spread(taps, taps_in[...])
-    add_products([xa_ref[...], xb_ref[...]], held, total)
-    for copy in ahead:
-        copy.wait()
+    multiply_beside(ahead, xa_ref, xb_ref, held, total)
 
 
 def filtered(taps, p_ref, s, t):
@@ -134,7 +137,9 @@
 
 
 def last_kernel(xa_ref, xb_ref, held, taps, table, _, total, source, out_ref, p_ref, tail):
-    add_products([jnp.concatenate([xa_ref[...], xb_ref[...]], axis=0)], held, total)
+    x = jnp.concatenate([xa_ref[...], xb_ref[...]], axis=0)
+    for s in range(total.shape[0]):
+        add_products([x], held, total, s)
     rows, groups, lanes = source.shape
     modes = table.shape[1]
     for s in (1, 2):
@@ -210,34 +215,80 @@
     )
 
 
+def lead_sources(taps, heads, rims):
+    one = edge(taps, 1, heads[0], heads[1], rims[2], rims[3])
+    two = edge(taps, 2, heads[2], heads[3], rims[4], rims[5])
+    return one[0] * two[0], one[1] * two[1]
+
+
+class Summary:
+    def __init__(self, rows, modes):
+        self.state = rows[:modes]
+        self.heads = rows[modes : modes + 4]
+        self.rims = rows[modes + 4 :]
+
+    @classmethod
+    def read(cls, ref, modes):
+        return cls([ref[i] for i in range(ref.shape[0])], modes)
+
+    @classmethod
+    def chosen(cls, odd, when_odd, when_even, modes):
+        pairs = zip(when_odd.rows(), when_even.rows())
+        return cls([jnp.where(odd, a, b) for a, b in pairs], modes)
+
+    def rows(self):
+        return self.state + self.heads + self.rims
+
+    def complete(self, taps, rims, by_first, by_second):
+        u0, u1 = lead_sources(taps, self.heads, rims)
+        return [x + f * u0 + g * u1 for x, f, g in zip(self.state, by_first, by_second)]
+
+
+def powers(table):
+    return [[table[i, n] for n in range(table.shape[1])] for i in range(table.shape[0])]
+
+
+def chip_kernel(local, partner, taps, table, out_ref):
+    modes = table.shape[1]
+    odd = lax.rem(lax.axis_index("ctx"), 2) == 1
+    mine, other = Summary.read(local, modes), Summary.read(partner, modes)
+    first = Summary.chosen(odd, other, mine, modes)
+    second = Summary.chosen(odd, mine, other, modes)
+    _, block, less_one, less_two, _ = powers(table)
+    end = second.complete(taps, first.rims, less_one, less_two)
+    joined = [d * x + y for d, x, y in zip(block, first.state, end)]
+    for i, value in enumerate(joined + first.heads + second.rims):
+        out_ref[i] = value
+
+
 def final_kernel(count, *refs):
     sent = refs[:count]
-    local, query, response, taps, table, out_ref, work = refs[count:]
+    local, partner, query, response, taps, table, out_ref, work = refs[count:]
     rows, groups, lanes = query.shape
     modes = table.shape[1]
-    zero = jnp.zeros((groups, lanes), jnp.float32)
-
-    def rim(d, s):
-        if d >= count:
-            return zero, zero
-        return sent[d][modes + 4 + s * 2], sent[d][modes + 4 + s * 2 + 1]
-
-    def sources(block, d):
-        ends = [
-            edge(taps, s, block[modes + s * 2 - 2], block[modes + s * 2 - 1], *rim(d, s))
-            for s in (1, 2)
-        ]
-        return ends[0][0] * ends[1][0], ends[0][1] * ends[1][1]
-
-    state = [zero] * modes
+    nothing = [jnp.zeros((groups, lanes), jnp.float32)] * 6
+    odd = lax.rem(lax.axis_index("ctx"), 2) == 1
+    _, block, less_one, less_two, _ = powers(table)
+    chips = [Summary.read(ref, modes) for ref in sent]
+    rims = [chip.rims for chip in chips] + [nothing]
+
+    state = [nothing[0]] * modes
     for d in reversed(range(count)):
-        u0, u1 = sources(sent[d], d + 1)
-        state = [
-            table[1, n] * state[n] + (sent[d][n] + table[2, n] * u0 + table[3, n] * u1)
-            for n in range(modes)
-        ]
-    heads = edge(taps, 0, query[0], query[1], *rim(0, 0))
-    for t, u in enumerate(sources(local, 0)):
+        end = chips[d].complete(
+            taps,
+            rims[d + 1],
+            [a * b for a, b in zip(block, less_one)],
+            [a * b for a, b in zip(block, less_two)],
+        )
+        state = [d * d * x + y for d, x, y in zip(block, state, end)]
+    before = Summary.read(partner, modes)
+    end = before.complete(taps, rims[0], less_one, less_two)
+    state = [jnp.where(odd, d * x + y, x) for d, x, y in zip(block, state, end)]
+    rim = [jnp.where(odd, a, b) for a, b in zip(before.rims, rims[0])]
+
+    leads = lead_sources(taps, Summary.read(local, modes).heads, rim)
+    heads = edge(taps, 0, query[0], query[1], rim[0], rim[1])
+    for t, u in enumerate(leads):
         state = [table[0, n] * state[n] + u for n in range(modes)]
         work[t] = heads[t] * tree_sum([table[4, n] * state[n] for n in range(modes)])
     carried = [table[4, n] * state[n] for n in range(modes)]
@@ -340,8 +391,17 @@
         name="project_last",
     )(fore, aft, weights, taps, table, total)
 
+    partner = lax.ppermute(local, "ctx", [(j, j ^ 1) for j in range(ctx)])
+    chip = pl.pallas_call(
+        chip_kernel,
+        out_shape=f32(modes + EDGE, groups, LANES),
+        in_specs=[VMEM] * 4,
+        out_specs=VMEM,
+        compiler_params=params,
+        name="chip_state",
+    )(local, partner, taps, table)
     sent = [
-        lax.ppermute(local, "ctx", [(j, j + d) for j in range(ctx - d)]) for d in range(1, ctx)
+        lax.ppermute(chip, "ctx", [(j, j + d) for j in range(ctx - d)]) for d in range(2, ctx, 2)
     ]
     query, response = pl.pallas_call(
         local_kernel,
@@ -356,12 +416,12 @@
     return pl.pallas_call(
         functools.partial(final_kernel, len(sent)),
         out_shape=jax.ShapeDtypeStruct((rows, chans), jnp.bfloat16),
-        in_specs=[VMEM] * (len(sent) + 5),
+        in_specs=[VMEM] * (len(sent) + 6),
         out_specs=VMEM,
         scratch_shapes=[pltpu.VMEM((rows, groups, LANES), jnp.float32)],
         compiler_params=params,
         name="carried_response",
-    )(*sent, local, query, response, taps, table)
+    )(*sent, local, partner, query, response, taps, table)
 
 
 def solution(mesh):

time: 47.9 us -> 46.3 us (0.967)
  waiting for transfers between devices: 1.32 us -> 7.38 us
  Pallas kernels: 30 us -> 25 us
  starting transfers between devices: 15.2 us -> 12.7 us
    pallas_call x3, Pallas kernels: 17.4 us -> 12.3 us  [on_device(): pl.pallas_call(functools.partial(second_kernel if with_tables else middle...]
    ppermute x3 -> x2, starting transfers between devices: 5.99 us -> 3.48 us  [the longest x1 3.41 us: on_device(): lax.ppermute(chip, 'ctx', [(j, j + d) for j in range(ctx - d)])]
    ppermute x3, waiting for transfers between devices: 0.76 us -> 2.91 us  [on_device(): aft = lax.ppermute(aft, 'tp', back)]
    ppermute x1, waiting for transfers between devices: 0.01 us -> 1.62 us  [on_device(): aft = lax.ppermute(aft[rows // 2:], 'tp', back)]
    ppermute x3 -> x2, waiting for transfers between devices: 0.55 us -> 2.12 us  [the longest x1 1.3 us: on_device(): partner = lax.ppermute(local, 'ctx', [(j, j ^ 1) for j in range(ctx)])]
    ppermute x3, waiting for transfers between devices: 0.01 us -> 0.73 us  [on_device(): fore = lax.ppermute(fore, 'tp', ahead)]
  transfers between devices with their start and end apart: 11 -> 10, of which waited for: 3 -> 7; matrix products, arithmetic and copies ran while one was open for 0% -> 0% of each run, Pallas kernels for 54% -> 45%
where the time goes in v3:
time: 46.3 us; the launch traced here: 46.2 us
  Pallas kernels  25 us (54%)
  starting transfers between devices  12.7 us (27%)
  waiting for transfers between devices  7.38 us (16%)
  local copies, waits for them, and re-layouts  1.03 us (2%)
    pallas_call x3, Pallas kernels, on_device(): pl.pallas_call(functools.partial(second_kernel if with_tables else middle...  12.3 us
    pallas_call x1, Pallas kernels, on_device(): pl.pallas_call(functools.partial(first_kernel, order, loads(1)), out_shap...  6.57 us
    ppermute x3, starting transfers between devices, on_device(): fore = lax.ppermute(fore, 'tp', ahead)  6.23 us
    ppermute x1, starting transfers between devices, on_device(): lax.ppermute(chip, 'ctx', [(j, j + d) for j in range(ctx - d)])  3.41 us
    ppermute x3, waiting for transfers between devices, on_device(): aft = lax.ppermute(aft, 'tp', back)  2.91 us
    pallas_call x1, Pallas kernels, on_device(): pl.pallas_call(last_kernel, out_shape=[sums, wide, f32(modes + EDGE, grou...  2.4 us
    pallas_call x1, Pallas kernels, on_device(): pl.pallas_call(functools.partial(final_kernel, len(sent)), out_shape=jax....  1.95 us
    pallas_call x1, Pallas kernels, on_device(): pl.pallas_call(local_kernel, out_shape=[wide, wide], in_specs=[VMEM] * 4,...  1.7 us
  transfers between devices with their start and end apart: 10, of which 7 were waited for; matrix products, arithmetic and copies ran while one was open for 0% of the time, Pallas kernels for 45%

profile of v3, /device:TPU:0, one launch (start us, length us, event | category | flops | bytes accessed | tf_op | source)
XLA Modules:
  0.0 46.2 jit_solution(7861998177416701958)
XLA Ops:
  0.0 3.0 %collective-permute-start = (bf16[128,1024]{1,0:T(8,128)(2,1)}, bf16[128,1024]{1,0:T(8,128)(2,1)S(1)}, u32[]{:S(2)}, u32[]{:S(2)}) collective-permute-start(bf16[128,1024]{1,0:T(8,128)(2,1)} %x_ref.1), channel_id=1, source_target_pairs={{0,1},{1,3},{3,5},{5,7},{7,6},{6,4},{4,2},{2,0},{8,9},{9,11},{11,1... | collective-permute-start | bytes 786440 | tf_op jit(solution)/shard_map/ppermute | solution.py:358
  3.0 0.1 collective-permute-start.1
  3.0 0.0 copy-start
  3.0 1.0 %copy-done = bf16[128,1024]{1,0:T(8,128)(2,1)S(1)} copy-done((bf16[128,1024]{1,0:T(8,128)(2,1)S(1)}, bf16[128,1024]{1,0:T(8,128)(2,1)}, u32[]{:S(2)}) %copy-start) | copy-done | bytes 262168
  4.0 6.6 %project_own.1 = (f32[3,128,1024]{2,1,0:T(8,128)S(1)}, bf16[2,3,1024,1024]{3,2,1,0:T(8,128)(2,1)S(1)}) custom-call(bf16[128,1024]{1,0:T(8,128)(2,1)S(1)} %copy-done, bf16[3,8192,1024]{2,1,0:T(8,128)(2,1)} %bitcast.1), custom_call_target="tpu_custom_call" | custom-call | bytes 16777216 | tf_op jit(solution)/shard_map/project_own/pallas_call | solution.py:342
  10.6 0.0 collective-permute-done.xa_ref
  10.6 0.3 collective-permute-done.1.xb_ref
  10.9 1.7 %collective-permute-start.2 = (bf16[128,1024]{1,0:T(8,128)(2,1)S(1)}, bf16[128,1024]{1,0:T(8,128)(2,1)S(1)}, u32[]{:S(2)}, u32[]{:S(2)}) collective-permute-start(bf16[128,1024]{1,0:T(8,128)(2,1)S(1)} %collective-permute-done.xa_ref), channel_id=1, source_target_pairs={{0,1},{1,3},{3,5},{5,7},{7,6},{6,4},{4,2},{2,0},{8,9},{9,11},{11,1... | collective-permute-start | bytes 786440 | tf_op jit(solution)/shard_map/ppermute | solution.py:358
  12.6 0.3 collective-permute-start.3
  13.0 0.0 copy-done.1
  13.0 0.0 copy-done.2
  13.0 0.0 copy-done.3
  13.0 4.7 %project_pair.3 = (f32[3,128,1024]{2,1,0:T(8,128)S(1)}, bf16[2,3,1024,1024]{3,2,1,0:T(8,128)(2,1)S(1)}, f32[3,3,8,128]{3,2,1,0:T(8,128)S(1)}, f32[5,16,8,128]{3,2,1,0:T(8,128)S(1)}) custom-call(bf16[128,1024]{1,0:T(8,128)(2,1)S(1)} %collective-permute-done.xa_ref, ...), custom_call_target="tpu_custom_call", output_to_operand_aliasing={{0}: (4, {})} | custom-call | bytes 16777216 | tf_op jit(solution)/shard_map/project_pair/pallas_call | solution.py:364
  17.7 0.7 %collective-permute-done.2.xa_ref = bf16[128,1024]{1,0:T(8,128)(2,1)S(1)} collective-permute-done((bf16[128,1024]{1,0:T(8,128)(2,1)S(1)}, bf16[128,1024]{1,0:T(8,128)(2,1)S(1)}, u32[]{:S(2)}, u32[]{:S(2)}) %collective-permute-start.2) | collective-permute-done | bytes 262176 | tf_op jit(solution)/shard_map/ppermute | solution.py:358
  18.4 1.4 %collective-permute-done.3.xb_ref = bf16[128,1024]{1,0:T(8,128)(2,1)S(1)} collective-permute-done((bf16[128,1024]{1,0:T(8,128)(2,1)S(1)}, bf16[128,1024]{1,0:T(8,128)(2,1)S(1)}, u32[]{:S(2)}, u32[]{:S(2)}) %collective-permute-start.3) | collective-permute-done | bytes 262176 | tf_op jit(solution)/shard_map/ppermute | solution.py:359
  19.8 1.6 %collective-permute-start.4 = (bf16[128,1024]{1,0:T(8,128)(2,1)S(1)}, bf16[128,1024]{1,0:T(8,128)(2,1)S(1)}, u32[]{:S(2)}, u32[]{:S(2)}) collective-permute-start(bf16[128,1024]{1,0:T(8,128)(2,1)S(1)} %collective-permute-done.2.xa_ref), channel_id=1, source_target_pairs={{0,1},{1,3},{3,5},{5,7},{7,6},{6,4},{4,2},{2,0},{8,9},{9,11},{11,1... | collective-permute-start | bytes 786440 | tf_op jit(solution)/shard_map/ppermute | solution.py:358
  21.4 0.4 collective-permute-start.5
  21.9 4.7 %project_pair.4 = (f32[3,128,1024]{2,1,0:T(8,128)S(1)}, bf16[2,3,1024,1024]{3,2,1,0:T(8,128)(2,1)S(1)}) custom-call(bf16[128,1024]{1,0:T(8,128)(2,1)S(1)} %collective-permute-done.2.xa_ref, bf16[128,1024]{1,0:T(8,128)(2,1)S(1)} %collective-permute-done.3.xb_ref, ...), custom_call_target="tpu_custom_call", output_to_operand_aliasing={{0}: (4, {})} | custom-call | bytes 16777216 | tf_op jit(solution)/shard_map/project_pair/pallas_call | solution.py:364
  26.6 0.0 collective-permute-done.4.xa_ref
  26.6 1.2 %collective-permute-done.5.xb_ref = bf16[128,1024]{1,0:T(8,128)(2,1)S(1)} collective-permute-done((bf16[128,1024]{1,0:T(8,128)(2,1)S(1)}, bf16[128,1024]{1,0:T(8,128)(2,1)S(1)}, u32[]{:S(2)}, u32[]{:S(2)}) %collective-permute-start.5) | collective-permute-done | bytes 262176 | tf_op jit(solution)/shard_map/ppermute | solution.py:359
  27.8 1.6 %collective-permute-start.6 = (bf16[64,1024]{1,0:T(8,128)(2,1)S(1)}, bf16[64,1024]{1,0:T(8,128)(2,1)S(1)}, u32[]{:S(2)}, u32[]{:S(2)}) collective-permute-start(bf16[64,1024]{1,0:T(8,128)(2,1)S(1)} %slice.6), channel_id=1, source_target_pairs={{0,1},{1,3},{3,5},{5,7},{7,6},{6,4},{4,2},{2,0},{8,9},{9,11},{11,1... | collective-permute-start | bytes 393224 | tf_op jit(solution)/shard_map/ppermute | solution.py:377
  29.4 0.5 %collective-permute-start.7 = (bf16[64,1024]{1,0:T(8,128)(2,1)S(1)}, bf16[64,1024]{1,0:T(8,128)(2,1)S(1)}, u32[]{:S(2)}, u32[]{:S(2)}) collective-permute-start(bf16[64,1024]{1,0:T(8,128)(2,1)S(1)} %slice.7), channel_id=1, source_target_pairs={{1,0},{3,1},{5,3},{7,5},{6,7},{4,6},{2,4},{0,2},{9,8},{11,9},{13,1... | collective-permute-start | bytes 393224 | tf_op jit(solution)/shard_map/ppermute | solution.py:378
  29.9 2.9 %project_pair.5 = (f32[3,128,1024]{2,1,0:T(8,128)S(1)}, bf16[1,3,1024,1024]{3,2,1,0:T(8,128)(2,1)S(1)}) custom-call(bf16[128,1024]{1,0:T(8,128)(2,1)S(1)} %collective-permute-done.4.xa_ref, bf16[128,1024]{1,0:T(8,128)(2,1)S(1)} %collective-permute-done.5.xb_ref, ...), custom_call_target="tpu_custom_call", output_to_operand_aliasing={{0}: (4, {})} | custom-call | bytes 16777216 | tf_op jit(solution)/shard_map/project_pair/pallas_call | solution.py:364
  32.8 0.0 collective-permute-done.6.xa_ref
  32.8 1.6 %collective-permute-done.7.xb_ref = bf16[64,1024]{1,0:T(8,128)(2,1)S(1)} collective-permute-done((bf16[64,1024]{1,0:T(8,128)(2,1)S(1)}, bf16[64,1024]{1,0:T(8,128)(2,1)S(1)}, u32[]{:S(2)}, u32[]{:S(2)}) %collective-permute-start.7) | collective-permute-done | bytes 131104 | tf_op jit(solution)/shard_map/ppermute | solution.py:378
  34.5 2.4 %project_last.1 = (f32[3,128,1024]{2,1,0:T(8,128)S(1)}, f32[128,8,128]{2,1,0:T(8,128)S(1)}, f32[26,8,128]{2,1,0:T(8,128)S(1)}) custom-call(bf16[64,1024]{1,0:T(8,128)(2,1)S(1)} %collective-permute-done.6.xa_ref, bf16[64,1024]{1,0:T(8,128)(2,1)S(1)} %collective-permute-done.7.xb_ref, ...), custom_call_target="tpu_custom_call", output_to_operand_aliasing={{0}: (5, {})} | custom-call | bytes 16777216 | tf_op jit(solution)/shard_map/project_last/pallas_call | solution.py:379
  36.9 0.1 collective-permute-start.8
  37.0 1.3 %collective-permute-done.8.partner.refs_2_ = f32[26,8,128]{2,1,0:T(8,128)S(1)} collective-permute-done((f32[26,8,128]{2,1,0:T(8,128)S(1)}, f32[26,8,128]{2,1,0:T(8,128)S(1)}, u32[]{:S(2)}, u32[]{:S(2)}) %collective-permute-start.8) | collective-permute-done | bytes 106528 | tf_op jit(solution)/shard_map/ppermute | solution.py:394
  38.3 3.4 %collective-permute-start.9 = (f32[26,8,128]{2,1,0:T(8,128)S(1)}, f32[26,8,128]{2,1,0:T(8,128)S(1)}, u32[]{:S(2)}, u32[]{:S(2)}) collective-permute-start(f32[26,8,128]{2,1,0:T(8,128)S(1)} %chip_state.1), channel_id=1, source_target_pairs={{0,16},{8,24},{1,17},{9,25},{2,18},{10,26},{3,19},{11,27},{4,20},{... | collective-permute-start | bytes 319496 | tf_op jit(solution)/shard_map/ppermute | solution.py:404
  41.7 1.7 %local_response.1 = (f32[128,8,128]{2,1,0:T(8,128)S(1)}, f32[128,8,128]{2,1,0:T(8,128)S(1)}) custom-call(f32[3,128,1024]{2,1,0:T(8,128)S(1)} %get-tuple-element.55.total, f32[128,8,128]{2,1,0:T(8,128)S(1)} %get-tuple-element.56.source, f32[3,3,8,128]{3,2,1,0:T(8,128)S(1)} %get-tuple-element.51.taps.refs_5_, f32[5,16,8,128]{3,2,1,0:T(8,128)S(1)} %get-tuple-element.52.table.refs_6_), custom_call_target="tpu_custom_call" | custom-call | bytes 16777216 | tf_op jit(solution)/shard_map/local_response/pallas_call | solution.py:406
  43.4 0.8 %collective-permute-done.9.refs_0_ = f32[26,8,128]{2,1,0:T(8,128)S(1)} collective-permute-done((f32[26,8,128]{2,1,0:T(8,128)S(1)}, f32[26,8,128]{2,1,0:T(8,128)S(1)}, u32[]{:S(2)}, u32[]{:S(2)}) %collective-permute-start.9) | collective-permute-done | bytes 106528 | tf_op jit(solution)/shard_map/ppermute | solution.py:404
  44.2 1.9 %carried_response.1 = bf16[128,1024]{1,0:T(8,128)(2,1)} custom-call(f32[26,8,128]{2,1,0:T(8,128)S(1)} %collective-permute-done.9.refs_0_, f32[26,8,128]{2,1,0:T(8,128)S(1)} %get-tuple-element.54.local.refs_1_, f32[26,8,128]{2,1,0:T(8,128)S(1)} %collective-permute-done.8.partner.refs_2_, f32[128,8,128]{2,1,0:T(8,128)S(1)} %get-tuple-element.57.refs_3_, ...), custom_call_target="tpu_custom_call" | custom-call | tf_op jit(solution)/shard_map/carried_response/pallas_call | solution.py:416
  (6 shorter events, 0.1 us)
Async XLA Ops:
  0.0 10.6 %collective-permute-start = (bf16[128,1024]{1,0:T(8,128)(2,1)}, bf16[128,1024]{1,0:T(8,128)(2,1)S(1)}, u32[]{:S(2)}, u32[]{:S(2)}) collective-permute-start(bf16[128,1024]{1,0:T(8,128)(2,1)} %x_ref.1), channel_id=1, source_target_pairs={{0,1},{1,3},{3,5},{5,7},{7,6},{6,4},{4,2},{2,0},{8,9},{9,11},{11,1... | collective-permute-start | bytes 786440 | tf_op jit(solution)/shard_map/ppermute | solution.py:358
  3.0 8.0 %collective-permute-start.1 = (bf16[128,1024]{1,0:T(8,128)(2,1)}, bf16[128,1024]{1,0:T(8,128)(2,1)S(1)}, u32[]{:S(2)}, u32[]{:S(2)}) collective-permute-start(bf16[128,1024]{1,0:T(8,128)(2,1)} %x_ref.1), channel_id=1, source_target_pairs={{1,0},{3,1},{5,3},{7,5},{6,7},{4,6},{2,4},{0,2},{9,8},{11,9},{13,1... | collective-permute-start | bytes 786440 | tf_op jit(solution)/shard_map/ppermute | solution.py:359
  3.0 1.0 %copy-start = (bf16[128,1024]{1,0:T(8,128)(2,1)S(1)}, bf16[128,1024]{1,0:T(8,128)(2,1)}, u32[]{:S(2)}) copy-start(bf16[128,1024]{1,0:T(8,128)(2,1)} %x_ref.1) | copy-start | bytes 786436
  4.0 8.9 %copy-start.1 = (f32[16,1024]{1,0:T(8,128)S(1)}, f32[16,1024]{1,0:T(8,128)}, u32[]{:S(2)}) copy-start(f32[16,1024]{1,0:T(8,128)} %decay.1) | copy-start | bytes 196612
  4.0 8.9 %copy-start.2 = (f32[16,1024]{1,0:T(8,128)S(1)}, f32[16,1024]{1,0:T(8,128)}, u32[]{:S(2)}) copy-start(f32[16,1024]{1,0:T(8,128)} %residue.1) | copy-start | bytes 196612
  4.0 8.9 %copy-start.3 = (f32[3,3,1024]{2,1,0:T(4,128)S(1)}, f32[3,3,1024]{2,1,0:T(4,128)}, u32[]{:S(2)}) copy-start(f32[3,3,1024]{2,1,0:T(4,128)} %taps_in.1) | copy-start | bytes 110596
  10.9 7.5 %collective-permute-start.2 = (bf16[128,1024]{1,0:T(8,128)(2,1)S(1)}, bf16[128,1024]{1,0:T(8,128)(2,1)S(1)}, u32[]{:S(2)}, u32[]{:S(2)}) collective-permute-start(bf16[128,1024]{1,0:T(8,128)(2,1)S(1)} %collective-permute-done.xa_ref), channel_id=1, source_target_pairs={{0,1},{1,3},{3,5},{5,7},{7,6},{6,4},{4,2},{2,0},{8,9},{9,11},{11,1... | collective-permute-start | bytes 786440 | tf_op jit(solution)/shard_map/ppermute | solution.py:358
  12.6 7.2 %collective-permute-start.3 = (bf16[128,1024]{1,0:T(8,128)(2,1)S(1)}, bf16[128,1024]{1,0:T(8,128)(2,1)S(1)}, u32[]{:S(2)}, u32[]{:S(2)}) collective-permute-start(bf16[128,1024]{1,0:T(8,128)(2,1)S(1)} %collective-permute-done.1.xb_ref), channel_id=1, source_target_pairs={{1,0},{3,1},{5,3},{7,5},{6,7},{4,6},{2,4},{0,2},{9,8},{11,9},{13,1... | collective-permute-start | bytes 786440 | tf_op jit(solution)/shard_map/ppermute | solution.py:359
  19.8 6.7 %collective-permute-start.4 = (bf16[128,1024]{1,0:T(8,128)(2,1)S(1)}, bf16[128,1024]{1,0:T(8,128)(2,1)S(1)}, u32[]{:S(2)}, u32[]{:S(2)}) collective-permute-start(bf16[128,1024]{1,0:T(8,128)(2,1)S(1)} %collective-permute-done.2.xa_ref), channel_id=1, source_target_pairs={{0,1},{1,3},{3,5},{5,7},{7,6},{6,4},{4,2},{2,0},{8,9},{9,11},{11,1... | collective-permute-start | bytes 786440 | tf_op jit(solution)/shard_map/ppermute | solution.py:358
  21.4 6.4 %collective-permute-start.5 = (bf16[128,1024]{1,0:T(8,128)(2,1)S(1)}, bf16[128,1024]{1,0:T(8,128)(2,1)S(1)}, u32[]{:S(2)}, u32[]{:S(2)}) collective-permute-start(bf16[128,1024]{1,0:T(8,128)(2,1)S(1)} %collective-permute-done.3.xb_ref), channel_id=1, source_target_pairs={{1,0},{3,1},{5,3},{7,5},{6,7},{4,6},{2,4},{0,2},{9,8},{11,9},{13,1... | collective-permute-start | bytes 786440 | tf_op jit(solution)/shard_map/ppermute | solution.py:359
  27.8 5.0 %collective-permute-start.6 = (bf16[64,1024]{1,0:T(8,128)(2,1)S(1)}, bf16[64,1024]{1,0:T(8,128)(2,1)S(1)}, u32[]{:S(2)}, u32[]{:S(2)}) collective-permute-start(bf16[64,1024]{1,0:T(8,128)(2,1)S(1)} %slice.6), channel_id=1, source_target_pairs={{0,1},{1,3},{3,5},{5,7},{7,6},{6,4},{4,2},{2,0},{8,9},{9,11},{11,1... | collective-permute-start | bytes 393224 | tf_op jit(solution)/shard_map/ppermute | solution.py:377
  29.4 5.0 %collective-permute-start.7 = (bf16[64,1024]{1,0:T(8,128)(2,1)S(1)}, bf16[64,1024]{1,0:T(8,128)(2,1)S(1)}, u32[]{:S(2)}, u32[]{:S(2)}) collective-permute-start(bf16[64,1024]{1,0:T(8,128)(2,1)S(1)} %slice.7), channel_id=1, source_target_pairs={{1,0},{3,1},{5,3},{7,5},{6,7},{4,6},{2,4},{0,2},{9,8},{11,9},{13,1... | collective-permute-start | bytes 393224 | tf_op jit(solution)/shard_map/ppermute | solution.py:378
  36.9 1.4 %collective-permute-start.8 = (f32[26,8,128]{2,1,0:T(8,128)S(1)}, f32[26,8,128]{2,1,0:T(8,128)S(1)}, u32[]{:S(2)}, u32[]{:S(2)}) collective-permute-start(f32[26,8,128]{2,1,0:T(8,128)S(1)} %get-tuple-element.54.local.refs_1_), channel_id=1, source_target_pairs={{0,8},{8,0},{16,24},{24,16},{1,9},{9,1},{17,25},{25,17},{2,10},{10... | collective-permute-start | bytes 319496 | tf_op jit(solution)/shard_map/ppermute | solution.py:394
  38.3 5.9 %collective-permute-start.9 = (f32[26,8,128]{2,1,0:T(8,128)S(1)}, f32[26,8,128]{2,1,0:T(8,128)S(1)}, u32[]{:S(2)}, u32[]{:S(2)}) collective-permute-start(f32[26,8,128]{2,1,0:T(8,128)S(1)} %chip_state.1), channel_id=1, source_target_pairs={{0,16},{8,24},{1,17},{9,25},{2,18},{10,26},{3,19},{11,27},{4,20},{... | collective-permute-start | bytes 319496 | tf_op jit(solution)/shard_map/ppermute | solution.py:404

commit v4 on v3

--- a/solution.py
+++ b/solution.py
@@ -12,6 +12,8 @@
 DEPTH = 256
 GRID_ROWS = 4
 EDGE = 10
+EARLY = 2
+PIECE = 32
 VMEM = pl.BlockSpec(memory_space=pltpu.VMEM)
 HBM = pl.BlockSpec(memory_space=pltpu.HBM)
 
@@ -36,37 +38,34 @@
     return owner
 
 
-def block_loads(order, steps, w_ref, held, sem):
-    count, streams, width, _ = held.shape
+def block_loads(order, steps, w_ref, held, sem, first=0):
+    _, streams, width, _ = held.shape
     copies = []
     for b, step in enumerate(steps):
         start = pl.multiple_of(owner_at(order, step) * width, width)
         for s in range(streams):
             copies.append(
                 pltpu.make_async_copy(
-                    w_ref.at[s, pl.ds(start, width), :], held.at[b, s], sem.at[b, s]
+                    w_ref.at[first + s, pl.ds(start, width), :], held.at[b, s], sem.at[b, s]
                 )
             )
     return copies
 
 
-def add_products(xs, held, total, s):
+def add_products(xs, held, total, s, first=0):
     for c in range(0, total.shape[2], COLS):
         at = slice(c, c + COLS)
         terms = [
             jnp.dot(x, held[b, s, :, at], preferred_element_type=jnp.float32)
             for b, x in enumerate(xs)
         ]
-        total[s, :, at] += sum(terms)
-
-
-def multiply_beside(loads, xa_ref, xb_ref, held, total):
-    @pl.loop(0, total.shape[0])
+        total[first + s, :, at] += sum(terms)
+
+
+def add_held(xa_ref, xb_ref, held, total):
+    @pl.loop(0, held.shape[1])
     def _(s):
         add_products([xa_ref[...], xb_ref[...]], held, total, s)
-
-    for copy in loads:
-        copy.wait()
 
 
 def spread(out_ref, value):
@@ -109,15 +108,19 @@
     ahead = block_loads(order, steps, w_ref, next_held, sem)
     for copy in ahead:
         copy.start()
-    multiply_beside(ahead, xa_ref, xb_ref, held, total)
+    add_held(xa_ref, xb_ref, held, total)
+    for copy in ahead:
+        copy.wait()
 
 
 def second_kernel(
-    order, steps, xa_ref, xb_ref, held, w_ref, _, taps_in, decay, residue,
-    total, next_held, taps, table, sem,
+    order, here, steps, xa_ref, xb_ref, held, w_ref, _, taps_in, decay, residue,
+    total, next_held, taps, table, rest, rest_sem, sem,
 ):
+    first = held.shape[1]
+    late = block_loads(order, here, w_ref, rest, rest_sem, first)
     ahead = block_loads(order, steps, w_ref, next_held, sem)
-    for copy in ahead:
+    for copy in late + ahead:
         copy.start()
     rate = decay[...]
     rows = total.shape[1]
@@ -125,7 +128,13 @@
         spread(table.at[i], jnp.exp(-rate * power))
     spread(table.at[4], residue[...] * jnp.sqrt(1.0 - jnp.exp(-2.0 * rate)))
     spread(taps, taps_in[...])
-    multiply_beside(ahead, xa_ref, xb_ref, held, total)
+    add_held(xa_ref, xb_ref, held, total)
+    for copy in late:
+        copy.wait()
+    for s in range(rest.shape[1]):
+        add_products([xa_ref[...], xb_ref[...]], rest, total, s, first)
+    for copy in ahead:
+        copy.wait()
 
 
 def filtered(taps, p_ref, s, t):
@@ -248,38 +257,46 @@
     return [[table[i, n] for n in range(table.shape[1])] for i in range(table.shape[0])]
 
 
-def chip_kernel(local, partner, taps, table, out_ref):
+def chip_kernel(lone, local, partner, taps, table, out_ref):
     modes = table.shape[1]
     odd = lax.rem(lax.axis_index("ctx"), 2) == 1
     mine, other = Summary.read(local, modes), Summary.read(partner, modes)
     first = Summary.chosen(odd, other, mine, modes)
     second = Summary.chosen(odd, mine, other, modes)
     _, block, less_one, less_two, _ = powers(table)
+    start, heads = first.state, first.heads
+    if lone:
+        start, heads = first.complete(taps, [jnp.zeros_like(heads[0])] * 6, less_one, less_two), []
     end = second.complete(taps, first.rims, less_one, less_two)
-    joined = [d * x + y for d, x, y in zip(block, first.state, end)]
-    for i, value in enumerate(joined + first.heads + second.rims):
+    joined = [d * x + y for d, x, y in zip(block, start, end)]
+    for i, value in enumerate(joined + heads + second.rims):
         out_ref[i] = value
 
 
-def final_kernel(count, *refs):
+def final_kernel(lone, count, *refs):
     sent = refs[:count]
-    local, partner, query, response, taps, table, out_ref, work = refs[count:]
+    local, partner, query, response, taps, table, out_ref, work, rounded_out, out_sem = refs[count:]
     rows, groups, lanes = query.shape
     modes = table.shape[1]
-    nothing = [jnp.zeros((groups, lanes), jnp.float32)] * 6
-    odd = lax.rem(lax.axis_index("ctx"), 2) == 1
+    zero = jnp.zeros((groups, lanes), jnp.float32)
+    index = lax.axis_index("ctx")
+    odd = lax.rem(index, 2) == 1
     _, block, less_one, less_two, _ = powers(table)
-    chips = [Summary.read(ref, modes) for ref in sent]
-    rims = [chip.rims for chip in chips] + [nothing]
-
-    state = [nothing[0]] * modes
+    values = [
+        [jnp.where(index >= 2 * (d + 1), ref[i], zero) for i in range(ref.shape[0])]
+        for d, ref in enumerate(sent)
+    ]
+    rims = [value[-6:] for value in values] + [[zero] * 6]
+    state = [zero] * modes
     for d in reversed(range(count)):
-        end = chips[d].complete(
-            taps,
-            rims[d + 1],
-            [a * b for a, b in zip(block, less_one)],
-            [a * b for a, b in zip(block, less_two)],
-        )
+        end = values[d][:modes]
+        if not lone:
+            end = Summary(values[d], modes).complete(
+                taps,
+                rims[d + 1],
+                [a * b for a, b in zip(block, less_one)],
+                [a * b for a, b in zip(block, less_two)],
+            )
         state = [d * d * x + y for d, x, y in zip(block, state, end)]
     before = Summary.read(partner, modes)
     end = before.complete(taps, rims[0], less_one, less_two)
@@ -298,17 +315,24 @@
         work[t] = query[t] * (response[t] + tree_sum(carried))
         return carried
 
-    for t in range(2, 8):
-        carried = row(t, carried)
-
     def eight(i, carried):
         for j in range(8):
             carried = row(i * 8 + j, carried)
         return carried
 
-    lax.fori_loop(1, rows // 8, eight, carried)
-    for g in range(groups):
-        out_ref[:, g * lanes : (g + 1) * lanes] = work[:, g, :].astype(out_ref.dtype)
+    for t in range(2, 8):
+        carried = row(t, carried)
+    copies = []
+    for i in range(rows // PIECE):
+        at = slice(i * PIECE, (i + 1) * PIECE)
+        first = 0 if i else 1
+        carried = lax.fori_loop(i * PIECE // 8 + first, (i + 1) * PIECE // 8, eight, carried)
+        for g in range(groups):
+            rounded_out[at, g * lanes : (g + 1) * lanes] = work[at, g, :].astype(out_ref.dtype)
+        copies.append(pltpu.make_async_copy(rounded_out.at[at], out_ref.at[at], out_sem.at[i]))
+        copies[-1].start()
+    for copy in copies:
+        copy.wait()
 
 
 def on_device(tokens, in_weight, filter_taps, decay_rate, residue):
@@ -327,7 +351,7 @@
     def f32(*shape):
         return jax.ShapeDtypeStruct(shape, jnp.float32)
 
-    def held(count):
+    def held(count, streams=streams):
         return jax.ShapeDtypeStruct((count, streams, width, chans), jnp.bfloat16)
 
     def loads(step):
@@ -341,13 +365,13 @@
     depth = min(DEPTH, width)
     total, weights = pl.pallas_call(
         functools.partial(first_kernel, order, loads(1)),
-        out_shape=[sums, held(len(loads(1)))],
+        out_shape=[sums, held(2, EARLY)],
         in_specs=[VMEM, HBM],
         out_specs=[VMEM] * 2,
         scratch_shapes=[
             pltpu.VMEM((streams, width, chans), jnp.bfloat16),
             pltpu.SemaphoreType.DMA((width // depth,)),
-            pltpu.SemaphoreType.DMA((len(loads(1)), streams)),
+            pltpu.SemaphoreType.DMA((2, EARLY)),
         ],
         compiler_params=params,
         cost_estimate=cost,
@@ -359,20 +383,27 @@
         aft = lax.ppermute(aft, "tp", back)
         fore, aft, total, weights = lax.optimization_barrier((fore, aft, total, weights))
         coming = loads(step + 1)
-        tables = [f32(lags, streams, groups, LANES), f32(5, modes, groups, LANES)]
-        with_tables = step == 1
+        body, extra, made, scratch = functools.partial(middle_kernel, order), [], [], []
+        if step == 1:
+            body = functools.partial(second_kernel, order, loads(1))
+            extra = [filter_taps, decay_rate, residue]
+            made = [f32(lags, streams, groups, LANES), f32(5, modes, groups, LANES)]
+            scratch = [
+                pltpu.VMEM((2, streams - EARLY, width, chans), jnp.bfloat16),
+                pltpu.SemaphoreType.DMA((2, streams - EARLY)),
+            ]
         total, weights, *made = pl.pallas_call(
-            functools.partial(second_kernel if with_tables else middle_kernel, order, coming),
-            out_shape=[sums, held(len(coming))] + tables * with_tables,
-            in_specs=[VMEM, VMEM, VMEM, HBM, VMEM] + [VMEM] * 3 * with_tables,
-            out_specs=[VMEM, VMEM] + [VMEM] * 2 * with_tables,
-            scratch_shapes=[pltpu.SemaphoreType.DMA((len(coming), streams))],
+            functools.partial(body, coming),
+            out_shape=[sums, held(len(coming))] + made,
+            in_specs=[VMEM, VMEM, VMEM, HBM, VMEM] + [VMEM] * len(extra),
+            out_specs=[VMEM] * (2 + len(made)),
+            scratch_shapes=scratch + [pltpu.SemaphoreType.DMA((len(coming), streams))],
             input_output_aliases={4: 0},
             compiler_params=params,
             cost_estimate=cost,
             name="project_pair",
-        )(fore, aft, weights, weight, total, *[filter_taps, decay_rate, residue][: 3 * with_tables])
-        if with_tables:
+        )(fore, aft, weights, weight, total, *extra)
+        if made:
             taps, table = made
     fore = lax.ppermute(fore[: rows // 2], "tp", ahead)
     aft = lax.ppermute(aft[rows // 2 :], "tp", back)
@@ -392,16 +423,18 @@
     )(fore, aft, weights, taps, table, total)
 
     partner = lax.ppermute(local, "ctx", [(j, j ^ 1) for j in range(ctx)])
+    lone = ctx == 4
     chip = pl.pallas_call(
-        chip_kernel,
-        out_shape=f32(modes + EDGE, groups, LANES),
+        functools.partial(chip_kernel, lone),
+        out_shape=f32(modes + (6 if lone else EDGE), groups, LANES),
         in_specs=[VMEM] * 4,
         out_specs=VMEM,
         compiler_params=params,
         name="chip_state",
     )(local, partner, taps, table)
     sent = [
-        lax.ppermute(chip, "ctx", [(j, j + d) for j in range(ctx - d)]) for d in range(2, ctx, 2)
+        lax.ppermute(chip, "ctx", [(j, (j + d) % ctx) for j in range(ctx)])
+        for d in range(2, ctx, 2)
     ]
     query, response = pl.pallas_call(
         local_kernel,
@@ -414,11 +447,15 @@
         name="local_response",
     )(total, source, taps, table)
     return pl.pallas_call(
-        functools.partial(final_kernel, len(sent)),
+        functools.partial(final_kernel, lone, len(sent)),
         out_shape=jax.ShapeDtypeStruct((rows, chans), jnp.bfloat16),
         in_specs=[VMEM] * (len(sent) + 6),
-        out_specs=VMEM,
-        scratch_shapes=[pltpu.VMEM((rows, groups, LANES), jnp.float32)],
+        out_specs=HBM,
+        scratch_shapes=[
+            pltpu.VMEM((rows, groups, LANES), jnp.float32),
+            pltpu.VMEM((rows, chans), jnp.bfloat16),
+            pltpu.SemaphoreType.DMA((rows // PIECE,)),
+        ],
         compiler_params=params,
         name="carried_response",
     )(*sent, local, partner, query, response, taps, table)

time: 46.3 us -> 45 us (0.972)
  starting transfers between devices: 12.7 us -> 10.8 us
  Pallas kernels: 25 us -> 25.8 us
    pallas_call x5, Pallas kernels: 14.3 us -> 16.3 us  [the longest x3 14.4 us: on_device(): pl.pallas_call(functools.partial(body, coming), out_shape=[sums, held(len...]
    ppermute x1, starting transfers between devices: 3.41 us -> 1.55 us  [on_device(): lax.ppermute(chip, 'ctx', [(j, (j + d) % ctx) for j in range(ctx)])]
    pallas_call x1, Pallas kernels: 6.57 us -> 5.36 us  [on_device(): pl.pallas_call(functools.partial(first_kernel, order, loads(1)), out_shap...]
    ppermute x1, waiting for transfers between devices: 0.82 us -> 1.45 us  [on_device(): lax.ppermute(chip, 'ctx', [(j, (j + d) % ctx) for j in range(ctx)])]
    ppermute x3, waiting for transfers between devices: 0.73 us -> 0.14 us  [on_device(): fore = lax.ppermute(fore, 'tp', ahead)]
  transfers between devices with their start and end apart: 10 -> 10, of which waited for: 7 -> 6; matrix products, arithmetic and copies ran while one was open for 0% -> 0% of each run, Pallas kernels for 45% -> 48%
where the time goes in v4:
time: 45 us; the launch traced here: 44.8 us
  Pallas kernels  25.8 us (57%)
  starting transfers between devices  10.8 us (24%)
  waiting for transfers between devices  7.06 us (16%)
  local copies, waits for them, and re-layouts  1.03 us (2%)
    pallas_call x3, Pallas kernels, on_device(): pl.pallas_call(functools.partial(body, coming), out_shape=[sums, held(len...  14.4 us
    ppermute x3, starting transfers between devices, on_device(): fore = lax.ppermute(fore, 'tp', ahead)  6.22 us
    pallas_call x1, Pallas kernels, on_device(): pl.pallas_call(functools.partial(first_kernel, order, loads(1)), out_shap...  5.36 us
    ppermute x3, waiting for transfers between devices, on_device(): aft = lax.ppermute(aft, 'tp', back)  2.65 us
    pallas_call x1, Pallas kernels, on_device(): pl.pallas_call(last_kernel, out_shape=[sums, wide, f32(modes + EDGE, grou...  2.41 us
    pallas_call x1, Pallas kernels, on_device(): pl.pallas_call(functools.partial(final_kernel, lone, len(sent)), out_shap...  1.92 us
    pallas_call x1, Pallas kernels, on_device(): pl.pallas_call(local_kernel, out_shape=[wide, wide], in_specs=[VMEM] * 4,...  1.74 us
    ppermute x1, starting transfers between devices, on_device(): lax.ppermute(chip, 'ctx', [(j, (j + d) % ctx) for j in range(ctx)])  1.55 us
  transfers between devices with their start and end apart: 10, of which 6 were waited for; matrix products, arithmetic and copies ran while one was open for 0% of the time, Pallas kernels for 48%

profile of v4, /device:TPU:0, one launch (start us, length us, event | category | flops | bytes accessed | tf_op | source)
XLA Modules:
  0.0 44.8 jit_solution(6903233864959821834)
XLA Ops:
  0.0 3.0 %collective-permute-start = (bf16[128,1024]{1,0:T(8,128)(2,1)}, bf16[128,1024]{1,0:T(8,128)(2,1)S(1)}, u32[]{:S(2)}, u32[]{:S(2)}) collective-permute-start(bf16[128,1024]{1,0:T(8,128)(2,1)} %x_ref.1), channel_id=1, source_target_pairs={{0,1},{1,3},{3,5},{5,7},{7,6},{6,4},{4,2},{2,0},{8,9},{9,11},{11,1... | collective-permute-start | bytes 786440 | tf_op jit(solution)/shard_map/ppermute | solution.py:382
  3.0 0.1 collective-permute-start.1
  3.0 1.0 %copy-done = bf16[128,1024]{1,0:T(8,128)(2,1)S(1)} copy-done((bf16[128,1024]{1,0:T(8,128)(2,1)S(1)}, bf16[128,1024]{1,0:T(8,128)(2,1)}, u32[]{:S(2)}) %copy-start) | copy-done | bytes 262168
  4.0 5.4 %project_own.1 = (f32[3,128,1024]{2,1,0:T(8,128)S(1)}, bf16[2,2,1024,1024]{3,2,1,0:T(8,128)(2,1)S(1)}) custom-call(bf16[128,1024]{1,0:T(8,128)(2,1)S(1)} %copy-done, bf16[3,8192,1024]{2,1,0:T(8,128)(2,1)} %bitcast.1), custom_call_target="tpu_custom_call" | custom-call | bytes 16777216 | tf_op jit(solution)/shard_map/project_own/pallas_call | solution.py:366
  9.4 0.1 collective-permute-done.xa_ref
  9.5 1.4 %collective-permute-done.1.xb_ref = bf16[128,1024]{1,0:T(8,128)(2,1)S(1)} collective-permute-done((bf16[128,1024]{1,0:T(8,128)(2,1)}, bf16[128,1024]{1,0:T(8,128)(2,1)S(1)}, u32[]{:S(2)}, u32[]{:S(2)}) %collective-permute-start.1) | collective-permute-done | bytes 262176 | tf_op jit(solution)/shard_map/ppermute | solution.py:383
  10.9 1.6 %collective-permute-start.2 = (bf16[128,1024]{1,0:T(8,128)(2,1)S(1)}, bf16[128,1024]{1,0:T(8,128)(2,1)S(1)}, u32[]{:S(2)}, u32[]{:S(2)}) collective-permute-start(bf16[128,1024]{1,0:T(8,128)(2,1)S(1)} %collective-permute-done.xa_ref), channel_id=1, source_target_pairs={{0,1},{1,3},{3,5},{5,7},{7,6},{6,4},{4,2},{2,0},{8,9},{9,11},{11,1... | collective-permute-start | bytes 786440 | tf_op jit(solution)/shard_map/ppermute | solution.py:382
  12.5 0.4 %collective-permute-start.3 = (bf16[128,1024]{1,0:T(8,128)(2,1)S(1)}, bf16[128,1024]{1,0:T(8,128)(2,1)S(1)}, u32[]{:S(2)}, u32[]{:S(2)}) collective-permute-start(bf16[128,1024]{1,0:T(8,128)(2,1)S(1)} %collective-permute-done.1.xb_ref), channel_id=1, source_target_pairs={{1,0},{3,1},{5,3},{7,5},{6,7},{4,6},{2,4},{0,2},{9,8},{11,9},{13,1... | collective-permute-start | bytes 786440 | tf_op jit(solution)/shard_map/ppermute | solution.py:383
  13.0 0.0 copy-done.1
  13.0 0.0 copy-done.2
  13.0 0.0 copy-done.3
  13.0 6.8 %project_pair.3 = (f32[3,128,1024]{2,1,0:T(8,128)S(1)}, bf16[2,3,1024,1024]{3,2,1,0:T(8,128)(2,1)S(1)}, f32[3,3,8,128]{3,2,1,0:T(8,128)S(1)}, f32[5,16,8,128]{3,2,1,0:T(8,128)S(1)}) custom-call(bf16[128,1024]{1,0:T(8,128)(2,1)S(1)} %collective-permute-done.xa_ref, ...), custom_call_target="tpu_custom_call", output_to_operand_aliasing={{0}: (4, {})} | custom-call | bytes 16777216 | tf_op jit(solution)/shard_map/project_pair/pallas_call | solution.py:395
  19.7 0.0 collective-permute-done.2.xa_ref
  19.8 0.0 collective-permute-done.3.xb_ref
  19.8 1.7 %collective-permute-start.4 = (bf16[128,1024]{1,0:T(8,128)(2,1)S(1)}, bf16[128,1024]{1,0:T(8,128)(2,1)S(1)}, u32[]{:S(2)}, u32[]{:S(2)}) collective-permute-start(bf16[128,1024]{1,0:T(8,128)(2,1)S(1)} %collective-permute-done.2.xa_ref), channel_id=1, source_target_pairs={{0,1},{1,3},{3,5},{5,7},{7,6},{6,4},{4,2},{2,0},{8,9},{9,11},{11,1... | collective-permute-start | bytes 786440 | tf_op jit(solution)/shard_map/ppermute | solution.py:382
  21.4 0.4 collective-permute-start.5
  21.8 4.7 %project_pair.4 = (f32[3,128,1024]{2,1,0:T(8,128)S(1)}, bf16[2,3,1024,1024]{3,2,1,0:T(8,128)(2,1)S(1)}) custom-call(bf16[128,1024]{1,0:T(8,128)(2,1)S(1)} %collective-permute-done.2.xa_ref, bf16[128,1024]{1,0:T(8,128)(2,1)S(1)} %collective-permute-done.3.xb_ref, ...), custom_call_target="tpu_custom_call", output_to_operand_aliasing={{0}: (4, {})} | custom-call | bytes 16777216 | tf_op jit(solution)/shard_map/project_pair/pallas_call | solution.py:395
  26.6 0.0 collective-permute-done.4.xa_ref
  26.6 1.2 %collective-permute-done.5.xb_ref = bf16[128,1024]{1,0:T(8,128)(2,1)S(1)} collective-permute-done((bf16[128,1024]{1,0:T(8,128)(2,1)S(1)}, bf16[128,1024]{1,0:T(8,128)(2,1)S(1)}, u32[]{:S(2)}, u32[]{:S(2)}) %collective-permute-start.5) | collective-permute-done | bytes 262176 | tf_op jit(solution)/shard_map/ppermute | solution.py:383
  27.8 1.5 %collective-permute-start.6 = (bf16[64,1024]{1,0:T(8,128)(2,1)S(1)}, bf16[64,1024]{1,0:T(8,128)(2,1)S(1)}, u32[]{:S(2)}, u32[]{:S(2)}) collective-permute-start(bf16[64,1024]{1,0:T(8,128)(2,1)S(1)} %slice.6), channel_id=1, source_target_pairs={{0,1},{1,3},{3,5},{5,7},{7,6},{6,4},{4,2},{2,0},{8,9},{9,11},{11,1... | collective-permute-start | bytes 393224 | tf_op jit(solution)/shard_map/ppermute | solution.py:408
  29.4 0.6 %collective-permute-start.7 = (bf16[64,1024]{1,0:T(8,128)(2,1)S(1)}, bf16[64,1024]{1,0:T(8,128)(2,1)S(1)}, u32[]{:S(2)}, u32[]{:S(2)}) collective-permute-start(bf16[64,1024]{1,0:T(8,128)(2,1)S(1)} %slice.7), channel_id=1, source_target_pairs={{1,0},{3,1},{5,3},{7,5},{6,7},{4,6},{2,4},{0,2},{9,8},{11,9},{13,1... | collective-permute-start | bytes 393224 | tf_op jit(solution)/shard_map/ppermute | solution.py:409
  29.9 2.9 %project_pair.5 = (f32[3,128,1024]{2,1,0:T(8,128)S(1)}, bf16[1,3,1024,1024]{3,2,1,0:T(8,128)(2,1)S(1)}) custom-call(bf16[128,1024]{1,0:T(8,128)(2,1)S(1)} %collective-permute-done.4.xa_ref, bf16[128,1024]{1,0:T(8,128)(2,1)S(1)} %collective-permute-done.5.xb_ref, ...), custom_call_target="tpu_custom_call", output_to_operand_aliasing={{0}: (4, {})} | custom-call | bytes 16777216 | tf_op jit(solution)/shard_map/project_pair/pallas_call | solution.py:395
  32.8 0.0 collective-permute-done.6.xa_ref
  32.9 1.5 %collective-permute-done.7.xb_ref = bf16[64,1024]{1,0:T(8,128)(2,1)S(1)} collective-permute-done((bf16[64,1024]{1,0:T(8,128)(2,1)S(1)}, bf16[64,1024]{1,0:T(8,128)(2,1)S(1)}, u32[]{:S(2)}, u32[]{:S(2)}) %collective-permute-start.7) | collective-permute-done | bytes 131104 | tf_op jit(solution)/shard_map/ppermute | solution.py:409
  34.3 2.4 %project_last.1 = (f32[3,128,1024]{2,1,0:T(8,128)S(1)}, f32[128,8,128]{2,1,0:T(8,128)S(1)}, f32[26,8,128]{2,1,0:T(8,128)S(1)}) custom-call(bf16[64,1024]{1,0:T(8,128)(2,1)S(1)} %collective-permute-done.6.xa_ref, bf16[64,1024]{1,0:T(8,128)(2,1)S(1)} %collective-permute-done.7.xb_ref, ...), custom_call_target="tpu_custom_call", output_to_operand_aliasing={{0}: (5, {})} | custom-call | bytes 16777216 | tf_op jit(solution)/shard_map/project_last/pallas_call | solution.py:410
  36.7 0.1 collective-permute-start.8
  36.8 1.3 %collective-permute-done.8.partner.refs_2_ = f32[26,8,128]{2,1,0:T(8,128)S(1)} collective-permute-done((f32[26,8,128]{2,1,0:T(8,128)S(1)}, f32[26,8,128]{2,1,0:T(8,128)S(1)}, u32[]{:S(2)}, u32[]{:S(2)}) %collective-permute-start.8) | collective-permute-done | bytes 106528 | tf_op jit(solution)/shard_map/ppermute | solution.py:425
  38.1 0.1 chip_state.1
  38.2 1.6 %collective-permute-start.9 = (f32[22,8,128]{2,1,0:T(8,128)S(1)}, f32[22,8,128]{2,1,0:T(8,128)S(1)}, u32[]{:S(2)}, u32[]{:S(2)}) collective-permute-start(f32[22,8,128]{2,1,0:T(8,128)S(1)} %chip_state.1), channel_id=1, source_target_pairs={{0,16},{8,24},{16,0},{24,8},{1,17},{9,25},{17,1},{25,9},{2,18},{10... | collective-permute-start | bytes 270344 | tf_op jit(solution)/shard_map/ppermute | solution.py:436
  39.7 1.7 %local_response.1 = (f32[128,8,128]{2,1,0:T(8,128)S(1)}, f32[128,8,128]{2,1,0:T(8,128)S(1)}) custom-call(f32[3,128,1024]{2,1,0:T(8,128)S(1)} %get-tuple-element.55.total, f32[128,8,128]{2,1,0:T(8,128)S(1)} %get-tuple-element.56.source, f32[3,3,8,128]{3,2,1,0:T(8,128)S(1)} %get-tuple-element.51.taps.refs_5_, f32[5,16,8,128]{3,2,1,0:T(8,128)S(1)} %get-tuple-element.52.table.refs_6_), custom_call_target="tpu_custom_call" | custom-call | bytes 16777216 | tf_op jit(solution)/shard_map/local_response/pallas_call | solution.py:439
  41.5 1.4 %collective-permute-done.9.refs_0_ = f32[22,8,128]{2,1,0:T(8,128)S(1)} collective-permute-done((f32[22,8,128]{2,1,0:T(8,128)S(1)}, f32[22,8,128]{2,1,0:T(8,128)S(1)}, u32[]{:S(2)}, u32[]{:S(2)}) %collective-permute-start.9) | collective-permute-done | bytes 90144 | tf_op jit(solution)/shard_map/ppermute | solution.py:436
  42.9 1.9 %carried_response.1 = bf16[128,1024]{1,0:T(8,128)(2,1)} custom-call(f32[22,8,128]{2,1,0:T(8,128)S(1)} %collective-permute-done.9.refs_0_, f32[26,8,128]{2,1,0:T(8,128)S(1)} %get-tuple-element.54.local.refs_1_, f32[26,8,128]{2,1,0:T(8,128)S(1)} %collective-permute-done.8.partner.refs_2_, f32[128,8,128]{2,1,0:T(8,128)S(1)} %get-tuple-element.57.refs_3_, ...), custom_call_target="tpu_custom_call" | custom-call | tf_op jit(solution)/shard_map/carried_response/pallas_call | solution.py:449
  (6 shorter events, 0.0 us)
Async XLA Ops:
  0.0 9.5 %collective-permute-start = (bf16[128,1024]{1,0:T(8,128)(2,1)}, bf16[128,1024]{1,0:T(8,128)(2,1)S(1)}, u32[]{:S(2)}, u32[]{:S(2)}) collective-permute-start(bf16[128,1024]{1,0:T(8,128)(2,1)} %x_ref.1), channel_id=1, source_target_pairs={{0,1},{1,3},{3,5},{5,7},{7,6},{6,4},{4,2},{2,0},{8,9},{9,11},{11,1... | collective-permute-start | bytes 786440 | tf_op jit(solution)/shard_map/ppermute | solution.py:382
  3.0 8.0 %collective-permute-start.1 = (bf16[128,1024]{1,0:T(8,128)(2,1)}, bf16[128,1024]{1,0:T(8,128)(2,1)S(1)}, u32[]{:S(2)}, u32[]{:S(2)}) collective-permute-start(bf16[128,1024]{1,0:T(8,128)(2,1)} %x_ref.1), channel_id=1, source_target_pairs={{1,0},{3,1},{5,3},{7,5},{6,7},{4,6},{2,4},{0,2},{9,8},{11,9},{13,1... | collective-permute-start | bytes 786440 | tf_op jit(solution)/shard_map/ppermute | solution.py:383
  3.0 1.0 %copy-start = (bf16[128,1024]{1,0:T(8,128)(2,1)S(1)}, bf16[128,1024]{1,0:T(8,128)(2,1)}, u32[]{:S(2)}) copy-start(bf16[128,1024]{1,0:T(8,128)(2,1)} %x_ref.1) | copy-start | bytes 786436
  4.0 8.9 %copy-start.1 = (f32[16,1024]{1,0:T(8,128)S(1)}, f32[16,1024]{1,0:T(8,128)}, u32[]{:S(2)}) copy-start(f32[16,1024]{1,0:T(8,128)} %decay.1) | copy-start | bytes 196612
  4.0 8.9 %copy-start.2 = (f32[16,1024]{1,0:T(8,128)S(1)}, f32[16,1024]{1,0:T(8,128)}, u32[]{:S(2)}) copy-start(f32[16,1024]{1,0:T(8,128)} %residue.1) | copy-start | bytes 196612
  4.0 8.9 %copy-start.3 = (f32[3,3,1024]{2,1,0:T(4,128)S(1)}, f32[3,3,1024]{2,1,0:T(4,128)}, u32[]{:S(2)}) copy-start(f32[3,3,1024]{2,1,0:T(4,128)} %taps_in.1) | copy-start | bytes 110596
  10.9 8.8 %collective-permute-start.2 = (bf16[128,1024]{1,0:T(8,128)(2,1)S(1)}, bf16[128,1024]{1,0:T(8,128)(2,1)S(1)}, u32[]{:S(2)}, u32[]{:S(2)}) collective-permute-start(bf16[128,1024]{1,0:T(8,128)(2,1)S(1)} %collective-permute-done.xa_ref), channel_id=1, source_target_pairs={{0,1},{1,3},{3,5},{5,7},{7,6},{6,4},{4,2},{2,0},{8,9},{9,11},{11,1... | collective-permute-start | bytes 786440 | tf_op jit(solution)/shard_map/ppermute | solution.py:382
  12.5 7.2 %collective-permute-start.3 = (bf16[128,1024]{1,0:T(8,128)(2,1)S(1)}, bf16[128,1024]{1,0:T(8,128)(2,1)S(1)}, u32[]{:S(2)}, u32[]{:S(2)}) collective-permute-start(bf16[128,1024]{1,0:T(8,128)(2,1)S(1)} %collective-permute-done.1.xb_ref), channel_id=1, source_target_pairs={{1,0},{3,1},{5,3},{7,5},{6,7},{4,6},{2,4},{0,2},{9,8},{11,9},{13,1... | collective-permute-start | bytes 786440 | tf_op jit(solution)/shard_map/ppermute | solution.py:383
  19.8 6.8 %collective-permute-start.4 = (bf16[128,1024]{1,0:T(8,128)(2,1)S(1)}, bf16[128,1024]{1,0:T(8,128)(2,1)S(1)}, u32[]{:S(2)}, u32[]{:S(2)}) collective-permute-start(bf16[128,1024]{1,0:T(8,128)(2,1)S(1)} %collective-permute-done.2.xa_ref), channel_id=1, source_target_pairs={{0,1},{1,3},{3,5},{5,7},{7,6},{6,4},{4,2},{2,0},{8,9},{9,11},{11,1... | collective-permute-start | bytes 786440 | tf_op jit(solution)/shard_map/ppermute | solution.py:382
  21.4 6.4 %collective-permute-start.5 = (bf16[128,1024]{1,0:T(8,128)(2,1)S(1)}, bf16[128,1024]{1,0:T(8,128)(2,1)S(1)}, u32[]{:S(2)}, u32[]{:S(2)}) collective-permute-start(bf16[128,1024]{1,0:T(8,128)(2,1)S(1)} %collective-permute-done.3.xb_ref), channel_id=1, source_target_pairs={{1,0},{3,1},{5,3},{7,5},{6,7},{4,6},{2,4},{0,2},{9,8},{11,9},{13,1... | collective-permute-start | bytes 786440 | tf_op jit(solution)/shard_map/ppermute | solution.py:383
  27.8 5.0 %collective-permute-start.6 = (bf16[64,1024]{1,0:T(8,128)(2,1)S(1)}, bf16[64,1024]{1,0:T(8,128)(2,1)S(1)}, u32[]{:S(2)}, u32[]{:S(2)}) collective-permute-start(bf16[64,1024]{1,0:T(8,128)(2,1)S(1)} %slice.6), channel_id=1, source_target_pairs={{0,1},{1,3},{3,5},{5,7},{7,6},{6,4},{4,2},{2,0},{8,9},{9,11},{11,1... | collective-permute-start | bytes 393224 | tf_op jit(solution)/shard_map/ppermute | solution.py:408
  29.4 5.0 %collective-permute-start.7 = (bf16[64,1024]{1,0:T(8,128)(2,1)S(1)}, bf16[64,1024]{1,0:T(8,128)(2,1)S(1)}, u32[]{:S(2)}, u32[]{:S(2)}) collective-permute-start(bf16[64,1024]{1,0:T(8,128)(2,1)S(1)} %slice.7), channel_id=1, source_target_pairs={{1,0},{3,1},{5,3},{7,5},{6,7},{4,6},{2,4},{0,2},{9,8},{11,9},{13,1... | collective-permute-start | bytes 393224 | tf_op jit(solution)/shard_map/ppermute | solution.py:409
  36.7 1.4 %collective-permute-start.8 = (f32[26,8,128]{2,1,0:T(8,128)S(1)}, f32[26,8,128]{2,1,0:T(8,128)S(1)}, u32[]{:S(2)}, u32[]{:S(2)}) collective-permute-start(f32[26,8,128]{2,1,0:T(8,128)S(1)} %get-tuple-element.54.local.refs_1_), channel_id=1, source_target_pairs={{0,8},{8,0},{16,24},{24,16},{1,9},{9,1},{17,25},{25,17},{2,10},{10... | collective-permute-start | bytes 319496 | tf_op jit(solution)/shard_map/ppermute | solution.py:425
  38.2 4.7 %collective-permute-start.9 = (f32[22,8,128]{2,1,0:T(8,128)S(1)}, f32[22,8,128]{2,1,0:T(8,128)S(1)}, u32[]{:S(2)}, u32[]{:S(2)}) collective-permute-start(f32[22,8,128]{2,1,0:T(8,128)S(1)} %chip_state.1), channel_id=1, source_target_pairs={{0,16},{8,24},{16,0},{24,8},{1,17},{9,25},{17,1},{25,9},{2,18},{10... | collective-permute-start | bytes 270344 | tf_op jit(solution)/shard_map/ppermute | solution.py:436

commit v5 on v4

--- a/solution.py
+++ b/solution.py
@@ -62,10 +62,8 @@
         total[first + s, :, at] += sum(terms)
 
 
-def add_held(xa_ref, xb_ref, held, total):
-    @pl.loop(0, held.shape[1])
-    def _(s):
-        add_products([xa_ref[...], xb_ref[...]], held, total, s)
+def joined(parts):
+    return jnp.concatenate([part[...] for part in parts], axis=0)
 
 
 def spread(out_ref, value):
@@ -104,37 +102,40 @@
         copy.wait()
 
 
-def middle_kernel(order, steps, xa_ref, xb_ref, held, w_ref, _, total, next_held, sem):
-    ahead = block_loads(order, steps, w_ref, next_held, sem)
-    for copy in ahead:
-        copy.start()
-    add_held(xa_ref, xb_ref, held, total)
-    for copy in ahead:
-        copy.wait()
-
-
-def second_kernel(
-    order, here, steps, xa_ref, xb_ref, held, w_ref, _, taps_in, decay, residue,
-    total, next_held, taps, table, rest, rest_sem, sem,
-):
+def middle_kernel(order, here, steps, count, inputs_count, *refs):
+    fore, aft = refs[:count], refs[count : 2 * count]
+    held, w_ref, _, *refs = refs[2 * count :]
+    *refs, rest, rest_sem, sem = refs
+    inputs, (total, next_held, *made) = refs[:inputs_count], refs[inputs_count:]
     first = held.shape[1]
     late = block_loads(order, here, w_ref, rest, rest_sem, first)
     ahead = block_loads(order, steps, w_ref, next_held, sem)
     for copy in late + ahead:
         copy.start()
+    if made:
+        make_tables(*inputs, *made, total.shape[1])
+
+    @pl.loop(0, first)
+    def _(s):
+        add_products([joined(fore), joined(aft)], held, total, s)
+
+    for copy in late:
+        copy.wait()
+
+    @pl.loop(0, rest.shape[1])
+    def _(s):
+        add_products([joined(fore), joined(aft)], rest, total, s, first)
+
+    for copy in ahead:
+        copy.wait()
+
+
+def make_tables(taps_in, decay, residue, taps, table, rows):
     rate = decay[...]
-    rows = total.shape[1]
     for i, power in enumerate((1, rows, rows - 1, rows - 2)):
         spread(table.at[i], jnp.exp(-rate * power))
     spread(table.at[4], residue[...] * jnp.sqrt(1.0 - jnp.exp(-2.0 * rate)))
     spread(taps, taps_in[...])
-    add_held(xa_ref, xb_ref, held, total)
-    for copy in late:
-        copy.wait()
-    for s in range(rest.shape[1]):
-        add_products([xa_ref[...], xb_ref[...]], rest, total, s, first)
-    for copy in ahead:
-        copy.wait()
 
 
 def filtered(taps, p_ref, s, t):
@@ -145,8 +146,9 @@
     )
 
 
-def last_kernel(xa_ref, xb_ref, held, taps, table, _, total, source, out_ref, p_ref, tail):
-    x = jnp.concatenate([xa_ref[...], xb_ref[...]], axis=0)
+def last_kernel(count, *refs):
+    x = joined(refs[:count])
+    held, taps, table, _, total, source, out_ref, p_ref, tail = refs[count:]
     for s in range(total.shape[0]):
         add_products([x], held, total, s)
     rows, groups, lanes = source.shape
@@ -377,50 +379,57 @@
         cost_estimate=cost,
         name="project_own",
     )(tokens, weight)
-    fore, aft = tokens, tokens
+    def passed(parts, pairs):
+        return [lax.ppermute(part, "tp", pairs) for part in parts]
+
+    def halves(part):
+        middle = part.shape[0] // 2
+        return [part[:middle], part[middle:]]
+
+    fore, aft = [tokens], [tokens]
     for step in range(1, half):
-        fore = lax.ppermute(fore, "tp", ahead)
-        aft = lax.ppermute(aft, "tp", back)
+        fore, aft = passed(fore, ahead), passed(aft, back)
         fore, aft, total, weights = lax.optimization_barrier((fore, aft, total, weights))
+        if step == 1:
+            fore, aft = halves(fore[0]), halves(aft[0])
         coming = loads(step + 1)
-        body, extra, made, scratch = functools.partial(middle_kernel, order), [], [], []
-        if step == 1:
-            body = functools.partial(second_kernel, order, loads(1))
-            extra = [filter_taps, decay_rate, residue]
-            made = [f32(lags, streams, groups, LANES), f32(5, modes, groups, LANES)]
-            scratch = [
+        extra = [filter_taps, decay_rate, residue] if step == 1 else []
+        made = [f32(lags, streams, groups, LANES), f32(5, modes, groups, LANES)] if step == 1 else []
+        early = EARLY if step + 1 < half else streams
+        total, weights, *made = pl.pallas_call(
+            functools.partial(
+                middle_kernel, order, loads(step), coming, len(fore), len(extra)
+            ),
+            out_shape=[sums, held(len(coming), early)] + made,
+            in_specs=[VMEM] * (2 * len(fore) + 1) + [HBM, VMEM] + [VMEM] * len(extra),
+            out_specs=[VMEM] * (2 + len(made)),
+            scratch_shapes=[
                 pltpu.VMEM((2, streams - EARLY, width, chans), jnp.bfloat16),
                 pltpu.SemaphoreType.DMA((2, streams - EARLY)),
-            ]
-        total, weights, *made = pl.pallas_call(
-            functools.partial(body, coming),
-            out_shape=[sums, held(len(coming))] + made,
-            in_specs=[VMEM, VMEM, VMEM, HBM, VMEM] + [VMEM] * len(extra),
-            out_specs=[VMEM] * (2 + len(made)),
-            scratch_shapes=scratch + [pltpu.SemaphoreType.DMA((len(coming), streams))],
-            input_output_aliases={4: 0},
+                pltpu.SemaphoreType.DMA((len(coming), early)),
+            ],
+            input_output_aliases={2 * len(fore) + 2: 0},
             compiler_params=params,
             cost_estimate=cost,
             name="project_pair",
-        )(fore, aft, weights, weight, total, *extra)
+        )(*fore, *aft, weights, weight, total, *extra)
         if made:
             taps, table = made
-    fore = lax.ppermute(fore[: rows // 2], "tp", ahead)
-    aft = lax.ppermute(aft[rows // 2 :], "tp", back)
+    last = passed(halves(fore[0]), ahead) + passed(halves(aft[1]), back)
     total, source, local = pl.pallas_call(
-        last_kernel,
+        functools.partial(last_kernel, len(last)),
         out_shape=[sums, wide, f32(modes + EDGE, groups, LANES)],
-        in_specs=[VMEM] * 6,
+        in_specs=[VMEM] * (len(last) + 4),
         out_specs=[VMEM] * 3,
         scratch_shapes=[
             pltpu.VMEM((2, rows, groups, LANES), jnp.float32),
             pltpu.VMEM((8, groups, LANES), jnp.float32),
         ],
-        input_output_aliases={5: 0},
+        input_output_aliases={len(last) + 3: 0},
         compiler_params=params,
         cost_estimate=cost,
         name="project_last",
-    )(fore, aft, weights, taps, table, total)
+    )(*last, weights, taps, table, total)
 
     partner = lax.ppermute(local, "ctx", [(j, j ^ 1) for j in range(ctx)])
     lone = ctx == 4

time: 45 us -> 49.3 us (1.096)
  starting transfers between devices: 10.8 us -> 17 us
  waiting for transfers between devices: 7.06 us -> 4.96 us
    ppermute x8 -> x14, starting transfers between devices: 9.21 us -> 15.3 us  [passed(): return [lax.ppermute(part, 'tp', pairs) for part in parts]]
    ppermute x8 -> x14, waiting for transfers between devices: 4.31 us -> 2.17 us  [passed(): return [lax.ppermute(part, 'tp', pairs) for part in parts]]
  transfers between devices with their start and end apart: 10 -> 16, of which waited for: 6 -> 6; matrix products, arithmetic and copies ran while one was open for 0% -> 0% of each run, Pallas kernels for 48% -> 44%
where the time goes in v5:
time: 49.3 us; the launch traced here: 49.2 us
  Pallas kernels  26 us (53%)
  starting transfers between devices  17 us (34%)
  waiting for transfers between devices  4.96 us (10%)
  local copies, waits for them, and re-layouts  1.06 us (2%)
    ppermute x14, starting transfers between devices, passed(): return [lax.ppermute(part, 'tp', pairs) for part in parts]  15.3 us
    pallas_call x3, Pallas kernels, on_device(): pl.pallas_call(functools.partial(middle_kernel, order, loads(step), comin...  14.6 us
    pallas_call x1, Pallas kernels, on_device(): pl.pallas_call(functools.partial(first_kernel, order, loads(1)), out_shap...  5.36 us
    pallas_call x1, Pallas kernels, on_device(): pl.pallas_call(functools.partial(last_kernel, len(last)), out_shape=[sums...  2.39 us
    ppermute x14, waiting for transfers between devices, passed(): return [lax.ppermute(part, 'tp', pairs) for part in parts]  2.17 us
    pallas_call x1, Pallas kernels, on_device(): pl.pallas_call(functools.partial(final_kernel, lone, len(sent)), out_shap...  1.92 us
    pallas_call x1, Pallas kernels, on_device(): pl.pallas_call(local_kernel, out_shape=[wide, wide], in_specs=[VMEM] * 4,...  1.7 us
    ppermute x1, starting transfers between devices, on_device(): lax.ppermute(chip, 'ctx', [(j, (j + d) % ctx) for j in range(ctx)])  1.56 us
  transfers between devices with their start and end apart: 16, of which 6 were waited for; matrix products, arithmetic and copies ran while one was open for 0% of the time, Pallas kernels for 44%

profile of v5, /device:TPU:0, one launch (start us, length us, event | category | flops | bytes accessed | tf_op | source)
XLA Modules:
  0.0 49.2 jit_solution(15495921701312586086)
XLA Ops:
  0.0 3.0 %collective-permute-start = (bf16[128,1024]{1,0:T(8,128)(2,1)}, bf16[128,1024]{1,0:T(8,128)(2,1)S(1)}, u32[]{:S(2)}, u32[]{:S(2)}) collective-permute-start(bf16[128,1024]{1,0:T(8,128)(2,1)} %x_ref.1), channel_id=1, source_target_pairs={{0,1},{1,3},{3,5},{5,7},{7,6},{6,4},{4,2},{2,0},{8,9},{9,11},{11,1... | collective-permute-start | bytes 786440 | tf_op jit(solution)/shard_map/ppermute | solution.py:383
  3.0 0.1 collective-permute-start.1
  3.0 1.0 %copy-done = bf16[128,1024]{1,0:T(8,128)(2,1)S(1)} copy-done((bf16[128,1024]{1,0:T(8,128)(2,1)S(1)}, bf16[128,1024]{1,0:T(8,128)(2,1)}, u32[]{:S(2)}) %copy-start) | copy-done | bytes 262168
  4.0 5.4 %project_own.1 = (f32[3,128,1024]{2,1,0:T(8,128)S(1)}, bf16[2,2,1024,1024]{3,2,1,0:T(8,128)(2,1)S(1)}) custom-call(bf16[128,1024]{1,0:T(8,128)(2,1)S(1)} %copy-done, bf16[3,8192,1024]{2,1,0:T(8,128)(2,1)} %bitcast.1), custom_call_target="tpu_custom_call" | custom-call | bytes 16777216 | tf_op jit(solution)/shard_map/project_own/pallas_call | solution.py:368
  9.4 0.1 collective-permute-done
  9.5 1.4 %collective-permute-done.1 = bf16[128,1024]{1,0:T(8,128)(2,1)S(1)} collective-permute-done((bf16[128,1024]{1,0:T(8,128)(2,1)}, bf16[128,1024]{1,0:T(8,128)(2,1)S(1)}, u32[]{:S(2)}, u32[]{:S(2)}) %collective-permute-start.1) | collective-permute-done | bytes 262176 | tf_op jit(solution)/shard_map/ppermute | solution.py:383
  11.0 1.6 %collective-permute-start.2 = (bf16[64,1024]{1,0:T(8,128)(2,1)S(1)}, bf16[64,1024]{1,0:T(8,128)(2,1)S(1)}, u32[]{:S(2)}, u32[]{:S(2)}) collective-permute-start(bf16[64,1024]{1,0:T(8,128)(2,1)S(1)} %get-tuple-element.70.refs_0_), channel_id=1, source_target_pairs={{0,1},{1,3},{3,5},{5,7},{7,6},{6,4},{4,2},{2,0},{8,9},{9,11},{11,1... | collective-permute-start | bytes 393224 | tf_op jit(solution)/shard_map/ppermute | solution.py:383
  12.6 1.6 %collective-permute-start.3 = (bf16[64,1024]{1,0:T(8,128)(2,1)S(1)}, bf16[64,1024]{1,0:T(8,128)(2,1)S(1)}, u32[]{:S(2)}, u32[]{:S(2)}) collective-permute-start(bf16[64,1024]{1,0:T(8,128)(2,1)S(1)} %get-tuple-element.69.refs_1_), channel_id=1, source_target_pairs={{0,1},{1,3},{3,5},{5,7},{7,6},{6,4},{4,2},{2,0},{8,9},{9,11},{11,1... | collective-permute-start | bytes 393224 | tf_op jit(solution)/shard_map/ppermute | solution.py:383
  14.2 0.4 collective-permute-start.4
  14.6 0.4 collective-permute-start.5
  15.1 4.9 %project_pair.3 = (f32[3,128,1024]{2,1,0:T(8,128)S(1)}, bf16[2,2,1024,1024]{3,2,1,0:T(8,128)(2,1)S(1)}, f32[3,3,8,128]{3,2,1,0:T(8,128)S(1)}, f32[5,16,8,128]{3,2,1,0:T(8,128)S(1)}) custom-call(bf16[64,1024]{1,0:T(8,128)(2,1)S(1)} %get-tuple-element.70.refs_0_, bf16[64,1024]{1,0:T(8,128)(2,1)S(1)} %get-tuple-element.69.refs_1_, ...), custom_call_target="tpu_custom_call", output_to_operand_aliasing={{0}: (6, {})} | custom-call | bytes 16777216 | tf_op jit(solution)/shard_map/project_pair/pallas_call | solution.py:399
  20.0 0.0 collective-permute-done.3.refs_1_
  20.0 0.0 collective-permute-done.4.refs_2_
  20.0 0.5 %collective-permute-done.5.refs_3_ = bf16[64,1024]{1,0:T(8,128)(2,1)S(1)} collective-permute-done((bf16[64,1024]{1,0:T(8,128)(2,1)S(1)}, bf16[64,1024]{1,0:T(8,128)(2,1)S(1)}, u32[]{:S(2)}, u32[]{:S(2)}) %collective-permute-start.5) | collective-permute-done | bytes 131104 | tf_op jit(solution)/shard_map/ppermute | solution.py:383
  20.6 1.6 %collective-permute-start.6 = (bf16[64,1024]{1,0:T(8,128)(2,1)S(1)}, bf16[64,1024]{1,0:T(8,128)(2,1)S(1)}, u32[]{:S(2)}, u32[]{:S(2)}) collective-permute-start(bf16[64,1024]{1,0:T(8,128)(2,1)S(1)} %collective-permute-done.2.refs_0_), channel_id=1, source_target_pairs={{0,1},{1,3},{3,5},{5,7},{7,6},{6,4},{4,2},{2,0},{8,9},{9,11},{11,1... | collective-permute-start | bytes 393224 | tf_op jit(solution)/shard_map/ppermute | solution.py:383
  22.1 1.1 %collective-permute-start.7 = (bf16[64,1024]{1,0:T(8,128)(2,1)S(1)}, bf16[64,1024]{1,0:T(8,128)(2,1)S(1)}, u32[]{:S(2)}, u32[]{:S(2)}) collective-permute-start(bf16[64,1024]{1,0:T(8,128)(2,1)S(1)} %collective-permute-done.3.refs_1_), channel_id=1, source_target_pairs={{0,1},{1,3},{3,5},{5,7},{7,6},{6,4},{4,2},{2,0},{8,9},{9,11},{11,1... | collective-permute-start | bytes 393224 | tf_op jit(solution)/shard_map/ppermute | solution.py:383
  23.2 0.9 %collective-permute-start.8 = (bf16[64,1024]{1,0:T(8,128)(2,1)S(1)}, bf16[64,1024]{1,0:T(8,128)(2,1)S(1)}, u32[]{:S(2)}, u32[]{:S(2)}) collective-permute-start(bf16[64,1024]{1,0:T(8,128)(2,1)S(1)} %collective-permute-done.4.refs_2_), channel_id=1, source_target_pairs={{1,0},{3,1},{5,3},{7,5},{6,7},{4,6},{2,4},{0,2},{9,8},{11,9},{13,1... | collective-permute-start | bytes 393224 | tf_op jit(solution)/shard_map/ppermute | solution.py:383
  24.2 0.4 collective-permute-start.9
  24.6 4.9 %project_pair.4 = (f32[3,128,1024]{2,1,0:T(8,128)S(1)}, bf16[2,2,1024,1024]{3,2,1,0:T(8,128)(2,1)S(1)}) custom-call(bf16[64,1024]{1,0:T(8,128)(2,1)S(1)} %collective-permute-done.2.refs_0_, bf16[64,1024]{1,0:T(8,128)(2,1)S(1)} %collective-permute-done.3.refs_1_, ...), custom_call_target="tpu_custom_call", output_to_operand_aliasing={{0}: (6, {})} | custom-call | bytes 16777216 | tf_op jit(solution)/shard_map/project_pair/pallas_call | solution.py:399
  29.6 0.1 collective-permute-done.9.refs_3_
  29.6 1.6 %collective-permute-start.10 = (bf16[32,1024]{1,0:T(8,128)(2,1)S(1)}, bf16[32,1024]{1,0:T(8,128)(2,1)S(1)}, u32[]{:S(2)}, u32[]{:S(2)}) collective-permute-start(bf16[32,1024]{1,0:T(8,128)(2,1)S(1)} %get-tuple-element.74), channel_id=1, source_target_pairs={{0,1},{1,3},{3,5},{5,7},{7,6},{6,4},{4,2},{2,0},{8,9},{9,11},{11,1... | collective-permute-start | bytes 196616 | tf_op jit(solution)/shard_map/ppermute | solution.py:383
  31.3 1.0 %collective-permute-start.11 = (bf16[32,1024]{1,0:T(8,128)(2,1)S(1)}, bf16[32,1024]{1,0:T(8,128)(2,1)S(1)}, u32[]{:S(2)}, u32[]{:S(2)}) collective-permute-start(bf16[32,1024]{1,0:T(8,128)(2,1)S(1)} %get-tuple-element.73), channel_id=1, source_target_pairs={{0,1},{1,3},{3,5},{5,7},{7,6},{6,4},{4,2},{2,0},{8,9},{9,11},{11,1... | collective-permute-start | bytes 196616 | tf_op jit(solution)/shard_map/ppermute | solution.py:383
  32.3 1.1 %collective-permute-start.12 = (bf16[32,1024]{1,0:T(8,128)(2,1)S(1)}, bf16[32,1024]{1,0:T(8,128)(2,1)S(1)}, u32[]{:S(2)}, u32[]{:S(2)}) collective-permute-start(bf16[32,1024]{1,0:T(8,128)(2,1)S(1)} %get-tuple-element.72), channel_id=1, source_target_pairs={{1,0},{3,1},{5,3},{7,5},{6,7},{4,6},{2,4},{0,2},{9,8},{11,9},{13,1... | collective-permute-start | bytes 196616 | tf_op jit(solution)/shard_map/ppermute | solution.py:383
  33.3 0.4 collective-permute-start.13
  33.8 4.8 %project_pair.5 = (f32[3,128,1024]{2,1,0:T(8,128)S(1)}, bf16[1,3,1024,1024]{3,2,1,0:T(8,128)(2,1)S(1)}) custom-call(bf16[64,1024]{1,0:T(8,128)(2,1)S(1)} %collective-permute-done.6.refs_0_, bf16[64,1024]{1,0:T(8,128)(2,1)S(1)} %collective-permute-done.7.refs_1_, ...), custom_call_target="tpu_custom_call", output_to_operand_aliasing={{0}: (6, {})} | custom-call | bytes 16777216 | tf_op jit(solution)/shard_map/project_pair/pallas_call | solution.py:399
  38.7 2.4 %project_last.1 = (f32[3,128,1024]{2,1,0:T(8,128)S(1)}, f32[128,8,128]{2,1,0:T(8,128)S(1)}, f32[26,8,128]{2,1,0:T(8,128)S(1)}) custom-call(bf16[32,1024]{1,0:T(8,128)(2,1)S(1)} %collective-permute-done.10.refs_0_, bf16[32,1024]{1,0:T(8,128)(2,1)S(1)} %collective-permute-done.11.refs_1_, ...), custom_call_target="tpu_custom_call", output_to_operand_aliasing={{0}: (7, {})} | custom-call | bytes 16777216 | tf_op jit(solution)/shard_map/project_last/pallas_call | solution.py:419
  41.1 0.1 collective-permute-start.14
  41.2 1.3 %collective-permute-done.14.partner.refs_2_ = f32[26,8,128]{2,1,0:T(8,128)S(1)} collective-permute-done((f32[26,8,128]{2,1,0:T(8,128)S(1)}, f32[26,8,128]{2,1,0:T(8,128)S(1)}, u32[]{:S(2)}, u32[]{:S(2)}) %collective-permute-start.14) | collective-permute-done | bytes 106528 | tf_op jit(solution)/shard_map/ppermute | solution.py:434
  42.5 1.6 %collective-permute-start.15 = (f32[22,8,128]{2,1,0:T(8,128)S(1)}, f32[22,8,128]{2,1,0:T(8,128)S(1)}, u32[]{:S(2)}, u32[]{:S(2)}) collective-permute-start(f32[22,8,128]{2,1,0:T(8,128)S(1)} %chip_state.1), channel_id=1, source_target_pairs={{0,16},{8,24},{16,0},{24,8},{1,17},{9,25},{17,1},{25,9},{2,18},{10... | collective-permute-start | bytes 270344 | tf_op jit(solution)/shard_map/ppermute | solution.py:445
  44.1 1.7 %local_response.1 = (f32[128,8,128]{2,1,0:T(8,128)S(1)}, f32[128,8,128]{2,1,0:T(8,128)S(1)}) custom-call(f32[3,128,1024]{2,1,0:T(8,128)S(1)} %get-tuple-element.63.total, f32[128,8,128]{2,1,0:T(8,128)S(1)} %get-tuple-element.64.source, f32[3,3,8,128]{3,2,1,0:T(8,128)S(1)} %get-tuple-element.59.refs_5_.taps, f32[5,16,8,128]{3,2,1,0:T(8,128)S(1)} %get-tuple-element.60.refs_6_.table), custom_call_target="tpu_custom_call" | custom-call | bytes 16777216 | tf_op jit(solution)/shard_map/local_response/pallas_call | solution.py:448
  45.8 1.5 %collective-permute-done.15.refs_0_ = f32[22,8,128]{2,1,0:T(8,128)S(1)} collective-permute-done((f32[22,8,128]{2,1,0:T(8,128)S(1)}, f32[22,8,128]{2,1,0:T(8,128)S(1)}, u32[]{:S(2)}, u32[]{:S(2)}) %collective-permute-start.15) | collective-permute-done | bytes 90144 | tf_op jit(solution)/shard_map/ppermute | solution.py:445
  47.3 1.9 %carried_response.1 = bf16[128,1024]{1,0:T(8,128)(2,1)} custom-call(f32[22,8,128]{2,1,0:T(8,128)S(1)} %collective-permute-done.15.refs_0_, f32[26,8,128]{2,1,0:T(8,128)S(1)} %get-tuple-element.62.local.refs_1_, f32[26,8,128]{2,1,0:T(8,128)S(1)} %collective-permute-done.14.partner.refs_2_, f32[128,8,128]{2,1,0:T(8,128)S(1)} %get-tuple-element.65.refs_3_, ...), custom_call_target="tpu_custom_call" | custom-call | tf_op jit(solution)/shard_map/carried_response/pallas_call | solution.py:458
  (20 shorter events, 0.1 us)
Async XLA Ops:
  0.0 9.5 %collective-permute-start = (bf16[128,1024]{1,0:T(8,128)(2,1)}, bf16[128,1024]{1,0:T(8,128)(2,1)S(1)}, u32[]{:S(2)}, u32[]{:S(2)}) collective-permute-start(bf16[128,1024]{1,0:T(8,128)(2,1)} %x_ref.1), channel_id=1, source_target_pairs={{0,1},{1,3},{3,5},{5,7},{7,6},{6,4},{4,2},{2,0},{8,9},{9,11},{11,1... | collective-permute-start | bytes 786440 | tf_op jit(solution)/shard_map/ppermute | solution.py:383
  3.0 8.0 %collective-permute-start.1 = (bf16[128,1024]{1,0:T(8,128)(2,1)}, bf16[128,1024]{1,0:T(8,128)(2,1)S(1)}, u32[]{:S(2)}, u32[]{:S(2)}) collective-permute-start(bf16[128,1024]{1,0:T(8,128)(2,1)} %x_ref.1), channel_id=1, source_target_pairs={{1,0},{3,1},{5,3},{7,5},{6,7},{4,6},{2,4},{0,2},{9,8},{11,9},{13,1... | collective-permute-start | bytes 786440 | tf_op jit(solution)/shard_map/ppermute | solution.py:383
  3.0 1.0 %copy-start = (bf16[128,1024]{1,0:T(8,128)(2,1)S(1)}, bf16[128,1024]{1,0:T(8,128)(2,1)}, u32[]{:S(2)}) copy-start(bf16[128,1024]{1,0:T(8,128)(2,1)} %x_ref.1) | copy-start | bytes 786436
  4.0 11.1 %copy-start.1 = (f32[16,1024]{1,0:T(8,128)S(1)}, f32[16,1024]{1,0:T(8,128)}, u32[]{:S(2)}) copy-start(f32[16,1024]{1,0:T(8,128)} %refs_8_.1) | copy-start | bytes 196612
  4.0 11.1 %copy-start.2 = (f32[16,1024]{1,0:T(8,128)S(1)}, f32[16,1024]{1,0:T(8,128)}, u32[]{:S(2)}) copy-start(f32[16,1024]{1,0:T(8,128)} %refs_9_.1) | copy-start | bytes 196612
  4.0 11.1 %copy-start.3 = (f32[3,3,1024]{2,1,0:T(4,128)S(1)}, f32[3,3,1024]{2,1,0:T(4,128)}, u32[]{:S(2)}) copy-start(f32[3,3,1024]{2,1,0:T(4,128)} %refs_7_.1) | copy-start | bytes 110596
  11.0 9.0 %collective-permute-start.2 = (bf16[64,1024]{1,0:T(8,128)(2,1)S(1)}, bf16[64,1024]{1,0:T(8,128)(2,1)S(1)}, u32[]{:S(2)}, u32[]{:S(2)}) collective-permute-start(bf16[64,1024]{1,0:T(8,128)(2,1)S(1)} %get-tuple-element.70.refs_0_), channel_id=1, source_target_pairs={{0,1},{1,3},{3,5},{5,7},{7,6},{6,4},{4,2},{2,0},{8,9},{9,11},{11,1... | collective-permute-start | bytes 393224 | tf_op jit(solution)/shard_map/ppermute | solution.py:383
  12.6 7.4 %collective-permute-start.3 = (bf16[64,1024]{1,0:T(8,128)(2,1)S(1)}, bf16[64,1024]{1,0:T(8,128)(2,1)S(1)}, u32[]{:S(2)}, u32[]{:S(2)}) collective-permute-start(bf16[64,1024]{1,0:T(8,128)(2,1)S(1)} %get-tuple-element.69.refs_1_), channel_id=1, source_target_pairs={{0,1},{1,3},{3,5},{5,7},{7,6},{6,4},{4,2},{2,0},{8,9},{9,11},{11,1... | collective-permute-start | bytes 393224 | tf_op jit(solution)/shard_map/ppermute | solution.py:383
  14.2 5.8 %collective-permute-start.4 = (bf16[64,1024]{1,0:T(8,128)(2,1)S(1)}, bf16[64,1024]{1,0:T(8,128)(2,1)S(1)}, u32[]{:S(2)}, u32[]{:S(2)}) collective-permute-start(bf16[64,1024]{1,0:T(8,128)(2,1)S(1)} %get-tuple-element.68.refs_2_), channel_id=1, source_target_pairs={{1,0},{3,1},{5,3},{7,5},{6,7},{4,6},{2,4},{0,2},{9,8},{11,9},{13,1... | collective-permute-start | bytes 393224 | tf_op jit(solution)/shard_map/ppermute | solution.py:383
  14.6 5.9 %collective-permute-start.5 = (bf16[64,1024]{1,0:T(8,128)(2,1)S(1)}, bf16[64,1024]{1,0:T(8,128)(2,1)S(1)}, u32[]{:S(2)}, u32[]{:S(2)}) collective-permute-start(bf16[64,1024]{1,0:T(8,128)(2,1)S(1)} %get-tuple-element.67.refs_3_), channel_id=1, source_target_pairs={{1,0},{3,1},{5,3},{7,5},{6,7},{4,6},{2,4},{0,2},{9,8},{11,9},{13,1... | collective-permute-start | bytes 393224 | tf_op jit(solution)/shard_map/ppermute | solution.py:383
  20.6 8.9 %collective-permute-start.6 = (bf16[64,1024]{1,0:T(8,128)(2,1)S(1)}, bf16[64,1024]{1,0:T(8,128)(2,1)S(1)}, u32[]{:S(2)}, u32[]{:S(2)}) collective-permute-start(bf16[64,1024]{1,0:T(8,128)(2,1)S(1)} %collective-permute-done.2.refs_0_), channel_id=1, source_target_pairs={{0,1},{1,3},{3,5},{5,7},{7,6},{6,4},{4,2},{2,0},{8,9},{9,11},{11,1... | collective-permute-start | bytes 393224 | tf_op jit(solution)/shard_map/ppermute | solution.py:383
  22.1 7.4 %collective-permute-start.7 = (bf16[64,1024]{1,0:T(8,128)(2,1)S(1)}, bf16[64,1024]{1,0:T(8,128)(2,1)S(1)}, u32[]{:S(2)}, u32[]{:S(2)}) collective-permute-start(bf16[64,1024]{1,0:T(8,128)(2,1)S(1)} %collective-permute-done.3.refs_1_), channel_id=1, source_target_pairs={{0,1},{1,3},{3,5},{5,7},{7,6},{6,4},{4,2},{2,0},{8,9},{9,11},{11,1... | collective-permute-start | bytes 393224 | tf_op jit(solution)/shard_map/ppermute | solution.py:383
  23.2 6.3 %collective-permute-start.8 = (bf16[64,1024]{1,0:T(8,128)(2,1)S(1)}, bf16[64,1024]{1,0:T(8,128)(2,1)S(1)}, u32[]{:S(2)}, u32[]{:S(2)}) collective-permute-start(bf16[64,1024]{1,0:T(8,128)(2,1)S(1)} %collective-permute-done.4.refs_2_), channel_id=1, source_target_pairs={{1,0},{3,1},{5,3},{7,5},{6,7},{4,6},{2,4},{0,2},{9,8},{11,9},{13,1... | collective-permute-start | bytes 393224 | tf_op jit(solution)/shard_map/ppermute | solution.py:383
  24.2 5.4 %collective-permute-start.9 = (bf16[64,1024]{1,0:T(8,128)(2,1)S(1)}, bf16[64,1024]{1,0:T(8,128)(2,1)S(1)}, u32[]{:S(2)}, u32[]{:S(2)}) collective-permute-start(bf16[64,1024]{1,0:T(8,128)(2,1)S(1)} %collective-permute-done.5.refs_3_), channel_id=1, source_target_pairs={{1,0},{3,1},{5,3},{7,5},{6,7},{4,6},{2,4},{0,2},{9,8},{11,9},{13,1... | collective-permute-start | bytes 393224 | tf_op jit(solution)/shard_map/ppermute | solution.py:383
  29.6 9.0 %collective-permute-start.10 = (bf16[32,1024]{1,0:T(8,128)(2,1)S(1)}, bf16[32,1024]{1,0:T(8,128)(2,1)S(1)}, u32[]{:S(2)}, u32[]{:S(2)}) collective-permute-start(bf16[32,1024]{1,0:T(8,128)(2,1)S(1)} %get-tuple-element.74), channel_id=1, source_target_pairs={{0,1},{1,3},{3,5},{5,7},{7,6},{6,4},{4,2},{2,0},{8,9},{9,11},{11,1... | collective-permute-start | bytes 196616 | tf_op jit(solution)/shard_map/ppermute | solution.py:383
  31.3 7.4 %collective-permute-start.11 = (bf16[32,1024]{1,0:T(8,128)(2,1)S(1)}, bf16[32,1024]{1,0:T(8,128)(2,1)S(1)}, u32[]{:S(2)}, u32[]{:S(2)}) collective-permute-start(bf16[32,1024]{1,0:T(8,128)(2,1)S(1)} %get-tuple-element.73), channel_id=1, source_target_pairs={{0,1},{1,3},{3,5},{5,7},{7,6},{6,4},{4,2},{2,0},{8,9},{9,11},{11,1... | collective-permute-start | bytes 196616 | tf_op jit(solution)/shard_map/ppermute | solution.py:383
  32.3 6.4 %collective-permute-start.12 = (bf16[32,1024]{1,0:T(8,128)(2,1)S(1)}, bf16[32,1024]{1,0:T(8,128)(2,1)S(1)}, u32[]{:S(2)}, u32[]{:S(2)}) collective-permute-start(bf16[32,1024]{1,0:T(8,128)(2,1)S(1)} %get-tuple-element.72), channel_id=1, source_target_pairs={{1,0},{3,1},{5,3},{7,5},{6,7},{4,6},{2,4},{0,2},{9,8},{11,9},{13,1... | collective-permute-start | bytes 196616 | tf_op jit(solution)/shard_map/ppermute | solution.py:383
  33.3 5.3 %collective-permute-start.13 = (bf16[32,1024]{1,0:T(8,128)(2,1)S(1)}, bf16[32,1024]{1,0:T(8,128)(2,1)S(1)}, u32[]{:S(2)}, u32[]{:S(2)}) collective-permute-start(bf16[32,1024]{1,0:T(8,128)(2,1)S(1)} %get-tuple-element.71), channel_id=1, source_target_pairs={{1,0},{3,1},{5,3},{7,5},{6,7},{4,6},{2,4},{0,2},{9,8},{11,9},{13,1... | collective-permute-start | bytes 196616 | tf_op jit(solution)/shard_map/ppermute | solution.py:383
  41.1 1.4 %collective-permute-start.14 = (f32[26,8,128]{2,1,0:T(8,128)S(1)}, f32[26,8,128]{2,1,0:T(8,128)S(1)}, u32[]{:S(2)}, u32[]{:S(2)}) collective-permute-start(f32[26,8,128]{2,1,0:T(8,128)S(1)} %get-tuple-element.62.local.refs_1_), channel_id=1, source_target_pairs={{0,8},{8,0},{16,24},{24,16},{1,9},{9,1},{17,25},{25,17},{2,10},{10... | collective-permute-start | bytes 319496 | tf_op jit(solution)/shard_map/ppermute | solution.py:434
  42.5 4.7 %collective-permute-start.15 = (f32[22,8,128]{2,1,0:T(8,128)S(1)}, f32[22,8,128]{2,1,0:T(8,128)S(1)}, u32[]{:S(2)}, u32[]{:S(2)}) collective-permute-start(f32[22,8,128]{2,1,0:T(8,128)S(1)} %chip_state.1), channel_id=1, source_target_pairs={{0,16},{8,24},{16,0},{24,8},{1,17},{9,25},{17,1},{25,9},{2,18},{10... | collective-permute-start | bytes 270344 | tf_op jit(solution)/shard_map/ppermute | solution.py:445

commit v6 on v5

--- a/solution.py
+++ b/solution.py
@@ -12,7 +12,7 @@
 DEPTH = 256
 GRID_ROWS = 4
 EDGE = 10
-EARLY = 2
+UNROLL = 16
 PIECE = 32
 VMEM = pl.BlockSpec(memory_space=pltpu.VMEM)
 HBM = pl.BlockSpec(memory_space=pltpu.HBM)
@@ -38,32 +38,24 @@
     return owner
 
 
-def block_loads(order, steps, w_ref, held, sem, first=0):
-    _, streams, width, _ = held.shape
-    copies = []
-    for b, step in enumerate(steps):
-        start = pl.multiple_of(owner_at(order, step) * width, width)
-        for s in range(streams):
-            copies.append(
-                pltpu.make_async_copy(
-                    w_ref.at[first + s, pl.ds(start, width), :], held.at[b, s], sem.at[b, s]
-                )
-            )
-    return copies
-
-
-def add_products(xs, held, total, s, first=0):
+def piece_loads(order, steps, pieces, w_ref, target, sem):
+    width = w_ref.shape[1] // len(order)
+    starts = [pl.multiple_of(owner_at(order, step) * width, width) for step in steps]
+    return [
+        pltpu.make_async_copy(
+            w_ref.at[s, pl.ds(starts[b], width), :], target(i, b, s), sem.at[i]
+        )
+        for i, (b, s) in enumerate(pieces)
+    ]
+
+
+def add_products(xs, weights, total, s):
     for c in range(0, total.shape[2], COLS):
         at = slice(c, c + COLS)
         terms = [
-            jnp.dot(x, held[b, s, :, at], preferred_element_type=jnp.float32)
-            for b, x in enumerate(xs)
+            jnp.dot(x, weights(b, at), preferred_element_type=jnp.float32) for b, x in enumerate(xs)
         ]
-        total[first + s, :, at] += sum(terms)
-
-
-def joined(parts):
-    return jnp.concatenate([part[...] for part in parts], axis=0)
+        total[s, :, at] += sum(terms)
 
 
 def spread(out_ref, value):
@@ -72,7 +64,7 @@
         out_ref[..., g, :] = value[..., g * lanes : (g + 1) * lanes]
 
 
-def first_kernel(order, steps, x_ref, w_ref, total, held, own, own_sem, held_sem):
+def first_kernel(order, steps, pieces, x_ref, w_ref, total, held, own, own_sem, held_sem):
     width = x_ref.shape[1]
     depth = min(DEPTH, width)
     start = pl.multiple_of(owner_at(order, 0) * width, width)
@@ -84,7 +76,7 @@
         )
         for k in range(width // depth)
     ]
-    ahead = block_loads(order, steps, w_ref, held, held_sem)
+    ahead = piece_loads(order, steps, pieces, w_ref, lambda i, b, s: held.at[b, s], held_sem)
     for copy in chunks + ahead:
         copy.start()
     for k, copy in enumerate(chunks):
@@ -102,32 +94,41 @@
         copy.wait()
 
 
-def middle_kernel(order, here, steps, count, inputs_count, *refs):
-    fore, aft = refs[:count], refs[count : 2 * count]
-    held, w_ref, _, *refs = refs[2 * count :]
+def middle_kernel(order, here, missing, steps, pieces, inputs_count, fore, aft, held, w_ref, _, *refs):
     *refs, rest, rest_sem, sem = refs
     inputs, (total, next_held, *made) = refs[:inputs_count], refs[inputs_count:]
-    first = held.shape[1]
-    late = block_loads(order, here, w_ref, rest, rest_sem, first)
-    ahead = block_loads(order, steps, w_ref, next_held, sem)
+    late = piece_loads(order, here, missing, w_ref, lambda i, b, s: rest.at[i], rest_sem)
+    ahead = piece_loads(order, steps, pieces, w_ref, lambda i, b, s: next_held.at[b, s], sem)
     for copy in late + ahead:
         copy.start()
     if made:
         make_tables(*inputs, *made, total.shape[1])
-
-    @pl.loop(0, first)
+    whole = min([s for _, s in missing], default=held.shape[1])
+
+    @pl.loop(0, whole)
     def _(s):
-        add_products([joined(fore), joined(aft)], held, total, s)
+        add_products([fore[...], aft[...]], lambda b, at: held[b, s, :, at], total, s)
 
     for copy in late:
         copy.wait()
 
-    @pl.loop(0, rest.shape[1])
-    def _(s):
-        add_products([joined(fore), joined(aft)], rest, total, s, first)
+    for s in range(whole, held.shape[1]):
+
+        def weights(b, at):
+            if (b, s) in missing:
+                return rest[missing.index((b, s)), :, at]
+            return held[b, s, :, at]
+
+        add_products([fore[...], aft[...]], weights, total, s)
 
     for copy in ahead:
         copy.wait()
+
+
+def half_kernel(x_ref, held, _, total):
+    depth = x_ref.shape[1]
+    for s in range(total.shape[0]):
+        add_products([x_ref[...]], lambda b, at: held[0, s, :depth, at], total, s)
 
 
 def make_tables(taps_in, decay, residue, taps, table, rows):
@@ -138,6 +139,19 @@
     spread(taps, taps_in[...])
 
 
+def over_rows(step, start, stop, carry):
+    aligned = -(-start // UNROLL) * UNROLL
+    for t in range(start, aligned):
+        carry = step(t, carry)
+
+    def group(i, carry):
+        for j in range(UNROLL):
+            carry = step(i * UNROLL + j, carry)
+        return carry
+
+    return lax.fori_loop(aligned // UNROLL, stop // UNROLL, group, carry)
+
+
 def filtered(taps, p_ref, s, t):
     return (
         taps[0, s] * p_ref[s - 1, t]
@@ -146,11 +160,10 @@
     )
 
 
-def last_kernel(count, *refs):
-    x = joined(refs[:count])
-    held, taps, table, _, total, source, out_ref, p_ref, tail = refs[count:]
+def last_kernel(x_ref, held, taps, table, _, total, source, out_ref, p_ref, tail):
+    depth = x_ref.shape[1]
     for s in range(total.shape[0]):
-        add_products([x], held, total, s)
+        add_products([x_ref[...]], lambda b, at: held[0, s, depth:, at], total, s)
     rows, groups, lanes = source.shape
     modes = table.shape[1]
     for s in (1, 2):
@@ -164,15 +177,7 @@
         return [r * s + u for r, s in zip(rate, state)]
 
     state = [jnp.zeros((groups, lanes), jnp.float32)] * modes
-    for t in range(2, 8):
-        state = step_row(t, state)
-
-    def eight(i, state):
-        for j in range(8):
-            state = step_row(i * 8 + j, state)
-        return state
-
-    state = lax.fori_loop(1, rows // 8, eight, state)
+    state = over_rows(step_row, 2, rows, state)
     for n in range(modes):
         out_ref[n] = state[n]
     for s in (1, 2):
@@ -208,15 +213,7 @@
         return state
 
     state = [jnp.zeros((groups, lanes), jnp.float32)] * modes
-    for t in range(2, 8):
-        state = step_row(t, state)
-
-    def eight(i, state):
-        for j in range(8):
-            state = step_row(i * 8 + j, state)
-        return state
-
-    lax.fori_loop(1, rows // 8, eight, state)
+    over_rows(step_row, 2, rows, state)
 
 
 def edge(taps, s, first, second, before, last):
@@ -317,18 +314,10 @@
         work[t] = query[t] * (response[t] + tree_sum(carried))
         return carried
 
-    def eight(i, carried):
-        for j in range(8):
-            carried = row(i * 8 + j, carried)
-        return carried
-
-    for t in range(2, 8):
-        carried = row(t, carried)
     copies = []
     for i in range(rows // PIECE):
         at = slice(i * PIECE, (i + 1) * PIECE)
-        first = 0 if i else 1
-        carried = lax.fori_loop(i * PIECE // 8 + first, (i + 1) * PIECE // 8, eight, carried)
+        carried = over_rows(row, max(i * PIECE, 2), (i + 1) * PIECE, carried)
         for g in range(groups):
             rounded_out[at, g * lanes : (g + 1) * lanes] = work[at, g, :].astype(out_ref.dtype)
         copies.append(pltpu.make_async_copy(rounded_out.at[at], out_ref.at[at], out_sem.at[i]))
@@ -353,7 +342,7 @@
     def f32(*shape):
         return jax.ShapeDtypeStruct(shape, jnp.float32)
 
-    def held(count, streams=streams):
+    def held(count):
         return jax.ShapeDtypeStruct((count, streams, width, chans), jnp.bfloat16)
 
     def loads(step):
@@ -365,71 +354,81 @@
     cost = pl.CostEstimate(flops=0, bytes_accessed=16 << 20, transcendentals=0)
 
     depth = min(DEPTH, width)
+    left = {1: [(0, streams - 1), (1, streams - 1)], 2: [(1, streams - 1)]}
+
+    def pieces(step):
+        every = [(b, s) for s in range(streams) for b in range(len(loads(step)))]
+        return [piece for piece in every if piece not in left.get(step, [])]
+
     total, weights = pl.pallas_call(
-        functools.partial(first_kernel, order, loads(1)),
-        out_shape=[sums, held(2, EARLY)],
+        functools.partial(first_kernel, order, loads(1), pieces(1)),
+        out_shape=[sums, held(2)],
         in_specs=[VMEM, HBM],
         out_specs=[VMEM] * 2,
         scratch_shapes=[
             pltpu.VMEM((streams, width, chans), jnp.bfloat16),
             pltpu.SemaphoreType.DMA((width // depth,)),
-            pltpu.SemaphoreType.DMA((2, EARLY)),
+            pltpu.SemaphoreType.DMA((len(pieces(1)),)),
         ],
         compiler_params=params,
         cost_estimate=cost,
         name="project_own",
     )(tokens, weight)
-    def passed(parts, pairs):
-        return [lax.ppermute(part, "tp", pairs) for part in parts]
-
-    def halves(part):
-        middle = part.shape[0] // 2
-        return [part[:middle], part[middle:]]
-
-    fore, aft = [tokens], [tokens]
+    fore, aft = tokens, tokens
     for step in range(1, half):
-        fore, aft = passed(fore, ahead), passed(aft, back)
-        fore, aft, total, weights = lax.optimization_barrier((fore, aft, total, weights))
-        if step == 1:
-            fore, aft = halves(fore[0]), halves(aft[0])
+        fore = lax.ppermute(fore, "tp", ahead)
+        aft = lax.ppermute(aft, "tp", back)
+        fore, total, weights = lax.optimization_barrier((fore, total, weights))
+        aft, total, weights = lax.optimization_barrier((aft, total, weights))
         coming = loads(step + 1)
+        missing = left.get(step, [])
         extra = [filter_taps, decay_rate, residue] if step == 1 else []
         made = [f32(lags, streams, groups, LANES), f32(5, modes, groups, LANES)] if step == 1 else []
-        early = EARLY if step + 1 < half else streams
         total, weights, *made = pl.pallas_call(
             functools.partial(
-                middle_kernel, order, loads(step), coming, len(fore), len(extra)
+                middle_kernel, order, loads(step), missing, coming, pieces(step + 1), len(extra)
             ),
-            out_shape=[sums, held(len(coming), early)] + made,
-            in_specs=[VMEM] * (2 * len(fore) + 1) + [HBM, VMEM] + [VMEM] * len(extra),
+            out_shape=[sums, held(len(coming))] + made,
+            in_specs=[VMEM, VMEM, VMEM, HBM, VMEM] + [VMEM] * len(extra),
             out_specs=[VMEM] * (2 + len(made)),
             scratch_shapes=[
-                pltpu.VMEM((2, streams - EARLY, width, chans), jnp.bfloat16),
-                pltpu.SemaphoreType.DMA((2, streams - EARLY)),
-                pltpu.SemaphoreType.DMA((len(coming), early)),
+                pltpu.VMEM((max(len(missing), 1), width, chans), jnp.bfloat16),
+                pltpu.SemaphoreType.DMA((max(len(missing), 1),)),
+                pltpu.SemaphoreType.DMA((len(pieces(step + 1)),)),
             ],
-            input_output_aliases={2 * len(fore) + 2: 0},
+            input_output_aliases={4: 0},
             compiler_params=params,
             cost_estimate=cost,
             name="project_pair",
-        )(*fore, *aft, weights, weight, total, *extra)
+        )(fore, aft, weights, weight, total, *extra)
         if made:
             taps, table = made
-    last = passed(halves(fore[0]), ahead) + passed(halves(aft[1]), back)
+    fore = lax.ppermute(fore[:, : width // 2], "tp", ahead)
+    aft = lax.ppermute(aft[:, width // 2 :], "tp", back)
+    total = pl.pallas_call(
+        half_kernel,
+        out_shape=sums,
+        in_specs=[VMEM] * 3,
+        out_specs=VMEM,
+        input_output_aliases={2: 0},
+        compiler_params=params,
+        cost_estimate=cost,
+        name="project_half",
+    )(fore, weights, total)
     total, source, local = pl.pallas_call(
-        functools.partial(last_kernel, len(last)),
+        last_kernel,
         out_shape=[sums, wide, f32(modes + EDGE, groups, LANES)],
-        in_specs=[VMEM] * (len(last) + 4),
+        in_specs=[VMEM] * 5,
         out_specs=[VMEM] * 3,
         scratch_shapes=[
             pltpu.VMEM((2, rows, groups, LANES), jnp.float32),
             pltpu.VMEM((8, groups, LANES), jnp.float32),
         ],
-        input_output_aliases={len(last) + 3: 0},
+        input_output_aliases={4: 0},
         compiler_params=params,
         cost_estimate=cost,
         name="project_last",
-    )(*last, weights, taps, table, total)
+    )(aft, weights, taps, table, total)
 
     partner = lax.ppermute(local, "ctx", [(j, j ^ 1) for j in range(ctx)])
     lone = ctx == 4

time: 49.3 us -> 42.9 us (0.87)
  starting transfers between devices: 17 us -> 10.9 us
  waiting for transfers between devices: 4.96 us -> 4.16 us
  Pallas kernels: 26 us -> 26.6 us
    ppermute x14 -> x8, starting transfers between devices: 15.3 us -> 9.26 us  [the longest x3 6.62 us: on_device(): fore = lax.ppermute(fore, 'tp', ahead)]
    ppermute x14 -> x8, waiting for transfers between devices: 2.17 us -> 1.29 us  [the longest x1 1.14 us: on_device(): aft = lax.ppermute(aft[:, width // 2:], 'tp', back)]
    pallas_call x5 -> x6, Pallas kernels: 22.4 us -> 23.1 us  [the longest x3 15.2 us: on_device(): pl.pallas_call(functools.partial(middle_kernel, order, loads(step), missi...]
  transfers between devices with their start and end apart: 16 -> 10, of which waited for: 6 -> 4; matrix products, arithmetic and copies ran while one was open for 0% -> 0% of each run, Pallas kernels for 44% -> 53%
where the time goes in v6:
time: 42.9 us; the launch traced here: 42.8 us
  Pallas kernels  26.6 us (62%)
  starting transfers between devices  10.9 us (25%)
  waiting for transfers between devices  4.16 us (10%)
  local copies, waits for them, and re-layouts  1.03 us (2%)
    pallas_call x3, Pallas kernels, on_device(): pl.pallas_call(functools.partial(middle_kernel, order, loads(step), missi...  15.2 us
    ppermute x3, starting transfers between devices, on_device(): fore = lax.ppermute(fore, 'tp', ahead)  6.62 us
    pallas_call x1, Pallas kernels, on_device(): pl.pallas_call(functools.partial(first_kernel, order, loads(1), pieces(1)...  5.36 us
    pallas_call x1, Pallas kernels, on_device(): pl.pallas_call(last_kernel, out_shape=[sums, wide, f32(modes + EDGE, grou...  1.92 us
    pallas_call x1, Pallas kernels, on_device(): pl.pallas_call(functools.partial(final_kernel, lone, len(sent)), out_shap...  1.86 us
    ppermute x1, starting transfers between devices, on_device(): fore = lax.ppermute(fore[:, :width // 2], 'tp', ahead)  1.78 us
    pallas_call x1, Pallas kernels, on_device(): pl.pallas_call(local_kernel, out_shape=[wide, wide], in_specs=[VMEM] * 4,...  1.62 us
    ppermute x1, waiting for transfers between devices, on_device(): lax.ppermute(chip, 'ctx', [(j, (j + d) % ctx) for j in range(ctx)])  1.57 us
  transfers between devices with their start and end apart: 10, of which 4 were waited for; matrix products, arithmetic and copies ran while one was open for 0% of the time, Pallas kernels for 53%

profile of v6, /device:TPU:0, one launch (start us, length us, event | category | flops | bytes accessed | tf_op | source)
XLA Modules:
  0.0 42.8 jit_solution(7633742740218597604)
XLA Ops:
  0.0 3.0 %collective-permute-start.1 = (bf16[128,1024]{1,0:T(8,128)(2,1)}, bf16[128,1024]{1,0:T(8,128)(2,1)S(1)}, u32[]{:S(2)}, u32[]{:S(2)}) collective-permute-start(bf16[128,1024]{1,0:T(8,128)(2,1)} %x_ref.1), channel_id=1, source_target_pairs={{0,1},{1,3},{3,5},{5,7},{7,6},{6,4},{4,2},{2,0},{8,9},{9,11},{11,1... | collective-permute-start | bytes 786440 | tf_op jit(solution)/shard_map/ppermute | solution.py:379
  3.0 0.1 collective-permute-start
  3.0 1.0 %copy-done = bf16[128,1024]{1,0:T(8,128)(2,1)S(1)} copy-done((bf16[128,1024]{1,0:T(8,128)(2,1)S(1)}, bf16[128,1024]{1,0:T(8,128)(2,1)}, u32[]{:S(2)}) %copy-start) | copy-done | bytes 262168
  4.0 5.4 %project_own.1 = (f32[3,128,1024]{2,1,0:T(8,128)S(1)}, bf16[2,3,1024,1024]{3,2,1,0:T(8,128)(2,1)S(1)}) custom-call(bf16[128,1024]{1,0:T(8,128)(2,1)S(1)} %copy-done, bf16[3,8192,1024]{2,1,0:T(8,128)(2,1)} %bitcast.1), custom_call_target="tpu_custom_call" | custom-call | bytes 16777216 | tf_op jit(solution)/shard_map/project_own/pallas_call | solution.py:363
  9.4 0.1 collective-permute-done.1.fore
  9.5 1.9 %collective-permute-start.3 = (bf16[128,1024]{1,0:T(8,128)(2,1)S(1)}, bf16[128,1024]{1,0:T(8,128)(2,1)S(1)}, u32[]{:S(2)}, u32[]{:S(2)}) collective-permute-start(bf16[128,1024]{1,0:T(8,128)(2,1)S(1)} %collective-permute-done.1.fore), channel_id=1, source_target_pairs={{0,1},{1,3},{3,5},{5,7},{7,6},{6,4},{4,2},{2,0},{8,9},{9,11},{11,1... | collective-permute-start | bytes 786440 | tf_op jit(solution)/shard_map/ppermute | solution.py:379
  11.4 0.0 collective-permute-done.aft
  11.4 0.2 collective-permute-start.2
  11.6 0.0 copy-done.1
  11.6 0.0 copy-done.2
  11.6 6.3 %project_pair.3 = (f32[3,128,1024]{2,1,0:T(8,128)S(1)}, bf16[2,3,1024,1024]{3,2,1,0:T(8,128)(2,1)S(1)}, f32[3,3,8,128]{3,2,1,0:T(8,128)S(1)}, f32[5,16,8,128]{3,2,1,0:T(8,128)S(1)}) custom-call(bf16[128,1024]{1,0:T(8,128)(2,1)S(1)} %collective-permute-done.1.fore, bf16[128,1024]{1,0:T(8,128)(2,1)S(1)} %collective-permute-done.aft, ...), custom_call_target="tpu_custom_call", output_to_operand_aliasing={{0}: (4, {})} | custom-call | bytes 16777216 | tf_op jit(solution)/shard_map/project_pair/pallas_call | solution.py:387
  17.8 0.0 collective-permute-done.3.fore
  17.8 1.8 %collective-permute-start.5 = (bf16[128,1024]{1,0:T(8,128)(2,1)S(1)}, bf16[128,1024]{1,0:T(8,128)(2,1)S(1)}, u32[]{:S(2)}, u32[]{:S(2)}) collective-permute-start(bf16[128,1024]{1,0:T(8,128)(2,1)S(1)} %collective-permute-done.3.fore), channel_id=1, source_target_pairs={{0,1},{1,3},{3,5},{5,7},{7,6},{6,4},{4,2},{2,0},{8,9},{9,11},{11,1... | collective-permute-start | bytes 786440 | tf_op jit(solution)/shard_map/ppermute | solution.py:379
  19.6 0.0 collective-permute-done.2.aft
  19.6 0.3 collective-permute-start.4
  19.9 6.1 %project_pair.4 = (f32[3,128,1024]{2,1,0:T(8,128)S(1)}, bf16[2,3,1024,1024]{3,2,1,0:T(8,128)(2,1)S(1)}) custom-call(bf16[128,1024]{1,0:T(8,128)(2,1)S(1)} %collective-permute-done.3.fore, bf16[128,1024]{1,0:T(8,128)(2,1)S(1)} %collective-permute-done.2.aft, bf16[2,3,1024,1024]{3,2,1,0:T(8,128)(2,1)S(1)} %get-tuple-element.52.held, ...), custom_call_target="tpu_custom_call", output_to_operand_aliasing={{0}: (4, {})} | custom-call | bytes 16777216 | tf_op jit(solution)/shard_map/project_pair/pallas_call | solution.py:387
  26.0 0.0 collective-permute-done.5.fore
  26.0 1.8 %collective-permute-start.7 = (bf16[128,512]{1,0:T(8,128)(2,1)S(1)}, bf16[128,512]{1,0:T(8,128)(2,1)S(1)}, u32[]{:S(2)}, u32[]{:S(2)}) collective-permute-start(bf16[128,512]{1,0:T(8,128)(2,1)S(1)} %slice.7), channel_id=1, source_target_pairs={{0,1},{1,3},{3,5},{5,7},{7,6},{6,4},{4,2},{2,0},{8,9},{9,11},{11,1... | collective-permute-start | bytes 393224 | tf_op jit(solution)/shard_map/ppermute | solution.py:406
  27.8 0.0 collective-permute-done.4.aft
  27.8 0.4 collective-permute-start.6
  28.2 2.9 %project_pair.5 = (f32[3,128,1024]{2,1,0:T(8,128)S(1)}, bf16[1,3,1024,1024]{3,2,1,0:T(8,128)(2,1)S(1)}) custom-call(bf16[128,1024]{1,0:T(8,128)(2,1)S(1)} %collective-permute-done.5.fore, bf16[128,1024]{1,0:T(8,128)(2,1)S(1)} %collective-permute-done.4.aft, bf16[2,3,1024,1024]{3,2,1,0:T(8,128)(2,1)S(1)} %get-tuple-element.60.held, ...), custom_call_target="tpu_custom_call", output_to_operand_aliasing={{0}: (4, {})} | custom-call | bytes 16777216 | tf_op jit(solution)/shard_map/project_pair/pallas_call | solution.py:387
  31.1 0.0 collective-permute-done.7.x_ref
  31.1 0.6 %project_half.1._ = f32[3,128,1024]{2,1,0:T(8,128)S(1)} custom-call(bf16[128,512]{1,0:T(8,128)(2,1)S(1)} %collective-permute-done.7.x_ref, bf16[1,3,1024,1024]{3,2,1,0:T(8,128)(2,1)S(1)} %get-tuple-element.62.held, f32[3,128,1024]{2,1,0:T(8,128)S(1)} %get-tuple-element.65._), custom_call_target="tpu_custom_call", output_to_operand_aliasing={{}: (2, {})} | custom-call | bytes 16777216 | tf_op jit(solution)/shard_map/project_half/pallas_call | solution.py:408
  31.7 1.1 %collective-permute-done.6.x_ref = bf16[128,512]{1,0:T(8,128)(2,1)S(1)} collective-permute-done((bf16[128,512]{1,0:T(8,128)(2,1)S(1)}, bf16[128,512]{1,0:T(8,128)(2,1)S(1)}, u32[]{:S(2)}, u32[]{:S(2)}) %collective-permute-start.6) | collective-permute-done | bytes 131104 | tf_op jit(solution)/shard_map/ppermute | solution.py:407
  32.8 1.9 %project_last.1 = (f32[3,128,1024]{2,1,0:T(8,128)S(1)}, f32[128,8,128]{2,1,0:T(8,128)S(1)}, f32[26,8,128]{2,1,0:T(8,128)S(1)}) custom-call(bf16[128,512]{1,0:T(8,128)(2,1)S(1)} %collective-permute-done.6.x_ref, bf16[1,3,1024,1024]{3,2,1,0:T(8,128)(2,1)S(1)} %get-tuple-element.62.held, ...), custom_call_target="tpu_custom_call", output_to_operand_aliasing={{0}: (4, {})} | custom-call | bytes 16777216 | tf_op jit(solution)/shard_map/project_last/pallas_call | solution.py:418
  34.8 0.1 collective-permute-start.8
  34.9 1.3 %collective-permute-done.8.partner.refs_2_ = f32[26,8,128]{2,1,0:T(8,128)S(1)} collective-permute-done((f32[26,8,128]{2,1,0:T(8,128)S(1)}, f32[26,8,128]{2,1,0:T(8,128)S(1)}, u32[]{:S(2)}, u32[]{:S(2)}) %collective-permute-start.8) | collective-permute-done | bytes 106528 | tf_op jit(solution)/shard_map/ppermute | solution.py:433
  36.2 0.1 chip_state.1
  36.2 1.6 %collective-permute-start.9 = (f32[22,8,128]{2,1,0:T(8,128)S(1)}, f32[22,8,128]{2,1,0:T(8,128)S(1)}, u32[]{:S(2)}, u32[]{:S(2)}) collective-permute-start(f32[22,8,128]{2,1,0:T(8,128)S(1)} %chip_state.1), channel_id=1, source_target_pairs={{0,16},{8,24},{16,0},{24,8},{1,17},{9,25},{17,1},{25,9},{2,18},{10... | collective-permute-start | bytes 270344 | tf_op jit(solution)/shard_map/ppermute | solution.py:444
  37.8 1.6 %local_response.1 = (f32[128,8,128]{2,1,0:T(8,128)S(1)}, f32[128,8,128]{2,1,0:T(8,128)S(1)}) custom-call(f32[3,128,1024]{2,1,0:T(8,128)S(1)} %get-tuple-element.67.total, f32[128,8,128]{2,1,0:T(8,128)S(1)} %get-tuple-element.68.source, f32[3,3,8,128]{3,2,1,0:T(8,128)S(1)} %get-tuple-element.63.taps.refs_5_, f32[5,16,8,128]{3,2,1,0:T(8,128)S(1)} %get-tuple-element.64.table.refs_6_), custom_call_target="tpu_custom_call" | custom-call | bytes 16777216 | tf_op jit(solution)/shard_map/local_response/pallas_call | solution.py:447
  39.4 1.6 %collective-permute-done.9.refs_0_ = f32[22,8,128]{2,1,0:T(8,128)S(1)} collective-permute-done((f32[22,8,128]{2,1,0:T(8,128)S(1)}, f32[22,8,128]{2,1,0:T(8,128)S(1)}, u32[]{:S(2)}, u32[]{:S(2)}) %collective-permute-start.9) | collective-permute-done | bytes 90144 | tf_op jit(solution)/shard_map/ppermute | solution.py:444
  40.9 1.9 %carried_response.1 = bf16[128,1024]{1,0:T(8,128)(2,1)} custom-call(f32[22,8,128]{2,1,0:T(8,128)S(1)} %collective-permute-done.9.refs_0_, f32[26,8,128]{2,1,0:T(8,128)S(1)} %get-tuple-element.66.local.refs_1_, f32[26,8,128]{2,1,0:T(8,128)S(1)} %collective-permute-done.8.partner.refs_2_, f32[128,8,128]{2,1,0:T(8,128)S(1)} %get-tuple-element.69.refs_3_, ...), custom_call_target="tpu_custom_call" | custom-call | tf_op jit(solution)/shard_map/carried_response/pallas_call | solution.py:457
  (7 shorter events, 0.0 us)
Async XLA Ops:
  0.0 9.5 %collective-permute-start.1 = (bf16[128,1024]{1,0:T(8,128)(2,1)}, bf16[128,1024]{1,0:T(8,128)(2,1)S(1)}, u32[]{:S(2)}, u32[]{:S(2)}) collective-permute-start(bf16[128,1024]{1,0:T(8,128)(2,1)} %x_ref.1), channel_id=1, source_target_pairs={{0,1},{1,3},{3,5},{5,7},{7,6},{6,4},{4,2},{2,0},{8,9},{9,11},{11,1... | collective-permute-start | bytes 786440 | tf_op jit(solution)/shard_map/ppermute | solution.py:379
  3.0 8.4 %collective-permute-start = (bf16[128,1024]{1,0:T(8,128)(2,1)}, bf16[128,1024]{1,0:T(8,128)(2,1)S(1)}, u32[]{:S(2)}, u32[]{:S(2)}) collective-permute-start(bf16[128,1024]{1,0:T(8,128)(2,1)} %x_ref.1), channel_id=1, source_target_pairs={{1,0},{3,1},{5,3},{7,5},{6,7},{4,6},{2,4},{0,2},{9,8},{11,9},{13,1... | collective-permute-start | bytes 786440 | tf_op jit(solution)/shard_map/ppermute | solution.py:380
  3.0 1.0 %copy-start = (bf16[128,1024]{1,0:T(8,128)(2,1)S(1)}, bf16[128,1024]{1,0:T(8,128)(2,1)}, u32[]{:S(2)}) copy-start(bf16[128,1024]{1,0:T(8,128)(2,1)} %x_ref.1) | copy-start | bytes 786436
  4.0 7.5 %copy-start.1 = (f32[16,1024]{1,0:T(8,128)S(1)}, f32[16,1024]{1,0:T(8,128)}, u32[]{:S(2)}) copy-start(f32[16,1024]{1,0:T(8,128)} %refs_1_.1) | copy-start | bytes 196612
  4.0 7.5 %copy-start.2 = (f32[16,1024]{1,0:T(8,128)S(1)}, f32[16,1024]{1,0:T(8,128)}, u32[]{:S(2)}) copy-start(f32[16,1024]{1,0:T(8,128)} %refs_2_.1) | copy-start | bytes 196612
  4.0 7.5 %copy-start.3 = (f32[3,3,1024]{2,1,0:T(4,128)S(1)}, f32[3,3,1024]{2,1,0:T(4,128)}, u32[]{:S(2)}) copy-start(f32[3,3,1024]{2,1,0:T(4,128)} %refs_0_.1) | copy-start | bytes 110596
  9.5 8.3 %collective-permute-start.3 = (bf16[128,1024]{1,0:T(8,128)(2,1)S(1)}, bf16[128,1024]{1,0:T(8,128)(2,1)S(1)}, u32[]{:S(2)}, u32[]{:S(2)}) collective-permute-start(bf16[128,1024]{1,0:T(8,128)(2,1)S(1)} %collective-permute-done.1.fore), channel_id=1, source_target_pairs={{0,1},{1,3},{3,5},{5,7},{7,6},{6,4},{4,2},{2,0},{8,9},{9,11},{11,1... | collective-permute-start | bytes 786440 | tf_op jit(solution)/shard_map/ppermute | solution.py:379
  11.4 8.2 %collective-permute-start.2 = (bf16[128,1024]{1,0:T(8,128)(2,1)S(1)}, bf16[128,1024]{1,0:T(8,128)(2,1)S(1)}, u32[]{:S(2)}, u32[]{:S(2)}) collective-permute-start(bf16[128,1024]{1,0:T(8,128)(2,1)S(1)} %collective-permute-done.aft), channel_id=1, source_target_pairs={{1,0},{3,1},{5,3},{7,5},{6,7},{4,6},{2,4},{0,2},{9,8},{11,9},{13,1... | collective-permute-start | bytes 786440 | tf_op jit(solution)/shard_map/ppermute | solution.py:380
  17.8 8.1 %collective-permute-start.5 = (bf16[128,1024]{1,0:T(8,128)(2,1)S(1)}, bf16[128,1024]{1,0:T(8,128)(2,1)S(1)}, u32[]{:S(2)}, u32[]{:S(2)}) collective-permute-start(bf16[128,1024]{1,0:T(8,128)(2,1)S(1)} %collective-permute-done.3.fore), channel_id=1, source_target_pairs={{0,1},{1,3},{3,5},{5,7},{7,6},{6,4},{4,2},{2,0},{8,9},{9,11},{11,1... | collective-permute-start | bytes 786440 | tf_op jit(solution)/shard_map/ppermute | solution.py:379
  19.6 8.2 %collective-permute-start.4 = (bf16[128,1024]{1,0:T(8,128)(2,1)S(1)}, bf16[128,1024]{1,0:T(8,128)(2,1)S(1)}, u32[]{:S(2)}, u32[]{:S(2)}) collective-permute-start(bf16[128,1024]{1,0:T(8,128)(2,1)S(1)} %collective-permute-done.2.aft), channel_id=1, source_target_pairs={{1,0},{3,1},{5,3},{7,5},{6,7},{4,6},{2,4},{0,2},{9,8},{11,9},{13,1... | collective-permute-start | bytes 786440 | tf_op jit(solution)/shard_map/ppermute | solution.py:380
  26.0 5.1 %collective-permute-start.7 = (bf16[128,512]{1,0:T(8,128)(2,1)S(1)}, bf16[128,512]{1,0:T(8,128)(2,1)S(1)}, u32[]{:S(2)}, u32[]{:S(2)}) collective-permute-start(bf16[128,512]{1,0:T(8,128)(2,1)S(1)} %slice.7), channel_id=1, source_target_pairs={{0,1},{1,3},{3,5},{5,7},{7,6},{6,4},{4,2},{2,0},{8,9},{9,11},{11,1... | collective-permute-start | bytes 393224 | tf_op jit(solution)/shard_map/ppermute | solution.py:406
  27.8 5.0 %collective-permute-start.6 = (bf16[128,512]{1,0:T(8,128)(2,1)S(1)}, bf16[128,512]{1,0:T(8,128)(2,1)S(1)}, u32[]{:S(2)}, u32[]{:S(2)}) collective-permute-start(bf16[128,512]{1,0:T(8,128)(2,1)S(1)} %slice.6), channel_id=1, source_target_pairs={{1,0},{3,1},{5,3},{7,5},{6,7},{4,6},{2,4},{0,2},{9,8},{11,9},{13,1... | collective-permute-start | bytes 393224 | tf_op jit(solution)/shard_map/ppermute | solution.py:407
  34.8 1.4 %collective-permute-start.8 = (f32[26,8,128]{2,1,0:T(8,128)S(1)}, f32[26,8,128]{2,1,0:T(8,128)S(1)}, u32[]{:S(2)}, u32[]{:S(2)}) collective-permute-start(f32[26,8,128]{2,1,0:T(8,128)S(1)} %get-tuple-element.66.local.refs_1_), channel_id=1, source_target_pairs={{0,8},{8,0},{16,24},{24,16},{1,9},{9,1},{17,25},{25,17},{2,10},{10... | collective-permute-start | bytes 319496 | tf_op jit(solution)/shard_map/ppermute | solution.py:433
  36.2 4.7 %collective-permute-start.9 = (f32[22,8,128]{2,1,0:T(8,128)S(1)}, f32[22,8,128]{2,1,0:T(8,128)S(1)}, u32[]{:S(2)}, u32[]{:S(2)}) collective-permute-start(f32[22,8,128]{2,1,0:T(8,128)S(1)} %chip_state.1), channel_id=1, source_target_pairs={{0,16},{8,24},{16,0},{24,8},{1,17},{9,25},{17,1},{25,9},{2,18},{10... | collective-permute-start | bytes 270344 | tf_op jit(solution)/shard_map/ppermute | solution.py:444

commit v7 on v6

--- a/solution.py
+++ b/solution.py
@@ -9,7 +9,7 @@
 
 LANES = 128
 COLS = 256
-DEPTH = 256
+SOON = 2
 GRID_ROWS = 4
 EDGE = 10
 UNROLL = 16
@@ -49,13 +49,13 @@
     ]
 
 
-def add_products(xs, weights, total, s):
+def add_products(xs, weights, total, s, fresh=False):
     for c in range(0, total.shape[2], COLS):
         at = slice(c, c + COLS)
         terms = [
             jnp.dot(x, weights(b, at), preferred_element_type=jnp.float32) for b, x in enumerate(xs)
         ]
-        total[s, :, at] += sum(terms)
+        total[s, :, at] = sum(terms) if fresh else total[s, :, at] + sum(terms)
 
 
 def spread(out_ref, value):
@@ -64,51 +64,33 @@
         out_ref[..., g, :] = value[..., g * lanes : (g + 1) * lanes]
 
 
-def first_kernel(order, steps, pieces, x_ref, w_ref, total, held, own, own_sem, held_sem):
-    width = x_ref.shape[1]
-    depth = min(DEPTH, width)
-    start = pl.multiple_of(owner_at(order, 0) * width, width)
-    chunks = [
-        pltpu.make_async_copy(
-            w_ref.at[:, pl.ds(start + k * depth, depth), :],
-            own.at[:, pl.ds(k * depth, depth), :],
-            own_sem.at[k],
-        )
-        for k in range(width // depth)
-    ]
-    ahead = piece_loads(order, steps, pieces, w_ref, lambda i, b, s: held.at[b, s], held_sem)
-    for copy in chunks + ahead:
+def load_kernel(order, steps, pieces, w_ref, held, sem):
+    copies = piece_loads(order, steps, pieces, w_ref, lambda i, b, s: held.at[b, s], sem)
+    for copy in copies:
         copy.start()
-    for k, copy in enumerate(chunks):
+    for copy in copies:
         copy.wait()
-        at = slice(k * depth, (k + 1) * depth)
-        for s in range(total.shape[0]):
-            for c in range(0, total.shape[2], COLS):
-                to = slice(c, c + COLS)
-                term = jnp.dot(x_ref[:, at], own[s, at, to], preferred_element_type=jnp.float32)
-                if k:
-                    total[s, :, to] += term
-                else:
-                    total[s, :, to] = term
-    for copy in ahead:
-        copy.wait()
-
-
-def middle_kernel(order, here, missing, steps, pieces, inputs_count, fore, aft, held, w_ref, _, *refs):
+
+
+def middle_kernel(order, here, missing, steps, pieces, inputs_count, *refs):
+    xs, (held, w_ref, *refs) = refs[: len(here)], refs[len(here) :]
     *refs, rest, rest_sem, sem = refs
     inputs, (total, next_held, *made) = refs[:inputs_count], refs[inputs_count:]
+    fresh = bool(made)
     late = piece_loads(order, here, missing, w_ref, lambda i, b, s: rest.at[i], rest_sem)
     ahead = piece_loads(order, steps, pieces, w_ref, lambda i, b, s: next_held.at[b, s], sem)
-    for copy in late + ahead:
+    for copy in late + ahead[:SOON]:
         copy.start()
     if made:
         make_tables(*inputs, *made, total.shape[1])
-    whole = min([s for _, s in missing], default=held.shape[1])
+    whole = min(s for _, s in missing)
 
     @pl.loop(0, whole)
     def _(s):
-        add_products([fore[...], aft[...]], lambda b, at: held[b, s, :, at], total, s)
-
+        add_products([x[...] for x in xs], lambda b, at: held[b, s, :, at], total, s, fresh)
+
+    for copy in ahead[SOON:]:
+        copy.start()
     for copy in late:
         copy.wait()
 
@@ -119,7 +101,7 @@
                 return rest[missing.index((b, s)), :, at]
             return held[b, s, :, at]
 
-        add_products([fore[...], aft[...]], weights, total, s)
+        add_products([x[...] for x in xs], weights, total, s, fresh)
 
     for copy in ahead:
         copy.wait()
@@ -353,55 +335,55 @@
     params = pltpu.CompilerParams(vmem_limit_bytes=12 << 20)
     cost = pl.CostEstimate(flops=0, bytes_accessed=16 << 20, transcendentals=0)
 
-    depth = min(DEPTH, width)
-    left = {1: [(0, streams - 1), (1, streams - 1)], 2: [(1, streams - 1)]}
+    def blocks(step):
+        return [0] + loads(1) if step == 1 else loads(step)
+
+    def left(step):
+        return [(len(blocks(step)) - 1, streams - 1)] if step < half else []
 
     def pieces(step):
-        every = [(b, s) for s in range(streams) for b in range(len(loads(step)))]
-        return [piece for piece in every if piece not in left.get(step, [])]
-
-    total, weights = pl.pallas_call(
-        functools.partial(first_kernel, order, loads(1), pieces(1)),
-        out_shape=[sums, held(2)],
-        in_specs=[VMEM, HBM],
-        out_specs=[VMEM] * 2,
-        scratch_shapes=[
-            pltpu.VMEM((streams, width, chans), jnp.bfloat16),
-            pltpu.SemaphoreType.DMA((width // depth,)),
-            pltpu.SemaphoreType.DMA((len(pieces(1)),)),
-        ],
+        every = [(b, s) for s in range(streams) for b in range(len(blocks(step)))]
+        return [piece for piece in every if piece not in left(step)]
+
+    weights = pl.pallas_call(
+        functools.partial(load_kernel, order, blocks(1), pieces(1)),
+        out_shape=held(len(blocks(1))),
+        in_specs=[HBM],
+        out_specs=VMEM,
+        scratch_shapes=[pltpu.SemaphoreType.DMA((len(pieces(1)),))],
         compiler_params=params,
         cost_estimate=cost,
-        name="project_own",
-    )(tokens, weight)
-    fore, aft = tokens, tokens
+        name="load_first",
+    )(weight)
+    fore, aft, total = tokens, tokens, None
     for step in range(1, half):
         fore = lax.ppermute(fore, "tp", ahead)
         aft = lax.ppermute(aft, "tp", back)
         fore, total, weights = lax.optimization_barrier((fore, total, weights))
         aft, total, weights = lax.optimization_barrier((aft, total, weights))
-        coming = loads(step + 1)
-        missing = left.get(step, [])
-        extra = [filter_taps, decay_rate, residue] if step == 1 else []
-        made = [f32(lags, streams, groups, LANES), f32(5, modes, groups, LANES)] if step == 1 else []
+        first = step == 1
+        xs = [tokens, fore, aft] if first else [fore, aft]
+        extra = [filter_taps, decay_rate, residue] if first else [total]
+        made = [f32(lags, streams, groups, LANES), f32(5, modes, groups, LANES)] if first else []
         total, weights, *made = pl.pallas_call(
             functools.partial(
-                middle_kernel, order, loads(step), missing, coming, pieces(step + 1), len(extra)
+                middle_kernel, order, blocks(step), left(step), blocks(step + 1), pieces(step + 1),
+                len(extra),
             ),
-            out_shape=[sums, held(len(coming))] + made,
-            in_specs=[VMEM, VMEM, VMEM, HBM, VMEM] + [VMEM] * len(extra),
+            out_shape=[sums, held(len(blocks(step + 1)))] + made,
+            in_specs=[VMEM] * (len(xs) + 1) + [HBM] + [VMEM] * len(extra),
             out_specs=[VMEM] * (2 + len(made)),
             scratch_shapes=[
-                pltpu.VMEM((max(len(missing), 1), width, chans), jnp.bfloat16),
-                pltpu.SemaphoreType.DMA((max(len(missing), 1),)),
+                pltpu.VMEM((len(left(step)), width, chans), jnp.bfloat16),
+                pltpu.SemaphoreType.DMA((len(left(step)),)),
                 pltpu.SemaphoreType.DMA((len(pieces(step + 1)),)),
             ],
-            input_output_aliases={4: 0},
+            input_output_aliases={} if first else {len(xs) + 2: 0},
             compiler_params=params,
             cost_estimate=cost,
-            name="project_pair",
-        )(fore, aft, weights, weight, total, *extra)
-        if made:
+            name="project_blocks",
+        )(*xs, weights, weight, *extra)
+        if first:
             taps, table = made
     fore = lax.ppermute(fore[:, : width // 2], "tp", ahead)
     aft = lax.ppermute(aft[:, width // 2 :], "tp", back)

time: 42.9 us -> 40.7 us (0.949)
  Pallas kernels: 26.6 us -> 25.6 us
  local copies, waits for them, and re-layouts: 1.03 us -> 0.03 us
    ppermute x1, waiting for transfers between devices: 1.14 us -> 0.1 us  [on_device(): aft = lax.ppermute(aft[:, width // 2:], 'tp', back)]
    pallas_call x4, Pallas kernels: 20.6 us -> 19.5 us  [the longest x3 13.6 us: on_device(): pl.pallas_call(functools.partial(middle_kernel, order, blocks(step), left...]
    unnamed x8, local copies, waits for them, and re-layouts: 1.01 us -> 0.01 us
    ppermute x3, waiting for transfers between devices: 0.14 us -> 0.98 us  [on_device(): fore = lax.ppermute(fore, 'tp', ahead)]
    ppermute x3, starting transfers between devices: 6.62 us -> 6.16 us  [on_device(): fore = lax.ppermute(fore, 'tp', ahead)]
  transfers between devices with their start and end apart: 10 -> 10, of which waited for: 4 -> 5; matrix products, arithmetic and copies ran while one was open for 0% -> 0% of each run, Pallas kernels for 53% -> 54%
where the time goes in v7:
time: 40.7 us; the launch traced here: 40.6 us
  Pallas kernels  25.6 us (63%)
  starting transfers between devices  10.8 us (27%)
  waiting for transfers between devices  3.96 us (10%)
    pallas_call x3, Pallas kernels, on_device(): pl.pallas_call(functools.partial(middle_kernel, order, blocks(step), left...  13.6 us
    ppermute x3, starting transfers between devices, on_device(): fore = lax.ppermute(fore, 'tp', ahead)  6.16 us
    pallas_call x1, Pallas kernels, on_device(): pl.pallas_call(functools.partial(load_kernel, order, blocks(1), pieces(1)...  5.97 us
    pallas_call x1, Pallas kernels, on_device(): pl.pallas_call(last_kernel, out_shape=[sums, wide, f32(modes + EDGE, grou...  1.94 us
    pallas_call x1, Pallas kernels, on_device(): pl.pallas_call(functools.partial(final_kernel, lone, len(sent)), out_shap...  1.85 us
    pallas_call x1, Pallas kernels, on_device(): pl.pallas_call(local_kernel, out_shape=[wide, wide], in_specs=[VMEM] * 4,...  1.62 us
    ppermute x1, waiting for transfers between devices, on_device(): lax.ppermute(chip, 'ctx', [(j, (j + d) % ctx) for j in range(ctx)])  1.57 us
    ppermute x1, starting transfers between devices, on_device(): fore = lax.ppermute(fore[:, :width // 2], 'tp', ahead)  1.56 us
  transfers between devices with their start and end apart: 10, of which 5 were waited for; matrix products, arithmetic and copies ran while one was open for 0% of the time, Pallas kernels for 54%

profile of v7, /device:TPU:0, one launch (start us, length us, event | category | flops | bytes accessed | tf_op | source)
XLA Modules:
  0.0 40.6 jit_solution(4676123196967350100)
XLA Ops:
  0.0 3.0 %collective-permute-start.1 = (bf16[128,1024]{1,0:T(8,128)(2,1)}, bf16[128,1024]{1,0:T(8,128)(2,1)S(1)}, u32[]{:S(2)}, u32[]{:S(2)}) collective-permute-start(bf16[128,1024]{1,0:T(8,128)(2,1)} %refs_0_.1), channel_id=1, source_target_pairs={{0,1},{1,3},{3,5},{5,7},{7,6},{6,4},{4,2},{2,0},{8,9},{9,11},{11,1... | collective-permute-start | bytes 786440 | tf_op jit(solution)/shard_map/ppermute | solution.py:360
  3.0 0.1 collective-permute-start
  3.0 6.0 %load_first.1.refs_3_ = bf16[3,3,1024,1024]{3,2,1,0:T(8,128)(2,1)S(1)} custom-call(bf16[3,8192,1024]{2,1,0:T(8,128)(2,1)} %bitcast.1), custom_call_target="tpu_custom_call" | custom-call | bytes 16777216 | tf_op jit(solution)/shard_map/load_first/pallas_call | solution.py:348
  9.0 0.5 %collective-permute-done.1.refs_1_ = bf16[128,1024]{1,0:T(8,128)(2,1)S(1)} collective-permute-done((bf16[128,1024]{1,0:T(8,128)(2,1)}, bf16[128,1024]{1,0:T(8,128)(2,1)S(1)}, u32[]{:S(2)}, u32[]{:S(2)}) %collective-permute-start.1) | collective-permute-done | bytes 262176 | tf_op jit(solution)/shard_map/ppermute | solution.py:360
  9.5 1.7 %collective-permute-start.3 = (bf16[128,1024]{1,0:T(8,128)(2,1)S(1)}, bf16[128,1024]{1,0:T(8,128)(2,1)S(1)}, u32[]{:S(2)}, u32[]{:S(2)}) collective-permute-start(bf16[128,1024]{1,0:T(8,128)(2,1)S(1)} %collective-permute-done.1.refs_1_), channel_id=1, source_target_pairs={{0,1},{1,3},{3,5},{5,7},{7,6},{6,4},{4,2},{2,0},{8,9},{9,11},{11,1... | collective-permute-start | bytes 786440 | tf_op jit(solution)/shard_map/ppermute | solution.py:360
  11.2 0.0 collective-permute-done.refs_2_
  11.2 0.3 collective-permute-start.2
  11.6 0.0 copy-done
  11.6 0.0 copy-done.1
  11.6 0.0 copy-done.2
  11.6 0.0 copy-done.3
  11.6 5.0 %project_blocks.3 = (f32[3,128,1024]{2,1,0:T(8,128)S(1)}, bf16[2,3,1024,1024]{3,2,1,0:T(8,128)(2,1)S(1)}, f32[3,3,8,128]{3,2,1,0:T(8,128)S(1)}, f32[5,16,8,128]{3,2,1,0:T(8,128)S(1)}) custom-call(bf16[128,1024]{1,0:T(8,128)(2,1)S(1)} %copy-done, bf16[128,1024]{1,0:T(8,128)(2,1)S(1)} %collective-permute-done.1.refs_1_, ...), custom_call_target="tpu_custom_call" | custom-call | bytes 16777216 | tf_op jit(solution)/shard_map/project_blocks/pallas_call | solution.py:368
  16.6 0.5 %collective-permute-done.3.refs_0_ = bf16[128,1024]{1,0:T(8,128)(2,1)S(1)} collective-permute-done((bf16[128,1024]{1,0:T(8,128)(2,1)S(1)}, bf16[128,1024]{1,0:T(8,128)(2,1)S(1)}, u32[]{:S(2)}, u32[]{:S(2)}) %collective-permute-start.3) | collective-permute-done | bytes 262176 | tf_op jit(solution)/shard_map/ppermute | solution.py:360
  17.0 1.5 %collective-permute-start.5 = (bf16[128,1024]{1,0:T(8,128)(2,1)S(1)}, bf16[128,1024]{1,0:T(8,128)(2,1)S(1)}, u32[]{:S(2)}, u32[]{:S(2)}) collective-permute-start(bf16[128,1024]{1,0:T(8,128)(2,1)S(1)} %collective-permute-done.3.refs_0_), channel_id=1, source_target_pairs={{0,1},{1,3},{3,5},{5,7},{7,6},{6,4},{4,2},{2,0},{8,9},{9,11},{11,1... | collective-permute-start | bytes 786440 | tf_op jit(solution)/shard_map/ppermute | solution.py:360
  18.5 0.0 collective-permute-done.2.refs_1_
  18.5 0.5 %collective-permute-start.4 = (bf16[128,1024]{1,0:T(8,128)(2,1)S(1)}, bf16[128,1024]{1,0:T(8,128)(2,1)S(1)}, u32[]{:S(2)}, u32[]{:S(2)}) collective-permute-start(bf16[128,1024]{1,0:T(8,128)(2,1)S(1)} %collective-permute-done.2.refs_1_), channel_id=1, source_target_pairs={{1,0},{3,1},{5,3},{7,5},{6,7},{4,6},{2,4},{0,2},{9,8},{11,9},{13,1... | collective-permute-start | bytes 786440 | tf_op jit(solution)/shard_map/ppermute | solution.py:361
  19.1 4.9 %project_blocks.4 = (f32[3,128,1024]{2,1,0:T(8,128)S(1)}, bf16[2,3,1024,1024]{3,2,1,0:T(8,128)(2,1)S(1)}) custom-call(bf16[128,1024]{1,0:T(8,128)(2,1)S(1)} %collective-permute-done.3.refs_0_, bf16[128,1024]{1,0:T(8,128)(2,1)S(1)} %collective-permute-done.2.refs_1_, ...), custom_call_target="tpu_custom_call", output_to_operand_aliasing={{0}: (4, {})} | custom-call | bytes 16777216 | tf_op jit(solution)/shard_map/project_blocks/pallas_call | solution.py:368
  24.0 0.0 collective-permute-done.5.refs_0_
  24.0 1.6 %collective-permute-start.7 = (bf16[128,512]{1,0:T(8,128)(2,1)S(1)}, bf16[128,512]{1,0:T(8,128)(2,1)S(1)}, u32[]{:S(2)}, u32[]{:S(2)}) collective-permute-start(bf16[128,512]{1,0:T(8,128)(2,1)S(1)} %slice.7), channel_id=1, source_target_pairs={{0,1},{1,3},{3,5},{5,7},{7,6},{6,4},{4,2},{2,0},{8,9},{9,11},{11,1... | collective-permute-start | bytes 393224 | tf_op jit(solution)/shard_map/ppermute | solution.py:388
  25.6 0.0 collective-permute-done.4.refs_1_
  25.6 0.6 %collective-permute-start.6 = (bf16[128,512]{1,0:T(8,128)(2,1)S(1)}, bf16[128,512]{1,0:T(8,128)(2,1)S(1)}, u32[]{:S(2)}, u32[]{:S(2)}) collective-permute-start(bf16[128,512]{1,0:T(8,128)(2,1)S(1)} %slice.6), channel_id=1, source_target_pairs={{1,0},{3,1},{5,3},{7,5},{6,7},{4,6},{2,4},{0,2},{9,8},{11,9},{13,1... | collective-permute-start | bytes 393224 | tf_op jit(solution)/shard_map/ppermute | solution.py:389
  26.1 3.7 %project_blocks.5 = (f32[3,128,1024]{2,1,0:T(8,128)S(1)}, bf16[1,3,1024,1024]{3,2,1,0:T(8,128)(2,1)S(1)}) custom-call(bf16[128,1024]{1,0:T(8,128)(2,1)S(1)} %collective-permute-done.5.refs_0_, bf16[128,1024]{1,0:T(8,128)(2,1)S(1)} %collective-permute-done.4.refs_1_, ...), custom_call_target="tpu_custom_call", output_to_operand_aliasing={{0}: (4, {})} | custom-call | bytes 16777216 | tf_op jit(solution)/shard_map/project_blocks/pallas_call | solution.py:368
  29.8 0.0 collective-permute-done.7.x_ref
  29.9 0.6 %project_half.1._ = f32[3,128,1024]{2,1,0:T(8,128)S(1)} custom-call(bf16[128,512]{1,0:T(8,128)(2,1)S(1)} %collective-permute-done.7.x_ref, bf16[1,3,1024,1024]{3,2,1,0:T(8,128)(2,1)S(1)} %get-tuple-element.54.held, f32[3,128,1024]{2,1,0:T(8,128)S(1)} %get-tuple-element.57._), custom_call_target="tpu_custom_call", output_to_operand_aliasing={{}: (2, {})} | custom-call | bytes 16777216 | tf_op jit(solution)/shard_map/project_half/pallas_call | solution.py:390
  30.5 0.1 collective-permute-done.6.x_ref
  30.6 1.9 %project_last.1 = (f32[3,128,1024]{2,1,0:T(8,128)S(1)}, f32[128,8,128]{2,1,0:T(8,128)S(1)}, f32[26,8,128]{2,1,0:T(8,128)S(1)}) custom-call(bf16[128,512]{1,0:T(8,128)(2,1)S(1)} %collective-permute-done.6.x_ref, bf16[1,3,1024,1024]{3,2,1,0:T(8,128)(2,1)S(1)} %get-tuple-element.54.held, ...), custom_call_target="tpu_custom_call", output_to_operand_aliasing={{0}: (4, {})} | custom-call | bytes 16777216 | tf_op jit(solution)/shard_map/project_last/pallas_call | solution.py:400
  32.5 0.1 collective-permute-start.8
  32.6 1.3 %collective-permute-done.8.partner.refs_2_ = f32[26,8,128]{2,1,0:T(8,128)S(1)} collective-permute-done((f32[26,8,128]{2,1,0:T(8,128)S(1)}, f32[26,8,128]{2,1,0:T(8,128)S(1)}, u32[]{:S(2)}, u32[]{:S(2)}) %collective-permute-start.8) | collective-permute-done | bytes 106528 | tf_op jit(solution)/shard_map/ppermute | solution.py:415
  34.0 1.6 %collective-permute-start.9 = (f32[22,8,128]{2,1,0:T(8,128)S(1)}, f32[22,8,128]{2,1,0:T(8,128)S(1)}, u32[]{:S(2)}, u32[]{:S(2)}) collective-permute-start(f32[22,8,128]{2,1,0:T(8,128)S(1)} %chip_state.1), channel_id=1, source_target_pairs={{0,16},{8,24},{16,0},{24,8},{1,17},{9,25},{17,1},{25,9},{2,18},{10... | collective-permute-start | bytes 270344 | tf_op jit(solution)/shard_map/ppermute | solution.py:426
  35.5 1.6 %local_response.1 = (f32[128,8,128]{2,1,0:T(8,128)S(1)}, f32[128,8,128]{2,1,0:T(8,128)S(1)}) custom-call(f32[3,128,1024]{2,1,0:T(8,128)S(1)} %get-tuple-element.59.total, f32[128,8,128]{2,1,0:T(8,128)S(1)} %get-tuple-element.60.source, f32[3,3,8,128]{3,2,1,0:T(8,128)S(1)} %get-tuple-element.55.taps.refs_5_, f32[5,16,8,128]{3,2,1,0:T(8,128)S(1)} %get-tuple-element.56.table.refs_6_), custom_call_target="tpu_custom_call" | custom-call | bytes 16777216 | tf_op jit(solution)/shard_map/local_response/pallas_call | solution.py:429
  37.1 1.6 %collective-permute-done.9.refs_0_ = f32[22,8,128]{2,1,0:T(8,128)S(1)} collective-permute-done((f32[22,8,128]{2,1,0:T(8,128)S(1)}, f32[22,8,128]{2,1,0:T(8,128)S(1)}, u32[]{:S(2)}, u32[]{:S(2)}) %collective-permute-start.9) | collective-permute-done | bytes 90144 | tf_op jit(solution)/shard_map/ppermute | solution.py:426
  38.7 1.9 %carried_response.1 = bf16[128,1024]{1,0:T(8,128)(2,1)} custom-call(f32[22,8,128]{2,1,0:T(8,128)S(1)} %collective-permute-done.9.refs_0_, f32[26,8,128]{2,1,0:T(8,128)S(1)} %get-tuple-element.58.local.refs_1_, f32[26,8,128]{2,1,0:T(8,128)S(1)} %collective-permute-done.8.partner.refs_2_, f32[128,8,128]{2,1,0:T(8,128)S(1)} %get-tuple-element.61.refs_3_, ...), custom_call_target="tpu_custom_call" | custom-call | tf_op jit(solution)/shard_map/carried_response/pallas_call | solution.py:439
  (7 shorter events, 0.1 us)
Async XLA Ops:
  0.0 9.5 %collective-permute-start.1 = (bf16[128,1024]{1,0:T(8,128)(2,1)}, bf16[128,1024]{1,0:T(8,128)(2,1)S(1)}, u32[]{:S(2)}, u32[]{:S(2)}) collective-permute-start(bf16[128,1024]{1,0:T(8,128)(2,1)} %refs_0_.1), channel_id=1, source_target_pairs={{0,1},{1,3},{3,5},{5,7},{7,6},{6,4},{4,2},{2,0},{8,9},{9,11},{11,1... | collective-permute-start | bytes 786440 | tf_op jit(solution)/shard_map/ppermute | solution.py:360
  3.0 8.3 %collective-permute-start = (bf16[128,1024]{1,0:T(8,128)(2,1)}, bf16[128,1024]{1,0:T(8,128)(2,1)S(1)}, u32[]{:S(2)}, u32[]{:S(2)}) collective-permute-start(bf16[128,1024]{1,0:T(8,128)(2,1)} %refs_0_.1), channel_id=1, source_target_pairs={{1,0},{3,1},{5,3},{7,5},{6,7},{4,6},{2,4},{0,2},{9,8},{11,9},{13,1... | collective-permute-start | bytes 786440 | tf_op jit(solution)/shard_map/ppermute | solution.py:361
  3.0 8.5 %copy-start = (bf16[128,1024]{1,0:T(8,128)(2,1)S(1)}, bf16[128,1024]{1,0:T(8,128)(2,1)}, u32[]{:S(2)}) copy-start(bf16[128,1024]{1,0:T(8,128)(2,1)} %refs_0_.1) | copy-start | bytes 786436
  3.0 8.5 %copy-start.1 = (f32[16,1024]{1,0:T(8,128)S(1)}, f32[16,1024]{1,0:T(8,128)}, u32[]{:S(2)}) copy-start(f32[16,1024]{1,0:T(8,128)} %refs_6_.1) | copy-start | bytes 196612
  3.0 8.5 %copy-start.2 = (f32[16,1024]{1,0:T(8,128)S(1)}, f32[16,1024]{1,0:T(8,128)}, u32[]{:S(2)}) copy-start(f32[16,1024]{1,0:T(8,128)} %refs_7_.1) | copy-start | bytes 196612
  3.0 8.5 %copy-start.3 = (f32[3,3,1024]{2,1,0:T(4,128)S(1)}, f32[3,3,1024]{2,1,0:T(4,128)}, u32[]{:S(2)}) copy-start(f32[3,3,1024]{2,1,0:T(4,128)} %refs_5_.1) | copy-start | bytes 110596
  9.5 7.5 %collective-permute-start.3 = (bf16[128,1024]{1,0:T(8,128)(2,1)S(1)}, bf16[128,1024]{1,0:T(8,128)(2,1)S(1)}, u32[]{:S(2)}, u32[]{:S(2)}) collective-permute-start(bf16[128,1024]{1,0:T(8,128)(2,1)S(1)} %collective-permute-done.1.refs_1_), channel_id=1, source_target_pairs={{0,1},{1,3},{3,5},{5,7},{7,6},{6,4},{4,2},{2,0},{8,9},{9,11},{11,1... | collective-permute-start | bytes 786440 | tf_op jit(solution)/shard_map/ppermute | solution.py:360
  11.2 7.3 %collective-permute-start.2 = (bf16[128,1024]{1,0:T(8,128)(2,1)S(1)}, bf16[128,1024]{1,0:T(8,128)(2,1)S(1)}, u32[]{:S(2)}, u32[]{:S(2)}) collective-permute-start(bf16[128,1024]{1,0:T(8,128)(2,1)S(1)} %collective-permute-done.refs_2_), channel_id=1, source_target_pairs={{1,0},{3,1},{5,3},{7,5},{6,7},{4,6},{2,4},{0,2},{9,8},{11,9},{13,1... | collective-permute-start | bytes 786440 | tf_op jit(solution)/shard_map/ppermute | solution.py:361
  17.0 6.9 %collective-permute-start.5 = (bf16[128,1024]{1,0:T(8,128)(2,1)S(1)}, bf16[128,1024]{1,0:T(8,128)(2,1)S(1)}, u32[]{:S(2)}, u32[]{:S(2)}) collective-permute-start(bf16[128,1024]{1,0:T(8,128)(2,1)S(1)} %collective-permute-done.3.refs_0_), channel_id=1, source_target_pairs={{0,1},{1,3},{3,5},{5,7},{7,6},{6,4},{4,2},{2,0},{8,9},{9,11},{11,1... | collective-permute-start | bytes 786440 | tf_op jit(solution)/shard_map/ppermute | solution.py:360
  18.5 7.0 %collective-permute-start.4 = (bf16[128,1024]{1,0:T(8,128)(2,1)S(1)}, bf16[128,1024]{1,0:T(8,128)(2,1)S(1)}, u32[]{:S(2)}, u32[]{:S(2)}) collective-permute-start(bf16[128,1024]{1,0:T(8,128)(2,1)S(1)} %collective-permute-done.2.refs_1_), channel_id=1, source_target_pairs={{1,0},{3,1},{5,3},{7,5},{6,7},{4,6},{2,4},{0,2},{9,8},{11,9},{13,1... | collective-permute-start | bytes 786440 | tf_op jit(solution)/shard_map/ppermute | solution.py:361
  24.0 5.8 %collective-permute-start.7 = (bf16[128,512]{1,0:T(8,128)(2,1)S(1)}, bf16[128,512]{1,0:T(8,128)(2,1)S(1)}, u32[]{:S(2)}, u32[]{:S(2)}) collective-permute-start(bf16[128,512]{1,0:T(8,128)(2,1)S(1)} %slice.7), channel_id=1, source_target_pairs={{0,1},{1,3},{3,5},{5,7},{7,6},{6,4},{4,2},{2,0},{8,9},{9,11},{11,1... | collective-permute-start | bytes 393224 | tf_op jit(solution)/shard_map/ppermute | solution.py:388
  25.6 5.0 %collective-permute-start.6 = (bf16[128,512]{1,0:T(8,128)(2,1)S(1)}, bf16[128,512]{1,0:T(8,128)(2,1)S(1)}, u32[]{:S(2)}, u32[]{:S(2)}) collective-permute-start(bf16[128,512]{1,0:T(8,128)(2,1)S(1)} %slice.6), channel_id=1, source_target_pairs={{1,0},{3,1},{5,3},{7,5},{6,7},{4,6},{2,4},{0,2},{9,8},{11,9},{13,1... | collective-permute-start | bytes 393224 | tf_op jit(solution)/shard_map/ppermute | solution.py:389
  32.5 1.4 %collective-permute-start.8 = (f32[26,8,128]{2,1,0:T(8,128)S(1)}, f32[26,8,128]{2,1,0:T(8,128)S(1)}, u32[]{:S(2)}, u32[]{:S(2)}) collective-permute-start(f32[26,8,128]{2,1,0:T(8,128)S(1)} %get-tuple-element.58.local.refs_1_), channel_id=1, source_target_pairs={{0,8},{8,0},{16,24},{24,16},{1,9},{9,1},{17,25},{25,17},{2,10},{10... | collective-permute-start | bytes 319496 | tf_op jit(solution)/shard_map/ppermute | solution.py:415
  34.0 4.7 %collective-permute-start.9 = (f32[22,8,128]{2,1,0:T(8,128)S(1)}, f32[22,8,128]{2,1,0:T(8,128)S(1)}, u32[]{:S(2)}, u32[]{:S(2)}) collective-permute-start(f32[22,8,128]{2,1,0:T(8,128)S(1)} %chip_state.1), channel_id=1, source_target_pairs={{0,16},{8,24},{16,0},{24,8},{1,17},{9,25},{17,1},{25,9},{2,18},{10... | collective-permute-start | bytes 270344 | tf_op jit(solution)/shard_map/ppermute | solution.py:426

commit v8 on v7

--- a/solution.py
+++ b/solution.py
@@ -13,7 +13,6 @@
 GRID_ROWS = 4
 EDGE = 10
 UNROLL = 16
-PIECE = 32
 VMEM = pl.BlockSpec(memory_space=pltpu.VMEM)
 HBM = pl.BlockSpec(memory_space=pltpu.HBM)
 
@@ -43,9 +42,9 @@
     starts = [pl.multiple_of(owner_at(order, step) * width, width) for step in steps]
     return [
         pltpu.make_async_copy(
-            w_ref.at[s, pl.ds(starts[b], width), :], target(i, b, s), sem.at[i]
+            w_ref.at[s, pl.ds(starts[b] + low, high - low), :], target(i, b, s, low, high), sem.at[i]
         )
-        for i, (b, s) in enumerate(pieces)
+        for i, (b, s, low, high) in enumerate(pieces)
     ]
 
 
@@ -64,8 +63,12 @@
         out_ref[..., g, :] = value[..., g * lanes : (g + 1) * lanes]
 
 
+def held_part(held):
+    return lambda i, b, s, low, high: held.at[b, s, pl.ds(low, high - low), :]
+
+
 def load_kernel(order, steps, pieces, w_ref, held, sem):
-    copies = piece_loads(order, steps, pieces, w_ref, lambda i, b, s: held.at[b, s], sem)
+    copies = piece_loads(order, steps, pieces, w_ref, held_part(held), sem)
     for copy in copies:
         copy.start()
     for copy in copies:
@@ -77,13 +80,13 @@
     *refs, rest, rest_sem, sem = refs
     inputs, (total, next_held, *made) = refs[:inputs_count], refs[inputs_count:]
     fresh = bool(made)
-    late = piece_loads(order, here, missing, w_ref, lambda i, b, s: rest.at[i], rest_sem)
-    ahead = piece_loads(order, steps, pieces, w_ref, lambda i, b, s: next_held.at[b, s], sem)
+    late = piece_loads(order, here, missing, w_ref, lambda i, *_: rest.at[i], rest_sem)
+    ahead = piece_loads(order, steps, pieces, w_ref, held_part(next_held), sem)
     for copy in late + ahead[:SOON]:
         copy.start()
     if made:
         make_tables(*inputs, *made, total.shape[1])
-    whole = min(s for _, s in missing)
+    whole = held.shape[1] - len(missing)
 
     @pl.loop(0, whole)
     def _(s):
@@ -93,16 +96,12 @@
         copy.start()
     for copy in late:
         copy.wait()
-
-    for s in range(whole, held.shape[1]):
-
-        def weights(b, at):
-            if (b, s) in missing:
-                return rest[missing.index((b, s)), :, at]
-            return held[b, s, :, at]
-
-        add_products([x[...] for x in xs], weights, total, s, fresh)
-
+    for i, (b, s, low, _) in enumerate(missing):
+        parts = [(x[...], (lambda at, k=k: held[k, s, :, at])) for k, x in enumerate(xs) if k != b]
+        parts.append((xs[b][:, :low], lambda at: held[b, s, :low, at]))
+        parts.append((xs[b][:, low:], lambda at: rest[i, :, at]))
+        values, weights = zip(*parts)
+        add_products(values, lambda k, at: weights[k](at), total, s, fresh)
     for copy in ahead:
         copy.wait()
 
@@ -113,12 +112,16 @@
         add_products([x_ref[...]], lambda b, at: held[0, s, :depth, at], total, s)
 
 
-def make_tables(taps_in, decay, residue, taps, table, rows):
+def make_tables(taps_in, decay, residue, taps, table, tile, tile_step, rows):
     rate = decay[...]
+    coeffs = residue[...] * jnp.sqrt(1.0 - jnp.exp(-2.0 * rate))
     for i, power in enumerate((1, rows, rows - 1, rows - 2)):
         spread(table.at[i], jnp.exp(-rate * power))
-    spread(table.at[4], residue[...] * jnp.sqrt(1.0 - jnp.exp(-2.0 * rate)))
+    spread(table.at[4], coeffs)
     spread(taps, taps_in[...])
+    for r in range(tile.shape[1]):
+        tile[:, r, :] = coeffs * jnp.exp(-rate * (r - 1.0))
+    tile_step[...] = jnp.exp(-rate * tile.shape[1])
 
 
 def over_rows(step, start, stop, carry):
@@ -134,40 +137,41 @@
     return lax.fori_loop(aligned // UNROLL, stop // UNROLL, group, carry)
 
 
-def filtered(taps, p_ref, s, t):
-    return (
-        taps[0, s] * p_ref[s - 1, t]
-        + taps[1, s] * p_ref[s - 1, t - 1]
-        + taps[2, s] * p_ref[s - 1, t - 2]
-    )
-
-
-def last_kernel(x_ref, held, taps, table, _, total, source, out_ref, p_ref, tail):
+def filtered(taps, s, value, cols):
+    one, two = pltpu.roll(value, 1, 0), pltpu.roll(value, 2, 0)
+    lags = [taps[j, s : s + 1, cols] for j in range(3)]
+    return lags[0] * value + lags[1] * one + lags[2] * two
+
+
+def last_kernel(x_ref, held, taps, table, _, total, source, out_ref, low, high):
     depth = x_ref.shape[1]
     for s in range(total.shape[0]):
         add_products([x_ref[...]], lambda b, at: held[0, s, depth:, at], total, s)
     rows, groups, lanes = source.shape
     modes = table.shape[1]
-    for s in (1, 2):
-        spread(p_ref.at[s - 1], rounded(total[s]))
-    spread(tail, rounded(total[0, rows - 8 :]))
+    for g in range(groups):
+        cols = slice(g * lanes, (g + 1) * lanes)
+        one, two = rounded(total[1, :, cols]), rounded(total[2, :, cols])
+        source[:, g, :] = filtered(taps, 1, one, cols) * filtered(taps, 2, two, cols)
+        for s, value in ((1, one), (2, two)):
+            low[s - 1, :, g, :] = value[:8]
+            high[s, :, g, :] = value[rows - 8 :]
+        high[0, :, g, :] = rounded(total[0, rows - 8 :, cols])
     rate = [table[0, n] for n in range(modes)]
 
     def step_row(t, state):
-        u = filtered(taps, p_ref, 1, t) * filtered(taps, p_ref, 2, t)
-        source[t] = u
+        u = source[t]
         return [r * s + u for r, s in zip(rate, state)]
 
     state = [jnp.zeros((groups, lanes), jnp.float32)] * modes
     state = over_rows(step_row, 2, rows, state)
     for n in range(modes):
         out_ref[n] = state[n]
-    for s in (1, 2):
-        for j in range(2):
-            out_ref[modes + (s - 1) * 2 + j] = p_ref[s - 1, j]
-            out_ref[modes + 4 + s * 2 + j] = p_ref[s - 1, rows - 2 + j]
     for j in range(2):
-        out_ref[modes + 4 + j] = tail[6 + j]
+        for s in (1, 2):
+            out_ref[modes + (s - 1) * 2 + j] = low[s - 1, j]
+        for s in range(3):
+            out_ref[modes + 4 + s * 2 + j] = high[s, 6 + j]
 
 
 def rounded(value):
@@ -180,22 +184,27 @@
     return terms[0]
 
 
-def local_kernel(total, source, taps, table, query, response, p_ref):
+def local_kernel(total, source, taps, table, query, response, heads, work, low):
     rows, groups, lanes = source.shape
     modes = table.shape[1]
-    spread(p_ref, rounded(total[0]))
+    for g in range(groups):
+        cols = slice(g * lanes, (g + 1) * lanes)
+        value = rounded(total[0, :, cols])
+        query[:, cols] = filtered(taps, 0, value, cols)
+        low[:, g, :] = value[:8]
     for j in range(2):
-        query[j] = p_ref[j]
+        heads[j] = low[j]
+        work[j] = jnp.zeros((groups, lanes), jnp.float32)
 
     def step_row(t, state):
-        query[t] = taps[0, 0] * p_ref[t] + taps[1, 0] * p_ref[t - 1] + taps[2, 0] * p_ref[t - 2]
         u = source[t]
         state = [table[0, n] * state[n] + u for n in range(modes)]
-        response[t] = tree_sum([table[4, n] * state[n] for n in range(modes)])
+        work[t] = tree_sum([table[4, n] * state[n] for n in range(modes)])
         return state
 
-    state = [jnp.zeros((groups, lanes), jnp.float32)] * modes
-    over_rows(step_row, 2, rows, state)
+    over_rows(step_row, 2, rows, [jnp.zeros((groups, lanes), jnp.float32)] * modes)
+    for g in range(groups):
+        response[:, g * lanes : (g + 1) * lanes] = work[:, g, :]
 
 
 def edge(taps, s, first, second, before, last):
@@ -256,8 +265,10 @@
 
 def final_kernel(lone, count, *refs):
     sent = refs[:count]
-    local, partner, query, response, taps, table, out_ref, work, rounded_out, out_sem = refs[count:]
-    rows, groups, lanes = query.shape
+    local, partner, query, response, query_heads, taps, table, tile, tile_step, *refs = refs[count:]
+    out_ref, states, firsts, rounded_out, out_sem = refs
+    rows = query.shape[0]
+    groups, lanes = local.shape[1:]
     modes = table.shape[1]
     zero = jnp.zeros((groups, lanes), jnp.float32)
     index = lax.axis_index("ctx")
@@ -285,25 +296,37 @@
     rim = [jnp.where(odd, a, b) for a, b in zip(before.rims, rims[0])]
 
     leads = lead_sources(taps, Summary.read(local, modes).heads, rim)
-    heads = edge(taps, 0, query[0], query[1], rim[0], rim[1])
+    heads = edge(taps, 0, query_heads[0], query_heads[1], rim[0], rim[1])
     for t, u in enumerate(leads):
         state = [table[0, n] * state[n] + u for n in range(modes)]
-        work[t] = heads[t] * tree_sum([table[4, n] * state[n] for n in range(modes)])
-    carried = [table[4, n] * state[n] for n in range(modes)]
-
-    def row(t, carried):
-        carried = [table[0, n] * carried[n] for n in range(modes)]
-        work[t] = query[t] * (response[t] + tree_sum(carried))
-        return carried
-
+        firsts[t] = heads[t] * tree_sum([table[4, n] * state[n] for n in range(modes)])
+    for n in range(modes):
+        states[n] = state[n]
+
+    tall = tile.shape[1]
+    row = lax.broadcasted_iota(jnp.int32, (tall, lanes), 0)
     copies = []
-    for i in range(rows // PIECE):
-        at = slice(i * PIECE, (i + 1) * PIECE)
-        carried = over_rows(row, max(i * PIECE, 2), (i + 1) * PIECE, carried)
-        for g in range(groups):
-            rounded_out[at, g * lanes : (g + 1) * lanes] = work[at, g, :].astype(out_ref.dtype)
-        copies.append(pltpu.make_async_copy(rounded_out.at[at], out_ref.at[at], out_sem.at[i]))
-        copies[-1].start()
+    for g in range(groups):
+        cols = slice(g * lanes, (g + 1) * lanes)
+        carried = [tile[n, :, cols] * states[n, g : g + 1, :] for n in range(modes)]
+        step = [jnp.broadcast_to(tile_step[n : n + 1, cols], (tall, lanes)) for n in range(modes)]
+        for i in range(0, rows, 2 * tall):
+            pair = []
+            for at in (slice(i, i + tall), slice(i + tall, i + 2 * tall)):
+                value = query[at, cols] * (response[at, cols] + tree_sum(carried))
+                if at.start == 0:
+                    value = jnp.where(row == 0, firsts[0, g : g + 1, :], value)
+                    value = jnp.where(row == 1, firsts[1, g : g + 1, :], value)
+                pair.append(value)
+                carried = [a * b for a, b in zip(carried, step)]
+            rounded_out[i : i + 2 * tall, cols] = jnp.concatenate(pair, axis=0).astype(out_ref.dtype)
+        if g % 2:
+            wide = slice((g - 1) * lanes, (g + 1) * lanes)
+            k = g // 2
+            copies.append(
+                pltpu.make_async_copy(rounded_out.at[:, wide], out_ref.at[:, wide], out_sem.at[k])
+            )
+            copies[-1].start()
     for copy in copies:
         copy.wait()
 
@@ -339,11 +362,13 @@
         return [0] + loads(1) if step == 1 else loads(step)
 
     def left(step):
-        return [(len(blocks(step)) - 1, streams - 1)] if step < half else []
+        rows_left = (width // 2, width)
+        return [(len(blocks(step)) - 1, streams - 1, *rows_left)] if step % 2 and step < half else []
 
     def pieces(step):
+        lacking = {(b, s): low for b, s, low, _ in left(step)}
         every = [(b, s) for s in range(streams) for b in range(len(blocks(step)))]
-        return [piece for piece in every if piece not in left(step)]
+        return [(b, s, 0, lacking.get((b, s), width)) for b, s in every]
 
     weights = pl.pallas_call(
         functools.partial(load_kernel, order, blocks(1), pieces(1)),
@@ -364,7 +389,10 @@
         first = step == 1
         xs = [tokens, fore, aft] if first else [fore, aft]
         extra = [filter_taps, decay_rate, residue] if first else [total]
-        made = [f32(lags, streams, groups, LANES), f32(5, modes, groups, LANES)] if first else []
+        made = []
+        if first:
+            made = [f32(lags, streams, groups, LANES), f32(5, modes, groups, LANES)]
+            made += [f32(modes, 8, chans), f32(modes, chans)]
         total, weights, *made = pl.pallas_call(
             functools.partial(
                 middle_kernel, order, blocks(step), left(step), blocks(step + 1), pieces(step + 1),
@@ -374,8 +402,8 @@
             in_specs=[VMEM] * (len(xs) + 1) + [HBM] + [VMEM] * len(extra),
             out_specs=[VMEM] * (2 + len(made)),
             scratch_shapes=[
-                pltpu.VMEM((len(left(step)), width, chans), jnp.bfloat16),
-                pltpu.SemaphoreType.DMA((len(left(step)),)),
+                pltpu.VMEM((1, width // 2, chans), jnp.bfloat16),
+                pltpu.SemaphoreType.DMA((1,)),
                 pltpu.SemaphoreType.DMA((len(pieces(step + 1)),)),
             ],
             input_output_aliases={} if first else {len(xs) + 2: 0},
@@ -384,7 +412,7 @@
             name="project_blocks",
         )(*xs, weights, weight, *extra)
         if first:
-            taps, table = made
+            taps, table, *tiles = made
     fore = lax.ppermute(fore[:, : width // 2], "tp", ahead)
     aft = lax.ppermute(aft[:, width // 2 :], "tp", back)
     total = pl.pallas_call(
@@ -403,14 +431,14 @@
         in_specs=[VMEM] * 5,
         out_specs=[VMEM] * 3,
         scratch_shapes=[
-            pltpu.VMEM((2, rows, groups, LANES), jnp.float32),
-            pltpu.VMEM((8, groups, LANES), jnp.float32),
+            pltpu.VMEM((streams - 1, 8, groups, LANES), jnp.float32),
+            pltpu.VMEM((streams, 8, groups, LANES), jnp.float32),
         ],
         input_output_aliases={4: 0},
         compiler_params=params,
         cost_estimate=cost,
         name="project_last",
-    )(aft, weights, taps, table, total)
+    )(aft, weights, filter_taps, table, total)
 
     partner = lax.ppermute(local, "ctx", [(j, j ^ 1) for j in range(ctx)])
     lone = ctx == 4
@@ -426,29 +454,33 @@
         lax.ppermute(chip, "ctx", [(j, (j + d) % ctx) for j in range(ctx)])
         for d in range(2, ctx, 2)
     ]
-    query, response = pl.pallas_call(
+    query, response, heads = pl.pallas_call(
         local_kernel,
-        out_shape=[wide, wide],
+        out_shape=[f32(rows, chans), f32(rows, chans), f32(2, groups, LANES)],
         in_specs=[VMEM] * 4,
-        out_specs=[VMEM] * 2,
-        scratch_shapes=[pltpu.VMEM((rows, groups, LANES), jnp.float32)],
+        out_specs=[VMEM] * 3,
+        scratch_shapes=[
+            pltpu.VMEM((rows, groups, LANES), jnp.float32),
+            pltpu.VMEM((8, groups, LANES), jnp.float32),
+        ],
         compiler_params=params,
         cost_estimate=cost,
         name="local_response",
-    )(total, source, taps, table)
+    )(total, source, filter_taps, table)
     return pl.pallas_call(
         functools.partial(final_kernel, lone, len(sent)),
         out_shape=jax.ShapeDtypeStruct((rows, chans), jnp.bfloat16),
-        in_specs=[VMEM] * (len(sent) + 6),
+        in_specs=[VMEM] * (len(sent) + 9),
         out_specs=HBM,
         scratch_shapes=[
-            pltpu.VMEM((rows, groups, LANES), jnp.float32),
+            pltpu.VMEM((modes, groups, LANES), jnp.float32),
+            pltpu.VMEM((2, groups, LANES), jnp.float32),
             pltpu.VMEM((rows, chans), jnp.bfloat16),
-            pltpu.SemaphoreType.DMA((rows // PIECE,)),
+            pltpu.SemaphoreType.DMA((groups // 2,)),
         ],
         compiler_params=params,
         name="carried_response",
-    )(*sent, local, partner, query, response, taps, table)
+    )(*sent, local, partner, query, response, heads, taps, table, *tiles)
 
 
 def solution(mesh):

time: 40.7 us -> 40.1 us (0.985)
  Pallas kernels: 25.6 us -> 25 us
    pallas_call x1, Pallas kernels: 1.85 us -> 1.32 us  [on_device(): pl.pallas_call(functools.partial(final_kernel, lone, len(sent)), out_shap...]
    ppermute x1, waiting for transfers between devices: 0.1 us -> 0.52 us  [on_device(): aft = lax.ppermute(aft[:, width // 2:], 'tp', back)]
  transfers between devices with their start and end apart: 10 -> 10, of which waited for: 5 -> 6; matrix products, arithmetic and copies ran while one was open for 0% -> 0% of each run, Pallas kernels for 54% -> 55%
where the time goes in v8:
time: 40.1 us; the launch traced here: 40 us
  Pallas kernels  25 us (62%)
  starting transfers between devices  10.8 us (27%)
  waiting for transfers between devices  4.04 us (10%)
    pallas_call x3, Pallas kernels, on_device(): pl.pallas_call(functools.partial(middle_kernel, order, blocks(step), left...  13.4 us
    ppermute x3, starting transfers between devices, on_device(): fore = lax.ppermute(fore, 'tp', ahead)  6.41 us
    pallas_call x1, Pallas kernels, on_device(): pl.pallas_call(functools.partial(load_kernel, order, blocks(1), pieces(1)...  6.22 us
    pallas_call x1, Pallas kernels, on_device(): pl.pallas_call(last_kernel, out_shape=[sums, wide, f32(modes + EDGE, grou...  1.77 us
    ppermute x1, starting transfers between devices, on_device(): fore = lax.ppermute(fore[:, :width // 2], 'tp', ahead)  1.67 us
    pallas_call x1, Pallas kernels, on_device(): pl.pallas_call(local_kernel, out_shape=[f32(rows, chans), f32(rows, chans...  1.62 us
    ppermute x1, waiting for transfers between devices, on_device(): lax.ppermute(chip, 'ctx', [(j, (j + d) % ctx) for j in range(ctx)])  1.56 us
    ppermute x1, starting transfers between devices, on_device(): lax.ppermute(chip, 'ctx', [(j, (j + d) % ctx) for j in range(ctx)])  1.55 us
  transfers between devices with their start and end apart: 10, of which 6 were waited for; matrix products, arithmetic and copies ran while one was open for 0% of the time, Pallas kernels for 55%

profile of v8, /device:TPU:0, one launch (start us, length us, event | category | flops | bytes accessed | tf_op | source)
XLA Modules:
  0.0 40.0 jit_solution(17989018511858566623)
XLA Ops:
  0.0 3.0 %collective-permute-start.1 = (bf16[128,1024]{1,0:T(8,128)(2,1)}, bf16[128,1024]{1,0:T(8,128)(2,1)S(1)}, u32[]{:S(2)}, u32[]{:S(2)}) collective-permute-start(bf16[128,1024]{1,0:T(8,128)(2,1)} %refs_0_.1), channel_id=1, source_target_pairs={{0,1},{1,3},{3,5},{5,7},{7,6},{6,4},{4,2},{2,0},{8,9},{9,11},{11,1... | collective-permute-start | bytes 786440 | tf_op jit(solution)/shard_map/ppermute | solution.py:385
  3.0 0.1 collective-permute-start
  3.0 6.2 %load_first.1.refs_3_ = bf16[3,3,1024,1024]{3,2,1,0:T(8,128)(2,1)S(1)} custom-call(bf16[3,8192,1024]{2,1,0:T(8,128)(2,1)} %bitcast.1), custom_call_target="tpu_custom_call" | custom-call | bytes 16777216 | tf_op jit(solution)/shard_map/load_first/pallas_call | solution.py:373
  9.3 0.3 collective-permute-done.1.refs_1_
  9.5 1.8 %collective-permute-start.3 = (bf16[128,1024]{1,0:T(8,128)(2,1)S(1)}, bf16[128,1024]{1,0:T(8,128)(2,1)S(1)}, u32[]{:S(2)}, u32[]{:S(2)}) collective-permute-start(bf16[128,1024]{1,0:T(8,128)(2,1)S(1)} %collective-permute-done.1.refs_1_), channel_id=1, source_target_pairs={{0,1},{1,3},{3,5},{5,7},{7,6},{6,4},{4,2},{2,0},{8,9},{9,11},{11,1... | collective-permute-start | bytes 786440 | tf_op jit(solution)/shard_map/ppermute | solution.py:385
  11.3 0.0 collective-permute-done.refs_2_
  11.3 0.3 collective-permute-start.2
  11.6 0.0 copy-done
  11.6 0.0 copy-done.1
  11.6 0.0 copy-done.2
  11.6 5.3 %project_blocks.3 = (f32[3,128,1024]{2,1,0:T(8,128)S(1)}, bf16[2,3,1024,1024]{3,2,1,0:T(8,128)(2,1)S(1)}, f32[3,3,8,128]{3,2,1,0:T(8,128)S(1)}, f32[5,16,8,128]{...) custom-call(bf16[128,1024]{1,0:T(8,128)(2,1)S(1)} %copy-done.1, ...), custom_call_target="tpu_custom_call" | custom-call | bytes 16777216 | tf_op jit(solution)/shard_map/project_blocks/pallas_call | solution.py:396
  16.9 0.2 collective-permute-done.3.refs_0_
  17.1 1.7 %collective-permute-start.5 = (bf16[128,1024]{1,0:T(8,128)(2,1)S(1)}, bf16[128,1024]{1,0:T(8,128)(2,1)S(1)}, u32[]{:S(2)}, u32[]{:S(2)}) collective-permute-start(bf16[128,1024]{1,0:T(8,128)(2,1)S(1)} %collective-permute-done.3.refs_0_), channel_id=1, source_target_pairs={{0,1},{1,3},{3,5},{5,7},{7,6},{6,4},{4,2},{2,0},{8,9},{9,11},{11,1... | collective-permute-start | bytes 786440 | tf_op jit(solution)/shard_map/ppermute | solution.py:385
  18.8 0.0 collective-permute-done.2.refs_1_
  18.8 0.3 collective-permute-start.4
  19.1 4.7 %project_blocks.4 = (f32[3,128,1024]{2,1,0:T(8,128)S(1)}, bf16[2,3,1024,1024]{3,2,1,0:T(8,128)(2,1)S(1)}) custom-call(bf16[128,1024]{1,0:T(8,128)(2,1)S(1)} %collective-permute-done.3.refs_0_, bf16[128,1024]{1,0:T(8,128)(2,1)S(1)} %collective-permute-done.2.refs_1_, ...), custom_call_target="tpu_custom_call", output_to_operand_aliasing={{0}: (4, {})} | custom-call | bytes 16777216 | tf_op jit(solution)/shard_map/project_blocks/pallas_call | solution.py:396
  23.8 0.2 collective-permute-done.5.refs_0_
  24.0 1.7 %collective-permute-start.7 = (bf16[128,512]{1,0:T(8,128)(2,1)S(1)}, bf16[128,512]{1,0:T(8,128)(2,1)S(1)}, u32[]{:S(2)}, u32[]{:S(2)}) collective-permute-start(bf16[128,512]{1,0:T(8,128)(2,1)S(1)} %slice.7), channel_id=1, source_target_pairs={{0,1},{1,3},{3,5},{5,7},{7,6},{6,4},{4,2},{2,0},{8,9},{9,11},{11,1... | collective-permute-start | bytes 393224 | tf_op jit(solution)/shard_map/ppermute | solution.py:416
  25.7 0.0 collective-permute-done.4.refs_1_
  25.7 0.5 %collective-permute-start.6 = (bf16[128,512]{1,0:T(8,128)(2,1)S(1)}, bf16[128,512]{1,0:T(8,128)(2,1)S(1)}, u32[]{:S(2)}, u32[]{:S(2)}) collective-permute-start(bf16[128,512]{1,0:T(8,128)(2,1)S(1)} %slice.6), channel_id=1, source_target_pairs={{1,0},{3,1},{5,3},{7,5},{6,7},{4,6},{2,4},{0,2},{9,8},{11,9},{13,1... | collective-permute-start | bytes 393224 | tf_op jit(solution)/shard_map/ppermute | solution.py:417
  26.2 3.4 %project_blocks.5 = (f32[3,128,1024]{2,1,0:T(8,128)S(1)}, bf16[1,3,1024,1024]{3,2,1,0:T(8,128)(2,1)S(1)}) custom-call(bf16[128,1024]{1,0:T(8,128)(2,1)S(1)} %collective-permute-done.5.refs_0_, bf16[128,1024]{1,0:T(8,128)(2,1)S(1)} %collective-permute-done.4.refs_1_, ...), custom_call_target="tpu_custom_call", output_to_operand_aliasing={{0}: (4, {})} | custom-call | bytes 16777216 | tf_op jit(solution)/shard_map/project_blocks/pallas_call | solution.py:396
  29.6 0.0 collective-permute-done.7.x_ref
  29.6 0.6 %project_half.1._ = f32[3,128,1024]{2,1,0:T(8,128)S(1)} custom-call(bf16[128,512]{1,0:T(8,128)(2,1)S(1)} %collective-permute-done.7.x_ref, bf16[1,3,1024,1024]{3,2,1,0:T(8,128)(2,1)S(1)} %get-tuple-element.57.held, f32[3,128,1024]{2,1,0:T(8,128)S(1)} %get-tuple-element.59._), custom_call_target="tpu_custom_call", output_to_operand_aliasing={{}: (2, {})} | custom-call | bytes 16777216 | tf_op jit(solution)/shard_map/project_half/pallas_call | solution.py:418
  30.2 0.5 %collective-permute-done.6.x_ref = bf16[128,512]{1,0:T(8,128)(2,1)S(1)} collective-permute-done((bf16[128,512]{1,0:T(8,128)(2,1)S(1)}, bf16[128,512]{1,0:T(8,128)(2,1)S(1)}, u32[]{:S(2)}, u32[]{:S(2)}) %collective-permute-start.6) | collective-permute-done | bytes 131104 | tf_op jit(solution)/shard_map/ppermute | solution.py:417
  30.7 1.8 %project_last.1 = (f32[3,128,1024]{2,1,0:T(8,128)S(1)}, f32[128,8,128]{2,1,0:T(8,128)S(1)}, f32[26,8,128]{2,1,0:T(8,128)S(1)}) custom-call(bf16[128,512]{1,0:T(8,128)(2,1)S(1)} %collective-permute-done.6.x_ref, bf16[1,3,1024,1024]{3,2,1,0:T(8,128)(2,1)S(1)} %get-tuple-element.57.held, f32[3,3,1024]{2,1,0:T(4,128)S(1)} %copy-done, ...), custom_call_target="tpu_custom_call", output_to_operand_aliasing={{0}: (4, {})} | custom-call | bytes 16777216 | tf_op jit(solution)/shard_map/project_last/pallas_call | solution.py:428
  32.5 0.1 collective-permute-start.8
  32.6 1.3 %collective-permute-done.8.partner.refs_2_ = f32[26,8,128]{2,1,0:T(8,128)S(1)} collective-permute-done((f32[26,8,128]{2,1,0:T(8,128)S(1)}, f32[26,8,128]{2,1,0:T(8,128)S(1)}, u32[]{:S(2)}, u32[]{:S(2)}) %collective-permute-start.8) | collective-permute-done | bytes 106528 | tf_op jit(solution)/shard_map/ppermute | solution.py:443
  33.9 0.1 chip_state.1
  33.9 1.6 %collective-permute-start.9 = (f32[22,8,128]{2,1,0:T(8,128)S(1)}, f32[22,8,128]{2,1,0:T(8,128)S(1)}, u32[]{:S(2)}, u32[]{:S(2)}) collective-permute-start(f32[22,8,128]{2,1,0:T(8,128)S(1)} %chip_state.1), channel_id=1, source_target_pairs={{0,16},{8,24},{16,0},{24,8},{1,17},{9,25},{17,1},{25,9},{2,18},{10... | collective-permute-start | bytes 270344 | tf_op jit(solution)/shard_map/ppermute | solution.py:454
  35.5 1.6 %local_response.1 = (f32[128,1024]{1,0:T(8,128)S(1)}, f32[128,1024]{1,0:T(8,128)S(1)}, f32[2,8,128]{2,1,0:T(8,128)S(1)}) custom-call(f32[3,128,1024]{2,1,0:T(8,128)S(1)} %get-tuple-element.62.total, f32[128,8,128]{2,1,0:T(8,128)S(1)} %get-tuple-element.63.source, f32[3,3,1024]{2,1,0:T(4,128)S(1)} %copy-done, ...), custom_call_target="tpu_custom_call" | custom-call | bytes 16777216 | tf_op jit(solution)/shard_map/local_response/pallas_call | solution.py:457
  37.1 1.6 %collective-permute-done.9.refs_0_ = f32[22,8,128]{2,1,0:T(8,128)S(1)} collective-permute-done((f32[22,8,128]{2,1,0:T(8,128)S(1)}, f32[22,8,128]{2,1,0:T(8,128)S(1)}, u32[]{:S(2)}, u32[]{:S(2)}) %collective-permute-start.9) | collective-permute-done | bytes 90144 | tf_op jit(solution)/shard_map/ppermute | solution.py:454
  38.7 1.3 %carried_response.1 = bf16[128,1024]{1,0:T(8,128)(2,1)} custom-call(f32[22,8,128]{2,1,0:T(8,128)S(1)} %collective-permute-done.9.refs_0_, f32[26,8,128]{2,1,0:T(8,128)S(1)} %get-tuple-element.60.local.refs_1_, f32[26,8,128]{2,1,0:T(8,128)S(1)} %collective-permute-done.8.partner.refs_2_, f32[128,1024]{1,0:T(8,128)S(1)} %get-tuple-element.64.refs_3_, ...), custom_call_target="tpu_custom_call" | custom-call | tf_op jit(solution)/shard_map/carried_response/pallas_call | solution.py:470
  (7 shorter events, 0.0 us)
Async XLA Ops:
  0.0 9.5 %collective-permute-start.1 = (bf16[128,1024]{1,0:T(8,128)(2,1)}, bf16[128,1024]{1,0:T(8,128)(2,1)S(1)}, u32[]{:S(2)}, u32[]{:S(2)}) collective-permute-start(bf16[128,1024]{1,0:T(8,128)(2,1)} %refs_0_.1), channel_id=1, source_target_pairs={{0,1},{1,3},{3,5},{5,7},{7,6},{6,4},{4,2},{2,0},{8,9},{9,11},{11,1... | collective-permute-start | bytes 786440 | tf_op jit(solution)/shard_map/ppermute | solution.py:385
  3.0 8.3 %collective-permute-start = (bf16[128,1024]{1,0:T(8,128)(2,1)}, bf16[128,1024]{1,0:T(8,128)(2,1)S(1)}, u32[]{:S(2)}, u32[]{:S(2)}) collective-permute-start(bf16[128,1024]{1,0:T(8,128)(2,1)} %refs_0_.1), channel_id=1, source_target_pairs={{1,0},{3,1},{5,3},{7,5},{6,7},{4,6},{2,4},{0,2},{9,8},{11,9},{13,1... | collective-permute-start | bytes 786440 | tf_op jit(solution)/shard_map/ppermute | solution.py:386
  3.0 8.5 %copy-start = (f32[3,3,1024]{2,1,0:T(4,128)S(1)}, f32[3,3,1024]{2,1,0:T(4,128)}, u32[]{:S(2)}) copy-start(f32[3,3,1024]{2,1,0:T(4,128)} %taps.3) | copy-start | bytes 110596
  3.0 8.5 %copy-start.1 = (bf16[128,1024]{1,0:T(8,128)(2,1)S(1)}, bf16[128,1024]{1,0:T(8,128)(2,1)}, u32[]{:S(2)}) copy-start(bf16[128,1024]{1,0:T(8,128)(2,1)} %refs_0_.1) | copy-start | bytes 786436
  3.0 8.5 %copy-start.2 = (f32[16,1024]{1,0:T(8,128)S(1)}, f32[16,1024]{1,0:T(8,128)}, u32[]{:S(2)}) copy-start(f32[16,1024]{1,0:T(8,128)} %refs_6_.1) | copy-start | bytes 196612
  3.0 8.5 %copy-start.3 = (f32[16,1024]{1,0:T(8,128)S(1)}, f32[16,1024]{1,0:T(8,128)}, u32[]{:S(2)}) copy-start(f32[16,1024]{1,0:T(8,128)} %refs_7_.1) | copy-start | bytes 196612
  9.5 7.6 %collective-permute-start.3 = (bf16[128,1024]{1,0:T(8,128)(2,1)S(1)}, bf16[128,1024]{1,0:T(8,128)(2,1)S(1)}, u32[]{:S(2)}, u32[]{:S(2)}) collective-permute-start(bf16[128,1024]{1,0:T(8,128)(2,1)S(1)} %collective-permute-done.1.refs_1_), channel_id=1, source_target_pairs={{0,1},{1,3},{3,5},{5,7},{7,6},{6,4},{4,2},{2,0},{8,9},{9,11},{11,1... | collective-permute-start | bytes 786440 | tf_op jit(solution)/shard_map/ppermute | solution.py:385
  11.3 7.5 %collective-permute-start.2 = (bf16[128,1024]{1,0:T(8,128)(2,1)S(1)}, bf16[128,1024]{1,0:T(8,128)(2,1)S(1)}, u32[]{:S(2)}, u32[]{:S(2)}) collective-permute-start(bf16[128,1024]{1,0:T(8,128)(2,1)S(1)} %collective-permute-done.refs_2_), channel_id=1, source_target_pairs={{1,0},{3,1},{5,3},{7,5},{6,7},{4,6},{2,4},{0,2},{9,8},{11,9},{13,1... | collective-permute-start | bytes 786440 | tf_op jit(solution)/shard_map/ppermute | solution.py:386
  17.1 6.9 %collective-permute-start.5 = (bf16[128,1024]{1,0:T(8,128)(2,1)S(1)}, bf16[128,1024]{1,0:T(8,128)(2,1)S(1)}, u32[]{:S(2)}, u32[]{:S(2)}) collective-permute-start(bf16[128,1024]{1,0:T(8,128)(2,1)S(1)} %collective-permute-done.3.refs_0_), channel_id=1, source_target_pairs={{0,1},{1,3},{3,5},{5,7},{7,6},{6,4},{4,2},{2,0},{8,9},{9,11},{11,1... | collective-permute-start | bytes 786440 | tf_op jit(solution)/shard_map/ppermute | solution.py:385
  18.8 6.9 %collective-permute-start.4 = (bf16[128,1024]{1,0:T(8,128)(2,1)S(1)}, bf16[128,1024]{1,0:T(8,128)(2,1)S(1)}, u32[]{:S(2)}, u32[]{:S(2)}) collective-permute-start(bf16[128,1024]{1,0:T(8,128)(2,1)S(1)} %collective-permute-done.2.refs_1_), channel_id=1, source_target_pairs={{1,0},{3,1},{5,3},{7,5},{6,7},{4,6},{2,4},{0,2},{9,8},{11,9},{13,1... | collective-permute-start | bytes 786440 | tf_op jit(solution)/shard_map/ppermute | solution.py:386
  24.0 5.6 %collective-permute-start.7 = (bf16[128,512]{1,0:T(8,128)(2,1)S(1)}, bf16[128,512]{1,0:T(8,128)(2,1)S(1)}, u32[]{:S(2)}, u32[]{:S(2)}) collective-permute-start(bf16[128,512]{1,0:T(8,128)(2,1)S(1)} %slice.7), channel_id=1, source_target_pairs={{0,1},{1,3},{3,5},{5,7},{7,6},{6,4},{4,2},{2,0},{8,9},{9,11},{11,1... | collective-permute-start | bytes 393224 | tf_op jit(solution)/shard_map/ppermute | solution.py:416
  25.7 5.0 %collective-permute-start.6 = (bf16[128,512]{1,0:T(8,128)(2,1)S(1)}, bf16[128,512]{1,0:T(8,128)(2,1)S(1)}, u32[]{:S(2)}, u32[]{:S(2)}) collective-permute-start(bf16[128,512]{1,0:T(8,128)(2,1)S(1)} %slice.6), channel_id=1, source_target_pairs={{1,0},{3,1},{5,3},{7,5},{6,7},{4,6},{2,4},{0,2},{9,8},{11,9},{13,1... | collective-permute-start | bytes 393224 | tf_op jit(solution)/shard_map/ppermute | solution.py:417
  32.5 1.4 %collective-permute-start.8 = (f32[26,8,128]{2,1,0:T(8,128)S(1)}, f32[26,8,128]{2,1,0:T(8,128)S(1)}, u32[]{:S(2)}, u32[]{:S(2)}) collective-permute-start(f32[26,8,128]{2,1,0:T(8,128)S(1)} %get-tuple-element.60.local.refs_1_), channel_id=1, source_target_pairs={{0,8},{8,0},{16,24},{24,16},{1,9},{9,1},{17,25},{25,17},{2,10},{10... | collective-permute-start | bytes 319496 | tf_op jit(solution)/shard_map/ppermute | solution.py:443
  33.9 4.7 %collective-permute-start.9 = (f32[22,8,128]{2,1,0:T(8,128)S(1)}, f32[22,8,128]{2,1,0:T(8,128)S(1)}, u32[]{:S(2)}, u32[]{:S(2)}) collective-permute-start(f32[22,8,128]{2,1,0:T(8,128)S(1)} %chip_state.1), channel_id=1, source_target_pairs={{0,16},{8,24},{16,0},{24,8},{1,17},{9,25},{17,1},{25,9},{2,18},{10... | collective-permute-start | bytes 270344 | tf_op jit(solution)/shard_map/ppermute | solution.py:454

commit v9 on v8

--- a/solution.py
+++ b/solution.py
@@ -9,7 +9,8 @@
 
 LANES = 128
 COLS = 256
-SOON = 2
+WIDE = 512
+SOON = 4
 GRID_ROWS = 4
 EDGE = 10
 UNROLL = 16
@@ -48,9 +49,10 @@
     ]
 
 
-def add_products(xs, weights, total, s, fresh=False):
-    for c in range(0, total.shape[2], COLS):
-        at = slice(c, c + COLS)
+def add_products(xs, weights, total, s, fresh=False, cols=COLS):
+    cols = min(cols, total.shape[2])
+    for c in range(0, total.shape[2], cols):
+        at = slice(c, c + cols)
         terms = [
             jnp.dot(x, weights(b, at), preferred_element_type=jnp.float32) for b, x in enumerate(xs)
         ]
@@ -109,7 +111,7 @@
 def half_kernel(x_ref, held, _, total):
     depth = x_ref.shape[1]
     for s in range(total.shape[0]):
-        add_products([x_ref[...]], lambda b, at: held[0, s, :depth, at], total, s)
+        add_products([x_ref[...]], lambda b, at: held[0, s, :depth, at], total, s, cols=WIDE)
 
 
 def make_tables(taps_in, decay, residue, taps, table, tile, tile_step, rows):
@@ -146,7 +148,7 @@
 def last_kernel(x_ref, held, taps, table, _, total, source, out_ref, low, high):
     depth = x_ref.shape[1]
     for s in range(total.shape[0]):
-        add_products([x_ref[...]], lambda b, at: held[0, s, depth:, at], total, s)
+        add_products([x_ref[...]], lambda b, at: held[0, s, depth:, at], total, s, cols=WIDE)
     rows, groups, lanes = source.shape
     modes = table.shape[1]
     for g in range(groups):

time: 40.1 us -> 40.1 us (level)
  transfers between devices with their start and end apart: 10 -> 10, of which waited for: 6 -> 6; matrix products, arithmetic and copies ran while one was open for 0% -> 0% of each run, Pallas kernels for 55% -> 54%
where the time goes in v9:
time: 40.1 us; the launch traced here: 40 us
  Pallas kernels  24.7 us (62%)
  starting transfers between devices  10.8 us (27%)
  waiting for transfers between devices  4.31 us (11%)
    pallas_call x3, Pallas kernels, on_device(): pl.pallas_call(functools.partial(middle_kernel, order, blocks(step), left...  13.1 us
    ppermute x3, starting transfers between devices, on_device(): fore = lax.ppermute(fore, 'tp', ahead)  6.41 us
    pallas_call x1, Pallas kernels, on_device(): pl.pallas_call(functools.partial(load_kernel, order, blocks(1), pieces(1)...  6.22 us
    pallas_call x1, Pallas kernels, on_device(): pl.pallas_call(last_kernel, out_shape=[sums, wide, f32(modes + EDGE, grou...  1.76 us
    ppermute x1, starting transfers between devices, on_device(): fore = lax.ppermute(fore[:, :width // 2], 'tp', ahead)  1.67 us
    pallas_call x1, Pallas kernels, on_device(): pl.pallas_call(local_kernel, out_shape=[f32(rows, chans), f32(rows, chans...  1.62 us
    ppermute x1, starting transfers between devices, on_device(): lax.ppermute(chip, 'ctx', [(j, (j + d) % ctx) for j in range(ctx)])  1.56 us
    ppermute x1, waiting for transfers between devices, on_device(): lax.ppermute(chip, 'ctx', [(j, (j + d) % ctx) for j in range(ctx)])  1.55 us
  transfers between devices with their start and end apart: 10, of which 6 were waited for; matrix products, arithmetic and copies ran while one was open for 0% of the time, Pallas kernels for 54%

profile of v9, /device:TPU:0, one launch (start us, length us, event | category | flops | bytes accessed | tf_op | source)
XLA Modules:
  0.0 40.0 jit_solution(1167126588984302326)
XLA Ops:
  0.0 3.0 %collective-permute-start.1 = (bf16[128,1024]{1,0:T(8,128)(2,1)}, bf16[128,1024]{1,0:T(8,128)(2,1)S(1)}, u32[]{:S(2)}, u32[]{:S(2)}) collective-permute-start(bf16[128,1024]{1,0:T(8,128)(2,1)} %refs_0_.1), channel_id=1, source_target_pairs={{0,1},{1,3},{3,5},{5,7},{7,6},{6,4},{4,2},{2,0},{8,9},{9,11},{11,1... | collective-permute-start | bytes 786440 | tf_op jit(solution)/shard_map/ppermute | solution.py:387
  3.0 0.1 collective-permute-start
  3.0 6.2 %load_first.1.refs_3_ = bf16[3,3,1024,1024]{3,2,1,0:T(8,128)(2,1)S(1)} custom-call(bf16[3,8192,1024]{2,1,0:T(8,128)(2,1)} %bitcast.1), custom_call_target="tpu_custom_call" | custom-call | bytes 16777216 | tf_op jit(solution)/shard_map/load_first/pallas_call | solution.py:375
  9.3 0.3 collective-permute-done.1.refs_1_
  9.5 1.8 %collective-permute-start.3 = (bf16[128,1024]{1,0:T(8,128)(2,1)S(1)}, bf16[128,1024]{1,0:T(8,128)(2,1)S(1)}, u32[]{:S(2)}, u32[]{:S(2)}) collective-permute-start(bf16[128,1024]{1,0:T(8,128)(2,1)S(1)} %collective-permute-done.1.refs_1_), channel_id=1, source_target_pairs={{0,1},{1,3},{3,5},{5,7},{7,6},{6,4},{4,2},{2,0},{8,9},{9,11},{11,1... | collective-permute-start | bytes 786440 | tf_op jit(solution)/shard_map/ppermute | solution.py:387
  11.3 0.0 collective-permute-done.refs_2_
  11.3 0.3 collective-permute-start.2
  11.6 0.0 copy-done
  11.6 0.0 copy-done.1
  11.6 0.0 copy-done.2
  11.6 5.3 %project_blocks.3 = (f32[3,128,1024]{2,1,0:T(8,128)S(1)}, bf16[2,3,1024,1024]{3,2,1,0:T(8,128)(2,1)S(1)}, f32[3,3,8,128]{3,2,1,0:T(8,128)S(1)}, f32[5,16,8,128]{...) custom-call(bf16[128,1024]{1,0:T(8,128)(2,1)S(1)} %copy-done.1, ...), custom_call_target="tpu_custom_call" | custom-call | bytes 16777216 | tf_op jit(solution)/shard_map/project_blocks/pallas_call | solution.py:398
  16.9 0.2 collective-permute-done.3.refs_0_
  17.1 1.7 %collective-permute-start.5 = (bf16[128,1024]{1,0:T(8,128)(2,1)S(1)}, bf16[128,1024]{1,0:T(8,128)(2,1)S(1)}, u32[]{:S(2)}, u32[]{:S(2)}) collective-permute-start(bf16[128,1024]{1,0:T(8,128)(2,1)S(1)} %collective-permute-done.3.refs_0_), channel_id=1, source_target_pairs={{0,1},{1,3},{3,5},{5,7},{7,6},{6,4},{4,2},{2,0},{8,9},{9,11},{11,1... | collective-permute-start | bytes 786440 | tf_op jit(solution)/shard_map/ppermute | solution.py:387
  18.8 0.0 collective-permute-done.2.refs_1_
  18.8 0.3 collective-permute-start.4
  19.1 4.6 %project_blocks.4 = (f32[3,128,1024]{2,1,0:T(8,128)S(1)}, bf16[2,3,1024,1024]{3,2,1,0:T(8,128)(2,1)S(1)}) custom-call(bf16[128,1024]{1,0:T(8,128)(2,1)S(1)} %collective-permute-done.3.refs_0_, bf16[128,1024]{1,0:T(8,128)(2,1)S(1)} %collective-permute-done.2.refs_1_, ...), custom_call_target="tpu_custom_call", output_to_operand_aliasing={{0}: (4, {})} | custom-call | bytes 16777216 | tf_op jit(solution)/shard_map/project_blocks/pallas_call | solution.py:398
  23.7 0.3 collective-permute-done.5.refs_0_
  24.0 1.7 %collective-permute-start.7 = (bf16[128,512]{1,0:T(8,128)(2,1)S(1)}, bf16[128,512]{1,0:T(8,128)(2,1)S(1)}, u32[]{:S(2)}, u32[]{:S(2)}) collective-permute-start(bf16[128,512]{1,0:T(8,128)(2,1)S(1)} %slice.7), channel_id=1, source_target_pairs={{0,1},{1,3},{3,5},{5,7},{7,6},{6,4},{4,2},{2,0},{8,9},{9,11},{11,1... | collective-permute-start | bytes 393224 | tf_op jit(solution)/shard_map/ppermute | solution.py:418
  25.7 0.0 collective-permute-done.4.refs_1_
  25.7 0.5 %collective-permute-start.6 = (bf16[128,512]{1,0:T(8,128)(2,1)S(1)}, bf16[128,512]{1,0:T(8,128)(2,1)S(1)}, u32[]{:S(2)}, u32[]{:S(2)}) collective-permute-start(bf16[128,512]{1,0:T(8,128)(2,1)S(1)} %slice.6), channel_id=1, source_target_pairs={{1,0},{3,1},{5,3},{7,5},{6,7},{4,6},{2,4},{0,2},{9,8},{11,9},{13,1... | collective-permute-start | bytes 393224 | tf_op jit(solution)/shard_map/ppermute | solution.py:419
  26.2 3.3 %project_blocks.5 = (f32[3,128,1024]{2,1,0:T(8,128)S(1)}, bf16[1,3,1024,1024]{3,2,1,0:T(8,128)(2,1)S(1)}) custom-call(bf16[128,1024]{1,0:T(8,128)(2,1)S(1)} %collective-permute-done.5.refs_0_, bf16[128,1024]{1,0:T(8,128)(2,1)S(1)} %collective-permute-done.4.refs_1_, ...), custom_call_target="tpu_custom_call", output_to_operand_aliasing={{0}: (4, {})} | custom-call | bytes 16777216 | tf_op jit(solution)/shard_map/project_blocks/pallas_call | solution.py:398
  29.4 0.0 collective-permute-done.7.x_ref
  29.4 0.6 %project_half.1._ = f32[3,128,1024]{2,1,0:T(8,128)S(1)} custom-call(bf16[128,512]{1,0:T(8,128)(2,1)S(1)} %collective-permute-done.7.x_ref, bf16[1,3,1024,1024]{3,2,1,0:T(8,128)(2,1)S(1)} %get-tuple-element.57.held, f32[3,128,1024]{2,1,0:T(8,128)S(1)} %get-tuple-element.59._), custom_call_target="tpu_custom_call", output_to_operand_aliasing={{}: (2, {})} | custom-call | bytes 16777216 | tf_op jit(solution)/shard_map/project_half/pallas_call | solution.py:420
  30.1 0.7 %collective-permute-done.6.x_ref = bf16[128,512]{1,0:T(8,128)(2,1)S(1)} collective-permute-done((bf16[128,512]{1,0:T(8,128)(2,1)S(1)}, bf16[128,512]{1,0:T(8,128)(2,1)S(1)}, u32[]{:S(2)}, u32[]{:S(2)}) %collective-permute-start.6) | collective-permute-done | bytes 131104 | tf_op jit(solution)/shard_map/ppermute | solution.py:419
  30.7 1.8 %project_last.1 = (f32[3,128,1024]{2,1,0:T(8,128)S(1)}, f32[128,8,128]{2,1,0:T(8,128)S(1)}, f32[26,8,128]{2,1,0:T(8,128)S(1)}) custom-call(bf16[128,512]{1,0:T(8,128)(2,1)S(1)} %collective-permute-done.6.x_ref, bf16[1,3,1024,1024]{3,2,1,0:T(8,128)(2,1)S(1)} %get-tuple-element.57.held, f32[3,3,1024]{2,1,0:T(4,128)S(1)} %copy-done, ...), custom_call_target="tpu_custom_call", output_to_operand_aliasing={{0}: (4, {})} | custom-call | bytes 16777216 | tf_op jit(solution)/shard_map/project_last/pallas_call | solution.py:430
  32.5 0.1 collective-permute-start.8
  32.6 1.3 %collective-permute-done.8.partner.refs_2_ = f32[26,8,128]{2,1,0:T(8,128)S(1)} collective-permute-done((f32[26,8,128]{2,1,0:T(8,128)S(1)}, f32[26,8,128]{2,1,0:T(8,128)S(1)}, u32[]{:S(2)}, u32[]{:S(2)}) %collective-permute-start.8) | collective-permute-done | bytes 106528 | tf_op jit(solution)/shard_map/ppermute | solution.py:445
  33.9 0.1 chip_state.1
  33.9 1.6 %collective-permute-start.9 = (f32[22,8,128]{2,1,0:T(8,128)S(1)}, f32[22,8,128]{2,1,0:T(8,128)S(1)}, u32[]{:S(2)}, u32[]{:S(2)}) collective-permute-start(f32[22,8,128]{2,1,0:T(8,128)S(1)} %chip_state.1), channel_id=1, source_target_pairs={{0,16},{8,24},{16,0},{24,8},{1,17},{9,25},{17,1},{25,9},{2,18},{10... | collective-permute-start | bytes 270344 | tf_op jit(solution)/shard_map/ppermute | solution.py:456
  35.5 1.6 %local_response.1 = (f32[128,1024]{1,0:T(8,128)S(1)}, f32[128,1024]{1,0:T(8,128)S(1)}, f32[2,8,128]{2,1,0:T(8,128)S(1)}) custom-call(f32[3,128,1024]{2,1,0:T(8,128)S(1)} %get-tuple-element.62.total, f32[128,8,128]{2,1,0:T(8,128)S(1)} %get-tuple-element.63.source, f32[3,3,1024]{2,1,0:T(4,128)S(1)} %copy-done, ...), custom_call_target="tpu_custom_call" | custom-call | bytes 16777216 | tf_op jit(solution)/shard_map/local_response/pallas_call | solution.py:459
  37.1 1.6 %collective-permute-done.9.refs_0_ = f32[22,8,128]{2,1,0:T(8,128)S(1)} collective-permute-done((f32[22,8,128]{2,1,0:T(8,128)S(1)}, f32[22,8,128]{2,1,0:T(8,128)S(1)}, u32[]{:S(2)}, u32[]{:S(2)}) %collective-permute-start.9) | collective-permute-done | bytes 90144 | tf_op jit(solution)/shard_map/ppermute | solution.py:456
  38.7 1.3 %carried_response.1 = bf16[128,1024]{1,0:T(8,128)(2,1)} custom-call(f32[22,8,128]{2,1,0:T(8,128)S(1)} %collective-permute-done.9.refs_0_, f32[26,8,128]{2,1,0:T(8,128)S(1)} %get-tuple-element.60.local.refs_1_, f32[26,8,128]{2,1,0:T(8,128)S(1)} %collective-permute-done.8.partner.refs_2_, f32[128,1024]{1,0:T(8,128)S(1)} %get-tuple-element.64.refs_3_, ...), custom_call_target="tpu_custom_call" | custom-call | tf_op jit(solution)/shard_map/carried_response/pallas_call | solution.py:472
  (7 shorter events, 0.0 us)
Async XLA Ops:
  0.0 9.5 %collective-permute-start.1 = (bf16[128,1024]{1,0:T(8,128)(2,1)}, bf16[128,1024]{1,0:T(8,128)(2,1)S(1)}, u32[]{:S(2)}, u32[]{:S(2)}) collective-permute-start(bf16[128,1024]{1,0:T(8,128)(2,1)} %refs_0_.1), channel_id=1, source_target_pairs={{0,1},{1,3},{3,5},{5,7},{7,6},{6,4},{4,2},{2,0},{8,9},{9,11},{11,1... | collective-permute-start | bytes 786440 | tf_op jit(solution)/shard_map/ppermute | solution.py:387
  3.0 8.3 %collective-permute-start = (bf16[128,1024]{1,0:T(8,128)(2,1)}, bf16[128,1024]{1,0:T(8,128)(2,1)S(1)}, u32[]{:S(2)}, u32[]{:S(2)}) collective-permute-start(bf16[128,1024]{1,0:T(8,128)(2,1)} %refs_0_.1), channel_id=1, source_target_pairs={{1,0},{3,1},{5,3},{7,5},{6,7},{4,6},{2,4},{0,2},{9,8},{11,9},{13,1... | collective-permute-start | bytes 786440 | tf_op jit(solution)/shard_map/ppermute | solution.py:388
  3.0 8.5 %copy-start = (f32[3,3,1024]{2,1,0:T(4,128)S(1)}, f32[3,3,1024]{2,1,0:T(4,128)}, u32[]{:S(2)}) copy-start(f32[3,3,1024]{2,1,0:T(4,128)} %taps.3) | copy-start | bytes 110596
  3.0 8.5 %copy-start.1 = (bf16[128,1024]{1,0:T(8,128)(2,1)S(1)}, bf16[128,1024]{1,0:T(8,128)(2,1)}, u32[]{:S(2)}) copy-start(bf16[128,1024]{1,0:T(8,128)(2,1)} %refs_0_.1) | copy-start | bytes 786436
  3.0 8.5 %copy-start.2 = (f32[16,1024]{1,0:T(8,128)S(1)}, f32[16,1024]{1,0:T(8,128)}, u32[]{:S(2)}) copy-start(f32[16,1024]{1,0:T(8,128)} %refs_6_.1) | copy-start | bytes 196612
  3.0 8.5 %copy-start.3 = (f32[16,1024]{1,0:T(8,128)S(1)}, f32[16,1024]{1,0:T(8,128)}, u32[]{:S(2)}) copy-start(f32[16,1024]{1,0:T(8,128)} %refs_7_.1) | copy-start | bytes 196612
  9.5 7.6 %collective-permute-start.3 = (bf16[128,1024]{1,0:T(8,128)(2,1)S(1)}, bf16[128,1024]{1,0:T(8,128)(2,1)S(1)}, u32[]{:S(2)}, u32[]{:S(2)}) collective-permute-start(bf16[128,1024]{1,0:T(8,128)(2,1)S(1)} %collective-permute-done.1.refs_1_), channel_id=1, source_target_pairs={{0,1},{1,3},{3,5},{5,7},{7,6},{6,4},{4,2},{2,0},{8,9},{9,11},{11,1... | collective-permute-start | bytes 786440 | tf_op jit(solution)/shard_map/ppermute | solution.py:387
  11.3 7.5 %collective-permute-start.2 = (bf16[128,1024]{1,0:T(8,128)(2,1)S(1)}, bf16[128,1024]{1,0:T(8,128)(2,1)S(1)}, u32[]{:S(2)}, u32[]{:S(2)}) collective-permute-start(bf16[128,1024]{1,0:T(8,128)(2,1)S(1)} %collective-permute-done.refs_2_), channel_id=1, source_target_pairs={{1,0},{3,1},{5,3},{7,5},{6,7},{4,6},{2,4},{0,2},{9,8},{11,9},{13,1... | collective-permute-start | bytes 786440 | tf_op jit(solution)/shard_map/ppermute | solution.py:388
  17.1 6.9 %collective-permute-start.5 = (bf16[128,1024]{1,0:T(8,128)(2,1)S(1)}, bf16[128,1024]{1,0:T(8,128)(2,1)S(1)}, u32[]{:S(2)}, u32[]{:S(2)}) collective-permute-start(bf16[128,1024]{1,0:T(8,128)(2,1)S(1)} %collective-permute-done.3.refs_0_), channel_id=1, source_target_pairs={{0,1},{1,3},{3,5},{5,7},{7,6},{6,4},{4,2},{2,0},{8,9},{9,11},{11,1... | collective-permute-start | bytes 786440 | tf_op jit(solution)/shard_map/ppermute | solution.py:387
  18.8 6.9 %collective-permute-start.4 = (bf16[128,1024]{1,0:T(8,128)(2,1)S(1)}, bf16[128,1024]{1,0:T(8,128)(2,1)S(1)}, u32[]{:S(2)}, u32[]{:S(2)}) collective-permute-start(bf16[128,1024]{1,0:T(8,128)(2,1)S(1)} %collective-permute-done.2.refs_1_), channel_id=1, source_target_pairs={{1,0},{3,1},{5,3},{7,5},{6,7},{4,6},{2,4},{0,2},{9,8},{11,9},{13,1... | collective-permute-start | bytes 786440 | tf_op jit(solution)/shard_map/ppermute | solution.py:388
  24.0 5.4 %collective-permute-start.7 = (bf16[128,512]{1,0:T(8,128)(2,1)S(1)}, bf16[128,512]{1,0:T(8,128)(2,1)S(1)}, u32[]{:S(2)}, u32[]{:S(2)}) collective-permute-start(bf16[128,512]{1,0:T(8,128)(2,1)S(1)} %slice.7), channel_id=1, source_target_pairs={{0,1},{1,3},{3,5},{5,7},{7,6},{6,4},{4,2},{2,0},{8,9},{9,11},{11,1... | collective-permute-start | bytes 393224 | tf_op jit(solution)/shard_map/ppermute | solution.py:418
  25.7 5.0 %collective-permute-start.6 = (bf16[128,512]{1,0:T(8,128)(2,1)S(1)}, bf16[128,512]{1,0:T(8,128)(2,1)S(1)}, u32[]{:S(2)}, u32[]{:S(2)}) collective-permute-start(bf16[128,512]{1,0:T(8,128)(2,1)S(1)} %slice.6), channel_id=1, source_target_pairs={{1,0},{3,1},{5,3},{7,5},{6,7},{4,6},{2,4},{0,2},{9,8},{11,9},{13,1... | collective-permute-start | bytes 393224 | tf_op jit(solution)/shard_map/ppermute | solution.py:419
  32.5 1.4 %collective-permute-start.8 = (f32[26,8,128]{2,1,0:T(8,128)S(1)}, f32[26,8,128]{2,1,0:T(8,128)S(1)}, u32[]{:S(2)}, u32[]{:S(2)}) collective-permute-start(f32[26,8,128]{2,1,0:T(8,128)S(1)} %get-tuple-element.60.local.refs_1_), channel_id=1, source_target_pairs={{0,8},{8,0},{16,24},{24,16},{1,9},{9,1},{17,25},{25,17},{2,10},{10... | collective-permute-start | bytes 319496 | tf_op jit(solution)/shard_map/ppermute | solution.py:445
  33.9 4.7 %collective-permute-start.9 = (f32[22,8,128]{2,1,0:T(8,128)S(1)}, f32[22,8,128]{2,1,0:T(8,128)S(1)}, u32[]{:S(2)}, u32[]{:S(2)}) collective-permute-start(f32[22,8,128]{2,1,0:T(8,128)S(1)} %chip_state.1), channel_id=1, source_target_pairs={{0,16},{8,24},{16,0},{24,8},{1,17},{9,25},{17,1},{25,9},{2,18},{10... | collective-permute-start | bytes 270344 | tf_op jit(solution)/shard_map/ppermute | solution.py:456

commit v10 on v9

--- a/solution.py
+++ b/solution.py
@@ -145,7 +145,7 @@
     return lags[0] * value + lags[1] * one + lags[2] * two
 
 
-def last_kernel(x_ref, held, taps, table, _, total, source, out_ref, low, high):
+def last_kernel(x_ref, held, taps, table, _, total, source, states, edges, low, high):
     depth = x_ref.shape[1]
     for s in range(total.shape[0]):
         add_products([x_ref[...]], lambda b, at: held[0, s, depth:, at], total, s, cols=WIDE)
@@ -168,12 +168,12 @@
     state = [jnp.zeros((groups, lanes), jnp.float32)] * modes
     state = over_rows(step_row, 2, rows, state)
     for n in range(modes):
-        out_ref[n] = state[n]
+        states[n] = state[n]
     for j in range(2):
         for s in (1, 2):
-            out_ref[modes + (s - 1) * 2 + j] = low[s - 1, j]
+            edges[(s - 1) * 2 + j] = low[s - 1, j]
         for s in range(3):
-            out_ref[modes + 4 + s * 2 + j] = high[s, 6 + j]
+            edges[4 + s * 2 + j] = high[s, 6 + j]
 
 
 def rounded(value):
@@ -229,8 +229,8 @@
         self.rims = rows[modes + 4 :]
 
     @classmethod
-    def read(cls, ref, modes):
-        return cls([ref[i] for i in range(ref.shape[0])], modes)
+    def read(cls, states, edges):
+        return cls([ref[i] for ref in (states, edges) for i in range(ref.shape[0])], states.shape[0])
 
     @classmethod
     def chosen(cls, odd, when_odd, when_even, modes):
@@ -249,10 +249,10 @@
     return [[table[i, n] for n in range(table.shape[1])] for i in range(table.shape[0])]
 
 
-def chip_kernel(lone, local, partner, taps, table, out_ref):
+def chip_kernel(lone, states, edges, other_states, other_edges, taps, table, out_states, out_edges):
     modes = table.shape[1]
     odd = lax.rem(lax.axis_index("ctx"), 2) == 1
-    mine, other = Summary.read(local, modes), Summary.read(partner, modes)
+    mine, other = Summary.read(states, edges), Summary.read(other_states, other_edges)
     first = Summary.chosen(odd, other, mine, modes)
     second = Summary.chosen(odd, mine, other, modes)
     _, block, less_one, less_two, _ = powers(table)
@@ -261,24 +261,30 @@
         start, heads = first.complete(taps, [jnp.zeros_like(heads[0])] * 6, less_one, less_two), []
     end = second.complete(taps, first.rims, less_one, less_two)
     joined = [d * x + y for d, x, y in zip(block, start, end)]
-    for i, value in enumerate(joined + heads + second.rims):
-        out_ref[i] = value
+    for i, value in enumerate(joined):
+        out_states[i] = value
+    for i, value in enumerate(heads + second.rims):
+        out_edges[i] = value
 
 
 def final_kernel(lone, count, *refs):
-    sent = refs[:count]
-    local, partner, query, response, query_heads, taps, table, tile, tile_step, *refs = refs[count:]
-    out_ref, states, firsts, rounded_out, out_sem = refs
+    sent, sent_edges = refs[:count], refs[count : 2 * count]
+    own_edges, other_states, other_edges, query, response, *refs = refs[2 * count :]
+    query_heads, taps, table, tile, tile_step, out_ref, states, firsts, rounded_out, out_sem = refs
     rows = query.shape[0]
-    groups, lanes = local.shape[1:]
+    groups, lanes = own_edges.shape[1:]
     modes = table.shape[1]
     zero = jnp.zeros((groups, lanes), jnp.float32)
     index = lax.axis_index("ctx")
     odd = lax.rem(index, 2) == 1
     _, block, less_one, less_two, _ = powers(table)
     values = [
-        [jnp.where(index >= 2 * (d + 1), ref[i], zero) for i in range(ref.shape[0])]
-        for d, ref in enumerate(sent)
+        [
+            jnp.where(index >= 2 * (d + 1), ref[i], zero)
+            for ref in (sent[d], sent_edges[d])
+            for i in range(ref.shape[0])
+        ]
+        for d in range(count)
     ]
     rims = [value[-6:] for value in values] + [[zero] * 6]
     state = [zero] * modes
@@ -292,12 +298,12 @@
                 [a * b for a, b in zip(block, less_two)],
             )
         state = [d * d * x + y for d, x, y in zip(block, state, end)]
-    before = Summary.read(partner, modes)
+    before = Summary.read(other_states, other_edges)
     end = before.complete(taps, rims[0], less_one, less_two)
     state = [jnp.where(odd, d * x + y, x) for d, x, y in zip(block, state, end)]
     rim = [jnp.where(odd, a, b) for a, b in zip(before.rims, rims[0])]
 
-    leads = lead_sources(taps, Summary.read(local, modes).heads, rim)
+    leads = lead_sources(taps, [own_edges[i] for i in range(4)], rim)
     heads = edge(taps, 0, query_heads[0], query_heads[1], rim[0], rim[1])
     for t, u in enumerate(leads):
         state = [table[0, n] * state[n] + u for n in range(modes)]
@@ -417,6 +423,7 @@
             taps, table, *tiles = made
     fore = lax.ppermute(fore[:, : width // 2], "tp", ahead)
     aft = lax.ppermute(aft[:, width // 2 :], "tp", back)
+    states, edges = f32(modes, groups, LANES), f32(EDGE, groups, LANES)
     total = pl.pallas_call(
         half_kernel,
         out_shape=sums,
@@ -427,11 +434,11 @@
         cost_estimate=cost,
         name="project_half",
     )(fore, weights, total)
-    total, source, local = pl.pallas_call(
+    total, source, *local = pl.pallas_call(
         last_kernel,
-        out_shape=[sums, wide, f32(modes + EDGE, groups, LANES)],
+        out_shape=[sums, wide, states, edges],
         in_specs=[VMEM] * 5,
-        out_specs=[VMEM] * 3,
+        out_specs=[VMEM] * 4,
         scratch_shapes=[
             pltpu.VMEM((streams - 1, 8, groups, LANES), jnp.float32),
             pltpu.VMEM((streams, 8, groups, LANES), jnp.float32),
@@ -442,18 +449,19 @@
         name="project_last",
     )(aft, weights, filter_taps, table, total)
 
-    partner = lax.ppermute(local, "ctx", [(j, j ^ 1) for j in range(ctx)])
+    partner = [lax.ppermute(part, "ctx", [(j, j ^ 1) for j in range(ctx)]) for part in local]
     lone = ctx == 4
     chip = pl.pallas_call(
         functools.partial(chip_kernel, lone),
-        out_shape=f32(modes + (6 if lone else EDGE), groups, LANES),
-        in_specs=[VMEM] * 4,
-        out_specs=VMEM,
+        out_shape=[states, f32(6, groups, LANES) if lone else edges],
+        in_specs=[VMEM] * 6,
+        out_specs=[VMEM] * 2,
         compiler_params=params,
         name="chip_state",
-    )(local, partner, taps, table)
+    )(*local, *partner, taps, table)
     sent = [
-        lax.ppermute(chip, "ctx", [(j, (j + d) % ctx) for j in range(ctx)])
+        lax.ppermute(part, "ctx", [(j, (j + d) % ctx) for j in range(ctx)])
+        for part in chip
         for d in range(2, ctx, 2)
     ]
     query, response, heads = pl.pallas_call(
@@ -470,9 +478,9 @@
         name="local_response",
     )(total, source, filter_taps, table)
     return pl.pallas_call(
-        functools.partial(final_kernel, lone, len(sent)),
+        functools.partial(final_kernel, lone, len(sent) // 2),
         out_shape=jax.ShapeDtypeStruct((rows, chans), jnp.bfloat16),
-        in_specs=[VMEM] * (len(sent) + 9),
+        in_specs=[VMEM] * (len(sent) + 10),
         out_specs=HBM,
         scratch_shapes=[
             pltpu.VMEM((modes, groups, LANES), jnp.float32),
@@ -482,7 +490,7 @@
         ],
         compiler_params=params,
         name="carried_response",
-    )(*sent, local, partner, query, response, heads, taps, table, *tiles)
+    )(*sent, local[1], *partner, query, response, heads, taps, table, *tiles)
 
 
 def solution(mesh):

time: 40.1 us -> 40.8 us (1.017)
  starting transfers between devices: 10.8 us -> 11.9 us
    ppermute x2 -> x4, starting transfers between devices: 1.63 us -> 2.66 us  [the longest x2 2.09 us: on_device(): lax.ppermute(part, 'ctx', [(j, (j + d) % ctx) for j in range(ctx)])]
    ppermute x2 -> x4, waiting for transfers between devices: 2.85 us -> 2.55 us  [the longest x2 1.68 us: on_device(): lax.ppermute(part, 'ctx', [(j, (j + d) % ctx) for j in range(ctx)])]
  transfers between devices with their start and end apart: 10 -> 12, of which waited for: 6 -> 6; matrix products, arithmetic and copies ran while one was open for 0% -> 0% of each run, Pallas kernels for 54% -> 53%
where the time goes in v10:
time: 40.8 us; the launch traced here: 40.7 us
  Pallas kernels  24.7 us (61%)
  starting transfers between devices  11.9 us (29%)
  waiting for transfers between devices  4.01 us (10%)
    pallas_call x3, Pallas kernels, on_device(): pl.pallas_call(functools.partial(middle_kernel, order, blocks(step), left...  13.1 us
    ppermute x3, starting transfers between devices, on_device(): fore = lax.ppermute(fore, 'tp', ahead)  6.41 us
    pallas_call x1, Pallas kernels, on_device(): pl.pallas_call(functools.partial(load_kernel, order, blocks(1), pieces(1)...  6.22 us
    ppermute x2, starting transfers between devices, on_device(): lax.ppermute(part, 'ctx', [(j, (j + d) % ctx) for j in range(ctx)])  2.09 us
    pallas_call x1, Pallas kernels, on_device(): pl.pallas_call(last_kernel, out_shape=[sums, wide, states, edges], in_spe...  1.76 us
    ppermute x2, waiting for transfers between devices, on_device(): lax.ppermute(part, 'ctx', [(j, (j + d) % ctx) for j in range(ctx)])  1.68 us
    ppermute x1, starting transfers between devices, on_device(): fore = lax.ppermute(fore[:, :width // 2], 'tp', ahead)  1.67 us
    pallas_call x1, Pallas kernels, on_device(): pl.pallas_call(local_kernel, out_shape=[f32(rows, chans), f32(rows, chans...  1.62 us
  transfers between devices with their start and end apart: 12, of which 6 were waited for; matrix products, arithmetic and copies ran while one was open for 0% of the time, Pallas kernels for 53%

profile of v10, /device:TPU:0, one launch (start us, length us, event | category | flops | bytes accessed | tf_op | source)
XLA Modules:
  0.0 40.7 jit_solution(17522235808586128688)
XLA Ops:
  0.0 3.0 %collective-permute-start.1 = (bf16[128,1024]{1,0:T(8,128)(2,1)}, bf16[128,1024]{1,0:T(8,128)(2,1)S(1)}, u32[]{:S(2)}, u32[]{:S(2)}) collective-permute-start(bf16[128,1024]{1,0:T(8,128)(2,1)} %refs_0_.1), channel_id=1, source_target_pairs={{0,1},{1,3},{3,5},{5,7},{7,6},{6,4},{4,2},{2,0},{8,9},{9,11},{11,1... | collective-permute-start | bytes 786440 | tf_op jit(solution)/shard_map/ppermute | solution.py:393
  3.0 0.1 collective-permute-start
  3.0 6.2 %load_first.1.refs_3_ = bf16[3,3,1024,1024]{3,2,1,0:T(8,128)(2,1)S(1)} custom-call(bf16[3,8192,1024]{2,1,0:T(8,128)(2,1)} %bitcast.1), custom_call_target="tpu_custom_call" | custom-call | bytes 16777216 | tf_op jit(solution)/shard_map/load_first/pallas_call | solution.py:381
  9.3 0.3 collective-permute-done.1.refs_1_
  9.5 1.8 %collective-permute-start.3 = (bf16[128,1024]{1,0:T(8,128)(2,1)S(1)}, bf16[128,1024]{1,0:T(8,128)(2,1)S(1)}, u32[]{:S(2)}, u32[]{:S(2)}) collective-permute-start(bf16[128,1024]{1,0:T(8,128)(2,1)S(1)} %collective-permute-done.1.refs_1_), channel_id=1, source_target_pairs={{0,1},{1,3},{3,5},{5,7},{7,6},{6,4},{4,2},{2,0},{8,9},{9,11},{11,1... | collective-permute-start | bytes 786440 | tf_op jit(solution)/shard_map/ppermute | solution.py:393
  11.3 0.0 collective-permute-done.refs_2_
  11.3 0.3 collective-permute-start.2
  11.6 5.3 %project_blocks.3 = (f32[3,128,1024]{2,1,0:T(8,128)S(1)}, bf16[2,3,1024,1024]{3,2,1,0:T(8,128)(2,1)S(1)}, f32[3,3,8,128]{3,2,1,0:T(8,128)S(1)}, f32[5,16,8,128]{...) custom-call(bf16[128,1024]{1,0:T(8,128)(2,1)S(1)} %copy-done.1, ...), custom_call_target="tpu_custom_call" | custom-call | bytes 16777216 | tf_op jit(solution)/shard_map/project_blocks/pallas_call | solution.py:404
  16.9 0.2 collective-permute-done.3.refs_0_
  17.1 1.7 %collective-permute-start.5 = (bf16[128,1024]{1,0:T(8,128)(2,1)S(1)}, bf16[128,1024]{1,0:T(8,128)(2,1)S(1)}, u32[]{:S(2)}, u32[]{:S(2)}) collective-permute-start(bf16[128,1024]{1,0:T(8,128)(2,1)S(1)} %collective-permute-done.3.refs_0_), channel_id=1, source_target_pairs={{0,1},{1,3},{3,5},{5,7},{7,6},{6,4},{4,2},{2,0},{8,9},{9,11},{11,1... | collective-permute-start | bytes 786440 | tf_op jit(solution)/shard_map/ppermute | solution.py:393
  18.8 0.0 collective-permute-done.2.refs_1_
  18.8 0.3 collective-permute-start.4
  19.1 4.6 %project_blocks.4 = (f32[3,128,1024]{2,1,0:T(8,128)S(1)}, bf16[2,3,1024,1024]{3,2,1,0:T(8,128)(2,1)S(1)}) custom-call(bf16[128,1024]{1,0:T(8,128)(2,1)S(1)} %collective-permute-done.3.refs_0_, bf16[128,1024]{1,0:T(8,128)(2,1)S(1)} %collective-permute-done.2.refs_1_, ...), custom_call_target="tpu_custom_call", output_to_operand_aliasing={{0}: (4, {})} | custom-call | bytes 16777216 | tf_op jit(solution)/shard_map/project_blocks/pallas_call | solution.py:404
  23.7 0.3 collective-permute-done.5.refs_0_
  24.0 1.7 %collective-permute-start.7 = (bf16[128,512]{1,0:T(8,128)(2,1)S(1)}, bf16[128,512]{1,0:T(8,128)(2,1)S(1)}, u32[]{:S(2)}, u32[]{:S(2)}) collective-permute-start(bf16[128,512]{1,0:T(8,128)(2,1)S(1)} %slice.7), channel_id=1, source_target_pairs={{0,1},{1,3},{3,5},{5,7},{7,6},{6,4},{4,2},{2,0},{8,9},{9,11},{11,1... | collective-permute-start | bytes 393224 | tf_op jit(solution)/shard_map/ppermute | solution.py:424
  25.7 0.0 collective-permute-done.4.refs_1_
  25.7 0.5 %collective-permute-start.6 = (bf16[128,512]{1,0:T(8,128)(2,1)S(1)}, bf16[128,512]{1,0:T(8,128)(2,1)S(1)}, u32[]{:S(2)}, u32[]{:S(2)}) collective-permute-start(bf16[128,512]{1,0:T(8,128)(2,1)S(1)} %slice.6), channel_id=1, source_target_pairs={{1,0},{3,1},{5,3},{7,5},{6,7},{4,6},{2,4},{0,2},{9,8},{11,9},{13,1... | collective-permute-start | bytes 393224 | tf_op jit(solution)/shard_map/ppermute | solution.py:425
  26.2 3.3 %project_blocks.5 = (f32[3,128,1024]{2,1,0:T(8,128)S(1)}, bf16[1,3,1024,1024]{3,2,1,0:T(8,128)(2,1)S(1)}) custom-call(bf16[128,1024]{1,0:T(8,128)(2,1)S(1)} %collective-permute-done.5.refs_0_, bf16[128,1024]{1,0:T(8,128)(2,1)S(1)} %collective-permute-done.4.refs_1_, ...), custom_call_target="tpu_custom_call", output_to_operand_aliasing={{0}: (4, {})} | custom-call | bytes 16777216 | tf_op jit(solution)/shard_map/project_blocks/pallas_call | solution.py:404
  29.4 0.0 collective-permute-done.7.x_ref
  29.4 0.6 %project_half.1._ = f32[3,128,1024]{2,1,0:T(8,128)S(1)} custom-call(bf16[128,512]{1,0:T(8,128)(2,1)S(1)} %collective-permute-done.7.x_ref, bf16[1,3,1024,1024]{3,2,1,0:T(8,128)(2,1)S(1)} %get-tuple-element.60.held, f32[3,128,1024]{2,1,0:T(8,128)S(1)} %get-tuple-element.62._), custom_call_target="tpu_custom_call", output_to_operand_aliasing={{}: (2, {})} | custom-call | bytes 16777216 | tf_op jit(solution)/shard_map/project_half/pallas_call | solution.py:427
  30.1 0.7 %collective-permute-done.6.x_ref = bf16[128,512]{1,0:T(8,128)(2,1)S(1)} collective-permute-done((bf16[128,512]{1,0:T(8,128)(2,1)S(1)}, bf16[128,512]{1,0:T(8,128)(2,1)S(1)}, u32[]{:S(2)}, u32[]{:S(2)}) %collective-permute-start.6) | collective-permute-done | bytes 131104 | tf_op jit(solution)/shard_map/ppermute | solution.py:425
  30.7 1.8 %project_last.1 = (f32[3,128,1024]{2,1,0:T(8,128)S(1)}, f32[128,8,128]{2,1,0:T(8,128)S(1)}, f32[16,8,128]{2,1,0:T(8,128)S(1)}, f32[10,8,128]{2,1,0:T(8,128)S(1)}) custom-call(bf16[128,512]{1,0:T(8,128)(2,1)S(1)} %collective-permute-done.6.x_ref, bf16[1,3,1024,1024]{3,2,1,0:T(8,128)(2,1)S(1)} %get-tuple-element.60.held, ...), custom_call_target="tpu_custom_call", output_to_operand_aliasing={{0}: (4, {})} | custom-call | bytes 16777216 | tf_op jit(solution)/shard_map/project_last/pallas_call | solution.py:437
  32.5 0.1 collective-permute-start.8
  32.6 0.5 %collective-permute-start.9 = (f32[10,8,128]{2,1,0:T(8,128)S(1)}, f32[10,8,128]{2,1,0:T(8,128)S(1)}, u32[]{:S(2)}, u32[]{:S(2)}) collective-permute-start(f32[10,8,128]{2,1,0:T(8,128)S(1)} %get-tuple-element.64.edges.refs_2_), channel_id=1, source_target_pairs={{0,8},{8,0},{16,24},{24,16},{1,9},{9,1},{17,25},{25,17},{2,10},{10... | collective-permute-start | bytes 122888 | tf_op jit(solution)/shard_map/ppermute | solution.py:452
  33.1 0.9 %collective-permute-done.9.other_edges.refs_4_ = f32[10,8,128]{2,1,0:T(8,128)S(1)} collective-permute-done((f32[10,8,128]{2,1,0:T(8,128)S(1)}, f32[10,8,128]{2,1,0:T(8,128)S(1)}, u32[]{:S(2)}, u32[]{:S(2)}) %collective-permute-start.9) | collective-permute-done | bytes 40992 | tf_op jit(solution)/shard_map/ppermute | solution.py:452
  33.9 0.0 collective-permute-done.8.other_states.refs_3_
  34.0 1.6 %collective-permute-start.10 = (f32[16,8,128]{2,1,0:T(8,128)S(1)}, f32[16,8,128]{2,1,0:T(8,128)S(1)}, u32[]{:S(2)}, u32[]{:S(2)}) collective-permute-start(f32[16,8,128]{2,1,0:T(8,128)S(1)} %get-tuple-element.66), channel_id=1, source_target_pairs={{0,16},{8,24},{16,0},{24,8},{1,17},{9,25},{17,1},{25,9},{2,18},{10... | collective-permute-start | bytes 196616 | tf_op jit(solution)/shard_map/ppermute | solution.py:463
  35.5 0.5 %collective-permute-start.11 = (f32[6,8,128]{2,1,0:T(8,128)S(1)}, f32[6,8,128]{2,1,0:T(8,128)S(1)}, u32[]{:S(2)}, u32[]{:S(2)}) collective-permute-start(f32[6,8,128]{2,1,0:T(8,128)S(1)} %get-tuple-element.67), channel_id=1, source_target_pairs={{0,16},{8,24},{16,0},{24,8},{1,17},{9,25},{17,1},{25,9},{2,18},{10... | collective-permute-start | bytes 73736 | tf_op jit(solution)/shard_map/ppermute | solution.py:463
  36.1 1.6 %local_response.1 = (f32[128,1024]{1,0:T(8,128)S(1)}, f32[128,1024]{1,0:T(8,128)S(1)}, f32[2,8,128]{2,1,0:T(8,128)S(1)}) custom-call(f32[3,128,1024]{2,1,0:T(8,128)S(1)} %get-tuple-element.68.total, f32[128,8,128]{2,1,0:T(8,128)S(1)} %get-tuple-element.69.source, f32[3,3,1024]{2,1,0:T(4,128)S(1)} %copy-done, ...), custom_call_target="tpu_custom_call" | custom-call | bytes 16777216 | tf_op jit(solution)/shard_map/local_response/pallas_call | solution.py:467
  37.7 1.7 %collective-permute-done.11.refs_1_ = f32[6,8,128]{2,1,0:T(8,128)S(1)} collective-permute-done((f32[6,8,128]{2,1,0:T(8,128)S(1)}, f32[6,8,128]{2,1,0:T(8,128)S(1)}, u32[]{:S(2)}, u32[]{:S(2)}) %collective-permute-start.11) | collective-permute-done | bytes 24608 | tf_op jit(solution)/shard_map/ppermute | solution.py:463
  39.4 0.0 collective-permute-done.10.refs_0_
  39.4 1.3 %carried_response.1 = bf16[128,1024]{1,0:T(8,128)(2,1)} custom-call(f32[16,8,128]{2,1,0:T(8,128)S(1)} %collective-permute-done.10.refs_0_, f32[6,8,128]{2,1,0:T(8,128)S(1)} %collective-permute-done.11.refs_1_, f32[10,8,128]{2,1,0:T(8,128)S(1)} %get-tuple-element.64.edges.refs_2_, f32[16,8,128]{2,1,0:T(8,128)S(1)} %collective-permute-done.8.other_states.refs_3_, ...), custom_call_target="tpu_custom_call" | custom-call | tf_op jit(solution)/shard_map/carried_response/pallas_call | solution.py:480
  (11 shorter events, 0.1 us)
Async XLA Ops:
  0.0 9.5 %collective-permute-start.1 = (bf16[128,1024]{1,0:T(8,128)(2,1)}, bf16[128,1024]{1,0:T(8,128)(2,1)S(1)}, u32[]{:S(2)}, u32[]{:S(2)}) collective-permute-start(bf16[128,1024]{1,0:T(8,128)(2,1)} %refs_0_.1), channel_id=1, source_target_pairs={{0,1},{1,3},{3,5},{5,7},{7,6},{6,4},{4,2},{2,0},{8,9},{9,11},{11,1... | collective-permute-start | bytes 786440 | tf_op jit(solution)/shard_map/ppermute | solution.py:393
  3.0 8.3 %collective-permute-start = (bf16[128,1024]{1,0:T(8,128)(2,1)}, bf16[128,1024]{1,0:T(8,128)(2,1)S(1)}, u32[]{:S(2)}, u32[]{:S(2)}) collective-permute-start(bf16[128,1024]{1,0:T(8,128)(2,1)} %refs_0_.1), channel_id=1, source_target_pairs={{1,0},{3,1},{5,3},{7,5},{6,7},{4,6},{2,4},{0,2},{9,8},{11,9},{13,1... | collective-permute-start | bytes 786440 | tf_op jit(solution)/shard_map/ppermute | solution.py:394
  3.0 8.5 %copy-start = (f32[3,3,1024]{2,1,0:T(4,128)S(1)}, f32[3,3,1024]{2,1,0:T(4,128)}, u32[]{:S(2)}) copy-start(f32[3,3,1024]{2,1,0:T(4,128)} %taps.3) | copy-start | bytes 110596
  3.0 8.5 %copy-start.1 = (bf16[128,1024]{1,0:T(8,128)(2,1)S(1)}, bf16[128,1024]{1,0:T(8,128)(2,1)}, u32[]{:S(2)}) copy-start(bf16[128,1024]{1,0:T(8,128)(2,1)} %refs_0_.1) | copy-start | bytes 786436
  3.0 8.5 %copy-start.2 = (f32[16,1024]{1,0:T(8,128)S(1)}, f32[16,1024]{1,0:T(8,128)}, u32[]{:S(2)}) copy-start(f32[16,1024]{1,0:T(8,128)} %refs_6_.1) | copy-start | bytes 196612
  3.0 8.5 %copy-start.3 = (f32[16,1024]{1,0:T(8,128)S(1)}, f32[16,1024]{1,0:T(8,128)}, u32[]{:S(2)}) copy-start(f32[16,1024]{1,0:T(8,128)} %refs_7_.1) | copy-start | bytes 196612
  9.5 7.6 %collective-permute-start.3 = (bf16[128,1024]{1,0:T(8,128)(2,1)S(1)}, bf16[128,1024]{1,0:T(8,128)(2,1)S(1)}, u32[]{:S(2)}, u32[]{:S(2)}) collective-permute-start(bf16[128,1024]{1,0:T(8,128)(2,1)S(1)} %collective-permute-done.1.refs_1_), channel_id=1, source_target_pairs={{0,1},{1,3},{3,5},{5,7},{7,6},{6,4},{4,2},{2,0},{8,9},{9,11},{11,1... | collective-permute-start | bytes 786440 | tf_op jit(solution)/shard_map/ppermute | solution.py:393
  11.3 7.5 %collective-permute-start.2 = (bf16[128,1024]{1,0:T(8,128)(2,1)S(1)}, bf16[128,1024]{1,0:T(8,128)(2,1)S(1)}, u32[]{:S(2)}, u32[]{:S(2)}) collective-permute-start(bf16[128,1024]{1,0:T(8,128)(2,1)S(1)} %collective-permute-done.refs_2_), channel_id=1, source_target_pairs={{1,0},{3,1},{5,3},{7,5},{6,7},{4,6},{2,4},{0,2},{9,8},{11,9},{13,1... | collective-permute-start | bytes 786440 | tf_op jit(solution)/shard_map/ppermute | solution.py:394
  17.1 6.9 %collective-permute-start.5 = (bf16[128,1024]{1,0:T(8,128)(2,1)S(1)}, bf16[128,1024]{1,0:T(8,128)(2,1)S(1)}, u32[]{:S(2)}, u32[]{:S(2)}) collective-permute-start(bf16[128,1024]{1,0:T(8,128)(2,1)S(1)} %collective-permute-done.3.refs_0_), channel_id=1, source_target_pairs={{0,1},{1,3},{3,5},{5,7},{7,6},{6,4},{4,2},{2,0},{8,9},{9,11},{11,1... | collective-permute-start | bytes 786440 | tf_op jit(solution)/shard_map/ppermute | solution.py:393
  18.8 6.9 %collective-permute-start.4 = (bf16[128,1024]{1,0:T(8,128)(2,1)S(1)}, bf16[128,1024]{1,0:T(8,128)(2,1)S(1)}, u32[]{:S(2)}, u32[]{:S(2)}) collective-permute-start(bf16[128,1024]{1,0:T(8,128)(2,1)S(1)} %collective-permute-done.2.refs_1_), channel_id=1, source_target_pairs={{1,0},{3,1},{5,3},{7,5},{6,7},{4,6},{2,4},{0,2},{9,8},{11,9},{13,1... | collective-permute-start | bytes 786440 | tf_op jit(solution)/shard_map/ppermute | solution.py:394
  24.0 5.4 %collective-permute-start.7 = (bf16[128,512]{1,0:T(8,128)(2,1)S(1)}, bf16[128,512]{1,0:T(8,128)(2,1)S(1)}, u32[]{:S(2)}, u32[]{:S(2)}) collective-permute-start(bf16[128,512]{1,0:T(8,128)(2,1)S(1)} %slice.7), channel_id=1, source_target_pairs={{0,1},{1,3},{3,5},{5,7},{7,6},{6,4},{4,2},{2,0},{8,9},{9,11},{11,1... | collective-permute-start | bytes 393224 | tf_op jit(solution)/shard_map/ppermute | solution.py:424
  25.7 5.0 %collective-permute-start.6 = (bf16[128,512]{1,0:T(8,128)(2,1)S(1)}, bf16[128,512]{1,0:T(8,128)(2,1)S(1)}, u32[]{:S(2)}, u32[]{:S(2)}) collective-permute-start(bf16[128,512]{1,0:T(8,128)(2,1)S(1)} %slice.6), channel_id=1, source_target_pairs={{1,0},{3,1},{5,3},{7,5},{6,7},{4,6},{2,4},{0,2},{9,8},{11,9},{13,1... | collective-permute-start | bytes 393224 | tf_op jit(solution)/shard_map/ppermute | solution.py:425
  32.5 1.4 %collective-permute-start.8 = (f32[16,8,128]{2,1,0:T(8,128)S(1)}, f32[16,8,128]{2,1,0:T(8,128)S(1)}, u32[]{:S(2)}, u32[]{:S(2)}) collective-permute-start(f32[16,8,128]{2,1,0:T(8,128)S(1)} %get-tuple-element.63.states), channel_id=1, source_target_pairs={{0,8},{8,0},{16,24},{24,16},{1,9},{9,1},{17,25},{25,17},{2,10},{10... | collective-permute-start | bytes 196616 | tf_op jit(solution)/shard_map/ppermute | solution.py:452
  32.6 1.4 %collective-permute-start.9 = (f32[10,8,128]{2,1,0:T(8,128)S(1)}, f32[10,8,128]{2,1,0:T(8,128)S(1)}, u32[]{:S(2)}, u32[]{:S(2)}) collective-permute-start(f32[10,8,128]{2,1,0:T(8,128)S(1)} %get-tuple-element.64.edges.refs_2_), channel_id=1, source_target_pairs={{0,8},{8,0},{16,24},{24,16},{1,9},{9,1},{17,25},{25,17},{2,10},{10... | collective-permute-start | bytes 122888 | tf_op jit(solution)/shard_map/ppermute | solution.py:452
  34.0 5.4 %collective-permute-start.10 = (f32[16,8,128]{2,1,0:T(8,128)S(1)}, f32[16,8,128]{2,1,0:T(8,128)S(1)}, u32[]{:S(2)}, u32[]{:S(2)}) collective-permute-start(f32[16,8,128]{2,1,0:T(8,128)S(1)} %get-tuple-element.66), channel_id=1, source_target_pairs={{0,16},{8,24},{16,0},{24,8},{1,17},{9,25},{17,1},{25,9},{2,18},{10... | collective-permute-start | bytes 196616 | tf_op jit(solution)/shard_map/ppermute | solution.py:463
  35.5 3.8 %collective-permute-start.11 = (f32[6,8,128]{2,1,0:T(8,128)S(1)}, f32[6,8,128]{2,1,0:T(8,128)S(1)}, u32[]{:S(2)}, u32[]{:S(2)}) collective-permute-start(f32[6,8,128]{2,1,0:T(8,128)S(1)} %get-tuple-element.67), channel_id=1, source_target_pairs={{0,16},{8,24},{16,0},{24,8},{1,17},{9,25},{17,1},{25,9},{2,18},{10... | collective-permute-start | bytes 73736 | tf_op jit(solution)/shard_map/ppermute | solution.py:463

commit v11 on v9

--- a/solution.py
+++ b/solution.py
@@ -147,18 +147,25 @@
 
 def last_kernel(x_ref, held, taps, table, _, total, source, out_ref, low, high):
     depth = x_ref.shape[1]
-    for s in range(total.shape[0]):
-        add_products([x_ref[...]], lambda b, at: held[0, s, depth:, at], total, s, cols=WIDE)
     rows, groups, lanes = source.shape
     modes = table.shape[1]
-    for g in range(groups):
-        cols = slice(g * lanes, (g + 1) * lanes)
-        one, two = rounded(total[1, :, cols]), rounded(total[2, :, cols])
-        source[:, g, :] = filtered(taps, 1, one, cols) * filtered(taps, 2, two, cols)
-        for s, value in ((1, one), (2, two)):
-            low[s - 1, :, g, :] = value[:8]
-            high[s, :, g, :] = value[rows - 8 :]
-        high[0, :, g, :] = rounded(total[0, rows - 8 :, cols])
+    for c in range(0, total.shape[2], COLS):
+        at = slice(c, c + COLS)
+        sums = [
+            total[s, :, at]
+            + jnp.dot(x_ref[...], held[0, s, depth:, at], preferred_element_type=jnp.float32)
+            for s in range(3)
+        ]
+        total[0, :, at] = sums[0]
+        projected = [rounded(value) for value in sums[1:]]
+        for g in range(c // lanes, (c + COLS) // lanes):
+            cols = slice(g * lanes, (g + 1) * lanes)
+            one, two = [value[:, g * lanes - c : (g + 1) * lanes - c] for value in projected]
+            source[:, g, :] = filtered(taps, 1, one, cols) * filtered(taps, 2, two, cols)
+            for s, value in ((1, one), (2, two)):
+                low[s - 1, :, g, :] = value[:8]
+                high[s, :, g, :] = value[rows - 8 :]
+            high[0, :, g, :] = rounded(sums[0][rows - 8 :, g * lanes - c : (g + 1) * lanes - c])
     rate = [table[0, n] for n in range(modes)]
 
     def step_row(t, state):

time: 40.1 us -> 40.2 us (level)
  no operation moved by 1% of the time
where the time goes in v11:
time: 40.2 us; the launch traced here: 40 us
  Pallas kernels  24.8 us (62%)
  starting transfers between devices  10.8 us (27%)
  waiting for transfers between devices  4.3 us (11%)
    pallas_call x3, Pallas kernels, on_device(): pl.pallas_call(functools.partial(middle_kernel, order, blocks(step), left...  13.1 us
    ppermute x3, starting transfers between devices, on_device(): fore = lax.ppermute(fore, 'tp', ahead)  6.41 us
    pallas_call x1, Pallas kernels, on_device(): pl.pallas_call(functools.partial(load_kernel, order, blocks(1), pieces(1)...  6.22 us
    pallas_call x1, Pallas kernels, on_device(): pl.pallas_call(last_kernel, out_shape=[sums, wide, f32(modes + EDGE, grou...  1.83 us
    ppermute x1, starting transfers between devices, on_device(): fore = lax.ppermute(fore[:, :width // 2], 'tp', ahead)  1.67 us
    pallas_call x1, Pallas kernels, on_device(): pl.pallas_call(local_kernel, out_shape=[f32(rows, chans), f32(rows, chans...  1.62 us
    ppermute x1, starting transfers between devices, on_device(): lax.ppermute(chip, 'ctx', [(j, (j + d) % ctx) for j in range(ctx)])  1.57 us
    ppermute x1, waiting for transfers between devices, on_device(): lax.ppermute(chip, 'ctx', [(j, (j + d) % ctx) for j in range(ctx)])  1.55 us
  transfers between devices with their start and end apart: 10, of which 6 were waited for; matrix products, arithmetic and copies ran while one was open for 0% of the time, Pallas kernels for 54%

profile of v11, /device:TPU:0, one launch (start us, length us, event | category | flops | bytes accessed | tf_op | source)
XLA Modules:
  0.0 40.0 jit_solution(8307116484679816207)
XLA Ops:
  0.0 3.0 %collective-permute-start.1 = (bf16[128,1024]{1,0:T(8,128)(2,1)}, bf16[128,1024]{1,0:T(8,128)(2,1)S(1)}, u32[]{:S(2)}, u32[]{:S(2)}) collective-permute-start(bf16[128,1024]{1,0:T(8,128)(2,1)} %refs_0_.1), channel_id=1, source_target_pairs={{0,1},{1,3},{3,5},{5,7},{7,6},{6,4},{4,2},{2,0},{8,9},{9,11},{11,1... | collective-permute-start | bytes 786440 | tf_op jit(solution)/shard_map/ppermute | solution.py:394
  3.0 0.1 collective-permute-start
  3.0 6.2 %load_first.1.refs_3_ = bf16[3,3,1024,1024]{3,2,1,0:T(8,128)(2,1)S(1)} custom-call(bf16[3,8192,1024]{2,1,0:T(8,128)(2,1)} %bitcast.1), custom_call_target="tpu_custom_call" | custom-call | bytes 16777216 | tf_op jit(solution)/shard_map/load_first/pallas_call | solution.py:382
  9.3 0.3 collective-permute-done.1.refs_1_
  9.5 1.8 %collective-permute-start.3 = (bf16[128,1024]{1,0:T(8,128)(2,1)S(1)}, bf16[128,1024]{1,0:T(8,128)(2,1)S(1)}, u32[]{:S(2)}, u32[]{:S(2)}) collective-permute-start(bf16[128,1024]{1,0:T(8,128)(2,1)S(1)} %collective-permute-done.1.refs_1_), channel_id=1, source_target_pairs={{0,1},{1,3},{3,5},{5,7},{7,6},{6,4},{4,2},{2,0},{8,9},{9,11},{11,1... | collective-permute-start | bytes 786440 | tf_op jit(solution)/shard_map/ppermute | solution.py:394
  11.3 0.0 collective-permute-done.refs_2_
  11.3 0.3 collective-permute-start.2
  11.6 0.0 copy-done
  11.6 0.0 copy-done.1
  11.6 0.0 copy-done.3
  11.6 5.3 %project_blocks.3 = (f32[3,128,1024]{2,1,0:T(8,128)S(1)}, bf16[2,3,1024,1024]{3,2,1,0:T(8,128)(2,1)S(1)}, f32[3,3,8,128]{3,2,1,0:T(8,128)S(1)}, f32[5,16,8,128]{...) custom-call(bf16[128,1024]{1,0:T(8,128)(2,1)S(1)} %copy-done.1, ...), custom_call_target="tpu_custom_call" | custom-call | bytes 16777216 | tf_op jit(solution)/shard_map/project_blocks/pallas_call | solution.py:405
  16.9 0.2 collective-permute-done.3.refs_0_
  17.1 1.7 %collective-permute-start.5 = (bf16[128,1024]{1,0:T(8,128)(2,1)S(1)}, bf16[128,1024]{1,0:T(8,128)(2,1)S(1)}, u32[]{:S(2)}, u32[]{:S(2)}) collective-permute-start(bf16[128,1024]{1,0:T(8,128)(2,1)S(1)} %collective-permute-done.3.refs_0_), channel_id=1, source_target_pairs={{0,1},{1,3},{3,5},{5,7},{7,6},{6,4},{4,2},{2,0},{8,9},{9,11},{11,1... | collective-permute-start | bytes 786440 | tf_op jit(solution)/shard_map/ppermute | solution.py:394
  18.8 0.0 collective-permute-done.2.refs_1_
  18.8 0.3 collective-permute-start.4
  19.1 4.6 %project_blocks.4 = (f32[3,128,1024]{2,1,0:T(8,128)S(1)}, bf16[2,3,1024,1024]{3,2,1,0:T(8,128)(2,1)S(1)}) custom-call(bf16[128,1024]{1,0:T(8,128)(2,1)S(1)} %collective-permute-done.3.refs_0_, bf16[128,1024]{1,0:T(8,128)(2,1)S(1)} %collective-permute-done.2.refs_1_, ...), custom_call_target="tpu_custom_call", output_to_operand_aliasing={{0}: (4, {})} | custom-call | bytes 16777216 | tf_op jit(solution)/shard_map/project_blocks/pallas_call | solution.py:405
  23.7 0.3 collective-permute-done.5.refs_0_
  24.0 1.7 %collective-permute-start.7 = (bf16[128,512]{1,0:T(8,128)(2,1)S(1)}, bf16[128,512]{1,0:T(8,128)(2,1)S(1)}, u32[]{:S(2)}, u32[]{:S(2)}) collective-permute-start(bf16[128,512]{1,0:T(8,128)(2,1)S(1)} %slice.7), channel_id=1, source_target_pairs={{0,1},{1,3},{3,5},{5,7},{7,6},{6,4},{4,2},{2,0},{8,9},{9,11},{11,1... | collective-permute-start | bytes 393224 | tf_op jit(solution)/shard_map/ppermute | solution.py:425
  25.7 0.0 collective-permute-done.4.refs_1_
  25.7 0.5 %collective-permute-start.6 = (bf16[128,512]{1,0:T(8,128)(2,1)S(1)}, bf16[128,512]{1,0:T(8,128)(2,1)S(1)}, u32[]{:S(2)}, u32[]{:S(2)}) collective-permute-start(bf16[128,512]{1,0:T(8,128)(2,1)S(1)} %slice.6), channel_id=1, source_target_pairs={{1,0},{3,1},{5,3},{7,5},{6,7},{4,6},{2,4},{0,2},{9,8},{11,9},{13,1... | collective-permute-start | bytes 393224 | tf_op jit(solution)/shard_map/ppermute | solution.py:426
  26.2 3.3 %project_blocks.5 = (f32[3,128,1024]{2,1,0:T(8,128)S(1)}, bf16[1,3,1024,1024]{3,2,1,0:T(8,128)(2,1)S(1)}) custom-call(bf16[128,1024]{1,0:T(8,128)(2,1)S(1)} %collective-permute-done.5.refs_0_, bf16[128,1024]{1,0:T(8,128)(2,1)S(1)} %collective-permute-done.4.refs_1_, ...), custom_call_target="tpu_custom_call", output_to_operand_aliasing={{0}: (4, {})} | custom-call | bytes 16777216 | tf_op jit(solution)/shard_map/project_blocks/pallas_call | solution.py:405
  29.4 0.0 collective-permute-done.7.x_ref
  29.4 0.6 %project_half.1._ = f32[3,128,1024]{2,1,0:T(8,128)S(1)} custom-call(bf16[128,512]{1,0:T(8,128)(2,1)S(1)} %collective-permute-done.7.x_ref, bf16[1,3,1024,1024]{3,2,1,0:T(8,128)(2,1)S(1)} %get-tuple-element.57.held, f32[3,128,1024]{2,1,0:T(8,128)S(1)} %get-tuple-element.59._), custom_call_target="tpu_custom_call", output_to_operand_aliasing={{}: (2, {})} | custom-call | bytes 16777216 | tf_op jit(solution)/shard_map/project_half/pallas_call | solution.py:427
  30.1 0.7 %collective-permute-done.6.x_ref = bf16[128,512]{1,0:T(8,128)(2,1)S(1)} collective-permute-done((bf16[128,512]{1,0:T(8,128)(2,1)S(1)}, bf16[128,512]{1,0:T(8,128)(2,1)S(1)}, u32[]{:S(2)}, u32[]{:S(2)}) %collective-permute-start.6) | collective-permute-done | bytes 131104 | tf_op jit(solution)/shard_map/ppermute | solution.py:426
  30.7 1.8 %project_last.1 = (f32[3,128,1024]{2,1,0:T(8,128)S(1)}, f32[128,8,128]{2,1,0:T(8,128)S(1)}, f32[26,8,128]{2,1,0:T(8,128)S(1)}) custom-call(bf16[128,512]{1,0:T(8,128)(2,1)S(1)} %collective-permute-done.6.x_ref, bf16[1,3,1024,1024]{3,2,1,0:T(8,128)(2,1)S(1)} %get-tuple-element.57.held, f32[3,3,1024]{2,1,0:T(4,128)S(1)} %copy-done, ...), custom_call_target="tpu_custom_call", output_to_operand_aliasing={{0}: (4, {})} | custom-call | bytes 16777216 | tf_op jit(solution)/shard_map/project_last/pallas_call | solution.py:437
  32.6 0.1 collective-permute-start.8
  32.6 1.3 %collective-permute-done.8.partner.refs_2_ = f32[26,8,128]{2,1,0:T(8,128)S(1)} collective-permute-done((f32[26,8,128]{2,1,0:T(8,128)S(1)}, f32[26,8,128]{2,1,0:T(8,128)S(1)}, u32[]{:S(2)}, u32[]{:S(2)}) %collective-permute-start.8) | collective-permute-done | bytes 106528 | tf_op jit(solution)/shard_map/ppermute | solution.py:452
  33.9 0.1 chip_state.1
  34.0 1.6 %collective-permute-start.9 = (f32[22,8,128]{2,1,0:T(8,128)S(1)}, f32[22,8,128]{2,1,0:T(8,128)S(1)}, u32[]{:S(2)}, u32[]{:S(2)}) collective-permute-start(f32[22,8,128]{2,1,0:T(8,128)S(1)} %chip_state.1), channel_id=1, source_target_pairs={{0,16},{8,24},{16,0},{24,8},{1,17},{9,25},{17,1},{25,9},{2,18},{10... | collective-permute-start | bytes 270344 | tf_op jit(solution)/shard_map/ppermute | solution.py:463
  35.6 1.6 %local_response.1 = (f32[128,1024]{1,0:T(8,128)S(1)}, f32[128,1024]{1,0:T(8,128)S(1)}, f32[2,8,128]{2,1,0:T(8,128)S(1)}) custom-call(f32[3,128,1024]{2,1,0:T(8,128)S(1)} %get-tuple-element.62.total, f32[128,8,128]{2,1,0:T(8,128)S(1)} %get-tuple-element.63.source, f32[3,3,1024]{2,1,0:T(4,128)S(1)} %copy-done, ...), custom_call_target="tpu_custom_call" | custom-call | bytes 16777216 | tf_op jit(solution)/shard_map/local_response/pallas_call | solution.py:466
  37.2 1.5 %collective-permute-done.9.refs_0_ = f32[22,8,128]{2,1,0:T(8,128)S(1)} collective-permute-done((f32[22,8,128]{2,1,0:T(8,128)S(1)}, f32[22,8,128]{2,1,0:T(8,128)S(1)}, u32[]{:S(2)}, u32[]{:S(2)}) %collective-permute-start.9) | collective-permute-done | bytes 90144 | tf_op jit(solution)/shard_map/ppermute | solution.py:463
  38.7 1.3 %carried_response.1 = bf16[128,1024]{1,0:T(8,128)(2,1)} custom-call(f32[22,8,128]{2,1,0:T(8,128)S(1)} %collective-permute-done.9.refs_0_, f32[26,8,128]{2,1,0:T(8,128)S(1)} %get-tuple-element.60.local.refs_1_, f32[26,8,128]{2,1,0:T(8,128)S(1)} %collective-permute-done.8.partner.refs_2_, f32[128,1024]{1,0:T(8,128)S(1)} %get-tuple-element.64.refs_3_, ...), custom_call_target="tpu_custom_call" | custom-call | tf_op jit(solution)/shard_map/carried_response/pallas_call | solution.py:479
  (7 shorter events, 0.0 us)
Async XLA Ops:
  0.0 9.5 %collective-permute-start.1 = (bf16[128,1024]{1,0:T(8,128)(2,1)}, bf16[128,1024]{1,0:T(8,128)(2,1)S(1)}, u32[]{:S(2)}, u32[]{:S(2)}) collective-permute-start(bf16[128,1024]{1,0:T(8,128)(2,1)} %refs_0_.1), channel_id=1, source_target_pairs={{0,1},{1,3},{3,5},{5,7},{7,6},{6,4},{4,2},{2,0},{8,9},{9,11},{11,1... | collective-permute-start | bytes 786440 | tf_op jit(solution)/shard_map/ppermute | solution.py:394
  3.0 8.3 %collective-permute-start = (bf16[128,1024]{1,0:T(8,128)(2,1)}, bf16[128,1024]{1,0:T(8,128)(2,1)S(1)}, u32[]{:S(2)}, u32[]{:S(2)}) collective-permute-start(bf16[128,1024]{1,0:T(8,128)(2,1)} %refs_0_.1), channel_id=1, source_target_pairs={{1,0},{3,1},{5,3},{7,5},{6,7},{4,6},{2,4},{0,2},{9,8},{11,9},{13,1... | collective-permute-start | bytes 786440 | tf_op jit(solution)/shard_map/ppermute | solution.py:395
  3.0 8.5 %copy-start = (f32[3,3,1024]{2,1,0:T(4,128)S(1)}, f32[3,3,1024]{2,1,0:T(4,128)}, u32[]{:S(2)}) copy-start(f32[3,3,1024]{2,1,0:T(4,128)} %taps.3) | copy-start | bytes 110596
  3.0 8.5 %copy-start.1 = (bf16[128,1024]{1,0:T(8,128)(2,1)S(1)}, bf16[128,1024]{1,0:T(8,128)(2,1)}, u32[]{:S(2)}) copy-start(bf16[128,1024]{1,0:T(8,128)(2,1)} %refs_0_.1) | copy-start | bytes 786436
  3.0 8.5 %copy-start.2 = (f32[16,1024]{1,0:T(8,128)S(1)}, f32[16,1024]{1,0:T(8,128)}, u32[]{:S(2)}) copy-start(f32[16,1024]{1,0:T(8,128)} %refs_6_.1) | copy-start | bytes 196612
  3.0 8.5 %copy-start.3 = (f32[16,1024]{1,0:T(8,128)S(1)}, f32[16,1024]{1,0:T(8,128)}, u32[]{:S(2)}) copy-start(f32[16,1024]{1,0:T(8,128)} %refs_7_.1) | copy-start | bytes 196612
  9.5 7.6 %collective-permute-start.3 = (bf16[128,1024]{1,0:T(8,128)(2,1)S(1)}, bf16[128,1024]{1,0:T(8,128)(2,1)S(1)}, u32[]{:S(2)}, u32[]{:S(2)}) collective-permute-start(bf16[128,1024]{1,0:T(8,128)(2,1)S(1)} %collective-permute-done.1.refs_1_), channel_id=1, source_target_pairs={{0,1},{1,3},{3,5},{5,7},{7,6},{6,4},{4,2},{2,0},{8,9},{9,11},{11,1... | collective-permute-start | bytes 786440 | tf_op jit(solution)/shard_map/ppermute | solution.py:394
  11.3 7.5 %collective-permute-start.2 = (bf16[128,1024]{1,0:T(8,128)(2,1)S(1)}, bf16[128,1024]{1,0:T(8,128)(2,1)S(1)}, u32[]{:S(2)}, u32[]{:S(2)}) collective-permute-start(bf16[128,1024]{1,0:T(8,128)(2,1)S(1)} %collective-permute-done.refs_2_), channel_id=1, source_target_pairs={{1,0},{3,1},{5,3},{7,5},{6,7},{4,6},{2,4},{0,2},{9,8},{11,9},{13,1... | collective-permute-start | bytes 786440 | tf_op jit(solution)/shard_map/ppermute | solution.py:395
  17.1 6.9 %collective-permute-start.5 = (bf16[128,1024]{1,0:T(8,128)(2,1)S(1)}, bf16[128,1024]{1,0:T(8,128)(2,1)S(1)}, u32[]{:S(2)}, u32[]{:S(2)}) collective-permute-start(bf16[128,1024]{1,0:T(8,128)(2,1)S(1)} %collective-permute-done.3.refs_0_), channel_id=1, source_target_pairs={{0,1},{1,3},{3,5},{5,7},{7,6},{6,4},{4,2},{2,0},{8,9},{9,11},{11,1... | collective-permute-start | bytes 786440 | tf_op jit(solution)/shard_map/ppermute | solution.py:394
  18.8 6.9 %collective-permute-start.4 = (bf16[128,1024]{1,0:T(8,128)(2,1)S(1)}, bf16[128,1024]{1,0:T(8,128)(2,1)S(1)}, u32[]{:S(2)}, u32[]{:S(2)}) collective-permute-start(bf16[128,1024]{1,0:T(8,128)(2,1)S(1)} %collective-permute-done.2.refs_1_), channel_id=1, source_target_pairs={{1,0},{3,1},{5,3},{7,5},{6,7},{4,6},{2,4},{0,2},{9,8},{11,9},{13,1... | collective-permute-start | bytes 786440 | tf_op jit(solution)/shard_map/ppermute | solution.py:395
  24.0 5.4 %collective-permute-start.7 = (bf16[128,512]{1,0:T(8,128)(2,1)S(1)}, bf16[128,512]{1,0:T(8,128)(2,1)S(1)}, u32[]{:S(2)}, u32[]{:S(2)}) collective-permute-start(bf16[128,512]{1,0:T(8,128)(2,1)S(1)} %slice.7), channel_id=1, source_target_pairs={{0,1},{1,3},{3,5},{5,7},{7,6},{6,4},{4,2},{2,0},{8,9},{9,11},{11,1... | collective-permute-start | bytes 393224 | tf_op jit(solution)/shard_map/ppermute | solution.py:425
  25.7 5.0 %collective-permute-start.6 = (bf16[128,512]{1,0:T(8,128)(2,1)S(1)}, bf16[128,512]{1,0:T(8,128)(2,1)S(1)}, u32[]{:S(2)}, u32[]{:S(2)}) collective-permute-start(bf16[128,512]{1,0:T(8,128)(2,1)S(1)} %slice.6), channel_id=1, source_target_pairs={{1,0},{3,1},{5,3},{7,5},{6,7},{4,6},{2,4},{0,2},{9,8},{11,9},{13,1... | collective-permute-start | bytes 393224 | tf_op jit(solution)/shard_map/ppermute | solution.py:426
  32.6 1.4 %collective-permute-start.8 = (f32[26,8,128]{2,1,0:T(8,128)S(1)}, f32[26,8,128]{2,1,0:T(8,128)S(1)}, u32[]{:S(2)}, u32[]{:S(2)}) collective-permute-start(f32[26,8,128]{2,1,0:T(8,128)S(1)} %get-tuple-element.60.local.refs_1_), channel_id=1, source_target_pairs={{0,8},{8,0},{16,24},{24,16},{1,9},{9,1},{17,25},{25,17},{2,10},{10... | collective-permute-start | bytes 319496 | tf_op jit(solution)/shard_map/ppermute | solution.py:452
  34.0 4.7 %collective-permute-start.9 = (f32[22,8,128]{2,1,0:T(8,128)S(1)}, f32[22,8,128]{2,1,0:T(8,128)S(1)}, u32[]{:S(2)}, u32[]{:S(2)}) collective-permute-start(f32[22,8,128]{2,1,0:T(8,128)S(1)} %chip_state.1), channel_id=1, source_target_pairs={{0,16},{8,24},{16,0},{24,8},{1,17},{9,25},{17,1},{25,9},{2,18},{10... | collective-permute-start | bytes 270344 | tf_op jit(solution)/shard_map/ppermute | solution.py:463

commit v12 on v9

--- a/solution.py
+++ b/solution.py
@@ -82,26 +82,35 @@
     *refs, rest, rest_sem, sem = refs
     inputs, (total, next_held, *made) = refs[:inputs_count], refs[inputs_count:]
     fresh = bool(made)
-    late = piece_loads(order, here, missing, w_ref, lambda i, *_: rest.at[i], rest_sem)
+    late = piece_loads(
+        order, here, missing, w_ref,
+        lambda i, b, s, low, high: rest.at[i, pl.ds(0, high - low), :], rest_sem,
+    )
     ahead = piece_loads(order, steps, pieces, w_ref, held_part(next_held), sem)
-    for copy in late + ahead[:SOON]:
+    soon = max(SOON - len(late), 0)
+    for copy in late + ahead[:soon]:
         copy.start()
     if made:
         make_tables(*inputs, *made, total.shape[1])
-    whole = held.shape[1] - len(missing)
+    whole = min(s for _, s, _, _ in missing) if missing else held.shape[1]
 
     @pl.loop(0, whole)
     def _(s):
         add_products([x[...] for x in xs], lambda b, at: held[b, s, :, at], total, s, fresh)
 
-    for copy in ahead[SOON:]:
+    for copy in ahead[soon:]:
         copy.start()
     for copy in late:
         copy.wait()
-    for i, (b, s, low, _) in enumerate(missing):
-        parts = [(x[...], (lambda at, k=k: held[k, s, :, at])) for k, x in enumerate(xs) if k != b]
-        parts.append((xs[b][:, :low], lambda at: held[b, s, :low, at]))
-        parts.append((xs[b][:, low:], lambda at: rest[i, :, at]))
+    for s in range(whole, held.shape[1]):
+        gaps = {b: (i, low, high) for i, (b, k, low, high) in enumerate(missing) if k == s}
+        parts = []
+        for b, x in enumerate(xs):
+            i, low, high = gaps.get(b, (0, x.shape[1], x.shape[1]))
+            if low:
+                parts.append((x[:, :low], lambda at, b=b, low=low: held[b, s, :low, at]))
+            if low < high:
+                parts.append((x[:, low:], lambda at, i=i, n=high - low: rest[i, :n, at]))
         values, weights = zip(*parts)
         add_products(values, lambda k, at: weights[k](at), total, s, fresh)
     for copy in ahead:
@@ -364,13 +373,18 @@
         return [0] + loads(1) if step == 1 else loads(step)
 
     def left(step):
-        rows_left = (width // 2, width)
-        return [(len(blocks(step)) - 1, streams - 1, *rows_left)] if step % 2 and step < half else []
+        if step >= half:
+            return []
+        last, halfway = len(blocks(step)) - 1, (width // 2, width)
+        if step == 1:
+            return [(last, streams - 1, *halfway)]
+        return [(last, streams - 1, 0, width)] + [(0, streams - 1, *halfway)] * (step == half - 1)
 
     def pieces(step):
         lacking = {(b, s): low for b, s, low, _ in left(step)}
         every = [(b, s) for s in range(streams) for b in range(len(blocks(step)))]
-        return [(b, s, 0, lacking.get((b, s), width)) for b, s in every]
+        found = [(b, s, 0, lacking.get((b, s), width)) for b, s in every]
+        return [piece for piece in found if piece[3]]
 
     weights = pl.pallas_call(
         functools.partial(load_kernel, order, blocks(1), pieces(1)),
@@ -404,8 +418,8 @@
             in_specs=[VMEM] * (len(xs) + 1) + [HBM] + [VMEM] * len(extra),
             out_specs=[VMEM] * (2 + len(made)),
             scratch_shapes=[
-                pltpu.VMEM((1, width // 2, chans), jnp.bfloat16),
-                pltpu.SemaphoreType.DMA((1,)),
+                pltpu.VMEM((2, width, chans), jnp.bfloat16),
+                pltpu.SemaphoreType.DMA((2,)),
                 pltpu.SemaphoreType.DMA((len(pieces(step + 1)),)),
             ],
             input_output_aliases={} if first else {len(xs) + 2: 0},

time: 40.1 us -> 40 us (level)
    ppermute x1, waiting for transfers between devices: 0.65 us -> 0.01 us  [on_device(): aft = lax.ppermute(aft[:, width // 2:], 'tp', back)]
  transfers between devices with their start and end apart: 10 -> 10, of which waited for: 6 -> 5; matrix products, arithmetic and copies ran while one was open for 0% -> 0% of each run, Pallas kernels for 54% -> 54%
where the time goes in v12:
time: 40 us; the launch traced here: 39.8 us
  Pallas kernels  24.8 us (62%)
  starting transfers between devices  10.9 us (27%)
  waiting for transfers between devices  3.94 us (10%)
    pallas_call x3, Pallas kernels, on_device(): pl.pallas_call(functools.partial(middle_kernel, order, blocks(step), left...  13.2 us
    ppermute x3, starting transfers between devices, on_device(): fore = lax.ppermute(fore, 'tp', ahead)  6.41 us
    pallas_call x1, Pallas kernels, on_device(): pl.pallas_call(functools.partial(load_kernel, order, blocks(1), pieces(1)...  6.22 us
    pallas_call x1, Pallas kernels, on_device(): pl.pallas_call(last_kernel, out_shape=[sums, wide, f32(modes + EDGE, grou...  1.76 us
    ppermute x1, starting transfers between devices, on_device(): fore = lax.ppermute(fore[:, :width // 2], 'tp', ahead)  1.68 us
    ppermute x1, starting transfers between devices, on_device(): lax.ppermute(chip, 'ctx', [(j, (j + d) % ctx) for j in range(ctx)])  1.66 us
    pallas_call x1, Pallas kernels, on_device(): pl.pallas_call(local_kernel, out_shape=[f32(rows, chans), f32(rows, chans...  1.62 us
    ppermute x1, waiting for transfers between devices, on_device(): lax.ppermute(chip, 'ctx', [(j, (j + d) % ctx) for j in range(ctx)])  1.46 us
  transfers between devices with their start and end apart: 10, of which 5 were waited for; matrix products, arithmetic and copies ran while one was open for 0% of the time, Pallas kernels for 54%

profile of v12, /device:TPU:0, one launch (start us, length us, event | category | flops | bytes accessed | tf_op | source)
XLA Modules:
  0.0 39.8 jit_solution(509557745087877392)
XLA Ops:
  0.0 3.0 %collective-permute-start.1 = (bf16[128,1024]{1,0:T(8,128)(2,1)}, bf16[128,1024]{1,0:T(8,128)(2,1)S(1)}, u32[]{:S(2)}, u32[]{:S(2)}) collective-permute-start(bf16[128,1024]{1,0:T(8,128)(2,1)} %refs_0_.1), channel_id=1, source_target_pairs={{0,1},{1,3},{3,5},{5,7},{7,6},{6,4},{4,2},{2,0},{8,9},{9,11},{11,1... | collective-permute-start | bytes 786440 | tf_op jit(solution)/shard_map/ppermute | solution.py:401
  3.0 0.1 collective-permute-start
  3.0 6.2 %load_first.1.refs_3_ = bf16[3,3,1024,1024]{3,2,1,0:T(8,128)(2,1)S(1)} custom-call(bf16[3,8192,1024]{2,1,0:T(8,128)(2,1)} %bitcast.1), custom_call_target="tpu_custom_call" | custom-call | bytes 16777216 | tf_op jit(solution)/shard_map/load_first/pallas_call | solution.py:389
  9.3 0.3 collective-permute-done.1.refs_1_
  9.5 1.8 %collective-permute-start.3 = (bf16[128,1024]{1,0:T(8,128)(2,1)S(1)}, bf16[128,1024]{1,0:T(8,128)(2,1)S(1)}, u32[]{:S(2)}, u32[]{:S(2)}) collective-permute-start(bf16[128,1024]{1,0:T(8,128)(2,1)S(1)} %collective-permute-done.1.refs_1_), channel_id=1, source_target_pairs={{0,1},{1,3},{3,5},{5,7},{7,6},{6,4},{4,2},{2,0},{8,9},{9,11},{11,1... | collective-permute-start | bytes 786440 | tf_op jit(solution)/shard_map/ppermute | solution.py:401
  11.3 0.0 collective-permute-done.refs_2_
  11.3 0.3 collective-permute-start.2
  11.6 0.0 copy-done
  11.6 0.0 copy-done.1
  11.6 0.0 copy-done.2
  11.6 4.7 %project_blocks.3 = (f32[3,128,1024]{2,1,0:T(8,128)S(1)}, bf16[2,3,1024,1024]{3,2,1,0:T(8,128)(2,1)S(1)}, f32[3,3,8,128]{3,2,1,0:T(8,128)S(1)}, f32[5,16,8,128]{...) custom-call(bf16[128,1024]{1,0:T(8,128)(2,1)S(1)} %copy-done.1, ...), custom_call_target="tpu_custom_call" | custom-call | bytes 16777216 | tf_op jit(solution)/shard_map/project_blocks/pallas_call | solution.py:412
  16.3 0.8 %collective-permute-done.3.refs_0_ = bf16[128,1024]{1,0:T(8,128)(2,1)S(1)} collective-permute-done((bf16[128,1024]{1,0:T(8,128)(2,1)S(1)}, bf16[128,1024]{1,0:T(8,128)(2,1)S(1)}, u32[]{:S(2)}, u32[]{:S(2)}) %collective-permute-start.3) | collective-permute-done | bytes 262176 | tf_op jit(solution)/shard_map/ppermute | solution.py:401
  17.1 1.7 %collective-permute-start.5 = (bf16[128,1024]{1,0:T(8,128)(2,1)S(1)}, bf16[128,1024]{1,0:T(8,128)(2,1)S(1)}, u32[]{:S(2)}, u32[]{:S(2)}) collective-permute-start(bf16[128,1024]{1,0:T(8,128)(2,1)S(1)} %collective-permute-done.3.refs_0_), channel_id=1, source_target_pairs={{0,1},{1,3},{3,5},{5,7},{7,6},{6,4},{4,2},{2,0},{8,9},{9,11},{11,1... | collective-permute-start | bytes 786440 | tf_op jit(solution)/shard_map/ppermute | solution.py:401
  18.8 0.0 collective-permute-done.2.refs_1_
  18.8 0.3 collective-permute-start.4
  19.1 4.5 %project_blocks.4 = (f32[3,128,1024]{2,1,0:T(8,128)S(1)}, bf16[2,3,1024,1024]{3,2,1,0:T(8,128)(2,1)S(1)}) custom-call(bf16[128,1024]{1,0:T(8,128)(2,1)S(1)} %collective-permute-done.3.refs_0_, bf16[128,1024]{1,0:T(8,128)(2,1)S(1)} %collective-permute-done.2.refs_1_, ...), custom_call_target="tpu_custom_call", output_to_operand_aliasing={{0}: (4, {})} | custom-call | bytes 16777216 | tf_op jit(solution)/shard_map/project_blocks/pallas_call | solution.py:412
  23.7 0.1 collective-permute-done.5.refs_0_
  23.7 1.7 %collective-permute-start.7 = (bf16[128,512]{1,0:T(8,128)(2,1)S(1)}, bf16[128,512]{1,0:T(8,128)(2,1)S(1)}, u32[]{:S(2)}, u32[]{:S(2)}) collective-permute-start(bf16[128,512]{1,0:T(8,128)(2,1)S(1)} %slice.7), channel_id=1, source_target_pairs={{0,1},{1,3},{3,5},{5,7},{7,6},{6,4},{4,2},{2,0},{8,9},{9,11},{11,1... | collective-permute-start | bytes 393224 | tf_op jit(solution)/shard_map/ppermute | solution.py:432
  25.4 0.0 collective-permute-done.4.refs_1_
  25.4 0.5 %collective-permute-start.6 = (bf16[128,512]{1,0:T(8,128)(2,1)S(1)}, bf16[128,512]{1,0:T(8,128)(2,1)S(1)}, u32[]{:S(2)}, u32[]{:S(2)}) collective-permute-start(bf16[128,512]{1,0:T(8,128)(2,1)S(1)} %slice.6), channel_id=1, source_target_pairs={{1,0},{3,1},{5,3},{7,5},{6,7},{4,6},{2,4},{0,2},{9,8},{11,9},{13,1... | collective-permute-start | bytes 393224 | tf_op jit(solution)/shard_map/ppermute | solution.py:433
  25.9 4.0 %project_blocks.5 = (f32[3,128,1024]{2,1,0:T(8,128)S(1)}, bf16[1,3,1024,1024]{3,2,1,0:T(8,128)(2,1)S(1)}) custom-call(bf16[128,1024]{1,0:T(8,128)(2,1)S(1)} %collective-permute-done.5.refs_0_, bf16[128,1024]{1,0:T(8,128)(2,1)S(1)} %collective-permute-done.4.refs_1_, ...), custom_call_target="tpu_custom_call", output_to_operand_aliasing={{0}: (4, {})} | custom-call | bytes 16777216 | tf_op jit(solution)/shard_map/project_blocks/pallas_call | solution.py:412
  29.9 0.0 collective-permute-done.7.x_ref
  29.9 0.6 %project_half.1._ = f32[3,128,1024]{2,1,0:T(8,128)S(1)} custom-call(bf16[128,512]{1,0:T(8,128)(2,1)S(1)} %collective-permute-done.7.x_ref, bf16[1,3,1024,1024]{3,2,1,0:T(8,128)(2,1)S(1)} %get-tuple-element.57.held, f32[3,128,1024]{2,1,0:T(8,128)S(1)} %get-tuple-element.59._), custom_call_target="tpu_custom_call", output_to_operand_aliasing={{}: (2, {})} | custom-call | bytes 16777216 | tf_op jit(solution)/shard_map/project_half/pallas_call | solution.py:434
  30.5 0.0 collective-permute-done.6.x_ref
  30.5 1.8 %project_last.1 = (f32[3,128,1024]{2,1,0:T(8,128)S(1)}, f32[128,8,128]{2,1,0:T(8,128)S(1)}, f32[26,8,128]{2,1,0:T(8,128)S(1)}) custom-call(bf16[128,512]{1,0:T(8,128)(2,1)S(1)} %collective-permute-done.6.x_ref, bf16[1,3,1024,1024]{3,2,1,0:T(8,128)(2,1)S(1)} %get-tuple-element.57.held, f32[3,3,1024]{2,1,0:T(4,128)S(1)} %copy-done, ...), custom_call_target="tpu_custom_call", output_to_operand_aliasing={{0}: (4, {})} | custom-call | bytes 16777216 | tf_op jit(solution)/shard_map/project_last/pallas_call | solution.py:444
  32.3 0.1 collective-permute-start.8
  32.4 1.3 %collective-permute-done.8.partner.refs_2_ = f32[26,8,128]{2,1,0:T(8,128)S(1)} collective-permute-done((f32[26,8,128]{2,1,0:T(8,128)S(1)}, f32[26,8,128]{2,1,0:T(8,128)S(1)}, u32[]{:S(2)}, u32[]{:S(2)}) %collective-permute-start.8) | collective-permute-done | bytes 106528 | tf_op jit(solution)/shard_map/ppermute | solution.py:459
  33.7 0.1 chip_state.1
  33.7 1.7 %collective-permute-start.9 = (f32[22,8,128]{2,1,0:T(8,128)S(1)}, f32[22,8,128]{2,1,0:T(8,128)S(1)}, u32[]{:S(2)}, u32[]{:S(2)}) collective-permute-start(f32[22,8,128]{2,1,0:T(8,128)S(1)} %chip_state.1), channel_id=1, source_target_pairs={{0,16},{8,24},{16,0},{24,8},{1,17},{9,25},{17,1},{25,9},{2,18},{10... | collective-permute-start | bytes 270344 | tf_op jit(solution)/shard_map/ppermute | solution.py:470
  35.4 1.6 %local_response.1 = (f32[128,1024]{1,0:T(8,128)S(1)}, f32[128,1024]{1,0:T(8,128)S(1)}, f32[2,8,128]{2,1,0:T(8,128)S(1)}) custom-call(f32[3,128,1024]{2,1,0:T(8,128)S(1)} %get-tuple-element.62.total, f32[128,8,128]{2,1,0:T(8,128)S(1)} %get-tuple-element.63.source, f32[3,3,1024]{2,1,0:T(4,128)S(1)} %copy-done, ...), custom_call_target="tpu_custom_call" | custom-call | bytes 16777216 | tf_op jit(solution)/shard_map/local_response/pallas_call | solution.py:473
  37.0 1.5 %collective-permute-done.9.refs_0_ = f32[22,8,128]{2,1,0:T(8,128)S(1)} collective-permute-done((f32[22,8,128]{2,1,0:T(8,128)S(1)}, f32[22,8,128]{2,1,0:T(8,128)S(1)}, u32[]{:S(2)}, u32[]{:S(2)}) %collective-permute-start.9) | collective-permute-done | bytes 90144 | tf_op jit(solution)/shard_map/ppermute | solution.py:470
  38.5 1.3 %carried_response.1 = bf16[128,1024]{1,0:T(8,128)(2,1)} custom-call(f32[22,8,128]{2,1,0:T(8,128)S(1)} %collective-permute-done.9.refs_0_, f32[26,8,128]{2,1,0:T(8,128)S(1)} %get-tuple-element.60.local.refs_1_, f32[26,8,128]{2,1,0:T(8,128)S(1)} %collective-permute-done.8.partner.refs_2_, f32[128,1024]{1,0:T(8,128)S(1)} %get-tuple-element.64.refs_3_, ...), custom_call_target="tpu_custom_call" | custom-call | tf_op jit(solution)/shard_map/carried_response/pallas_call | solution.py:486
  (7 shorter events, 0.0 us)
Async XLA Ops:
  0.0 9.5 %collective-permute-start.1 = (bf16[128,1024]{1,0:T(8,128)(2,1)}, bf16[128,1024]{1,0:T(8,128)(2,1)S(1)}, u32[]{:S(2)}, u32[]{:S(2)}) collective-permute-start(bf16[128,1024]{1,0:T(8,128)(2,1)} %refs_0_.1), channel_id=1, source_target_pairs={{0,1},{1,3},{3,5},{5,7},{7,6},{6,4},{4,2},{2,0},{8,9},{9,11},{11,1... | collective-permute-start | bytes 786440 | tf_op jit(solution)/shard_map/ppermute | solution.py:401
  3.0 8.3 %collective-permute-start = (bf16[128,1024]{1,0:T(8,128)(2,1)}, bf16[128,1024]{1,0:T(8,128)(2,1)S(1)}, u32[]{:S(2)}, u32[]{:S(2)}) collective-permute-start(bf16[128,1024]{1,0:T(8,128)(2,1)} %refs_0_.1), channel_id=1, source_target_pairs={{1,0},{3,1},{5,3},{7,5},{6,7},{4,6},{2,4},{0,2},{9,8},{11,9},{13,1... | collective-permute-start | bytes 786440 | tf_op jit(solution)/shard_map/ppermute | solution.py:402
  3.0 8.5 %copy-start = (f32[3,3,1024]{2,1,0:T(4,128)S(1)}, f32[3,3,1024]{2,1,0:T(4,128)}, u32[]{:S(2)}) copy-start(f32[3,3,1024]{2,1,0:T(4,128)} %taps.3) | copy-start | bytes 110596
  3.0 8.5 %copy-start.1 = (bf16[128,1024]{1,0:T(8,128)(2,1)S(1)}, bf16[128,1024]{1,0:T(8,128)(2,1)}, u32[]{:S(2)}) copy-start(bf16[128,1024]{1,0:T(8,128)(2,1)} %refs_0_.1) | copy-start | bytes 786436
  3.0 8.5 %copy-start.2 = (f32[16,1024]{1,0:T(8,128)S(1)}, f32[16,1024]{1,0:T(8,128)}, u32[]{:S(2)}) copy-start(f32[16,1024]{1,0:T(8,128)} %refs_6_.1) | copy-start | bytes 196612
  3.0 8.5 %copy-start.3 = (f32[16,1024]{1,0:T(8,128)S(1)}, f32[16,1024]{1,0:T(8,128)}, u32[]{:S(2)}) copy-start(f32[16,1024]{1,0:T(8,128)} %refs_7_.1) | copy-start | bytes 196612
  9.5 7.6 %collective-permute-start.3 = (bf16[128,1024]{1,0:T(8,128)(2,1)S(1)}, bf16[128,1024]{1,0:T(8,128)(2,1)S(1)}, u32[]{:S(2)}, u32[]{:S(2)}) collective-permute-start(bf16[128,1024]{1,0:T(8,128)(2,1)S(1)} %collective-permute-done.1.refs_1_), channel_id=1, source_target_pairs={{0,1},{1,3},{3,5},{5,7},{7,6},{6,4},{4,2},{2,0},{8,9},{9,11},{11,1... | collective-permute-start | bytes 786440 | tf_op jit(solution)/shard_map/ppermute | solution.py:401
  11.3 7.5 %collective-permute-start.2 = (bf16[128,1024]{1,0:T(8,128)(2,1)S(1)}, bf16[128,1024]{1,0:T(8,128)(2,1)S(1)}, u32[]{:S(2)}, u32[]{:S(2)}) collective-permute-start(bf16[128,1024]{1,0:T(8,128)(2,1)S(1)} %collective-permute-done.refs_2_), channel_id=1, source_target_pairs={{1,0},{3,1},{5,3},{7,5},{6,7},{4,6},{2,4},{0,2},{9,8},{11,9},{13,1... | collective-permute-start | bytes 786440 | tf_op jit(solution)/shard_map/ppermute | solution.py:402
  17.1 6.6 %collective-permute-start.5 = (bf16[128,1024]{1,0:T(8,128)(2,1)S(1)}, bf16[128,1024]{1,0:T(8,128)(2,1)S(1)}, u32[]{:S(2)}, u32[]{:S(2)}) collective-permute-start(bf16[128,1024]{1,0:T(8,128)(2,1)S(1)} %collective-permute-done.3.refs_0_), channel_id=1, source_target_pairs={{0,1},{1,3},{3,5},{5,7},{7,6},{6,4},{4,2},{2,0},{8,9},{9,11},{11,1... | collective-permute-start | bytes 786440 | tf_op jit(solution)/shard_map/ppermute | solution.py:401
  18.8 6.6 %collective-permute-start.4 = (bf16[128,1024]{1,0:T(8,128)(2,1)S(1)}, bf16[128,1024]{1,0:T(8,128)(2,1)S(1)}, u32[]{:S(2)}, u32[]{:S(2)}) collective-permute-start(bf16[128,1024]{1,0:T(8,128)(2,1)S(1)} %collective-permute-done.2.refs_1_), channel_id=1, source_target_pairs={{1,0},{3,1},{5,3},{7,5},{6,7},{4,6},{2,4},{0,2},{9,8},{11,9},{13,1... | collective-permute-start | bytes 786440 | tf_op jit(solution)/shard_map/ppermute | solution.py:402
  23.7 6.2 %collective-permute-start.7 = (bf16[128,512]{1,0:T(8,128)(2,1)S(1)}, bf16[128,512]{1,0:T(8,128)(2,1)S(1)}, u32[]{:S(2)}, u32[]{:S(2)}) collective-permute-start(bf16[128,512]{1,0:T(8,128)(2,1)S(1)} %slice.7), channel_id=1, source_target_pairs={{0,1},{1,3},{3,5},{5,7},{7,6},{6,4},{4,2},{2,0},{8,9},{9,11},{11,1... | collective-permute-start | bytes 393224 | tf_op jit(solution)/shard_map/ppermute | solution.py:432
  25.4 5.1 %collective-permute-start.6 = (bf16[128,512]{1,0:T(8,128)(2,1)S(1)}, bf16[128,512]{1,0:T(8,128)(2,1)S(1)}, u32[]{:S(2)}, u32[]{:S(2)}) collective-permute-start(bf16[128,512]{1,0:T(8,128)(2,1)S(1)} %slice.6), channel_id=1, source_target_pairs={{1,0},{3,1},{5,3},{7,5},{6,7},{4,6},{2,4},{0,2},{9,8},{11,9},{13,1... | collective-permute-start | bytes 393224 | tf_op jit(solution)/shard_map/ppermute | solution.py:433
  32.3 1.4 %collective-permute-start.8 = (f32[26,8,128]{2,1,0:T(8,128)S(1)}, f32[26,8,128]{2,1,0:T(8,128)S(1)}, u32[]{:S(2)}, u32[]{:S(2)}) collective-permute-start(f32[26,8,128]{2,1,0:T(8,128)S(1)} %get-tuple-element.60.local.refs_1_), channel_id=1, source_target_pairs={{0,8},{8,0},{16,24},{24,16},{1,9},{9,1},{17,25},{25,17},{2,10},{10... | collective-permute-start | bytes 319496 | tf_op jit(solution)/shard_map/ppermute | solution.py:459
  33.7 4.7 %collective-permute-start.9 = (f32[22,8,128]{2,1,0:T(8,128)S(1)}, f32[22,8,128]{2,1,0:T(8,128)S(1)}, u32[]{:S(2)}, u32[]{:S(2)}) collective-permute-start(f32[22,8,128]{2,1,0:T(8,128)S(1)} %chip_state.1), channel_id=1, source_target_pairs={{0,16},{8,24},{16,0},{24,8},{1,17},{9,25},{17,1},{25,9},{2,18},{10... | collective-permute-start | bytes 270344 | tf_op jit(solution)/shard_map/ppermute | solution.py:470

commit v13 on v12

--- a/solution.py
+++ b/solution.py
@@ -376,9 +376,7 @@
         if step >= half:
             return []
         last, halfway = len(blocks(step)) - 1, (width // 2, width)
-        if step == 1:
-            return [(last, streams - 1, *halfway)]
-        return [(last, streams - 1, 0, width)] + [(0, streams - 1, *halfway)] * (step == half - 1)
+        return [(last, streams - 1, *halfway) if step < half - 1 else (last, streams - 1, 0, width)]
 
     def pieces(step):
         lacking = {(b, s): low for b, s, low, _ in left(step)}

time: 40 us -> 40 us (level)
  no operation moved by 1% of the time
where the time goes in v13:
time: 40 us; the launch traced here: 39.8 us
  Pallas kernels  24.7 us (62%)
  starting transfers between devices  10.8 us (27%)
  waiting for transfers between devices  4.08 us (10%)
    pallas_call x3, Pallas kernels, on_device(): pl.pallas_call(functools.partial(middle_kernel, order, blocks(step), left...  13.2 us
    ppermute x3, starting transfers between devices, on_device(): fore = lax.ppermute(fore, 'tp', ahead)  6.41 us
    pallas_call x1, Pallas kernels, on_device(): pl.pallas_call(functools.partial(load_kernel, order, blocks(1), pieces(1)...  6.22 us
    pallas_call x1, Pallas kernels, on_device(): pl.pallas_call(last_kernel, out_shape=[sums, wide, f32(modes + EDGE, grou...  1.76 us
    ppermute x1, starting transfers between devices, on_device(): fore = lax.ppermute(fore[:, :width // 2], 'tp', ahead)  1.73 us
    pallas_call x1, Pallas kernels, on_device(): pl.pallas_call(local_kernel, out_shape=[f32(rows, chans), f32(rows, chans...  1.62 us
    ppermute x1, starting transfers between devices, on_device(): lax.ppermute(chip, 'ctx', [(j, (j + d) % ctx) for j in range(ctx)])  1.56 us
    ppermute x1, waiting for transfers between devices, on_device(): lax.ppermute(chip, 'ctx', [(j, (j + d) % ctx) for j in range(ctx)])  1.56 us
  transfers between devices with their start and end apart: 10, of which 5 were waited for; matrix products, arithmetic and copies ran while one was open for 0% of the time, Pallas kernels for 54%

profile of v13, /device:TPU:0, one launch (start us, length us, event | category | flops | bytes accessed | tf_op | source)
XLA Modules:
  0.0 39.8 jit_solution(17253602798366854486)
XLA Ops:
  0.0 3.0 %collective-permute-start.1 = (bf16[128,1024]{1,0:T(8,128)(2,1)}, bf16[128,1024]{1,0:T(8,128)(2,1)S(1)}, u32[]{:S(2)}, u32[]{:S(2)}) collective-permute-start(bf16[128,1024]{1,0:T(8,128)(2,1)} %refs_0_.1), channel_id=1, source_target_pairs={{0,1},{1,3},{3,5},{5,7},{7,6},{6,4},{4,2},{2,0},{8,9},{9,11},{11,1... | collective-permute-start | bytes 786440 | tf_op jit(solution)/shard_map/ppermute | solution.py:399
  3.0 0.1 collective-permute-start
  3.0 6.2 %load_first.1.refs_3_ = bf16[3,3,1024,1024]{3,2,1,0:T(8,128)(2,1)S(1)} custom-call(bf16[3,8192,1024]{2,1,0:T(8,128)(2,1)} %bitcast.1), custom_call_target="tpu_custom_call" | custom-call | bytes 16777216 | tf_op jit(solution)/shard_map/load_first/pallas_call | solution.py:387
  9.3 0.3 collective-permute-done.1.refs_1_
  9.5 1.8 %collective-permute-start.3 = (bf16[128,1024]{1,0:T(8,128)(2,1)S(1)}, bf16[128,1024]{1,0:T(8,128)(2,1)S(1)}, u32[]{:S(2)}, u32[]{:S(2)}) collective-permute-start(bf16[128,1024]{1,0:T(8,128)(2,1)S(1)} %collective-permute-done.1.refs_1_), channel_id=1, source_target_pairs={{0,1},{1,3},{3,5},{5,7},{7,6},{6,4},{4,2},{2,0},{8,9},{9,11},{11,1... | collective-permute-start | bytes 786440 | tf_op jit(solution)/shard_map/ppermute | solution.py:399
  11.3 0.0 collective-permute-done.refs_2_
  11.3 0.3 collective-permute-start.2
  11.6 0.0 copy-done
  11.6 0.0 copy-done.1
  11.6 0.0 copy-done.2
  11.6 4.9 %project_blocks.3 = (f32[3,128,1024]{2,1,0:T(8,128)S(1)}, bf16[2,3,1024,1024]{3,2,1,0:T(8,128)(2,1)S(1)}, f32[3,3,8,128]{3,2,1,0:T(8,128)S(1)}, f32[5,16,8,128]{...) custom-call(bf16[128,1024]{1,0:T(8,128)(2,1)S(1)} %copy-done.1, ...), custom_call_target="tpu_custom_call" | custom-call | bytes 16777216 | tf_op jit(solution)/shard_map/project_blocks/pallas_call | solution.py:410
  16.5 0.6 %collective-permute-done.3.refs_0_ = bf16[128,1024]{1,0:T(8,128)(2,1)S(1)} collective-permute-done((bf16[128,1024]{1,0:T(8,128)(2,1)S(1)}, bf16[128,1024]{1,0:T(8,128)(2,1)S(1)}, u32[]{:S(2)}, u32[]{:S(2)}) %collective-permute-start.3) | collective-permute-done | bytes 262176 | tf_op jit(solution)/shard_map/ppermute | solution.py:399
  17.1 1.7 %collective-permute-start.5 = (bf16[128,1024]{1,0:T(8,128)(2,1)S(1)}, bf16[128,1024]{1,0:T(8,128)(2,1)S(1)}, u32[]{:S(2)}, u32[]{:S(2)}) collective-permute-start(bf16[128,1024]{1,0:T(8,128)(2,1)S(1)} %collective-permute-done.3.refs_0_), channel_id=1, source_target_pairs={{0,1},{1,3},{3,5},{5,7},{7,6},{6,4},{4,2},{2,0},{8,9},{9,11},{11,1... | collective-permute-start | bytes 786440 | tf_op jit(solution)/shard_map/ppermute | solution.py:399
  18.8 0.0 collective-permute-done.2.refs_1_
  18.8 0.3 collective-permute-start.4
  19.1 4.6 %project_blocks.4 = (f32[3,128,1024]{2,1,0:T(8,128)S(1)}, bf16[2,3,1024,1024]{3,2,1,0:T(8,128)(2,1)S(1)}) custom-call(bf16[128,1024]{1,0:T(8,128)(2,1)S(1)} %collective-permute-done.3.refs_0_, bf16[128,1024]{1,0:T(8,128)(2,1)S(1)} %collective-permute-done.2.refs_1_, ...), custom_call_target="tpu_custom_call", output_to_operand_aliasing={{0}: (4, {})} | custom-call | bytes 16777216 | tf_op jit(solution)/shard_map/project_blocks/pallas_call | solution.py:410
  23.7 0.0 collective-permute-done.5.refs_0_
  23.8 1.7 %collective-permute-start.7 = (bf16[128,512]{1,0:T(8,128)(2,1)S(1)}, bf16[128,512]{1,0:T(8,128)(2,1)S(1)}, u32[]{:S(2)}, u32[]{:S(2)}) collective-permute-start(bf16[128,512]{1,0:T(8,128)(2,1)S(1)} %slice.7), channel_id=1, source_target_pairs={{0,1},{1,3},{3,5},{5,7},{7,6},{6,4},{4,2},{2,0},{8,9},{9,11},{11,1... | collective-permute-start | bytes 393224 | tf_op jit(solution)/shard_map/ppermute | solution.py:430
  25.5 0.0 collective-permute-done.4.refs_1_
  25.5 0.4 collective-permute-start.6
  25.9 3.6 %project_blocks.5 = (f32[3,128,1024]{2,1,0:T(8,128)S(1)}, bf16[1,3,1024,1024]{3,2,1,0:T(8,128)(2,1)S(1)}) custom-call(bf16[128,1024]{1,0:T(8,128)(2,1)S(1)} %collective-permute-done.5.refs_0_, bf16[128,1024]{1,0:T(8,128)(2,1)S(1)} %collective-permute-done.4.refs_1_, ...), custom_call_target="tpu_custom_call", output_to_operand_aliasing={{0}: (4, {})} | custom-call | bytes 16777216 | tf_op jit(solution)/shard_map/project_blocks/pallas_call | solution.py:410
  29.6 0.0 collective-permute-done.7.x_ref
  29.6 0.6 %project_half.1._ = f32[3,128,1024]{2,1,0:T(8,128)S(1)} custom-call(bf16[128,512]{1,0:T(8,128)(2,1)S(1)} %collective-permute-done.7.x_ref, bf16[1,3,1024,1024]{3,2,1,0:T(8,128)(2,1)S(1)} %get-tuple-element.57.held, f32[3,128,1024]{2,1,0:T(8,128)S(1)} %get-tuple-element.59._), custom_call_target="tpu_custom_call", output_to_operand_aliasing={{}: (2, {})} | custom-call | bytes 16777216 | tf_op jit(solution)/shard_map/project_half/pallas_call | solution.py:432
  30.2 0.3 collective-permute-done.6.x_ref
  30.5 1.8 %project_last.1 = (f32[3,128,1024]{2,1,0:T(8,128)S(1)}, f32[128,8,128]{2,1,0:T(8,128)S(1)}, f32[26,8,128]{2,1,0:T(8,128)S(1)}) custom-call(bf16[128,512]{1,0:T(8,128)(2,1)S(1)} %collective-permute-done.6.x_ref, bf16[1,3,1024,1024]{3,2,1,0:T(8,128)(2,1)S(1)} %get-tuple-element.57.held, f32[3,3,1024]{2,1,0:T(4,128)S(1)} %copy-done, ...), custom_call_target="tpu_custom_call", output_to_operand_aliasing={{0}: (4, {})} | custom-call | bytes 16777216 | tf_op jit(solution)/shard_map/project_last/pallas_call | solution.py:442
  32.3 0.1 collective-permute-start.8
  32.4 1.3 %collective-permute-done.8.partner.refs_2_ = f32[26,8,128]{2,1,0:T(8,128)S(1)} collective-permute-done((f32[26,8,128]{2,1,0:T(8,128)S(1)}, f32[26,8,128]{2,1,0:T(8,128)S(1)}, u32[]{:S(2)}, u32[]{:S(2)}) %collective-permute-start.8) | collective-permute-done | bytes 106528 | tf_op jit(solution)/shard_map/ppermute | solution.py:457
  33.7 0.1 chip_state.1
  33.7 1.6 %collective-permute-start.9 = (f32[22,8,128]{2,1,0:T(8,128)S(1)}, f32[22,8,128]{2,1,0:T(8,128)S(1)}, u32[]{:S(2)}, u32[]{:S(2)}) collective-permute-start(f32[22,8,128]{2,1,0:T(8,128)S(1)} %chip_state.1), channel_id=1, source_target_pairs={{0,16},{8,24},{16,0},{24,8},{1,17},{9,25},{17,1},{25,9},{2,18},{10... | collective-permute-start | bytes 270344 | tf_op jit(solution)/shard_map/ppermute | solution.py:468
  35.3 1.6 %local_response.1 = (f32[128,1024]{1,0:T(8,128)S(1)}, f32[128,1024]{1,0:T(8,128)S(1)}, f32[2,8,128]{2,1,0:T(8,128)S(1)}) custom-call(f32[3,128,1024]{2,1,0:T(8,128)S(1)} %get-tuple-element.62.total, f32[128,8,128]{2,1,0:T(8,128)S(1)} %get-tuple-element.63.source, f32[3,3,1024]{2,1,0:T(4,128)S(1)} %copy-done, ...), custom_call_target="tpu_custom_call" | custom-call | bytes 16777216 | tf_op jit(solution)/shard_map/local_response/pallas_call | solution.py:471
  36.9 1.6 %collective-permute-done.9.refs_0_ = f32[22,8,128]{2,1,0:T(8,128)S(1)} collective-permute-done((f32[22,8,128]{2,1,0:T(8,128)S(1)}, f32[22,8,128]{2,1,0:T(8,128)S(1)}, u32[]{:S(2)}, u32[]{:S(2)}) %collective-permute-start.9) | collective-permute-done | bytes 90144 | tf_op jit(solution)/shard_map/ppermute | solution.py:468
  38.5 1.3 %carried_response.1 = bf16[128,1024]{1,0:T(8,128)(2,1)} custom-call(f32[22,8,128]{2,1,0:T(8,128)S(1)} %collective-permute-done.9.refs_0_, f32[26,8,128]{2,1,0:T(8,128)S(1)} %get-tuple-element.60.local.refs_1_, f32[26,8,128]{2,1,0:T(8,128)S(1)} %collective-permute-done.8.partner.refs_2_, f32[128,1024]{1,0:T(8,128)S(1)} %get-tuple-element.64.refs_3_, ...), custom_call_target="tpu_custom_call" | custom-call | tf_op jit(solution)/shard_map/carried_response/pallas_call | solution.py:484
  (7 shorter events, 0.0 us)
Async XLA Ops:
  0.0 9.5 %collective-permute-start.1 = (bf16[128,1024]{1,0:T(8,128)(2,1)}, bf16[128,1024]{1,0:T(8,128)(2,1)S(1)}, u32[]{:S(2)}, u32[]{:S(2)}) collective-permute-start(bf16[128,1024]{1,0:T(8,128)(2,1)} %refs_0_.1), channel_id=1, source_target_pairs={{0,1},{1,3},{3,5},{5,7},{7,6},{6,4},{4,2},{2,0},{8,9},{9,11},{11,1... | collective-permute-start | bytes 786440 | tf_op jit(solution)/shard_map/ppermute | solution.py:399
  3.0 8.3 %collective-permute-start = (bf16[128,1024]{1,0:T(8,128)(2,1)}, bf16[128,1024]{1,0:T(8,128)(2,1)S(1)}, u32[]{:S(2)}, u32[]{:S(2)}) collective-permute-start(bf16[128,1024]{1,0:T(8,128)(2,1)} %refs_0_.1), channel_id=1, source_target_pairs={{1,0},{3,1},{5,3},{7,5},{6,7},{4,6},{2,4},{0,2},{9,8},{11,9},{13,1... | collective-permute-start | bytes 786440 | tf_op jit(solution)/shard_map/ppermute | solution.py:400
  3.0 8.5 %copy-start = (f32[3,3,1024]{2,1,0:T(4,128)S(1)}, f32[3,3,1024]{2,1,0:T(4,128)}, u32[]{:S(2)}) copy-start(f32[3,3,1024]{2,1,0:T(4,128)} %taps.3) | copy-start | bytes 110596
  3.0 8.5 %copy-start.1 = (bf16[128,1024]{1,0:T(8,128)(2,1)S(1)}, bf16[128,1024]{1,0:T(8,128)(2,1)}, u32[]{:S(2)}) copy-start(bf16[128,1024]{1,0:T(8,128)(2,1)} %refs_0_.1) | copy-start | bytes 786436
  3.0 8.5 %copy-start.2 = (f32[16,1024]{1,0:T(8,128)S(1)}, f32[16,1024]{1,0:T(8,128)}, u32[]{:S(2)}) copy-start(f32[16,1024]{1,0:T(8,128)} %refs_6_.1) | copy-start | bytes 196612
  3.0 8.5 %copy-start.3 = (f32[16,1024]{1,0:T(8,128)S(1)}, f32[16,1024]{1,0:T(8,128)}, u32[]{:S(2)}) copy-start(f32[16,1024]{1,0:T(8,128)} %refs_7_.1) | copy-start | bytes 196612
  9.5 7.6 %collective-permute-start.3 = (bf16[128,1024]{1,0:T(8,128)(2,1)S(1)}, bf16[128,1024]{1,0:T(8,128)(2,1)S(1)}, u32[]{:S(2)}, u32[]{:S(2)}) collective-permute-start(bf16[128,1024]{1,0:T(8,128)(2,1)S(1)} %collective-permute-done.1.refs_1_), channel_id=1, source_target_pairs={{0,1},{1,3},{3,5},{5,7},{7,6},{6,4},{4,2},{2,0},{8,9},{9,11},{11,1... | collective-permute-start | bytes 786440 | tf_op jit(solution)/shard_map/ppermute | solution.py:399
  11.3 7.5 %collective-permute-start.2 = (bf16[128,1024]{1,0:T(8,128)(2,1)S(1)}, bf16[128,1024]{1,0:T(8,128)(2,1)S(1)}, u32[]{:S(2)}, u32[]{:S(2)}) collective-permute-start(bf16[128,1024]{1,0:T(8,128)(2,1)S(1)} %collective-permute-done.refs_2_), channel_id=1, source_target_pairs={{1,0},{3,1},{5,3},{7,5},{6,7},{4,6},{2,4},{0,2},{9,8},{11,9},{13,1... | collective-permute-start | bytes 786440 | tf_op jit(solution)/shard_map/ppermute | solution.py:400
  17.1 6.7 %collective-permute-start.5 = (bf16[128,1024]{1,0:T(8,128)(2,1)S(1)}, bf16[128,1024]{1,0:T(8,128)(2,1)S(1)}, u32[]{:S(2)}, u32[]{:S(2)}) collective-permute-start(bf16[128,1024]{1,0:T(8,128)(2,1)S(1)} %collective-permute-done.3.refs_0_), channel_id=1, source_target_pairs={{0,1},{1,3},{3,5},{5,7},{7,6},{6,4},{4,2},{2,0},{8,9},{9,11},{11,1... | collective-permute-start | bytes 786440 | tf_op jit(solution)/shard_map/ppermute | solution.py:399
  18.8 6.7 %collective-permute-start.4 = (bf16[128,1024]{1,0:T(8,128)(2,1)S(1)}, bf16[128,1024]{1,0:T(8,128)(2,1)S(1)}, u32[]{:S(2)}, u32[]{:S(2)}) collective-permute-start(bf16[128,1024]{1,0:T(8,128)(2,1)S(1)} %collective-permute-done.2.refs_1_), channel_id=1, source_target_pairs={{1,0},{3,1},{5,3},{7,5},{6,7},{4,6},{2,4},{0,2},{9,8},{11,9},{13,1... | collective-permute-start | bytes 786440 | tf_op jit(solution)/shard_map/ppermute | solution.py:400
  23.8 5.8 %collective-permute-start.7 = (bf16[128,512]{1,0:T(8,128)(2,1)S(1)}, bf16[128,512]{1,0:T(8,128)(2,1)S(1)}, u32[]{:S(2)}, u32[]{:S(2)}) collective-permute-start(bf16[128,512]{1,0:T(8,128)(2,1)S(1)} %slice.7), channel_id=1, source_target_pairs={{0,1},{1,3},{3,5},{5,7},{7,6},{6,4},{4,2},{2,0},{8,9},{9,11},{11,1... | collective-permute-start | bytes 393224 | tf_op jit(solution)/shard_map/ppermute | solution.py:430
  25.5 5.0 %collective-permute-start.6 = (bf16[128,512]{1,0:T(8,128)(2,1)S(1)}, bf16[128,512]{1,0:T(8,128)(2,1)S(1)}, u32[]{:S(2)}, u32[]{:S(2)}) collective-permute-start(bf16[128,512]{1,0:T(8,128)(2,1)S(1)} %slice.6), channel_id=1, source_target_pairs={{1,0},{3,1},{5,3},{7,5},{6,7},{4,6},{2,4},{0,2},{9,8},{11,9},{13,1... | collective-permute-start | bytes 393224 | tf_op jit(solution)/shard_map/ppermute | solution.py:431
  32.3 1.4 %collective-permute-start.8 = (f32[26,8,128]{2,1,0:T(8,128)S(1)}, f32[26,8,128]{2,1,0:T(8,128)S(1)}, u32[]{:S(2)}, u32[]{:S(2)}) collective-permute-start(f32[26,8,128]{2,1,0:T(8,128)S(1)} %get-tuple-element.60.local.refs_1_), channel_id=1, source_target_pairs={{0,8},{8,0},{16,24},{24,16},{1,9},{9,1},{17,25},{25,17},{2,10},{10... | collective-permute-start | bytes 319496 | tf_op jit(solution)/shard_map/ppermute | solution.py:457
  33.7 4.7 %collective-permute-start.9 = (f32[22,8,128]{2,1,0:T(8,128)S(1)}, f32[22,8,128]{2,1,0:T(8,128)S(1)}, u32[]{:S(2)}, u32[]{:S(2)}) collective-permute-start(f32[22,8,128]{2,1,0:T(8,128)S(1)} %chip_state.1), channel_id=1, source_target_pairs={{0,16},{8,24},{16,0},{24,8},{1,17},{9,25},{17,1},{25,9},{2,18},{10... | collective-permute-start | bytes 270344 | tf_op jit(solution)/shard_map/ppermute | solution.py:468

commit v14 on v13

--- a/solution.py
+++ b/solution.py
@@ -123,7 +123,7 @@
         add_products([x_ref[...]], lambda b, at: held[0, s, :depth, at], total, s, cols=WIDE)
 
 
-def make_tables(taps_in, decay, residue, taps, table, tile, tile_step, rows):
+def make_tables(taps_in, decay, residue, taps, table, tile, tile_step, fade, rows):
     rate = decay[...]
     coeffs = residue[...] * jnp.sqrt(1.0 - jnp.exp(-2.0 * rate))
     for i, power in enumerate((1, rows, rows - 1, rows - 2)):
@@ -132,6 +132,7 @@
     spread(taps, taps_in[...])
     for r in range(tile.shape[1]):
         tile[:, r, :] = coeffs * jnp.exp(-rate * (r - 1.0))
+        fade[:, r, :] = jnp.exp(-rate * (fade.shape[1] - 1.0 - r))
     tile_step[...] = jnp.exp(-rate * tile.shape[1])
 
 
@@ -154,35 +155,32 @@
     return lags[0] * value + lags[1] * one + lags[2] * two
 
 
-def last_kernel(x_ref, held, taps, table, _, total, source, out_ref, low, high):
+def last_kernel(x_ref, held, taps, tile_step, fade, _, total, source, out_ref):
     depth = x_ref.shape[1]
     for s in range(total.shape[0]):
         add_products([x_ref[...]], lambda b, at: held[0, s, depth:, at], total, s, cols=WIDE)
-    rows, groups, lanes = source.shape
-    modes = table.shape[1]
+    rows = source.shape[0]
+    modes, tall, _ = fade.shape
+    groups, lanes = out_ref.shape[1:]
+    row = lax.broadcasted_iota(jnp.int32, (tall, lanes), 0)
     for g in range(groups):
         cols = slice(g * lanes, (g + 1) * lanes)
         one, two = rounded(total[1, :, cols]), rounded(total[2, :, cols])
-        source[:, g, :] = filtered(taps, 1, one, cols) * filtered(taps, 2, two, cols)
-        for s, value in ((1, one), (2, two)):
-            low[s - 1, :, g, :] = value[:8]
-            high[s, :, g, :] = value[rows - 8 :]
-        high[0, :, g, :] = rounded(total[0, rows - 8 :, cols])
-    rate = [table[0, n] for n in range(modes)]
-
-    def step_row(t, state):
-        u = source[t]
-        return [r * s + u for r, s in zip(rate, state)]
-
-    state = [jnp.zeros((groups, lanes), jnp.float32)] * modes
-    state = over_rows(step_row, 2, rows, state)
-    for n in range(modes):
-        out_ref[n] = state[n]
-    for j in range(2):
-        for s in (1, 2):
-            out_ref[modes + (s - 1) * 2 + j] = low[s - 1, j]
-        for s in range(3):
-            out_ref[modes + 4 + s * 2 + j] = high[s, 6 + j]
+        value = filtered(taps, 1, one, cols) * filtered(taps, 2, two, cols)
+        source[:, cols] = value
+        step = [jnp.broadcast_to(tile_step[n : n + 1, cols], (tall, lanes)) for n in range(modes)]
+        first = jnp.where(row < 2, 0.0, value[:tall])
+        state = [first] * modes
+        for i in range(tall, rows, tall):
+            state = [a * b + value[i : i + tall] for a, b in zip(state, step)]
+        for n in range(modes):
+            out_ref[n, g : g + 1, :] = jnp.sum(state[n] * fade[n, :, cols], axis=0, keepdims=True)
+        query = rounded(total[0, rows - tall :, cols])
+        for s, ends in ((1, one), (2, two)):
+            out_ref[modes + s * 2 - 2 : modes + s * 2, g, :] = ends[:2]
+        for s, ends in ((0, query), (1, one), (2, two)):
+            low = modes + 4 + s * 2
+            out_ref[low : low + 2, g, :] = ends[-2:]
 
 
 def rounded(value):
@@ -195,7 +193,7 @@
     return terms[0]
 
 
-def local_kernel(total, source, taps, table, query, response, heads, work, low):
+def local_kernel(total, natural, taps, table, query, response, heads, work, low, source):
     rows, groups, lanes = source.shape
     modes = table.shape[1]
     for g in range(groups):
@@ -203,6 +201,7 @@
         value = rounded(total[0, :, cols])
         query[:, cols] = filtered(taps, 0, value, cols)
         low[:, g, :] = value[:8]
+        source[:, g, :] = natural[:, cols]
     for j in range(2):
         heads[j] = low[j]
         work[j] = jnp.zeros((groups, lanes), jnp.float32)
@@ -365,7 +364,6 @@
         return [step, -step] if step < half else [step]
 
     sums = f32(streams, rows, chans)
-    wide = f32(rows, groups, LANES)
     params = pltpu.CompilerParams(vmem_limit_bytes=12 << 20)
     cost = pl.CostEstimate(flops=0, bytes_accessed=16 << 20, transcendentals=0)
 
@@ -406,7 +404,7 @@
         made = []
         if first:
             made = [f32(lags, streams, groups, LANES), f32(5, modes, groups, LANES)]
-            made += [f32(modes, 8, chans), f32(modes, chans)]
+            made += [f32(modes, 8, chans), f32(modes, chans), f32(modes, 8, chans)]
         total, weights, *made = pl.pallas_call(
             functools.partial(
                 middle_kernel, order, blocks(step), left(step), blocks(step + 1), pieces(step + 1),
@@ -426,7 +424,7 @@
             name="project_blocks",
         )(*xs, weights, weight, *extra)
         if first:
-            taps, table, *tiles = made
+            taps, table, tile, tile_step, fade = made
     fore = lax.ppermute(fore[:, : width // 2], "tp", ahead)
     aft = lax.ppermute(aft[:, width // 2 :], "tp", back)
     total = pl.pallas_call(
@@ -441,18 +439,14 @@
     )(fore, weights, total)
     total, source, local = pl.pallas_call(
         last_kernel,
-        out_shape=[sums, wide, f32(modes + EDGE, groups, LANES)],
-        in_specs=[VMEM] * 5,
+        out_shape=[sums, f32(rows, chans), f32(modes + EDGE, groups, LANES)],
+        in_specs=[VMEM] * 6,
         out_specs=[VMEM] * 3,
-        scratch_shapes=[
-            pltpu.VMEM((streams - 1, 8, groups, LANES), jnp.float32),
-            pltpu.VMEM((streams, 8, groups, LANES), jnp.float32),
-        ],
-        input_output_aliases={4: 0},
+        input_output_aliases={5: 0},
         compiler_params=params,
         cost_estimate=cost,
         name="project_last",
-    )(aft, weights, filter_taps, table, total)
+    )(aft, weights, filter_taps, tile_step, fade, total)
 
     partner = lax.ppermute(local, "ctx", [(j, j ^ 1) for j in range(ctx)])
     lone = ctx == 4
@@ -476,6 +470,7 @@
         scratch_shapes=[
             pltpu.VMEM((rows, groups, LANES), jnp.float32),
             pltpu.VMEM((8, groups, LANES), jnp.float32),
+            pltpu.VMEM((rows, groups, LANES), jnp.float32),
         ],
         compiler_params=params,
         cost_estimate=cost,
@@ -494,7 +489,7 @@
         ],
         compiler_params=params,
         name="carried_response",
-    )(*sent, local, partner, query, response, heads, taps, table, *tiles)
+    )(*sent, local, partner, query, response, heads, taps, table, tile, tile_step)
 
 
 def solution(mesh):

time: 40 us -> 39.8 us (level)
  transfers between devices with their start and end apart: 10 -> 10, of which waited for: 5 -> 5; matrix products, arithmetic and copies ran while one was open for 0% -> 0% of each run, Pallas kernels for 54% -> 55%
where the time goes in v14:
time: 39.8 us; the launch traced here: 39.6 us
  Pallas kernels  24.8 us (62%)
  starting transfers between devices  10.8 us (27%)
  waiting for transfers between devices  3.8 us (10%)
    pallas_call x3, Pallas kernels, on_device(): pl.pallas_call(functools.partial(middle_kernel, order, blocks(step), left...  13.2 us
    ppermute x3, starting transfers between devices, on_device(): fore = lax.ppermute(fore, 'tp', ahead)  6.41 us
    pallas_call x1, Pallas kernels, on_device(): pl.pallas_call(functools.partial(load_kernel, order, blocks(1), pieces(1)...  6.22 us
    pallas_call x1, Pallas kernels, on_device(): pl.pallas_call(local_kernel, out_shape=[f32(rows, chans), f32(rows, chans...  1.9 us
    ppermute x1, starting transfers between devices, on_device(): fore = lax.ppermute(fore[:, :width // 2], 'tp', ahead)  1.74 us
    pallas_call x1, Pallas kernels, on_device(): pl.pallas_call(last_kernel, out_shape=[sums, f32(rows, chans), f32(modes...  1.57 us
    ppermute x1, starting transfers between devices, on_device(): lax.ppermute(chip, 'ctx', [(j, (j + d) % ctx) for j in range(ctx)])  1.55 us
    pallas_call x1, Pallas kernels, on_device(): pl.pallas_call(functools.partial(final_kernel, lone, len(sent)), out_shap...  1.33 us
  transfers between devices with their start and end apart: 10, of which 5 were waited for; matrix products, arithmetic and copies ran while one was open for 0% of the time, Pallas kernels for 55%

profile of v14, /device:TPU:0, one launch (start us, length us, event | category | flops | bytes accessed | tf_op | source)
XLA Modules:
  0.0 39.6 jit_solution(739831781155144981)
XLA Ops:
  0.0 3.0 %collective-permute-start.1 = (bf16[128,1024]{1,0:T(8,128)(2,1)}, bf16[128,1024]{1,0:T(8,128)(2,1)S(1)}, u32[]{:S(2)}, u32[]{:S(2)}) collective-permute-start(bf16[128,1024]{1,0:T(8,128)(2,1)} %refs_0_.1), channel_id=1, source_target_pairs={{0,1},{1,3},{3,5},{5,7},{7,6},{6,4},{4,2},{2,0},{8,9},{9,11},{11,1... | collective-permute-start | bytes 786440 | tf_op jit(solution)/shard_map/ppermute | solution.py:397
  3.0 0.1 collective-permute-start
  3.0 6.2 %load_first.1.refs_3_ = bf16[3,3,1024,1024]{3,2,1,0:T(8,128)(2,1)S(1)} custom-call(bf16[3,8192,1024]{2,1,0:T(8,128)(2,1)} %bitcast.1), custom_call_target="tpu_custom_call" | custom-call | bytes 16777216 | tf_op jit(solution)/shard_map/load_first/pallas_call | solution.py:385
  9.3 0.3 collective-permute-done.1.refs_1_
  9.5 1.8 %collective-permute-start.3 = (bf16[128,1024]{1,0:T(8,128)(2,1)S(1)}, bf16[128,1024]{1,0:T(8,128)(2,1)S(1)}, u32[]{:S(2)}, u32[]{:S(2)}) collective-permute-start(bf16[128,1024]{1,0:T(8,128)(2,1)S(1)} %collective-permute-done.1.refs_1_), channel_id=1, source_target_pairs={{0,1},{1,3},{3,5},{5,7},{7,6},{6,4},{4,2},{2,0},{8,9},{9,11},{11,1... | collective-permute-start | bytes 786440 | tf_op jit(solution)/shard_map/ppermute | solution.py:397
  11.3 0.0 collective-permute-done.refs_2_
  11.3 0.3 collective-permute-start.2
  11.6 0.0 copy-done
  11.6 0.0 copy-done.1
  11.6 0.0 copy-done.2
  11.6 0.0 copy-done.3
  11.6 4.9 %project_blocks.3 = (f32[3,128,1024]{2,1,0:T(8,128)S(1)}, bf16[2,3,1024,1024]{3,2,1,0:T(8,128)(2,1)S(1)}, f32[3,3,8,128]{3,2,1,0:T(8,128)S(1)}, f32[5,16,8,128]{...) custom-call(bf16[128,1024]{1,0:T(8,128)(2,1)S(1)} %copy-done.1, ...), custom_call_target="tpu_custom_call" | custom-call | bytes 16777216 | tf_op jit(solution)/shard_map/project_blocks/pallas_call | solution.py:408
  16.5 0.6 %collective-permute-done.3.refs_0_ = bf16[128,1024]{1,0:T(8,128)(2,1)S(1)} collective-permute-done((bf16[128,1024]{1,0:T(8,128)(2,1)S(1)}, bf16[128,1024]{1,0:T(8,128)(2,1)S(1)}, u32[]{:S(2)}, u32[]{:S(2)}) %collective-permute-start.3) | collective-permute-done | bytes 262176 | tf_op jit(solution)/shard_map/ppermute | solution.py:397
  17.1 1.7 %collective-permute-start.5 = (bf16[128,1024]{1,0:T(8,128)(2,1)S(1)}, bf16[128,1024]{1,0:T(8,128)(2,1)S(1)}, u32[]{:S(2)}, u32[]{:S(2)}) collective-permute-start(bf16[128,1024]{1,0:T(8,128)(2,1)S(1)} %collective-permute-done.3.refs_0_), channel_id=1, source_target_pairs={{0,1},{1,3},{3,5},{5,7},{7,6},{6,4},{4,2},{2,0},{8,9},{9,11},{11,1... | collective-permute-start | bytes 786440 | tf_op jit(solution)/shard_map/ppermute | solution.py:397
  18.8 0.0 collective-permute-done.2.refs_1_
  18.8 0.3 collective-permute-start.4
  19.1 4.6 %project_blocks.4 = (f32[3,128,1024]{2,1,0:T(8,128)S(1)}, bf16[2,3,1024,1024]{3,2,1,0:T(8,128)(2,1)S(1)}) custom-call(bf16[128,1024]{1,0:T(8,128)(2,1)S(1)} %collective-permute-done.3.refs_0_, bf16[128,1024]{1,0:T(8,128)(2,1)S(1)} %collective-permute-done.2.refs_1_, ...), custom_call_target="tpu_custom_call", output_to_operand_aliasing={{0}: (4, {})} | custom-call | bytes 16777216 | tf_op jit(solution)/shard_map/project_blocks/pallas_call | solution.py:408
  23.7 0.0 collective-permute-done.5.refs_0_
  23.8 1.7 %collective-permute-start.7 = (bf16[128,512]{1,0:T(8,128)(2,1)S(1)}, bf16[128,512]{1,0:T(8,128)(2,1)S(1)}, u32[]{:S(2)}, u32[]{:S(2)}) collective-permute-start(bf16[128,512]{1,0:T(8,128)(2,1)S(1)} %slice.7), channel_id=1, source_target_pairs={{0,1},{1,3},{3,5},{5,7},{7,6},{6,4},{4,2},{2,0},{8,9},{9,11},{11,1... | collective-permute-start | bytes 393224 | tf_op jit(solution)/shard_map/ppermute | solution.py:428
  25.5 0.0 collective-permute-done.4.refs_1_
  25.5 0.4 collective-permute-start.6
  25.9 3.7 %project_blocks.5 = (f32[3,128,1024]{2,1,0:T(8,128)S(1)}, bf16[1,3,1024,1024]{3,2,1,0:T(8,128)(2,1)S(1)}) custom-call(bf16[128,1024]{1,0:T(8,128)(2,1)S(1)} %collective-permute-done.5.refs_0_, bf16[128,1024]{1,0:T(8,128)(2,1)S(1)} %collective-permute-done.4.refs_1_, ...), custom_call_target="tpu_custom_call", output_to_operand_aliasing={{0}: (4, {})} | custom-call | bytes 16777216 | tf_op jit(solution)/shard_map/project_blocks/pallas_call | solution.py:408
  29.6 0.0 collective-permute-done.7.x_ref
  29.6 0.6 %project_half.1._ = f32[3,128,1024]{2,1,0:T(8,128)S(1)} custom-call(bf16[128,512]{1,0:T(8,128)(2,1)S(1)} %collective-permute-done.7.x_ref, bf16[1,3,1024,1024]{3,2,1,0:T(8,128)(2,1)S(1)} %get-tuple-element.58.held, f32[3,128,1024]{2,1,0:T(8,128)S(1)} %get-tuple-element.61._), custom_call_target="tpu_custom_call", output_to_operand_aliasing={{}: (2, {})} | custom-call | bytes 16777216 | tf_op jit(solution)/shard_map/project_half/pallas_call | solution.py:430
  30.2 0.3 collective-permute-done.6.x_ref
  30.6 1.6 %project_last.1 = (f32[3,128,1024]{2,1,0:T(8,128)S(1)}, f32[128,1024]{1,0:T(8,128)S(1)}, f32[26,8,128]{2,1,0:T(8,128)S(1)}) custom-call(bf16[128,512]{1,0:T(8,128)(2,1)S(1)} %collective-permute-done.6.x_ref, bf16[1,3,1024,1024]{3,2,1,0:T(8,128)(2,1)S(1)} %get-tuple-element.58.held, f32[3,3,1024]{2,1,0:T(4,128)S(1)} %copy-done, ...), custom_call_target="tpu_custom_call", output_to_operand_aliasing={{0}: (5, {})} | custom-call | bytes 16777216 | tf_op jit(solution)/shard_map/project_last/pallas_call | solution.py:440
  32.1 0.1 collective-permute-start.8
  32.2 1.3 %collective-permute-done.8.partner.refs_2_ = f32[26,8,128]{2,1,0:T(8,128)S(1)} collective-permute-done((f32[26,8,128]{2,1,0:T(8,128)S(1)}, f32[26,8,128]{2,1,0:T(8,128)S(1)}, u32[]{:S(2)}, u32[]{:S(2)}) %collective-permute-start.8) | collective-permute-done | bytes 106528 | tf_op jit(solution)/shard_map/ppermute | solution.py:451
  33.6 1.6 %collective-permute-start.9 = (f32[22,8,128]{2,1,0:T(8,128)S(1)}, f32[22,8,128]{2,1,0:T(8,128)S(1)}, u32[]{:S(2)}, u32[]{:S(2)}) collective-permute-start(f32[22,8,128]{2,1,0:T(8,128)S(1)} %chip_state.1), channel_id=1, source_target_pairs={{0,16},{8,24},{16,0},{24,8},{1,17},{9,25},{17,1},{25,9},{2,18},{10... | collective-permute-start | bytes 270344 | tf_op jit(solution)/shard_map/ppermute | solution.py:462
  35.1 1.9 %local_response.1 = (f32[128,1024]{1,0:T(8,128)S(1)}, f32[128,1024]{1,0:T(8,128)S(1)}, f32[2,8,128]{2,1,0:T(8,128)S(1)}) custom-call(f32[3,128,1024]{2,1,0:T(8,128)S(1)} %get-tuple-element.65.total, f32[128,1024]{1,0:T(8,128)S(1)} %get-tuple-element.66.natural, f32[3,3,1024]{2,1,0:T(4,128)S(1)} %copy-done, f32[5,16,8,128]{3,2,1,0:T(8,128)S(1)} %get-tuple-element.64.table.refs_7_), custom_call_target="tpu_custom_call" | custom-call | bytes 16777216 | tf_op jit(solution)/shard_map/local_response/pallas_call | solution.py:465
  37.0 1.3 %collective-permute-done.9.refs_0_ = f32[22,8,128]{2,1,0:T(8,128)S(1)} collective-permute-done((f32[22,8,128]{2,1,0:T(8,128)S(1)}, f32[22,8,128]{2,1,0:T(8,128)S(1)}, u32[]{:S(2)}, u32[]{:S(2)}) %collective-permute-start.9) | collective-permute-done | bytes 90144 | tf_op jit(solution)/shard_map/ppermute | solution.py:462
  38.3 1.3 %carried_response.1 = bf16[128,1024]{1,0:T(8,128)(2,1)} custom-call(f32[22,8,128]{2,1,0:T(8,128)S(1)} %collective-permute-done.9.refs_0_, f32[26,8,128]{2,1,0:T(8,128)S(1)} %get-tuple-element.62.local.refs_1_, f32[26,8,128]{2,1,0:T(8,128)S(1)} %collective-permute-done.8.partner.refs_2_, f32[128,1024]{1,0:T(8,128)S(1)} %get-tuple-element.67.refs_3_, ...), custom_call_target="tpu_custom_call" | custom-call | tf_op jit(solution)/shard_map/carried_response/pallas_call | solution.py:479
  (7 shorter events, 0.1 us)
Async XLA Ops:
  0.0 9.5 %collective-permute-start.1 = (bf16[128,1024]{1,0:T(8,128)(2,1)}, bf16[128,1024]{1,0:T(8,128)(2,1)S(1)}, u32[]{:S(2)}, u32[]{:S(2)}) collective-permute-start(bf16[128,1024]{1,0:T(8,128)(2,1)} %refs_0_.1), channel_id=1, source_target_pairs={{0,1},{1,3},{3,5},{5,7},{7,6},{6,4},{4,2},{2,0},{8,9},{9,11},{11,1... | collective-permute-start | bytes 786440 | tf_op jit(solution)/shard_map/ppermute | solution.py:397
  3.0 8.3 %collective-permute-start = (bf16[128,1024]{1,0:T(8,128)(2,1)}, bf16[128,1024]{1,0:T(8,128)(2,1)S(1)}, u32[]{:S(2)}, u32[]{:S(2)}) collective-permute-start(bf16[128,1024]{1,0:T(8,128)(2,1)} %refs_0_.1), channel_id=1, source_target_pairs={{1,0},{3,1},{5,3},{7,5},{6,7},{4,6},{2,4},{0,2},{9,8},{11,9},{13,1... | collective-permute-start | bytes 786440 | tf_op jit(solution)/shard_map/ppermute | solution.py:398
  3.0 8.5 %copy-start = (f32[3,3,1024]{2,1,0:T(4,128)S(1)}, f32[3,3,1024]{2,1,0:T(4,128)}, u32[]{:S(2)}) copy-start(f32[3,3,1024]{2,1,0:T(4,128)} %taps.3) | copy-start | bytes 110596
  3.0 8.5 %copy-start.1 = (bf16[128,1024]{1,0:T(8,128)(2,1)S(1)}, bf16[128,1024]{1,0:T(8,128)(2,1)}, u32[]{:S(2)}) copy-start(bf16[128,1024]{1,0:T(8,128)(2,1)} %refs_0_.1) | copy-start | bytes 786436
  3.0 8.5 %copy-start.2 = (f32[16,1024]{1,0:T(8,128)S(1)}, f32[16,1024]{1,0:T(8,128)}, u32[]{:S(2)}) copy-start(f32[16,1024]{1,0:T(8,128)} %refs_6_.1) | copy-start | bytes 196612
  3.0 8.5 %copy-start.3 = (f32[16,1024]{1,0:T(8,128)S(1)}, f32[16,1024]{1,0:T(8,128)}, u32[]{:S(2)}) copy-start(f32[16,1024]{1,0:T(8,128)} %refs_7_.1) | copy-start | bytes 196612
  9.5 7.6 %collective-permute-start.3 = (bf16[128,1024]{1,0:T(8,128)(2,1)S(1)}, bf16[128,1024]{1,0:T(8,128)(2,1)S(1)}, u32[]{:S(2)}, u32[]{:S(2)}) collective-permute-start(bf16[128,1024]{1,0:T(8,128)(2,1)S(1)} %collective-permute-done.1.refs_1_), channel_id=1, source_target_pairs={{0,1},{1,3},{3,5},{5,7},{7,6},{6,4},{4,2},{2,0},{8,9},{9,11},{11,1... | collective-permute-start | bytes 786440 | tf_op jit(solution)/shard_map/ppermute | solution.py:397
  11.3 7.5 %collective-permute-start.2 = (bf16[128,1024]{1,0:T(8,128)(2,1)S(1)}, bf16[128,1024]{1,0:T(8,128)(2,1)S(1)}, u32[]{:S(2)}, u32[]{:S(2)}) collective-permute-start(bf16[128,1024]{1,0:T(8,128)(2,1)S(1)} %collective-permute-done.refs_2_), channel_id=1, source_target_pairs={{1,0},{3,1},{5,3},{7,5},{6,7},{4,6},{2,4},{0,2},{9,8},{11,9},{13,1... | collective-permute-start | bytes 786440 | tf_op jit(solution)/shard_map/ppermute | solution.py:398
  17.1 6.7 %collective-permute-start.5 = (bf16[128,1024]{1,0:T(8,128)(2,1)S(1)}, bf16[128,1024]{1,0:T(8,128)(2,1)S(1)}, u32[]{:S(2)}, u32[]{:S(2)}) collective-permute-start(bf16[128,1024]{1,0:T(8,128)(2,1)S(1)} %collective-permute-done.3.refs_0_), channel_id=1, source_target_pairs={{0,1},{1,3},{3,5},{5,7},{7,6},{6,4},{4,2},{2,0},{8,9},{9,11},{11,1... | collective-permute-start | bytes 786440 | tf_op jit(solution)/shard_map/ppermute | solution.py:397
  18.8 6.7 %collective-permute-start.4 = (bf16[128,1024]{1,0:T(8,128)(2,1)S(1)}, bf16[128,1024]{1,0:T(8,128)(2,1)S(1)}, u32[]{:S(2)}, u32[]{:S(2)}) collective-permute-start(bf16[128,1024]{1,0:T(8,128)(2,1)S(1)} %collective-permute-done.2.refs_1_), channel_id=1, source_target_pairs={{1,0},{3,1},{5,3},{7,5},{6,7},{4,6},{2,4},{0,2},{9,8},{11,9},{13,1... | collective-permute-start | bytes 786440 | tf_op jit(solution)/shard_map/ppermute | solution.py:398
  23.8 5.8 %collective-permute-start.7 = (bf16[128,512]{1,0:T(8,128)(2,1)S(1)}, bf16[128,512]{1,0:T(8,128)(2,1)S(1)}, u32[]{:S(2)}, u32[]{:S(2)}) collective-permute-start(bf16[128,512]{1,0:T(8,128)(2,1)S(1)} %slice.7), channel_id=1, source_target_pairs={{0,1},{1,3},{3,5},{5,7},{7,6},{6,4},{4,2},{2,0},{8,9},{9,11},{11,1... | collective-permute-start | bytes 393224 | tf_op jit(solution)/shard_map/ppermute | solution.py:428
  25.5 5.0 %collective-permute-start.6 = (bf16[128,512]{1,0:T(8,128)(2,1)S(1)}, bf16[128,512]{1,0:T(8,128)(2,1)S(1)}, u32[]{:S(2)}, u32[]{:S(2)}) collective-permute-start(bf16[128,512]{1,0:T(8,128)(2,1)S(1)} %slice.6), channel_id=1, source_target_pairs={{1,0},{3,1},{5,3},{7,5},{6,7},{4,6},{2,4},{0,2},{9,8},{11,9},{13,1... | collective-permute-start | bytes 393224 | tf_op jit(solution)/shard_map/ppermute | solution.py:429
  32.1 1.4 %collective-permute-start.8 = (f32[26,8,128]{2,1,0:T(8,128)S(1)}, f32[26,8,128]{2,1,0:T(8,128)S(1)}, u32[]{:S(2)}, u32[]{:S(2)}) collective-permute-start(f32[26,8,128]{2,1,0:T(8,128)S(1)} %get-tuple-element.62.local.refs_1_), channel_id=1, source_target_pairs={{0,8},{8,0},{16,24},{24,16},{1,9},{9,1},{17,25},{25,17},{2,10},{10... | collective-permute-start | bytes 319496 | tf_op jit(solution)/shard_map/ppermute | solution.py:451
  33.6 4.7 %collective-permute-start.9 = (f32[22,8,128]{2,1,0:T(8,128)S(1)}, f32[22,8,128]{2,1,0:T(8,128)S(1)}, u32[]{:S(2)}, u32[]{:S(2)}) collective-permute-start(f32[22,8,128]{2,1,0:T(8,128)S(1)} %chip_state.1), channel_id=1, source_target_pairs={{0,16},{8,24},{16,0},{24,8},{1,17},{9,25},{17,1},{25,9},{2,18},{10... | collective-permute-start | bytes 270344 | tf_op jit(solution)/shard_map/ppermute | solution.py:462

commit v15 on v14

--- a/solution.py
+++ b/solution.py
@@ -165,7 +165,7 @@
     row = lax.broadcasted_iota(jnp.int32, (tall, lanes), 0)
     for g in range(groups):
         cols = slice(g * lanes, (g + 1) * lanes)
-        one, two = rounded(total[1, :, cols]), rounded(total[2, :, cols])
+        one, two = total[1, :, cols], total[2, :, cols]
         value = filtered(taps, 1, one, cols) * filtered(taps, 2, two, cols)
         source[:, cols] = value
         step = [jnp.broadcast_to(tile_step[n : n + 1, cols], (tall, lanes)) for n in range(modes)]
@@ -175,7 +175,7 @@
             state = [a * b + value[i : i + tall] for a, b in zip(state, step)]
         for n in range(modes):
             out_ref[n, g : g + 1, :] = jnp.sum(state[n] * fade[n, :, cols], axis=0, keepdims=True)
-        query = rounded(total[0, rows - tall :, cols])
+        query = total[0, rows - tall :, cols]
         for s, ends in ((1, one), (2, two)):
             out_ref[modes + s * 2 - 2 : modes + s * 2, g, :] = ends[:2]
         for s, ends in ((0, query), (1, one), (2, two)):
@@ -183,10 +183,6 @@
             out_ref[low : low + 2, g, :] = ends[-2:]
 
 
-def rounded(value):
-    return value.astype(jnp.bfloat16).astype(jnp.float32)
-
-
 def tree_sum(terms):
     while len(terms) > 1:
         terms = [a + b for a, b in zip(terms[::2], terms[1::2])] + terms[len(terms) & ~1 :]
@@ -198,7 +194,7 @@
     modes = table.shape[1]
     for g in range(groups):
         cols = slice(g * lanes, (g + 1) * lanes)
-        value = rounded(total[0, :, cols])
+        value = total[0, :, cols]
         query[:, cols] = filtered(taps, 0, value, cols)
         low[:, g, :] = value[:8]
         source[:, g, :] = natural[:, cols]

time: 39.8 us -> 39.7 us (level)
  no operation moved by 1% of the time
where the time goes in v15:
time: 39.7 us; the launch traced here: 39.6 us
  Pallas kernels  24.8 us (62%)
  starting transfers between devices  10.8 us (27%)
  waiting for transfers between devices  3.82 us (10%)
    pallas_call x3, Pallas kernels, on_device(): pl.pallas_call(functools.partial(middle_kernel, order, blocks(step), left...  13.2 us
    ppermute x3, starting transfers between devices, on_device(): fore = lax.ppermute(fore, 'tp', ahead)  6.41 us
    pallas_call x1, Pallas kernels, on_device(): pl.pallas_call(functools.partial(load_kernel, order, blocks(1), pieces(1)...  6.22 us
    pallas_call x1, Pallas kernels, on_device(): pl.pallas_call(local_kernel, out_shape=[f32(rows, chans), f32(rows, chans...  1.88 us
    ppermute x1, starting transfers between devices, on_device(): fore = lax.ppermute(fore[:, :width // 2], 'tp', ahead)  1.74 us
    ppermute x1, starting transfers between devices, on_device(): lax.ppermute(chip, 'ctx', [(j, (j + d) % ctx) for j in range(ctx)])  1.55 us
    pallas_call x1, Pallas kernels, on_device(): pl.pallas_call(last_kernel, out_shape=[sums, f32(rows, chans), f32(modes...  1.52 us
    pallas_call x1, Pallas kernels, on_device(): pl.pallas_call(functools.partial(final_kernel, lone, len(sent)), out_shap...  1.33 us
  transfers between devices with their start and end apart: 10, of which 5 were waited for; matrix products, arithmetic and copies ran while one was open for 0% of the time, Pallas kernels for 55%

profile of v15, /device:TPU:0, one launch (start us, length us, event | category | flops | bytes accessed | tf_op | source)
XLA Modules:
  0.0 39.6 jit_solution(13441844555377998260)
XLA Ops:
  0.0 3.0 %collective-permute-start.1 = (bf16[128,1024]{1,0:T(8,128)(2,1)}, bf16[128,1024]{1,0:T(8,128)(2,1)S(1)}, u32[]{:S(2)}, u32[]{:S(2)}) collective-permute-start(bf16[128,1024]{1,0:T(8,128)(2,1)} %refs_0_.1), channel_id=1, source_target_pairs={{0,1},{1,3},{3,5},{5,7},{7,6},{6,4},{4,2},{2,0},{8,9},{9,11},{11,1... | collective-permute-start | bytes 786440 | tf_op jit(solution)/shard_map/ppermute | solution.py:393
  3.0 0.1 collective-permute-start
  3.0 6.2 %load_first.1.refs_3_ = bf16[3,3,1024,1024]{3,2,1,0:T(8,128)(2,1)S(1)} custom-call(bf16[3,8192,1024]{2,1,0:T(8,128)(2,1)} %bitcast.1), custom_call_target="tpu_custom_call" | custom-call | bytes 16777216 | tf_op jit(solution)/shard_map/load_first/pallas_call | solution.py:381
  9.3 0.3 collective-permute-done.1.refs_1_
  9.5 1.8 %collective-permute-start.3 = (bf16[128,1024]{1,0:T(8,128)(2,1)S(1)}, bf16[128,1024]{1,0:T(8,128)(2,1)S(1)}, u32[]{:S(2)}, u32[]{:S(2)}) collective-permute-start(bf16[128,1024]{1,0:T(8,128)(2,1)S(1)} %collective-permute-done.1.refs_1_), channel_id=1, source_target_pairs={{0,1},{1,3},{3,5},{5,7},{7,6},{6,4},{4,2},{2,0},{8,9},{9,11},{11,1... | collective-permute-start | bytes 786440 | tf_op jit(solution)/shard_map/ppermute | solution.py:393
  11.3 0.0 collective-permute-done.refs_2_
  11.3 0.3 collective-permute-start.2
  11.6 0.0 copy-done
  11.6 0.0 copy-done.1
  11.6 0.0 copy-done.2
  11.6 0.0 copy-done.3
  11.6 4.9 %project_blocks.3 = (f32[3,128,1024]{2,1,0:T(8,128)S(1)}, bf16[2,3,1024,1024]{3,2,1,0:T(8,128)(2,1)S(1)}, f32[3,3,8,128]{3,2,1,0:T(8,128)S(1)}, f32[5,16,8,128]{...) custom-call(bf16[128,1024]{1,0:T(8,128)(2,1)S(1)} %copy-done.1, ...), custom_call_target="tpu_custom_call" | custom-call | bytes 16777216 | tf_op jit(solution)/shard_map/project_blocks/pallas_call | solution.py:404
  16.5 0.6 %collective-permute-done.3.refs_0_ = bf16[128,1024]{1,0:T(8,128)(2,1)S(1)} collective-permute-done((bf16[128,1024]{1,0:T(8,128)(2,1)S(1)}, bf16[128,1024]{1,0:T(8,128)(2,1)S(1)}, u32[]{:S(2)}, u32[]{:S(2)}) %collective-permute-start.3) | collective-permute-done | bytes 262176 | tf_op jit(solution)/shard_map/ppermute | solution.py:393
  17.1 1.7 %collective-permute-start.5 = (bf16[128,1024]{1,0:T(8,128)(2,1)S(1)}, bf16[128,1024]{1,0:T(8,128)(2,1)S(1)}, u32[]{:S(2)}, u32[]{:S(2)}) collective-permute-start(bf16[128,1024]{1,0:T(8,128)(2,1)S(1)} %collective-permute-done.3.refs_0_), channel_id=1, source_target_pairs={{0,1},{1,3},{3,5},{5,7},{7,6},{6,4},{4,2},{2,0},{8,9},{9,11},{11,1... | collective-permute-start | bytes 786440 | tf_op jit(solution)/shard_map/ppermute | solution.py:393
  18.8 0.0 collective-permute-done.2.refs_1_
  18.8 0.3 collective-permute-start.4
  19.1 4.6 %project_blocks.4 = (f32[3,128,1024]{2,1,0:T(8,128)S(1)}, bf16[2,3,1024,1024]{3,2,1,0:T(8,128)(2,1)S(1)}) custom-call(bf16[128,1024]{1,0:T(8,128)(2,1)S(1)} %collective-permute-done.3.refs_0_, bf16[128,1024]{1,0:T(8,128)(2,1)S(1)} %collective-permute-done.2.refs_1_, ...), custom_call_target="tpu_custom_call", output_to_operand_aliasing={{0}: (4, {})} | custom-call | bytes 16777216 | tf_op jit(solution)/shard_map/project_blocks/pallas_call | solution.py:404
  23.7 0.0 collective-permute-done.5.refs_0_
  23.8 1.7 %collective-permute-start.7 = (bf16[128,512]{1,0:T(8,128)(2,1)S(1)}, bf16[128,512]{1,0:T(8,128)(2,1)S(1)}, u32[]{:S(2)}, u32[]{:S(2)}) collective-permute-start(bf16[128,512]{1,0:T(8,128)(2,1)S(1)} %slice.7), channel_id=1, source_target_pairs={{0,1},{1,3},{3,5},{5,7},{7,6},{6,4},{4,2},{2,0},{8,9},{9,11},{11,1... | collective-permute-start | bytes 393224 | tf_op jit(solution)/shard_map/ppermute | solution.py:424
  25.5 0.0 collective-permute-done.4.refs_1_
  25.5 0.4 collective-permute-start.6
  25.9 3.7 %project_blocks.5 = (f32[3,128,1024]{2,1,0:T(8,128)S(1)}, bf16[1,3,1024,1024]{3,2,1,0:T(8,128)(2,1)S(1)}) custom-call(bf16[128,1024]{1,0:T(8,128)(2,1)S(1)} %collective-permute-done.5.refs_0_, bf16[128,1024]{1,0:T(8,128)(2,1)S(1)} %collective-permute-done.4.refs_1_, ...), custom_call_target="tpu_custom_call", output_to_operand_aliasing={{0}: (4, {})} | custom-call | bytes 16777216 | tf_op jit(solution)/shard_map/project_blocks/pallas_call | solution.py:404
  29.6 0.0 collective-permute-done.7.x_ref
  29.6 0.6 %project_half.1._ = f32[3,128,1024]{2,1,0:T(8,128)S(1)} custom-call(bf16[128,512]{1,0:T(8,128)(2,1)S(1)} %collective-permute-done.7.x_ref, bf16[1,3,1024,1024]{3,2,1,0:T(8,128)(2,1)S(1)} %get-tuple-element.58.held, f32[3,128,1024]{2,1,0:T(8,128)S(1)} %get-tuple-element.61._), custom_call_target="tpu_custom_call", output_to_operand_aliasing={{}: (2, {})} | custom-call | bytes 16777216 | tf_op jit(solution)/shard_map/project_half/pallas_call | solution.py:426
  30.2 0.3 collective-permute-done.6.x_ref
  30.6 1.5 %project_last.1 = (f32[3,128,1024]{2,1,0:T(8,128)S(1)}, f32[128,1024]{1,0:T(8,128)S(1)}, f32[26,8,128]{2,1,0:T(8,128)S(1)}) custom-call(bf16[128,512]{1,0:T(8,128)(2,1)S(1)} %collective-permute-done.6.x_ref, bf16[1,3,1024,1024]{3,2,1,0:T(8,128)(2,1)S(1)} %get-tuple-element.58.held, f32[3,3,1024]{2,1,0:T(4,128)S(1)} %copy-done, ...), custom_call_target="tpu_custom_call", output_to_operand_aliasing={{0}: (5, {})} | custom-call | bytes 16777216 | tf_op jit(solution)/shard_map/project_last/pallas_call | solution.py:436
  32.1 0.1 collective-permute-start.8
  32.2 1.3 %collective-permute-done.8.partner.refs_2_ = f32[26,8,128]{2,1,0:T(8,128)S(1)} collective-permute-done((f32[26,8,128]{2,1,0:T(8,128)S(1)}, f32[26,8,128]{2,1,0:T(8,128)S(1)}, u32[]{:S(2)}, u32[]{:S(2)}) %collective-permute-start.8) | collective-permute-done | bytes 106528 | tf_op jit(solution)/shard_map/ppermute | solution.py:447
  33.5 1.6 %collective-permute-start.9 = (f32[22,8,128]{2,1,0:T(8,128)S(1)}, f32[22,8,128]{2,1,0:T(8,128)S(1)}, u32[]{:S(2)}, u32[]{:S(2)}) collective-permute-start(f32[22,8,128]{2,1,0:T(8,128)S(1)} %chip_state.1), channel_id=1, source_target_pairs={{0,16},{8,24},{16,0},{24,8},{1,17},{9,25},{17,1},{25,9},{2,18},{10... | collective-permute-start | bytes 270344 | tf_op jit(solution)/shard_map/ppermute | solution.py:458
  35.1 1.9 %local_response.1 = (f32[128,1024]{1,0:T(8,128)S(1)}, f32[128,1024]{1,0:T(8,128)S(1)}, f32[2,8,128]{2,1,0:T(8,128)S(1)}) custom-call(f32[3,128,1024]{2,1,0:T(8,128)S(1)} %get-tuple-element.65.total, f32[128,1024]{1,0:T(8,128)S(1)} %get-tuple-element.66.natural, f32[3,3,1024]{2,1,0:T(4,128)S(1)} %copy-done, f32[5,16,8,128]{3,2,1,0:T(8,128)S(1)} %get-tuple-element.64.table.refs_7_), custom_call_target="tpu_custom_call" | custom-call | bytes 16777216 | tf_op jit(solution)/shard_map/local_response/pallas_call | solution.py:461
  37.0 1.3 %collective-permute-done.9.refs_0_ = f32[22,8,128]{2,1,0:T(8,128)S(1)} collective-permute-done((f32[22,8,128]{2,1,0:T(8,128)S(1)}, f32[22,8,128]{2,1,0:T(8,128)S(1)}, u32[]{:S(2)}, u32[]{:S(2)}) %collective-permute-start.9) | collective-permute-done | bytes 90144 | tf_op jit(solution)/shard_map/ppermute | solution.py:458
  38.3 1.3 %carried_response.1 = bf16[128,1024]{1,0:T(8,128)(2,1)} custom-call(f32[22,8,128]{2,1,0:T(8,128)S(1)} %collective-permute-done.9.refs_0_, f32[26,8,128]{2,1,0:T(8,128)S(1)} %get-tuple-element.62.local.refs_1_, f32[26,8,128]{2,1,0:T(8,128)S(1)} %collective-permute-done.8.partner.refs_2_, f32[128,1024]{1,0:T(8,128)S(1)} %get-tuple-element.67.refs_3_, ...), custom_call_target="tpu_custom_call" | custom-call | tf_op jit(solution)/shard_map/carried_response/pallas_call | solution.py:475
  (7 shorter events, 0.1 us)
Async XLA Ops:
  0.0 9.5 %collective-permute-start.1 = (bf16[128,1024]{1,0:T(8,128)(2,1)}, bf16[128,1024]{1,0:T(8,128)(2,1)S(1)}, u32[]{:S(2)}, u32[]{:S(2)}) collective-permute-start(bf16[128,1024]{1,0:T(8,128)(2,1)} %refs_0_.1), channel_id=1, source_target_pairs={{0,1},{1,3},{3,5},{5,7},{7,6},{6,4},{4,2},{2,0},{8,9},{9,11},{11,1... | collective-permute-start | bytes 786440 | tf_op jit(solution)/shard_map/ppermute | solution.py:393
  3.0 8.3 %collective-permute-start = (bf16[128,1024]{1,0:T(8,128)(2,1)}, bf16[128,1024]{1,0:T(8,128)(2,1)S(1)}, u32[]{:S(2)}, u32[]{:S(2)}) collective-permute-start(bf16[128,1024]{1,0:T(8,128)(2,1)} %refs_0_.1), channel_id=1, source_target_pairs={{1,0},{3,1},{5,3},{7,5},{6,7},{4,6},{2,4},{0,2},{9,8},{11,9},{13,1... | collective-permute-start | bytes 786440 | tf_op jit(solution)/shard_map/ppermute | solution.py:394
  3.0 8.5 %copy-start = (f32[3,3,1024]{2,1,0:T(4,128)S(1)}, f32[3,3,1024]{2,1,0:T(4,128)}, u32[]{:S(2)}) copy-start(f32[3,3,1024]{2,1,0:T(4,128)} %taps.3) | copy-start | bytes 110596
  3.0 8.5 %copy-start.1 = (bf16[128,1024]{1,0:T(8,128)(2,1)S(1)}, bf16[128,1024]{1,0:T(8,128)(2,1)}, u32[]{:S(2)}) copy-start(bf16[128,1024]{1,0:T(8,128)(2,1)} %refs_0_.1) | copy-start | bytes 786436
  3.0 8.5 %copy-start.2 = (f32[16,1024]{1,0:T(8,128)S(1)}, f32[16,1024]{1,0:T(8,128)}, u32[]{:S(2)}) copy-start(f32[16,1024]{1,0:T(8,128)} %refs_6_.1) | copy-start | bytes 196612
  3.0 8.5 %copy-start.3 = (f32[16,1024]{1,0:T(8,128)S(1)}, f32[16,1024]{1,0:T(8,128)}, u32[]{:S(2)}) copy-start(f32[16,1024]{1,0:T(8,128)} %refs_7_.1) | copy-start | bytes 196612
  9.5 7.6 %collective-permute-start.3 = (bf16[128,1024]{1,0:T(8,128)(2,1)S(1)}, bf16[128,1024]{1,0:T(8,128)(2,1)S(1)}, u32[]{:S(2)}, u32[]{:S(2)}) collective-permute-start(bf16[128,1024]{1,0:T(8,128)(2,1)S(1)} %collective-permute-done.1.refs_1_), channel_id=1, source_target_pairs={{0,1},{1,3},{3,5},{5,7},{7,6},{6,4},{4,2},{2,0},{8,9},{9,11},{11,1... | collective-permute-start | bytes 786440 | tf_op jit(solution)/shard_map/ppermute | solution.py:393
  11.3 7.5 %collective-permute-start.2 = (bf16[128,1024]{1,0:T(8,128)(2,1)S(1)}, bf16[128,1024]{1,0:T(8,128)(2,1)S(1)}, u32[]{:S(2)}, u32[]{:S(2)}) collective-permute-start(bf16[128,1024]{1,0:T(8,128)(2,1)S(1)} %collective-permute-done.refs_2_), channel_id=1, source_target_pairs={{1,0},{3,1},{5,3},{7,5},{6,7},{4,6},{2,4},{0,2},{9,8},{11,9},{13,1... | collective-permute-start | bytes 786440 | tf_op jit(solution)/shard_map/ppermute | solution.py:394
  17.1 6.7 %collective-permute-start.5 = (bf16[128,1024]{1,0:T(8,128)(2,1)S(1)}, bf16[128,1024]{1,0:T(8,128)(2,1)S(1)}, u32[]{:S(2)}, u32[]{:S(2)}) collective-permute-start(bf16[128,1024]{1,0:T(8,128)(2,1)S(1)} %collective-permute-done.3.refs_0_), channel_id=1, source_target_pairs={{0,1},{1,3},{3,5},{5,7},{7,6},{6,4},{4,2},{2,0},{8,9},{9,11},{11,1... | collective-permute-start | bytes 786440 | tf_op jit(solution)/shard_map/ppermute | solution.py:393
  18.8 6.7 %collective-permute-start.4 = (bf16[128,1024]{1,0:T(8,128)(2,1)S(1)}, bf16[128,1024]{1,0:T(8,128)(2,1)S(1)}, u32[]{:S(2)}, u32[]{:S(2)}) collective-permute-start(bf16[128,1024]{1,0:T(8,128)(2,1)S(1)} %collective-permute-done.2.refs_1_), channel_id=1, source_target_pairs={{1,0},{3,1},{5,3},{7,5},{6,7},{4,6},{2,4},{0,2},{9,8},{11,9},{13,1... | collective-permute-start | bytes 786440 | tf_op jit(solution)/shard_map/ppermute | solution.py:394
  23.8 5.8 %collective-permute-start.7 = (bf16[128,512]{1,0:T(8,128)(2,1)S(1)}, bf16[128,512]{1,0:T(8,128)(2,1)S(1)}, u32[]{:S(2)}, u32[]{:S(2)}) collective-permute-start(bf16[128,512]{1,0:T(8,128)(2,1)S(1)} %slice.7), channel_id=1, source_target_pairs={{0,1},{1,3},{3,5},{5,7},{7,6},{6,4},{4,2},{2,0},{8,9},{9,11},{11,1... | collective-permute-start | bytes 393224 | tf_op jit(solution)/shard_map/ppermute | solution.py:424
  25.5 5.0 %collective-permute-start.6 = (bf16[128,512]{1,0:T(8,128)(2,1)S(1)}, bf16[128,512]{1,0:T(8,128)(2,1)S(1)}, u32[]{:S(2)}, u32[]{:S(2)}) collective-permute-start(bf16[128,512]{1,0:T(8,128)(2,1)S(1)} %slice.6), channel_id=1, source_target_pairs={{1,0},{3,1},{5,3},{7,5},{6,7},{4,6},{2,4},{0,2},{9,8},{11,9},{13,1... | collective-permute-start | bytes 393224 | tf_op jit(solution)/shard_map/ppermute | solution.py:425
  32.1 1.4 %collective-permute-start.8 = (f32[26,8,128]{2,1,0:T(8,128)S(1)}, f32[26,8,128]{2,1,0:T(8,128)S(1)}, u32[]{:S(2)}, u32[]{:S(2)}) collective-permute-start(f32[26,8,128]{2,1,0:T(8,128)S(1)} %get-tuple-element.62.local.refs_1_), channel_id=1, source_target_pairs={{0,8},{8,0},{16,24},{24,16},{1,9},{9,1},{17,25},{25,17},{2,10},{10... | collective-permute-start | bytes 319496 | tf_op jit(solution)/shard_map/ppermute | solution.py:447
  33.5 4.7 %collective-permute-start.9 = (f32[22,8,128]{2,1,0:T(8,128)S(1)}, f32[22,8,128]{2,1,0:T(8,128)S(1)}, u32[]{:S(2)}, u32[]{:S(2)}) collective-permute-start(f32[22,8,128]{2,1,0:T(8,128)S(1)} %chip_state.1), channel_id=1, source_target_pairs={{0,16},{8,24},{16,0},{24,8},{1,17},{9,25},{17,1},{25,9},{2,18},{10... | collective-permute-start | bytes 270344 | tf_op jit(solution)/shard_map/ppermute | solution.py:458

commit v16 on v15

--- a/solution.py
+++ b/solution.py
@@ -157,9 +157,9 @@
 
 def last_kernel(x_ref, held, taps, tile_step, fade, _, total, source, out_ref):
     depth = x_ref.shape[1]
-    for s in range(total.shape[0]):
+    for s in (1, 2):
         add_products([x_ref[...]], lambda b, at: held[0, s, depth:, at], total, s, cols=WIDE)
-    rows = source.shape[0]
+    rows, chans = source.shape
     modes, tall, _ = fade.shape
     groups, lanes = out_ref.shape[1:]
     row = lax.broadcasted_iota(jnp.int32, (tall, lanes), 0)
@@ -175,12 +175,16 @@
             state = [a * b + value[i : i + tall] for a, b in zip(state, step)]
         for n in range(modes):
             out_ref[n, g : g + 1, :] = jnp.sum(state[n] * fade[n, :, cols], axis=0, keepdims=True)
-        query = total[0, rows - tall :, cols]
         for s, ends in ((1, one), (2, two)):
             out_ref[modes + s * 2 - 2 : modes + s * 2, g, :] = ends[:2]
-        for s, ends in ((0, query), (1, one), (2, two)):
-            low = modes + 4 + s * 2
-            out_ref[low : low + 2, g, :] = ends[-2:]
+            out_ref[modes + 4 + s * 2 : modes + 6 + s * 2, g, :] = ends[-2:]
+        if not g * lanes % min(WIDE, chans):
+            at = slice(g * lanes, g * lanes + min(WIDE, chans))
+            total[0, :, at] += jnp.dot(
+                x_ref[...], held[0, 0, depth:, at], preferred_element_type=jnp.float32
+            )
+    for g in range(groups):
+        out_ref[modes + 4 : modes + 6, g, :] = total[0, rows - 2 :, g * lanes : (g + 1) * lanes]
 
 
 def tree_sum(terms):

time: 39.7 us -> 39.8 us (level)
  no operation moved by 1% of the time
where the time goes in v16:
time: 39.8 us; the launch traced here: 39.6 us
  Pallas kernels  24.8 us (62%)
  starting transfers between devices  10.8 us (27%)
  waiting for transfers between devices  3.81 us (10%)
    pallas_call x3, Pallas kernels, on_device(): pl.pallas_call(functools.partial(middle_kernel, order, blocks(step), left...  13.2 us
    ppermute x3, starting transfers between devices, on_device(): fore = lax.ppermute(fore, 'tp', ahead)  6.41 us
    pallas_call x1, Pallas kernels, on_device(): pl.pallas_call(functools.partial(load_kernel, order, blocks(1), pieces(1)...  6.22 us
    pallas_call x1, Pallas kernels, on_device(): pl.pallas_call(local_kernel, out_shape=[f32(rows, chans), f32(rows, chans...  1.88 us
    ppermute x1, starting transfers between devices, on_device(): fore = lax.ppermute(fore[:, :width // 2], 'tp', ahead)  1.74 us
    pallas_call x1, Pallas kernels, on_device(): pl.pallas_call(last_kernel, out_shape=[sums, f32(rows, chans), f32(modes...  1.58 us
    ppermute x1, starting transfers between devices, on_device(): lax.ppermute(chip, 'ctx', [(j, (j + d) % ctx) for j in range(ctx)])  1.56 us
    pallas_call x1, Pallas kernels, on_device(): pl.pallas_call(functools.partial(final_kernel, lone, len(sent)), out_shap...  1.33 us
  transfers between devices with their start and end apart: 10, of which 5 were waited for; matrix products, arithmetic and copies ran while one was open for 0% of the time, Pallas kernels for 55%

profile of v16, /device:TPU:0, one launch (start us, length us, event | category | flops | bytes accessed | tf_op | source)
XLA Modules:
  0.0 39.6 jit_solution(10083646653618811427)
XLA Ops:
  0.0 3.0 %collective-permute-start.1 = (bf16[128,1024]{1,0:T(8,128)(2,1)}, bf16[128,1024]{1,0:T(8,128)(2,1)S(1)}, u32[]{:S(2)}, u32[]{:S(2)}) collective-permute-start(bf16[128,1024]{1,0:T(8,128)(2,1)} %refs_0_.1), channel_id=1, source_target_pairs={{0,1},{1,3},{3,5},{5,7},{7,6},{6,4},{4,2},{2,0},{8,9},{9,11},{11,1... | collective-permute-start | bytes 786440 | tf_op jit(solution)/shard_map/ppermute | solution.py:397
  3.0 0.1 collective-permute-start
  3.0 6.2 %load_first.1.refs_3_ = bf16[3,3,1024,1024]{3,2,1,0:T(8,128)(2,1)S(1)} custom-call(bf16[3,8192,1024]{2,1,0:T(8,128)(2,1)} %bitcast.1), custom_call_target="tpu_custom_call" | custom-call | bytes 16777216 | tf_op jit(solution)/shard_map/load_first/pallas_call | solution.py:385
  9.3 0.3 collective-permute-done.1.refs_1_
  9.5 1.8 %collective-permute-start.3 = (bf16[128,1024]{1,0:T(8,128)(2,1)S(1)}, bf16[128,1024]{1,0:T(8,128)(2,1)S(1)}, u32[]{:S(2)}, u32[]{:S(2)}) collective-permute-start(bf16[128,1024]{1,0:T(8,128)(2,1)S(1)} %collective-permute-done.1.refs_1_), channel_id=1, source_target_pairs={{0,1},{1,3},{3,5},{5,7},{7,6},{6,4},{4,2},{2,0},{8,9},{9,11},{11,1... | collective-permute-start | bytes 786440 | tf_op jit(solution)/shard_map/ppermute | solution.py:397
  11.3 0.0 collective-permute-done.refs_2_
  11.3 0.3 collective-permute-start.2
  11.6 0.0 copy-done
  11.6 0.0 copy-done.1
  11.6 0.0 copy-done.2
  11.6 0.0 copy-done.3
  11.6 4.9 %project_blocks.3 = (f32[3,128,1024]{2,1,0:T(8,128)S(1)}, bf16[2,3,1024,1024]{3,2,1,0:T(8,128)(2,1)S(1)}, f32[3,3,8,128]{3,2,1,0:T(8,128)S(1)}, f32[5,16,8,128]{...) custom-call(bf16[128,1024]{1,0:T(8,128)(2,1)S(1)} %copy-done.1, ...), custom_call_target="tpu_custom_call" | custom-call | bytes 16777216 | tf_op jit(solution)/shard_map/project_blocks/pallas_call | solution.py:408
  16.5 0.6 %collective-permute-done.3.refs_0_ = bf16[128,1024]{1,0:T(8,128)(2,1)S(1)} collective-permute-done((bf16[128,1024]{1,0:T(8,128)(2,1)S(1)}, bf16[128,1024]{1,0:T(8,128)(2,1)S(1)}, u32[]{:S(2)}, u32[]{:S(2)}) %collective-permute-start.3) | collective-permute-done | bytes 262176 | tf_op jit(solution)/shard_map/ppermute | solution.py:397
  17.1 1.7 %collective-permute-start.5 = (bf16[128,1024]{1,0:T(8,128)(2,1)S(1)}, bf16[128,1024]{1,0:T(8,128)(2,1)S(1)}, u32[]{:S(2)}, u32[]{:S(2)}) collective-permute-start(bf16[128,1024]{1,0:T(8,128)(2,1)S(1)} %collective-permute-done.3.refs_0_), channel_id=1, source_target_pairs={{0,1},{1,3},{3,5},{5,7},{7,6},{6,4},{4,2},{2,0},{8,9},{9,11},{11,1... | collective-permute-start | bytes 786440 | tf_op jit(solution)/shard_map/ppermute | solution.py:397
  18.8 0.0 collective-permute-done.2.refs_1_
  18.8 0.3 collective-permute-start.4
  19.1 4.6 %project_blocks.4 = (f32[3,128,1024]{2,1,0:T(8,128)S(1)}, bf16[2,3,1024,1024]{3,2,1,0:T(8,128)(2,1)S(1)}) custom-call(bf16[128,1024]{1,0:T(8,128)(2,1)S(1)} %collective-permute-done.3.refs_0_, bf16[128,1024]{1,0:T(8,128)(2,1)S(1)} %collective-permute-done.2.refs_1_, ...), custom_call_target="tpu_custom_call", output_to_operand_aliasing={{0}: (4, {})} | custom-call | bytes 16777216 | tf_op jit(solution)/shard_map/project_blocks/pallas_call | solution.py:408
  23.7 0.0 collective-permute-done.5.refs_0_
  23.8 1.7 %collective-permute-start.7 = (bf16[128,512]{1,0:T(8,128)(2,1)S(1)}, bf16[128,512]{1,0:T(8,128)(2,1)S(1)}, u32[]{:S(2)}, u32[]{:S(2)}) collective-permute-start(bf16[128,512]{1,0:T(8,128)(2,1)S(1)} %slice.7), channel_id=1, source_target_pairs={{0,1},{1,3},{3,5},{5,7},{7,6},{6,4},{4,2},{2,0},{8,9},{9,11},{11,1... | collective-permute-start | bytes 393224 | tf_op jit(solution)/shard_map/ppermute | solution.py:428
  25.5 0.0 collective-permute-done.4.refs_1_
  25.5 0.4 collective-permute-start.6
  25.9 3.7 %project_blocks.5 = (f32[3,128,1024]{2,1,0:T(8,128)S(1)}, bf16[1,3,1024,1024]{3,2,1,0:T(8,128)(2,1)S(1)}) custom-call(bf16[128,1024]{1,0:T(8,128)(2,1)S(1)} %collective-permute-done.5.refs_0_, bf16[128,1024]{1,0:T(8,128)(2,1)S(1)} %collective-permute-done.4.refs_1_, ...), custom_call_target="tpu_custom_call", output_to_operand_aliasing={{0}: (4, {})} | custom-call | bytes 16777216 | tf_op jit(solution)/shard_map/project_blocks/pallas_call | solution.py:408
  29.6 0.0 collective-permute-done.7.x_ref
  29.6 0.6 %project_half.1._ = f32[3,128,1024]{2,1,0:T(8,128)S(1)} custom-call(bf16[128,512]{1,0:T(8,128)(2,1)S(1)} %collective-permute-done.7.x_ref, bf16[1,3,1024,1024]{3,2,1,0:T(8,128)(2,1)S(1)} %get-tuple-element.58.held, f32[3,128,1024]{2,1,0:T(8,128)S(1)} %get-tuple-element.61._), custom_call_target="tpu_custom_call", output_to_operand_aliasing={{}: (2, {})} | custom-call | bytes 16777216 | tf_op jit(solution)/shard_map/project_half/pallas_call | solution.py:430
  30.2 0.3 collective-permute-done.6.x_ref
  30.6 1.6 %project_last.1 = (f32[3,128,1024]{2,1,0:T(8,128)S(1)}, f32[128,1024]{1,0:T(8,128)S(1)}, f32[26,8,128]{2,1,0:T(8,128)S(1)}) custom-call(bf16[128,512]{1,0:T(8,128)(2,1)S(1)} %collective-permute-done.6.x_ref, bf16[1,3,1024,1024]{3,2,1,0:T(8,128)(2,1)S(1)} %get-tuple-element.58.held, f32[3,3,1024]{2,1,0:T(4,128)S(1)} %copy-done, ...), custom_call_target="tpu_custom_call", output_to_operand_aliasing={{0}: (5, {})} | custom-call | bytes 16777216 | tf_op jit(solution)/shard_map/project_last/pallas_call | solution.py:440
  32.1 0.1 collective-permute-start.8
  32.2 1.3 %collective-permute-done.8.partner.refs_2_ = f32[26,8,128]{2,1,0:T(8,128)S(1)} collective-permute-done((f32[26,8,128]{2,1,0:T(8,128)S(1)}, f32[26,8,128]{2,1,0:T(8,128)S(1)}, u32[]{:S(2)}, u32[]{:S(2)}) %collective-permute-start.8) | collective-permute-done | bytes 106528 | tf_op jit(solution)/shard_map/ppermute | solution.py:451
  33.6 1.6 %collective-permute-start.9 = (f32[22,8,128]{2,1,0:T(8,128)S(1)}, f32[22,8,128]{2,1,0:T(8,128)S(1)}, u32[]{:S(2)}, u32[]{:S(2)}) collective-permute-start(f32[22,8,128]{2,1,0:T(8,128)S(1)} %chip_state.1), channel_id=1, source_target_pairs={{0,16},{8,24},{16,0},{24,8},{1,17},{9,25},{17,1},{25,9},{2,18},{10... | collective-permute-start | bytes 270344 | tf_op jit(solution)/shard_map/ppermute | solution.py:462
  35.1 1.9 %local_response.1 = (f32[128,1024]{1,0:T(8,128)S(1)}, f32[128,1024]{1,0:T(8,128)S(1)}, f32[2,8,128]{2,1,0:T(8,128)S(1)}) custom-call(f32[3,128,1024]{2,1,0:T(8,128)S(1)} %get-tuple-element.65.total, f32[128,1024]{1,0:T(8,128)S(1)} %get-tuple-element.66.natural, f32[3,3,1024]{2,1,0:T(4,128)S(1)} %copy-done, f32[5,16,8,128]{3,2,1,0:T(8,128)S(1)} %get-tuple-element.64.table.refs_7_), custom_call_target="tpu_custom_call" | custom-call | bytes 16777216 | tf_op jit(solution)/shard_map/local_response/pallas_call | solution.py:465
  37.0 1.3 %collective-permute-done.9.refs_0_ = f32[22,8,128]{2,1,0:T(8,128)S(1)} collective-permute-done((f32[22,8,128]{2,1,0:T(8,128)S(1)}, f32[22,8,128]{2,1,0:T(8,128)S(1)}, u32[]{:S(2)}, u32[]{:S(2)}) %collective-permute-start.9) | collective-permute-done | bytes 90144 | tf_op jit(solution)/shard_map/ppermute | solution.py:462
  38.3 1.3 %carried_response.1 = bf16[128,1024]{1,0:T(8,128)(2,1)} custom-call(f32[22,8,128]{2,1,0:T(8,128)S(1)} %collective-permute-done.9.refs_0_, f32[26,8,128]{2,1,0:T(8,128)S(1)} %get-tuple-element.62.local.refs_1_, f32[26,8,128]{2,1,0:T(8,128)S(1)} %collective-permute-done.8.partner.refs_2_, f32[128,1024]{1,0:T(8,128)S(1)} %get-tuple-element.67.refs_3_, ...), custom_call_target="tpu_custom_call" | custom-call | tf_op jit(solution)/shard_map/carried_response/pallas_call | solution.py:479
  (7 shorter events, 0.1 us)
Async XLA Ops:
  0.0 9.5 %collective-permute-start.1 = (bf16[128,1024]{1,0:T(8,128)(2,1)}, bf16[128,1024]{1,0:T(8,128)(2,1)S(1)}, u32[]{:S(2)}, u32[]{:S(2)}) collective-permute-start(bf16[128,1024]{1,0:T(8,128)(2,1)} %refs_0_.1), channel_id=1, source_target_pairs={{0,1},{1,3},{3,5},{5,7},{7,6},{6,4},{4,2},{2,0},{8,9},{9,11},{11,1... | collective-permute-start | bytes 786440 | tf_op jit(solution)/shard_map/ppermute | solution.py:397
  3.0 8.3 %collective-permute-start = (bf16[128,1024]{1,0:T(8,128)(2,1)}, bf16[128,1024]{1,0:T(8,128)(2,1)S(1)}, u32[]{:S(2)}, u32[]{:S(2)}) collective-permute-start(bf16[128,1024]{1,0:T(8,128)(2,1)} %refs_0_.1), channel_id=1, source_target_pairs={{1,0},{3,1},{5,3},{7,5},{6,7},{4,6},{2,4},{0,2},{9,8},{11,9},{13,1... | collective-permute-start | bytes 786440 | tf_op jit(solution)/shard_map/ppermute | solution.py:398
  3.0 8.5 %copy-start = (f32[3,3,1024]{2,1,0:T(4,128)S(1)}, f32[3,3,1024]{2,1,0:T(4,128)}, u32[]{:S(2)}) copy-start(f32[3,3,1024]{2,1,0:T(4,128)} %taps.3) | copy-start | bytes 110596
  3.0 8.5 %copy-start.1 = (bf16[128,1024]{1,0:T(8,128)(2,1)S(1)}, bf16[128,1024]{1,0:T(8,128)(2,1)}, u32[]{:S(2)}) copy-start(bf16[128,1024]{1,0:T(8,128)(2,1)} %refs_0_.1) | copy-start | bytes 786436
  3.0 8.5 %copy-start.2 = (f32[16,1024]{1,0:T(8,128)S(1)}, f32[16,1024]{1,0:T(8,128)}, u32[]{:S(2)}) copy-start(f32[16,1024]{1,0:T(8,128)} %refs_6_.1) | copy-start | bytes 196612
  3.0 8.5 %copy-start.3 = (f32[16,1024]{1,0:T(8,128)S(1)}, f32[16,1024]{1,0:T(8,128)}, u32[]{:S(2)}) copy-start(f32[16,1024]{1,0:T(8,128)} %refs_7_.1) | copy-start | bytes 196612
  9.5 7.6 %collective-permute-start.3 = (bf16[128,1024]{1,0:T(8,128)(2,1)S(1)}, bf16[128,1024]{1,0:T(8,128)(2,1)S(1)}, u32[]{:S(2)}, u32[]{:S(2)}) collective-permute-start(bf16[128,1024]{1,0:T(8,128)(2,1)S(1)} %collective-permute-done.1.refs_1_), channel_id=1, source_target_pairs={{0,1},{1,3},{3,5},{5,7},{7,6},{6,4},{4,2},{2,0},{8,9},{9,11},{11,1... | collective-permute-start | bytes 786440 | tf_op jit(solution)/shard_map/ppermute | solution.py:397
  11.3 7.5 %collective-permute-start.2 = (bf16[128,1024]{1,0:T(8,128)(2,1)S(1)}, bf16[128,1024]{1,0:T(8,128)(2,1)S(1)}, u32[]{:S(2)}, u32[]{:S(2)}) collective-permute-start(bf16[128,1024]{1,0:T(8,128)(2,1)S(1)} %collective-permute-done.refs_2_), channel_id=1, source_target_pairs={{1,0},{3,1},{5,3},{7,5},{6,7},{4,6},{2,4},{0,2},{9,8},{11,9},{13,1... | collective-permute-start | bytes 786440 | tf_op jit(solution)/shard_map/ppermute | solution.py:398
  17.1 6.7 %collective-permute-start.5 = (bf16[128,1024]{1,0:T(8,128)(2,1)S(1)}, bf16[128,1024]{1,0:T(8,128)(2,1)S(1)}, u32[]{:S(2)}, u32[]{:S(2)}) collective-permute-start(bf16[128,1024]{1,0:T(8,128)(2,1)S(1)} %collective-permute-done.3.refs_0_), channel_id=1, source_target_pairs={{0,1},{1,3},{3,5},{5,7},{7,6},{6,4},{4,2},{2,0},{8,9},{9,11},{11,1... | collective-permute-start | bytes 786440 | tf_op jit(solution)/shard_map/ppermute | solution.py:397
  18.8 6.7 %collective-permute-start.4 = (bf16[128,1024]{1,0:T(8,128)(2,1)S(1)}, bf16[128,1024]{1,0:T(8,128)(2,1)S(1)}, u32[]{:S(2)}, u32[]{:S(2)}) collective-permute-start(bf16[128,1024]{1,0:T(8,128)(2,1)S(1)} %collective-permute-done.2.refs_1_), channel_id=1, source_target_pairs={{1,0},{3,1},{5,3},{7,5},{6,7},{4,6},{2,4},{0,2},{9,8},{11,9},{13,1... | collective-permute-start | bytes 786440 | tf_op jit(solution)/shard_map/ppermute | solution.py:398
  23.8 5.8 %collective-permute-start.7 = (bf16[128,512]{1,0:T(8,128)(2,1)S(1)}, bf16[128,512]{1,0:T(8,128)(2,1)S(1)}, u32[]{:S(2)}, u32[]{:S(2)}) collective-permute-start(bf16[128,512]{1,0:T(8,128)(2,1)S(1)} %slice.7), channel_id=1, source_target_pairs={{0,1},{1,3},{3,5},{5,7},{7,6},{6,4},{4,2},{2,0},{8,9},{9,11},{11,1... | collective-permute-start | bytes 393224 | tf_op jit(solution)/shard_map/ppermute | solution.py:428
  25.5 5.0 %collective-permute-start.6 = (bf16[128,512]{1,0:T(8,128)(2,1)S(1)}, bf16[128,512]{1,0:T(8,128)(2,1)S(1)}, u32[]{:S(2)}, u32[]{:S(2)}) collective-permute-start(bf16[128,512]{1,0:T(8,128)(2,1)S(1)} %slice.6), channel_id=1, source_target_pairs={{1,0},{3,1},{5,3},{7,5},{6,7},{4,6},{2,4},{0,2},{9,8},{11,9},{13,1... | collective-permute-start | bytes 393224 | tf_op jit(solution)/shard_map/ppermute | solution.py:429
  32.1 1.4 %collective-permute-start.8 = (f32[26,8,128]{2,1,0:T(8,128)S(1)}, f32[26,8,128]{2,1,0:T(8,128)S(1)}, u32[]{:S(2)}, u32[]{:S(2)}) collective-permute-start(f32[26,8,128]{2,1,0:T(8,128)S(1)} %get-tuple-element.62.local.refs_1_), channel_id=1, source_target_pairs={{0,8},{8,0},{16,24},{24,16},{1,9},{9,1},{17,25},{25,17},{2,10},{10... | collective-permute-start | bytes 319496 | tf_op jit(solution)/shard_map/ppermute | solution.py:451
  33.6 4.7 %collective-permute-start.9 = (f32[22,8,128]{2,1,0:T(8,128)S(1)}, f32[22,8,128]{2,1,0:T(8,128)S(1)}, u32[]{:S(2)}, u32[]{:S(2)}) collective-permute-start(f32[22,8,128]{2,1,0:T(8,128)S(1)} %chip_state.1), channel_id=1, source_target_pairs={{0,16},{8,24},{16,0},{24,8},{1,17},{9,25},{17,1},{25,9},{2,18},{10... | collective-permute-start | bytes 270344 | tf_op jit(solution)/shard_map/ppermute | solution.py:462

commit v17 on v15

--- a/solution.py
+++ b/solution.py
@@ -10,7 +10,7 @@
 LANES = 128
 COLS = 256
 WIDE = 512
-SOON = 4
+SOON = 8
 GRID_ROWS = 4
 EDGE = 10
 UNROLL = 16
@@ -87,7 +87,7 @@
         lambda i, b, s, low, high: rest.at[i, pl.ds(0, high - low), :], rest_sem,
     )
     ahead = piece_loads(order, steps, pieces, w_ref, held_part(next_held), sem)
-    soon = max(SOON - len(late), 0)
+    soon = max(SOON - 2 * len(late), 0)
     for copy in late + ahead[:soon]:
         copy.start()
     if made:
@@ -376,7 +376,8 @@
         lacking = {(b, s): low for b, s, low, _ in left(step)}
         every = [(b, s) for s in range(streams) for b in range(len(blocks(step)))]
         found = [(b, s, 0, lacking.get((b, s), width)) for b, s in every]
-        return [piece for piece in found if piece[3]]
+        cuts = [(b, s, low, low + width // 2) for b, s, _, high in found for low in (0, width // 2)[: 2 * high // width]]
+        return cuts
 
     weights = pl.pallas_call(
         functools.partial(load_kernel, order, blocks(1), pieces(1)),

time: 39.7 us -> 39.9 us (level)
  Pallas kernels: 24.8 us -> 25.2 us
  transfers between devices with their start and end apart: 10 -> 10, of which waited for: 5 -> 5; matrix products, arithmetic and copies ran while one was open for 0% -> 0% of each run, Pallas kernels for 55% -> 56%
where the time goes in v17:
time: 39.9 us; the launch traced here: 39.8 us
  Pallas kernels  25.2 us (63%)
  starting transfers between devices  10.9 us (27%)
  waiting for transfers between devices  3.47 us (9%)
    pallas_call x3, Pallas kernels, on_device(): pl.pallas_call(functools.partial(middle_kernel, order, blocks(step), left...  13.5 us
    ppermute x3, starting transfers between devices, on_device(): fore = lax.ppermute(fore, 'tp', ahead)  6.48 us
    pallas_call x1, Pallas kernels, on_device(): pl.pallas_call(functools.partial(load_kernel, order, blocks(1), pieces(1)...  6.29 us
    pallas_call x1, Pallas kernels, on_device(): pl.pallas_call(local_kernel, out_shape=[f32(rows, chans), f32(rows, chans...  1.88 us
    ppermute x1, starting transfers between devices, on_device(): fore = lax.ppermute(fore[:, :width // 2], 'tp', ahead)  1.67 us
    ppermute x1, starting transfers between devices, on_device(): lax.ppermute(chip, 'ctx', [(j, (j + d) % ctx) for j in range(ctx)])  1.65 us
    pallas_call x1, Pallas kernels, on_device(): pl.pallas_call(last_kernel, out_shape=[sums, f32(rows, chans), f32(modes...  1.53 us
    pallas_call x1, Pallas kernels, on_device(): pl.pallas_call(functools.partial(final_kernel, lone, len(sent)), out_shap...  1.33 us
  transfers between devices with their start and end apart: 10, of which 5 were waited for; matrix products, arithmetic and copies ran while one was open for 0% of the time, Pallas kernels for 56%

profile of v17, /device:TPU:0, one launch (start us, length us, event | category | flops | bytes accessed | tf_op | source)
XLA Modules:
  0.0 39.8 jit_solution(12251299663597165171)
XLA Ops:
  0.0 3.0 %collective-permute-start.1 = (bf16[128,1024]{1,0:T(8,128)(2,1)}, bf16[128,1024]{1,0:T(8,128)(2,1)S(1)}, u32[]{:S(2)}, u32[]{:S(2)}) collective-permute-start(bf16[128,1024]{1,0:T(8,128)(2,1)} %refs_0_.1), channel_id=1, source_target_pairs={{0,1},{1,3},{3,5},{5,7},{7,6},{6,4},{4,2},{2,0},{8,9},{9,11},{11,1... | collective-permute-start | bytes 786440 | tf_op jit(solution)/shard_map/ppermute | solution.py:394
  3.0 0.1 collective-permute-start
  3.0 6.3 %load_first.1.refs_3_ = bf16[3,3,1024,1024]{3,2,1,0:T(8,128)(2,1)S(1)} custom-call(bf16[3,8192,1024]{2,1,0:T(8,128)(2,1)} %bitcast.1), custom_call_target="tpu_custom_call" | custom-call | bytes 16777216 | tf_op jit(solution)/shard_map/load_first/pallas_call | solution.py:382
  9.3 0.2 collective-permute-done.1.refs_1_
  9.5 1.8 %collective-permute-start.3 = (bf16[128,1024]{1,0:T(8,128)(2,1)S(1)}, bf16[128,1024]{1,0:T(8,128)(2,1)S(1)}, u32[]{:S(2)}, u32[]{:S(2)}) collective-permute-start(bf16[128,1024]{1,0:T(8,128)(2,1)S(1)} %collective-permute-done.1.refs_1_), channel_id=1, source_target_pairs={{0,1},{1,3},{3,5},{5,7},{7,6},{6,4},{4,2},{2,0},{8,9},{9,11},{11,1... | collective-permute-start | bytes 786440 | tf_op jit(solution)/shard_map/ppermute | solution.py:394
  11.4 0.0 collective-permute-done.refs_2_
  11.4 0.2 collective-permute-start.2
  11.6 0.0 copy-done
  11.6 0.0 copy-done.1
  11.6 0.0 copy-done.2
  11.6 0.0 copy-done.3
  11.6 4.9 %project_blocks.3 = (f32[3,128,1024]{2,1,0:T(8,128)S(1)}, bf16[2,3,1024,1024]{3,2,1,0:T(8,128)(2,1)S(1)}, f32[3,3,8,128]{3,2,1,0:T(8,128)S(1)}, f32[5,16,8,128]{...) custom-call(bf16[128,1024]{1,0:T(8,128)(2,1)S(1)} %copy-done.1, ...), custom_call_target="tpu_custom_call" | custom-call | bytes 16777216 | tf_op jit(solution)/shard_map/project_blocks/pallas_call | solution.py:405
  16.5 0.7 %collective-permute-done.3.refs_0_ = bf16[128,1024]{1,0:T(8,128)(2,1)S(1)} collective-permute-done((bf16[128,1024]{1,0:T(8,128)(2,1)S(1)}, bf16[128,1024]{1,0:T(8,128)(2,1)S(1)}, u32[]{:S(2)}, u32[]{:S(2)}) %collective-permute-start.3) | collective-permute-done | bytes 262176 | tf_op jit(solution)/shard_map/ppermute | solution.py:394
  17.2 1.7 %collective-permute-start.5 = (bf16[128,1024]{1,0:T(8,128)(2,1)S(1)}, bf16[128,1024]{1,0:T(8,128)(2,1)S(1)}, u32[]{:S(2)}, u32[]{:S(2)}) collective-permute-start(bf16[128,1024]{1,0:T(8,128)(2,1)S(1)} %collective-permute-done.3.refs_0_), channel_id=1, source_target_pairs={{0,1},{1,3},{3,5},{5,7},{7,6},{6,4},{4,2},{2,0},{8,9},{9,11},{11,1... | collective-permute-start | bytes 786440 | tf_op jit(solution)/shard_map/ppermute | solution.py:394
  18.9 0.0 collective-permute-done.2.refs_1_
  18.9 0.3 collective-permute-start.4
  19.2 4.6 %project_blocks.4 = (f32[3,128,1024]{2,1,0:T(8,128)S(1)}, bf16[2,3,1024,1024]{3,2,1,0:T(8,128)(2,1)S(1)}) custom-call(bf16[128,1024]{1,0:T(8,128)(2,1)S(1)} %collective-permute-done.3.refs_0_, bf16[128,1024]{1,0:T(8,128)(2,1)S(1)} %collective-permute-done.2.refs_1_, ...), custom_call_target="tpu_custom_call", output_to_operand_aliasing={{0}: (4, {})} | custom-call | bytes 16777216 | tf_op jit(solution)/shard_map/project_blocks/pallas_call | solution.py:405
  23.8 0.1 collective-permute-done.5.refs_0_
  23.9 1.7 %collective-permute-start.7 = (bf16[128,512]{1,0:T(8,128)(2,1)S(1)}, bf16[128,512]{1,0:T(8,128)(2,1)S(1)}, u32[]{:S(2)}, u32[]{:S(2)}) collective-permute-start(bf16[128,512]{1,0:T(8,128)(2,1)S(1)} %slice.7), channel_id=1, source_target_pairs={{0,1},{1,3},{3,5},{5,7},{7,6},{6,4},{4,2},{2,0},{8,9},{9,11},{11,1... | collective-permute-start | bytes 393224 | tf_op jit(solution)/shard_map/ppermute | solution.py:425
  25.6 0.0 collective-permute-done.4.refs_1_
  25.6 0.5 %collective-permute-start.6 = (bf16[128,512]{1,0:T(8,128)(2,1)S(1)}, bf16[128,512]{1,0:T(8,128)(2,1)S(1)}, u32[]{:S(2)}, u32[]{:S(2)}) collective-permute-start(bf16[128,512]{1,0:T(8,128)(2,1)S(1)} %slice.6), channel_id=1, source_target_pairs={{1,0},{3,1},{5,3},{7,5},{6,7},{4,6},{2,4},{0,2},{9,8},{11,9},{13,1... | collective-permute-start | bytes 393224 | tf_op jit(solution)/shard_map/ppermute | solution.py:426
  26.0 4.0 %project_blocks.5 = (f32[3,128,1024]{2,1,0:T(8,128)S(1)}, bf16[1,3,1024,1024]{3,2,1,0:T(8,128)(2,1)S(1)}) custom-call(bf16[128,1024]{1,0:T(8,128)(2,1)S(1)} %collective-permute-done.5.refs_0_, bf16[128,1024]{1,0:T(8,128)(2,1)S(1)} %collective-permute-done.4.refs_1_, ...), custom_call_target="tpu_custom_call", output_to_operand_aliasing={{0}: (4, {})} | custom-call | bytes 16777216 | tf_op jit(solution)/shard_map/project_blocks/pallas_call | solution.py:405
  30.1 0.0 collective-permute-done.7.x_ref
  30.1 0.6 %project_half.1._ = f32[3,128,1024]{2,1,0:T(8,128)S(1)} custom-call(bf16[128,512]{1,0:T(8,128)(2,1)S(1)} %collective-permute-done.7.x_ref, bf16[1,3,1024,1024]{3,2,1,0:T(8,128)(2,1)S(1)} %get-tuple-element.58.held, f32[3,128,1024]{2,1,0:T(8,128)S(1)} %get-tuple-element.61._), custom_call_target="tpu_custom_call", output_to_operand_aliasing={{}: (2, {})} | custom-call | bytes 16777216 | tf_op jit(solution)/shard_map/project_half/pallas_call | solution.py:427
  30.7 0.0 collective-permute-done.6.x_ref
  30.7 1.5 %project_last.1 = (f32[3,128,1024]{2,1,0:T(8,128)S(1)}, f32[128,1024]{1,0:T(8,128)S(1)}, f32[26,8,128]{2,1,0:T(8,128)S(1)}) custom-call(bf16[128,512]{1,0:T(8,128)(2,1)S(1)} %collective-permute-done.6.x_ref, bf16[1,3,1024,1024]{3,2,1,0:T(8,128)(2,1)S(1)} %get-tuple-element.58.held, f32[3,3,1024]{2,1,0:T(4,128)S(1)} %copy-done, ...), custom_call_target="tpu_custom_call", output_to_operand_aliasing={{0}: (5, {})} | custom-call | bytes 16777216 | tf_op jit(solution)/shard_map/project_last/pallas_call | solution.py:437
  32.3 0.1 collective-permute-start.8
  32.3 1.3 %collective-permute-done.8.partner.refs_2_ = f32[26,8,128]{2,1,0:T(8,128)S(1)} collective-permute-done((f32[26,8,128]{2,1,0:T(8,128)S(1)}, f32[26,8,128]{2,1,0:T(8,128)S(1)}, u32[]{:S(2)}, u32[]{:S(2)}) %collective-permute-start.8) | collective-permute-done | bytes 106528 | tf_op jit(solution)/shard_map/ppermute | solution.py:448
  33.7 1.6 %collective-permute-start.9 = (f32[22,8,128]{2,1,0:T(8,128)S(1)}, f32[22,8,128]{2,1,0:T(8,128)S(1)}, u32[]{:S(2)}, u32[]{:S(2)}) collective-permute-start(f32[22,8,128]{2,1,0:T(8,128)S(1)} %chip_state.1), channel_id=1, source_target_pairs={{0,16},{8,24},{16,0},{24,8},{1,17},{9,25},{17,1},{25,9},{2,18},{10... | collective-permute-start | bytes 270344 | tf_op jit(solution)/shard_map/ppermute | solution.py:459
  35.3 1.9 %local_response.1 = (f32[128,1024]{1,0:T(8,128)S(1)}, f32[128,1024]{1,0:T(8,128)S(1)}, f32[2,8,128]{2,1,0:T(8,128)S(1)}) custom-call(f32[3,128,1024]{2,1,0:T(8,128)S(1)} %get-tuple-element.65.total, f32[128,1024]{1,0:T(8,128)S(1)} %get-tuple-element.66.natural, f32[3,3,1024]{2,1,0:T(4,128)S(1)} %copy-done, f32[5,16,8,128]{3,2,1,0:T(8,128)S(1)} %get-tuple-element.64.table.refs_7_), custom_call_target="tpu_custom_call" | custom-call | bytes 16777216 | tf_op jit(solution)/shard_map/local_response/pallas_call | solution.py:462
  37.2 1.2 %collective-permute-done.9.refs_0_ = f32[22,8,128]{2,1,0:T(8,128)S(1)} collective-permute-done((f32[22,8,128]{2,1,0:T(8,128)S(1)}, f32[22,8,128]{2,1,0:T(8,128)S(1)}, u32[]{:S(2)}, u32[]{:S(2)}) %collective-permute-start.9) | collective-permute-done | bytes 90144 | tf_op jit(solution)/shard_map/ppermute | solution.py:459
  38.4 1.3 %carried_response.1 = bf16[128,1024]{1,0:T(8,128)(2,1)} custom-call(f32[22,8,128]{2,1,0:T(8,128)S(1)} %collective-permute-done.9.refs_0_, f32[26,8,128]{2,1,0:T(8,128)S(1)} %get-tuple-element.62.local.refs_1_, f32[26,8,128]{2,1,0:T(8,128)S(1)} %collective-permute-done.8.partner.refs_2_, f32[128,1024]{1,0:T(8,128)S(1)} %get-tuple-element.67.refs_3_, ...), custom_call_target="tpu_custom_call" | custom-call | tf_op jit(solution)/shard_map/carried_response/pallas_call | solution.py:476
  (7 shorter events, 0.1 us)
Async XLA Ops:
  0.0 9.5 %collective-permute-start.1 = (bf16[128,1024]{1,0:T(8,128)(2,1)}, bf16[128,1024]{1,0:T(8,128)(2,1)S(1)}, u32[]{:S(2)}, u32[]{:S(2)}) collective-permute-start(bf16[128,1024]{1,0:T(8,128)(2,1)} %refs_0_.1), channel_id=1, source_target_pairs={{0,1},{1,3},{3,5},{5,7},{7,6},{6,4},{4,2},{2,0},{8,9},{9,11},{11,1... | collective-permute-start | bytes 786440 | tf_op jit(solution)/shard_map/ppermute | solution.py:394
  3.0 8.4 %collective-permute-start = (bf16[128,1024]{1,0:T(8,128)(2,1)}, bf16[128,1024]{1,0:T(8,128)(2,1)S(1)}, u32[]{:S(2)}, u32[]{:S(2)}) collective-permute-start(bf16[128,1024]{1,0:T(8,128)(2,1)} %refs_0_.1), channel_id=1, source_target_pairs={{1,0},{3,1},{5,3},{7,5},{6,7},{4,6},{2,4},{0,2},{9,8},{11,9},{13,1... | collective-permute-start | bytes 786440 | tf_op jit(solution)/shard_map/ppermute | solution.py:395
  3.0 8.5 %copy-start = (f32[3,3,1024]{2,1,0:T(4,128)S(1)}, f32[3,3,1024]{2,1,0:T(4,128)}, u32[]{:S(2)}) copy-start(f32[3,3,1024]{2,1,0:T(4,128)} %taps.3) | copy-start | bytes 110596
  3.0 8.5 %copy-start.1 = (bf16[128,1024]{1,0:T(8,128)(2,1)S(1)}, bf16[128,1024]{1,0:T(8,128)(2,1)}, u32[]{:S(2)}) copy-start(bf16[128,1024]{1,0:T(8,128)(2,1)} %refs_0_.1) | copy-start | bytes 786436
  3.0 8.5 %copy-start.2 = (f32[16,1024]{1,0:T(8,128)S(1)}, f32[16,1024]{1,0:T(8,128)}, u32[]{:S(2)}) copy-start(f32[16,1024]{1,0:T(8,128)} %refs_6_.1) | copy-start | bytes 196612
  3.0 8.5 %copy-start.3 = (f32[16,1024]{1,0:T(8,128)S(1)}, f32[16,1024]{1,0:T(8,128)}, u32[]{:S(2)}) copy-start(f32[16,1024]{1,0:T(8,128)} %refs_7_.1) | copy-start | bytes 196612
  9.5 7.6 %collective-permute-start.3 = (bf16[128,1024]{1,0:T(8,128)(2,1)S(1)}, bf16[128,1024]{1,0:T(8,128)(2,1)S(1)}, u32[]{:S(2)}, u32[]{:S(2)}) collective-permute-start(bf16[128,1024]{1,0:T(8,128)(2,1)S(1)} %collective-permute-done.1.refs_1_), channel_id=1, source_target_pairs={{0,1},{1,3},{3,5},{5,7},{7,6},{6,4},{4,2},{2,0},{8,9},{9,11},{11,1... | collective-permute-start | bytes 786440 | tf_op jit(solution)/shard_map/ppermute | solution.py:394
  11.4 7.5 %collective-permute-start.2 = (bf16[128,1024]{1,0:T(8,128)(2,1)S(1)}, bf16[128,1024]{1,0:T(8,128)(2,1)S(1)}, u32[]{:S(2)}, u32[]{:S(2)}) collective-permute-start(bf16[128,1024]{1,0:T(8,128)(2,1)S(1)} %collective-permute-done.refs_2_), channel_id=1, source_target_pairs={{1,0},{3,1},{5,3},{7,5},{6,7},{4,6},{2,4},{0,2},{9,8},{11,9},{13,1... | collective-permute-start | bytes 786440 | tf_op jit(solution)/shard_map/ppermute | solution.py:395
  17.2 6.7 %collective-permute-start.5 = (bf16[128,1024]{1,0:T(8,128)(2,1)S(1)}, bf16[128,1024]{1,0:T(8,128)(2,1)S(1)}, u32[]{:S(2)}, u32[]{:S(2)}) collective-permute-start(bf16[128,1024]{1,0:T(8,128)(2,1)S(1)} %collective-permute-done.3.refs_0_), channel_id=1, source_target_pairs={{0,1},{1,3},{3,5},{5,7},{7,6},{6,4},{4,2},{2,0},{8,9},{9,11},{11,1... | collective-permute-start | bytes 786440 | tf_op jit(solution)/shard_map/ppermute | solution.py:394
  18.9 6.7 %collective-permute-start.4 = (bf16[128,1024]{1,0:T(8,128)(2,1)S(1)}, bf16[128,1024]{1,0:T(8,128)(2,1)S(1)}, u32[]{:S(2)}, u32[]{:S(2)}) collective-permute-start(bf16[128,1024]{1,0:T(8,128)(2,1)S(1)} %collective-permute-done.2.refs_1_), channel_id=1, source_target_pairs={{1,0},{3,1},{5,3},{7,5},{6,7},{4,6},{2,4},{0,2},{9,8},{11,9},{13,1... | collective-permute-start | bytes 786440 | tf_op jit(solution)/shard_map/ppermute | solution.py:395
  23.9 6.2 %collective-permute-start.7 = (bf16[128,512]{1,0:T(8,128)(2,1)S(1)}, bf16[128,512]{1,0:T(8,128)(2,1)S(1)}, u32[]{:S(2)}, u32[]{:S(2)}) collective-permute-start(bf16[128,512]{1,0:T(8,128)(2,1)S(1)} %slice.7), channel_id=1, source_target_pairs={{0,1},{1,3},{3,5},{5,7},{7,6},{6,4},{4,2},{2,0},{8,9},{9,11},{11,1... | collective-permute-start | bytes 393224 | tf_op jit(solution)/shard_map/ppermute | solution.py:425
  25.6 5.1 %collective-permute-start.6 = (bf16[128,512]{1,0:T(8,128)(2,1)S(1)}, bf16[128,512]{1,0:T(8,128)(2,1)S(1)}, u32[]{:S(2)}, u32[]{:S(2)}) collective-permute-start(bf16[128,512]{1,0:T(8,128)(2,1)S(1)} %slice.6), channel_id=1, source_target_pairs={{1,0},{3,1},{5,3},{7,5},{6,7},{4,6},{2,4},{0,2},{9,8},{11,9},{13,1... | collective-permute-start | bytes 393224 | tf_op jit(solution)/shard_map/ppermute | solution.py:426
  32.3 1.4 %collective-permute-start.8 = (f32[26,8,128]{2,1,0:T(8,128)S(1)}, f32[26,8,128]{2,1,0:T(8,128)S(1)}, u32[]{:S(2)}, u32[]{:S(2)}) collective-permute-start(f32[26,8,128]{2,1,0:T(8,128)S(1)} %get-tuple-element.62.local.refs_1_), channel_id=1, source_target_pairs={{0,8},{8,0},{16,24},{24,16},{1,9},{9,1},{17,25},{25,17},{2,10},{10... | collective-permute-start | bytes 319496 | tf_op jit(solution)/shard_map/ppermute | solution.py:448
  33.7 4.7 %collective-permute-start.9 = (f32[22,8,128]{2,1,0:T(8,128)S(1)}, f32[22,8,128]{2,1,0:T(8,128)S(1)}, u32[]{:S(2)}, u32[]{:S(2)}) collective-permute-start(f32[22,8,128]{2,1,0:T(8,128)S(1)} %chip_state.1), channel_id=1, source_target_pairs={{0,16},{8,24},{16,0},{24,8},{1,17},{9,25},{17,1},{25,9},{2,18},{10... | collective-permute-start | bytes 270344 | tf_op jit(solution)/shard_map/ppermute | solution.py:459

commit v18 on v15

--- a/solution.py
+++ b/solution.py
@@ -156,7 +156,7 @@
 
 
 def last_kernel(x_ref, held, taps, tile_step, fade, _, total, source, out_ref):
-    depth = x_ref.shape[1]
+    depth = held.shape[2] - x_ref.shape[1]
     for s in range(total.shape[0]):
         add_products([x_ref[...]], lambda b, at: held[0, s, depth:, at], total, s, cols=WIDE)
     rows = source.shape[0]
@@ -421,8 +421,9 @@
         )(*xs, weights, weight, *extra)
         if first:
             taps, table, tile, tile_step, fade = made
-    fore = lax.ppermute(fore[:, : width // 2], "tp", ahead)
-    aft = lax.ppermute(aft[:, width // 2 :], "tp", back)
+    cut = width // 2 if width % (4 * LANES) else width * 3 // 4
+    fore = lax.ppermute(fore[:, :cut], "tp", ahead)
+    aft = lax.ppermute(aft[:, cut:], "tp", back)
     total = pl.pallas_call(
         half_kernel,
         out_shape=sums,

time: 39.7 us -> 39.4 us (level)
  waiting for transfers between devices: 3.82 us -> 3.32 us
  transfers between devices with their start and end apart: 10 -> 10, of which waited for: 5 -> 4; matrix products, arithmetic and copies ran while one was open for 0% -> 0% of each run, Pallas kernels for 55% -> 56%
where the time goes in v18:
time: 39.4 us; the launch traced here: 39.3 us
  Pallas kernels  24.8 us (63%)
  starting transfers between devices  11 us (28%)
  waiting for transfers between devices  3.32 us (8%)
    pallas_call x3, Pallas kernels, on_device(): pl.pallas_call(functools.partial(middle_kernel, order, blocks(step), left...  13.2 us
    ppermute x3, starting transfers between devices, on_device(): fore = lax.ppermute(fore, 'tp', ahead)  6.41 us
    pallas_call x1, Pallas kernels, on_device(): pl.pallas_call(functools.partial(load_kernel, order, blocks(1), pieces(1)...  6.22 us
    pallas_call x1, Pallas kernels, on_device(): pl.pallas_call(local_kernel, out_shape=[f32(rows, chans), f32(rows, chans...  1.88 us
    ppermute x1, starting transfers between devices, on_device(): fore = lax.ppermute(fore[:, :cut], 'tp', ahead)  1.74 us
    ppermute x1, starting transfers between devices, on_device(): lax.ppermute(chip, 'ctx', [(j, (j + d) % ctx) for j in range(ctx)])  1.72 us
    pallas_call x1, Pallas kernels, on_device(): pl.pallas_call(last_kernel, out_shape=[sums, f32(rows, chans), f32(modes...  1.36 us
    pallas_call x1, Pallas kernels, on_device(): pl.pallas_call(functools.partial(final_kernel, lone, len(sent)), out_shap...  1.32 us
  transfers between devices with their start and end apart: 10, of which 4 were waited for; matrix products, arithmetic and copies ran while one was open for 0% of the time, Pallas kernels for 56%

profile of v18, /device:TPU:0, one launch (start us, length us, event | category | flops | bytes accessed | tf_op | source)
XLA Modules:
  0.0 39.3 jit_solution(13577148841412174082)
XLA Ops:
  0.0 3.0 %collective-permute-start.1 = (bf16[128,1024]{1,0:T(8,128)(2,1)}, bf16[128,1024]{1,0:T(8,128)(2,1)S(1)}, u32[]{:S(2)}, u32[]{:S(2)}) collective-permute-start(bf16[128,1024]{1,0:T(8,128)(2,1)} %refs_0_.1), channel_id=1, source_target_pairs={{0,1},{1,3},{3,5},{5,7},{7,6},{6,4},{4,2},{2,0},{8,9},{9,11},{11,1... | collective-permute-start | bytes 786440 | tf_op jit(solution)/shard_map/ppermute | solution.py:393
  3.0 0.1 collective-permute-start
  3.0 6.2 %load_first.1.refs_3_ = bf16[3,3,1024,1024]{3,2,1,0:T(8,128)(2,1)S(1)} custom-call(bf16[3,8192,1024]{2,1,0:T(8,128)(2,1)} %bitcast.1), custom_call_target="tpu_custom_call" | custom-call | bytes 16777216 | tf_op jit(solution)/shard_map/load_first/pallas_call | solution.py:381
  9.3 0.3 collective-permute-done.1.refs_1_
  9.5 1.8 %collective-permute-start.3 = (bf16[128,1024]{1,0:T(8,128)(2,1)S(1)}, bf16[128,1024]{1,0:T(8,128)(2,1)S(1)}, u32[]{:S(2)}, u32[]{:S(2)}) collective-permute-start(bf16[128,1024]{1,0:T(8,128)(2,1)S(1)} %collective-permute-done.1.refs_1_), channel_id=1, source_target_pairs={{0,1},{1,3},{3,5},{5,7},{7,6},{6,4},{4,2},{2,0},{8,9},{9,11},{11,1... | collective-permute-start | bytes 786440 | tf_op jit(solution)/shard_map/ppermute | solution.py:393
  11.3 0.0 collective-permute-done.refs_2_
  11.3 0.3 collective-permute-start.2
  11.6 0.0 copy-done
  11.6 0.0 copy-done.1
  11.6 0.0 copy-done.2
  11.6 0.0 copy-done.3
  11.6 4.9 %project_blocks.3 = (f32[3,128,1024]{2,1,0:T(8,128)S(1)}, bf16[2,3,1024,1024]{3,2,1,0:T(8,128)(2,1)S(1)}, f32[3,3,8,128]{3,2,1,0:T(8,128)S(1)}, f32[5,16,8,128]{...) custom-call(bf16[128,1024]{1,0:T(8,128)(2,1)S(1)} %copy-done.1, ...), custom_call_target="tpu_custom_call" | custom-call | bytes 16777216 | tf_op jit(solution)/shard_map/project_blocks/pallas_call | solution.py:404
  16.5 0.6 %collective-permute-done.3.refs_0_ = bf16[128,1024]{1,0:T(8,128)(2,1)S(1)} collective-permute-done((bf16[128,1024]{1,0:T(8,128)(2,1)S(1)}, bf16[128,1024]{1,0:T(8,128)(2,1)S(1)}, u32[]{:S(2)}, u32[]{:S(2)}) %collective-permute-start.3) | collective-permute-done | bytes 262176 | tf_op jit(solution)/shard_map/ppermute | solution.py:393
  17.1 1.7 %collective-permute-start.5 = (bf16[128,1024]{1,0:T(8,128)(2,1)S(1)}, bf16[128,1024]{1,0:T(8,128)(2,1)S(1)}, u32[]{:S(2)}, u32[]{:S(2)}) collective-permute-start(bf16[128,1024]{1,0:T(8,128)(2,1)S(1)} %collective-permute-done.3.refs_0_), channel_id=1, source_target_pairs={{0,1},{1,3},{3,5},{5,7},{7,6},{6,4},{4,2},{2,0},{8,9},{9,11},{11,1... | collective-permute-start | bytes 786440 | tf_op jit(solution)/shard_map/ppermute | solution.py:393
  18.8 0.0 collective-permute-done.2.refs_1_
  18.8 0.3 collective-permute-start.4
  19.1 4.6 %project_blocks.4 = (f32[3,128,1024]{2,1,0:T(8,128)S(1)}, bf16[2,3,1024,1024]{3,2,1,0:T(8,128)(2,1)S(1)}) custom-call(bf16[128,1024]{1,0:T(8,128)(2,1)S(1)} %collective-permute-done.3.refs_0_, bf16[128,1024]{1,0:T(8,128)(2,1)S(1)} %collective-permute-done.2.refs_1_, ...), custom_call_target="tpu_custom_call", output_to_operand_aliasing={{0}: (4, {})} | custom-call | bytes 16777216 | tf_op jit(solution)/shard_map/project_blocks/pallas_call | solution.py:404
  23.7 0.0 collective-permute-done.5.refs_0_
  23.8 1.7 %collective-permute-start.7 = (bf16[128,768]{1,0:T(8,128)(2,1)S(1)}, bf16[128,768]{1,0:T(8,128)(2,1)S(1)}, u32[]{:S(2)}, u32[]{:S(2)}) collective-permute-start(bf16[128,768]{1,0:T(8,128)(2,1)S(1)} %slice.7), channel_id=1, source_target_pairs={{0,1},{1,3},{3,5},{5,7},{7,6},{6,4},{4,2},{2,0},{8,9},{9,11},{11,1... | collective-permute-start | bytes 589832 | tf_op jit(solution)/shard_map/ppermute | solution.py:425
  25.5 0.0 collective-permute-done.4.refs_1_
  25.5 0.4 %collective-permute-start.6 = (bf16[128,256]{1,0:T(8,128)(2,1)S(1)}, bf16[128,256]{1,0:T(8,128)(2,1)S(1)}, u32[]{:S(2)}, u32[]{:S(2)}) collective-permute-start(bf16[128,256]{1,0:T(8,128)(2,1)S(1)} %slice.6), channel_id=1, source_target_pairs={{1,0},{3,1},{5,3},{7,5},{6,7},{4,6},{2,4},{0,2},{9,8},{11,9},{13,1... | collective-permute-start | bytes 196616 | tf_op jit(solution)/shard_map/ppermute | solution.py:426
  25.9 3.7 %project_blocks.5 = (f32[3,128,1024]{2,1,0:T(8,128)S(1)}, bf16[1,3,1024,1024]{3,2,1,0:T(8,128)(2,1)S(1)}) custom-call(bf16[128,1024]{1,0:T(8,128)(2,1)S(1)} %collective-permute-done.5.refs_0_, bf16[128,1024]{1,0:T(8,128)(2,1)S(1)} %collective-permute-done.4.refs_1_, ...), custom_call_target="tpu_custom_call", output_to_operand_aliasing={{0}: (4, {})} | custom-call | bytes 16777216 | tf_op jit(solution)/shard_map/project_blocks/pallas_call | solution.py:404
  29.6 0.0 collective-permute-done.7.x_ref
  29.6 0.8 %project_half.1._ = f32[3,128,1024]{2,1,0:T(8,128)S(1)} custom-call(bf16[128,768]{1,0:T(8,128)(2,1)S(1)} %collective-permute-done.7.x_ref, bf16[1,3,1024,1024]{3,2,1,0:T(8,128)(2,1)S(1)} %get-tuple-element.58.held, f32[3,128,1024]{2,1,0:T(8,128)S(1)} %get-tuple-element.61._), custom_call_target="tpu_custom_call", output_to_operand_aliasing={{}: (2, {})} | custom-call | bytes 16777216 | tf_op jit(solution)/shard_map/project_half/pallas_call | solution.py:427
  30.4 0.0 collective-permute-done.6.x_ref
  30.4 1.4 %project_last.1 = (f32[3,128,1024]{2,1,0:T(8,128)S(1)}, f32[128,1024]{1,0:T(8,128)S(1)}, f32[26,8,128]{2,1,0:T(8,128)S(1)}) custom-call(bf16[128,256]{1,0:T(8,128)(2,1)S(1)} %collective-permute-done.6.x_ref, bf16[1,3,1024,1024]{3,2,1,0:T(8,128)(2,1)S(1)} %get-tuple-element.58.held, f32[3,3,1024]{2,1,0:T(4,128)S(1)} %copy-done, ...), custom_call_target="tpu_custom_call", output_to_operand_aliasing={{0}: (5, {})} | custom-call | bytes 16777216 | tf_op jit(solution)/shard_map/project_last/pallas_call | solution.py:437
  31.8 0.1 collective-permute-start.8
  31.9 1.3 %collective-permute-done.8.partner.refs_2_ = f32[26,8,128]{2,1,0:T(8,128)S(1)} collective-permute-done((f32[26,8,128]{2,1,0:T(8,128)S(1)}, f32[26,8,128]{2,1,0:T(8,128)S(1)}, u32[]{:S(2)}, u32[]{:S(2)}) %collective-permute-start.8) | collective-permute-done | bytes 106528 | tf_op jit(solution)/shard_map/ppermute | solution.py:448
  33.2 1.7 %collective-permute-start.9 = (f32[22,8,128]{2,1,0:T(8,128)S(1)}, f32[22,8,128]{2,1,0:T(8,128)S(1)}, u32[]{:S(2)}, u32[]{:S(2)}) collective-permute-start(f32[22,8,128]{2,1,0:T(8,128)S(1)} %chip_state.1), channel_id=1, source_target_pairs={{0,16},{8,24},{16,0},{24,8},{1,17},{9,25},{17,1},{25,9},{2,18},{10... | collective-permute-start | bytes 270344 | tf_op jit(solution)/shard_map/ppermute | solution.py:459
  35.0 1.9 %local_response.1 = (f32[128,1024]{1,0:T(8,128)S(1)}, f32[128,1024]{1,0:T(8,128)S(1)}, f32[2,8,128]{2,1,0:T(8,128)S(1)}) custom-call(f32[3,128,1024]{2,1,0:T(8,128)S(1)} %get-tuple-element.65.total, f32[128,1024]{1,0:T(8,128)S(1)} %get-tuple-element.66.natural, f32[3,3,1024]{2,1,0:T(4,128)S(1)} %copy-done, f32[5,16,8,128]{3,2,1,0:T(8,128)S(1)} %get-tuple-element.64.table.refs_7_), custom_call_target="tpu_custom_call" | custom-call | bytes 16777216 | tf_op jit(solution)/shard_map/local_response/pallas_call | solution.py:462
  36.8 1.1 %collective-permute-done.9.refs_0_ = f32[22,8,128]{2,1,0:T(8,128)S(1)} collective-permute-done((f32[22,8,128]{2,1,0:T(8,128)S(1)}, f32[22,8,128]{2,1,0:T(8,128)S(1)}, u32[]{:S(2)}, u32[]{:S(2)}) %collective-permute-start.9) | collective-permute-done | bytes 90144 | tf_op jit(solution)/shard_map/ppermute | solution.py:459
  38.0 1.3 %carried_response.1 = bf16[128,1024]{1,0:T(8,128)(2,1)} custom-call(f32[22,8,128]{2,1,0:T(8,128)S(1)} %collective-permute-done.9.refs_0_, f32[26,8,128]{2,1,0:T(8,128)S(1)} %get-tuple-element.62.local.refs_1_, f32[26,8,128]{2,1,0:T(8,128)S(1)} %collective-permute-done.8.partner.refs_2_, f32[128,1024]{1,0:T(8,128)S(1)} %get-tuple-element.67.refs_3_, ...), custom_call_target="tpu_custom_call" | custom-call | tf_op jit(solution)/shard_map/carried_response/pallas_call | solution.py:476
  (7 shorter events, 0.1 us)
Async XLA Ops:
  0.0 9.5 %collective-permute-start.1 = (bf16[128,1024]{1,0:T(8,128)(2,1)}, bf16[128,1024]{1,0:T(8,128)(2,1)S(1)}, u32[]{:S(2)}, u32[]{:S(2)}) collective-permute-start(bf16[128,1024]{1,0:T(8,128)(2,1)} %refs_0_.1), channel_id=1, source_target_pairs={{0,1},{1,3},{3,5},{5,7},{7,6},{6,4},{4,2},{2,0},{8,9},{9,11},{11,1... | collective-permute-start | bytes 786440 | tf_op jit(solution)/shard_map/ppermute | solution.py:393
  3.0 8.3 %collective-permute-start = (bf16[128,1024]{1,0:T(8,128)(2,1)}, bf16[128,1024]{1,0:T(8,128)(2,1)S(1)}, u32[]{:S(2)}, u32[]{:S(2)}) collective-permute-start(bf16[128,1024]{1,0:T(8,128)(2,1)} %refs_0_.1), channel_id=1, source_target_pairs={{1,0},{3,1},{5,3},{7,5},{6,7},{4,6},{2,4},{0,2},{9,8},{11,9},{13,1... | collective-permute-start | bytes 786440 | tf_op jit(solution)/shard_map/ppermute | solution.py:394
  3.0 8.5 %copy-start = (f32[3,3,1024]{2,1,0:T(4,128)S(1)}, f32[3,3,1024]{2,1,0:T(4,128)}, u32[]{:S(2)}) copy-start(f32[3,3,1024]{2,1,0:T(4,128)} %taps.3) | copy-start | bytes 110596
  3.0 8.5 %copy-start.1 = (bf16[128,1024]{1,0:T(8,128)(2,1)S(1)}, bf16[128,1024]{1,0:T(8,128)(2,1)}, u32[]{:S(2)}) copy-start(bf16[128,1024]{1,0:T(8,128)(2,1)} %refs_0_.1) | copy-start | bytes 786436
  3.0 8.5 %copy-start.2 = (f32[16,1024]{1,0:T(8,128)S(1)}, f32[16,1024]{1,0:T(8,128)}, u32[]{:S(2)}) copy-start(f32[16,1024]{1,0:T(8,128)} %refs_6_.1) | copy-start | bytes 196612
  3.0 8.5 %copy-start.3 = (f32[16,1024]{1,0:T(8,128)S(1)}, f32[16,1024]{1,0:T(8,128)}, u32[]{:S(2)}) copy-start(f32[16,1024]{1,0:T(8,128)} %refs_7_.1) | copy-start | bytes 196612
  9.5 7.6 %collective-permute-start.3 = (bf16[128,1024]{1,0:T(8,128)(2,1)S(1)}, bf16[128,1024]{1,0:T(8,128)(2,1)S(1)}, u32[]{:S(2)}, u32[]{:S(2)}) collective-permute-start(bf16[128,1024]{1,0:T(8,128)(2,1)S(1)} %collective-permute-done.1.refs_1_), channel_id=1, source_target_pairs={{0,1},{1,3},{3,5},{5,7},{7,6},{6,4},{4,2},{2,0},{8,9},{9,11},{11,1... | collective-permute-start | bytes 786440 | tf_op jit(solution)/shard_map/ppermute | solution.py:393
  11.3 7.5 %collective-permute-start.2 = (bf16[128,1024]{1,0:T(8,128)(2,1)S(1)}, bf16[128,1024]{1,0:T(8,128)(2,1)S(1)}, u32[]{:S(2)}, u32[]{:S(2)}) collective-permute-start(bf16[128,1024]{1,0:T(8,128)(2,1)S(1)} %collective-permute-done.refs_2_), channel_id=1, source_target_pairs={{1,0},{3,1},{5,3},{7,5},{6,7},{4,6},{2,4},{0,2},{9,8},{11,9},{13,1... | collective-permute-start | bytes 786440 | tf_op jit(solution)/shard_map/ppermute | solution.py:394
  17.1 6.7 %collective-permute-start.5 = (bf16[128,1024]{1,0:T(8,128)(2,1)S(1)}, bf16[128,1024]{1,0:T(8,128)(2,1)S(1)}, u32[]{:S(2)}, u32[]{:S(2)}) collective-permute-start(bf16[128,1024]{1,0:T(8,128)(2,1)S(1)} %collective-permute-done.3.refs_0_), channel_id=1, source_target_pairs={{0,1},{1,3},{3,5},{5,7},{7,6},{6,4},{4,2},{2,0},{8,9},{9,11},{11,1... | collective-permute-start | bytes 786440 | tf_op jit(solution)/shard_map/ppermute | solution.py:393
  18.8 6.7 %collective-permute-start.4 = (bf16[128,1024]{1,0:T(8,128)(2,1)S(1)}, bf16[128,1024]{1,0:T(8,128)(2,1)S(1)}, u32[]{:S(2)}, u32[]{:S(2)}) collective-permute-start(bf16[128,1024]{1,0:T(8,128)(2,1)S(1)} %collective-permute-done.2.refs_1_), channel_id=1, source_target_pairs={{1,0},{3,1},{5,3},{7,5},{6,7},{4,6},{2,4},{0,2},{9,8},{11,9},{13,1... | collective-permute-start | bytes 786440 | tf_op jit(solution)/shard_map/ppermute | solution.py:394
  23.8 5.8 %collective-permute-start.7 = (bf16[128,768]{1,0:T(8,128)(2,1)S(1)}, bf16[128,768]{1,0:T(8,128)(2,1)S(1)}, u32[]{:S(2)}, u32[]{:S(2)}) collective-permute-start(bf16[128,768]{1,0:T(8,128)(2,1)S(1)} %slice.7), channel_id=1, source_target_pairs={{0,1},{1,3},{3,5},{5,7},{7,6},{6,4},{4,2},{2,0},{8,9},{9,11},{11,1... | collective-permute-start | bytes 589832 | tf_op jit(solution)/shard_map/ppermute | solution.py:425
  25.5 4.9 %collective-permute-start.6 = (bf16[128,256]{1,0:T(8,128)(2,1)S(1)}, bf16[128,256]{1,0:T(8,128)(2,1)S(1)}, u32[]{:S(2)}, u32[]{:S(2)}) collective-permute-start(bf16[128,256]{1,0:T(8,128)(2,1)S(1)} %slice.6), channel_id=1, source_target_pairs={{1,0},{3,1},{5,3},{7,5},{6,7},{4,6},{2,4},{0,2},{9,8},{11,9},{13,1... | collective-permute-start | bytes 196616 | tf_op jit(solution)/shard_map/ppermute | solution.py:426
  31.8 1.4 %collective-permute-start.8 = (f32[26,8,128]{2,1,0:T(8,128)S(1)}, f32[26,8,128]{2,1,0:T(8,128)S(1)}, u32[]{:S(2)}, u32[]{:S(2)}) collective-permute-start(f32[26,8,128]{2,1,0:T(8,128)S(1)} %get-tuple-element.62.local.refs_1_), channel_id=1, source_target_pairs={{0,8},{8,0},{16,24},{24,16},{1,9},{9,1},{17,25},{25,17},{2,10},{10... | collective-permute-start | bytes 319496 | tf_op jit(solution)/shard_map/ppermute | solution.py:448
  33.2 4.7 %collective-permute-start.9 = (f32[22,8,128]{2,1,0:T(8,128)S(1)}, f32[22,8,128]{2,1,0:T(8,128)S(1)}, u32[]{:S(2)}, u32[]{:S(2)}) collective-permute-start(f32[22,8,128]{2,1,0:T(8,128)S(1)} %chip_state.1), channel_id=1, source_target_pairs={{0,16},{8,24},{16,0},{24,8},{1,17},{9,25},{17,1},{25,9},{2,18},{10... | collective-permute-start | bytes 270344 | tf_op jit(solution)/shard_map/ppermute | solution.py:459
